TPU v7x, 32 devices: a whole 2x2x4 slice. The times are simulated.
32 devices in a mesh: lon: 8 (over y, x, core), lat: 4 (over z).
Axes of the slice: x: 2, y: 2, z: 4, core: 2. Of those that a mesh axis runs over, the one named last changes fastest.
Arguments:
- concentration: float32 [72, 8, 64, 1024], P(None, None, 'lat', 'lon'), may hold values from -0.3 to 0.3
- adjoint: float32 [72, 8, 64, 1024], P(None, None, 'lat', 'lon'), may hold values from -4 to 4
- wind_east: float32 [72, 64, 1024], P(None, 'lat', 'lon'), may hold values from -0.45 to 0.45
- wind_north: float32 [72, 64, 1024], P(None, 'lat', 'lon'), may hold values from -0.45 to 0.45
- mixing: float32 [72, 64, 1024], P(None, 'lat', 'lon'), may hold values from 0.01 to 100
- sound_col: int32 [1, 32, 1024], P(None, ('lon', 'lat')), may hold values from -1 to 2047, as said below
- kernel: float32 [72, 32, 1024], P(None, ('lon', 'lat')), may hold values from 0.5 to 3
- observed: float32 [1, 32, 1024], P(None, ('lon', 'lat')), may hold values from -12 to 12
- obs_error: float32 [1, 32, 1024], P(None, ('lon', 'lat')), may hold values from 1 to 3
Outputs:
- adjoint_out: float32 [72, 8, 64, 1024], P(None, None, 'lat', 'lon')
- residual: float32 [1, 32, 1024], P(None, ('lon', 'lat'))
Inputs may be any that keep to these rules, and one draw needn't show every extreme that they name: `sound_col`: each entry is a column index inside the brick of its slot (slots b * 32 to b * 32 + 31 of an owner belong to brick b in lon-major order), or -1 for an empty slot; for each owner and brick the used slots come first. In every draw some brick receives 32 soundings from every owner.
All inputs are finite; a program needn't handle non-finite values.
Results may differ from a plain program's by a relative error of at most 0.00022.
Values sent between devices are 32-bit elements; how exact they have to be, the bound alone decides.
No kernel may reach another device: no remote copies, remote signals or barrier semaphores. Data moves between devices by JAX's collectives and lax.ppermute only.
A program may use at most 192 MiB of HBM per device.

v0:
```python
import functools

import jax
import jax.numpy as jnp
from jax import lax
from jax.experimental import pallas as pl
from jax.experimental.pallas import tpu as pltpu
from jax.sharding import PartitionSpec as P

LANES = 128
SUB = 8
MIB = 1 << 20
ANY = pl.BlockSpec(memory_space=pl.ANY)
VMEM = pl.BlockSpec(memory_space=pltpu.VMEM)


def rim_chunks(levels):
    chunks = -(-levels // 63)
    return chunks, -(-levels // chunks)


def lane_iota():
    return lax.broadcasted_iota(jnp.int32, (SUB, LANES), 1)


def sub_iota():
    return lax.broadcasted_iota(jnp.int32, (SUB, LANES), 0)


def largest(count, *choices):
    return next(u for u in choices if count % u == 0)


def f32(*shape):
    return jax.ShapeDtypeStruct(shape, jnp.float32)


def vmem(*shape):
    return pltpu.VMEM(shape, jnp.float32)


def call(body, ins, outs, out_specs, scratch, mib, flops, size, name):
    return pl.pallas_call(
        body,
        in_specs=ins,
        out_specs=out_specs,
        out_shape=outs,
        scratch_shapes=scratch,
        compiler_params=pltpu.CompilerParams(vmem_limit_bytes=mib * MIB),
        cost_estimate=pl.CostEstimate(flops=flops, bytes_accessed=size, transcendentals=0),
        name=name,
    )


def put_rims(field, offset, levels, per_chunk, chunks, out, first, plane):
    lane = lane_iota()
    group = largest(plane // SUB, 4, 2, 1)
    for chunk in range(chunks):
        count = min(per_chunk, levels - chunk * per_chunk)

        def body(i, carry, chunk=chunk, count=count):
            r = pl.multiple_of(i * SUB * group, SUB * group)
            made = [jnp.zeros((SUB, LANES), jnp.float32)] * group
            for q in range(count):
                for g in range(group):
                    at = pl.multiple_of((chunk * per_chunk + q) * plane + offset + r + g * SUB, SUB)
                    turned = pltpu.roll(field[pl.ds(at, SUB), :], 2 * q + 2, 1)
                    made[g] = jnp.where(lane >= 2 * q + 1, turned, made[g])
            for g in range(group):
                out[chunk, pl.ds(pl.multiple_of(first + r + g * SUB, SUB), SUB), :] = made[g]
            return carry

        lax.fori_loop(0, plane // SUB // group, body, 0)


def put_rows(field, offset, north, south, rows, count):
    unroll = largest(count // SUB, 9, 8, 4, 2, 1)

    def body(i, carry):
        for u in range(unroll):
            start = pl.multiple_of((i * unroll + u) * SUB, SUB)
            at = start * rows + offset
            if south is not None:
                south[pl.ds(start, SUB), :] = field[pl.ds(at, SUB, stride=rows), :]
            north[pl.ds(start, SUB), :] = field[pl.ds(at + rows - 1, SUB, stride=rows), :]
        return carry

    lax.fori_loop(0, count // SUB // unroll, body, 0)


def first_rims(levels, tracers, rows, chunks, per_chunk, field, east, north, side, s_ref, n_ref, f, e, n, sems):
    plane = tracers * rows
    half = chunks * 2
    size = levels * plane // half
    wind_copies = [
        pltpu.make_async_copy(east, e, sems.at[half]),
        pltpu.make_async_copy(north, n, sems.at[half + 1]),
    ]
    copies = [
        pltpu.make_async_copy(field.at[pl.ds(i * size, size)], f.at[pl.ds(i * size, size)], sems.at[i])
        for i in range(half)
    ]
    for copy in wind_copies + copies:
        copy.start()
    wind_copies[0].wait()
    put_rims(e, 0, levels, per_chunk, chunks, side, plane, rows)
    wind_copies[1].wait()
    put_rows(n, 0, n_ref.at[pl.ds(levels * tracers, levels)], None, rows, levels)
    for copy in copies:
        copy.wait()
    put_rims(f, 0, levels, per_chunk, chunks, side, 0, plane)
    put_rows(f, 0, n_ref.at[pl.ds(0, levels * tracers)], s_ref, rows, levels * tracers)


def step(levels, tracers, rows, chunks, per_chunk, unroll, first, *refs):
    refs = list(refs)
    field, east, north, mixing, west0, south0 = refs[:6]
    west_in, east_in, north_in, south_in = refs[6:10]
    refs = refs[10:]
    if first:
        forcing, f_west, f_east, f_north, f_south = refs[:5]
        refs = refs[5:]
    out = refs.pop(0)
    if first:
        side_ref, s_ref, n_ref = refs[:3]
        refs = refs[3:]
    buf, e_buf, n_buf, m_buf, above, rim, sems = refs

    plane = tracers * rows
    halves = rows // SUB
    lane, sub = lane_iota(), sub_iota()
    blocks = levels // unroll
    flat = buf.reshape((levels * tracers + 2) * rows, LANES)
    south_flag = (lax.axis_index("lat") > 0).astype(jnp.float32)
    north_flag = (lax.axis_index("lat") < lax.axis_size("lat") - 1).astype(jnp.float32)
    north_mask = jnp.where(sub == SUB - 1, north_flag, 1.0)

    def load(b):
        at = b * unroll * tracers
        return pltpu.make_async_copy(
            field.at[pl.ds(at, unroll * tracers)], buf.at[pl.ds(at + 1, unroll * tracers)], sems.at[b]
        )

    def store(b):
        at = b * unroll * tracers
        return pltpu.make_async_copy(
            buf.at[pl.ds(at + 1, unroll * tracers)], out.at[pl.ds(at, unroll * tracers)], sems.at[b]
        )

    winds = [
        pltpu.make_async_copy(source, target, sems.at[blocks + i])
        for i, (source, target) in enumerate(((east, e_buf), (north, n_buf), (mixing, m_buf)))
    ]
    for copy in winds:
        copy.start()
    for b in range(blocks):
        load(b).start()

    def meet(target, from_west, from_east, source, count):
        for chunk in range(chunks):
            for r in range(0, count, SUB):
                a, b = pl.ds(target + r, SUB), pl.ds(source + r, SUB)
                turned = pltpu.roll(from_east[chunk, b, :], LANES - 2, 1)
                rim[chunk, a, :] = jnp.where(lane % 2 == 1, from_west[chunk, b, :], turned)

    meet(0, west_in, east_in, 0, plane)
    if first:
        meet(plane, f_west, f_east, 0, rows)
    for copy in winds:
        copy.wait()

    def stencil(source, at, rim_row, chunk, turn, edge_n, edge_s, co):
        values = []
        for h in range(halves):
            here = at + h * SUB
            cell = source[pl.ds(pl.multiple_of(here, SUB), SUB), :]
            side = pltpu.roll(rim[chunk, pl.ds(rim_row + h * SUB, SUB), :], turn, 1)
            e = jnp.where(lane == LANES - 1, side, pltpu.roll(cell, LANES - 1, 1))
            w = jnp.where(lane == 0, side, pltpu.roll(cell, 1, 1))
            if h == halves - 1:
                n = jnp.where(sub == SUB - 1, edge_n, pltpu.roll(cell, SUB - 1, 0))
            else:
                n = source[pl.ds(here + 1, SUB), :]
            s = source[pl.ds(here - 1, SUB), :]
            if h == 0:
                s = jnp.where(sub == 0, edge_s, s)
            c0, ce, cw, cn, cs = co[h][:5]
            values.append((c0 * cell + ce * e) + (cw * w + cn * n) + cs * s)
        return values

    def forward(k, carry):
        chunk, q = k // per_chunk, k % per_chunk
        turn = LANES - 1 - 2 * q
        has_up = (k < levels - 1).astype(jnp.float32)
        solved, pivots = carry
        co, new_pivots, edge = [], [], None
        for h in range(halves):
            blk = pl.ds(pl.multiple_of(k * rows + h * SUB, SUB), SUB)
            down, factor = pivots[h]
            up = m_buf[blk, :] * has_up
            inv = 1.0 / (1.0 + up + down - down * factor)
            factor = up * inv
            new_pivots.append((up, factor))
            above[blk, :] = factor
            e, n = e_buf[blk, :], n_buf[blk, :]
            side = pltpu.roll(west0[chunk, pl.ds(plane + h * SUB, SUB), :], turn, 1)
            w_in = jnp.minimum(jnp.where(lane == 0, side, pltpu.roll(e, 1, 1)), 0.0)
            if h == 0:
                edge = south0[pl.ds(levels * tracers + k, 1), :] * south_flag
            s_in = jnp.minimum(jnp.where(sub == 0, edge, pltpu.roll(n, 1, 0)), 0.0)
            edge = n[SUB - 1 : SUB, :]
            e_out, n_out = jnp.maximum(e, 0.0), jnp.maximum(n, 0.0)
            from_n = n_out * inv
            if h == halves - 1:
                from_n = from_n * north_mask
            stay = (1.0 - e_out + w_in - n_out + s_in) * inv
            co.append((stay, e_out * inv, -(w_in * inv), from_n, -(s_in * inv), down * inv))
        extra = None
        if first:
            extra = stencil(
                forcing, k * rows + SUB, plane, chunk, turn,
                f_north[pl.ds(k, 1), :], f_south[pl.ds(k, 1), :], co,
            )
        new = []
        for t in range(tracers):
            at = (k + 1) * plane - plane + (t + 1) * rows
            values = stencil(
                flat, at, t * rows, chunk, turn,
                north_in[pl.ds(k * tracers + t, 1), :], south_in[pl.ds(k * tracers + t, 1), :], co,
            )
            for h in range(halves):
                value = values[h] + co[h][5] * solved[t * halves + h]
                if first:
                    value = value + extra[h]
                new.append(value)
                flat[pl.ds(pl.multiple_of(at + h * SUB, SUB), SUB), :] = value
        return tuple(new), tuple(new_pivots)

    def forward_block(b, carry):
        load(b).wait()
        for u in range(unroll):
            carry = forward(b * unroll + u, carry)
        return carry

    zero = jnp.zeros((SUB, LANES), jnp.float32)
    zeros = (zero,) * (tracers * halves)
    lax.fori_loop(0, blocks, forward_block, (zeros, ((zero, zero),) * halves))

    def backward(k, carry):
        new = []
        for h in range(halves):
            f = above[pl.ds(pl.multiple_of(k * rows + h * SUB, SUB), SUB), :]
            for t in range(tracers):
                blk = pl.ds(pl.multiple_of(k * plane + (t + 1) * rows + h * SUB, SUB), SUB)
                value = flat[blk, :] + f * carry[h * tracers + t]
                flat[blk, :] = value
                new.append(value)
        return tuple(new)

    def backward_block(i, carry):
        b = blocks - 1 - i
        for u in reversed(range(unroll)):
            carry = backward(b * unroll + u, carry)
        store(b).start()
        return carry

    lax.fori_loop(0, blocks, backward_block, zeros)
    if first:
        put_rims(flat, rows, levels, per_chunk, chunks, side_ref, 0, plane)
        put_rows(flat, rows, n_ref, s_ref, rows, levels * tracers)
    for b in range(blocks):
        store(b).wait()


def pack(levels, group_rows, cap, kernel, columns, observed, errors, out, k_buf, c_buf, o_buf, e_buf, wide, sems):
    lane = lane_iota()
    copies = [
        pltpu.make_async_copy(source, target, sems.at[i])
        for i, (source, target) in enumerate(
            ((columns, c_buf), (observed, o_buf), (errors, e_buf), (kernel, k_buf))
        )
    ]
    for copy in copies:
        copy.start()
    for copy in copies:
        copy.wait()
    per_level = columns.shape[0]
    groups = LANES // cap
    pad = groups * group_rows - levels - 3

    def body(i, carry):
        one = pl.ds(i, 1)
        tail = [c_buf[one, :].astype(jnp.float32), o_buf[one, :], e_buf[one, :]]
        wide[pl.ds(0, levels), :] = k_buf[pl.ds(i, levels, stride=per_level), :]
        wide[pl.ds(levels, pad + 3), :] = jnp.concatenate(
            tail + [jnp.zeros((pad, LANES), jnp.float32)], axis=0
        )
        for j in range(groups):
            for m in range(group_rows // SUB):
                made = None
                for g in range(groups):
                    piece = wide[pl.ds(g * group_rows + m * SUB, SUB), :]
                    if g != j:
                        piece = pltpu.roll(piece, (g - j) * cap % LANES, 1)
                    made = piece if made is None else jnp.where(lane >= g * cap, piece, made)
                out[i * groups + j, pl.ds(m * SUB, SUB), :] = made
        return carry

    lax.fori_loop(0, per_level, body, 0)


def tracer_sum(block, concentration, out, buf, sems):
    levels, tracers, rows, cols = buf.shape

    def load(b):
        return pltpu.make_async_copy(
            concentration.at[pl.ds(b * block, block)], buf.at[pl.ds(b * block, block)], sems.at[b]
        )

    for b in range(levels // block):
        load(b).start()

    def body(b, carry):
        load(b).wait()
        for h in range(rows // SUB):
            tops, rests = [], []
            for k in range(block):
                part = jnp.sum(buf[b * block + k, :, pl.ds(h * SUB, SUB), :], axis=0)
                top = part.astype(jnp.bfloat16).astype(jnp.float32)
                tops.append(top)
                rests.append(part - top)
            at = pl.ds(pl.multiple_of(b * block * SUB, block * SUB), block * SUB)
            lanes = pl.ds(h * cols, cols)
            out[0, at, lanes] = jnp.concatenate(tops, axis=0).astype(jnp.bfloat16)
            out[1, at, lanes] = jnp.concatenate(rests, axis=0).astype(jnp.bfloat16)
        return carry

    lax.fori_loop(0, levels // block, body, 0)


def soundings(
    levels, rows, group_rows, cap, chunks, per_chunk, block,
    received, sums, forcing, side_ref, s_ref, n_ref, back, arrived, table, scaled
):
    lane = lane_iota()
    parts, _, width = arrived.shape
    halves = rows // SUB
    keys = halves * LANES
    groups = LANES // cap
    senders = width // cap

    def unpack(c, carry):
        part, col = c // (width // LANES), c % (width // LANES)
        for g in range(groups):
            for m in range(group_rows // SUB):
                made = None
                for p in range(groups):
                    piece = received[c * groups + p, pl.ds(m * SUB, SUB), :]
                    if p != g:
                        piece = pltpu.roll(piece, (p - g) * cap % LANES, 1)
                    made = piece if made is None else jnp.where(lane >= p * cap, piece, made)
                lanes = pl.ds(pl.multiple_of(col * LANES, LANES), LANES)
                arrived[part, pl.ds(g * group_rows + m * SUB, SUB), lanes] = made
        return carry

    lax.fori_loop(0, parts * width // LANES, unpack, 0)

    sub_index = lax.broadcasted_iota(jnp.int32, (SUB, width), 0)
    key_index = lax.broadcasted_iota(jnp.int32, (keys, width), 0)
    turned_index = lax.broadcasted_iota(jnp.int32, (LANES, keys), 1)

    def columns(j):
        return arrived[j, pl.ds(levels, 1), :].astype(jnp.int32)

    def key_of(col):
        return (col >> 10) * LANES + (col & (LANES - 1))

    def mask_of(j):
        return sub_index == ((columns(j) >> 7) & (SUB - 1))

    for j in range(parts):
        col = columns(j)
        key = key_of(col)
        look = jnp.where(key_index == key, 1.0, 0.0).astype(jnp.bfloat16)
        for c in range(width // LANES):
            piece = key[:, c * LANES : (c + 1) * LANES].astype(jnp.float32)
            across = jnp.broadcast_to(piece, (LANES, LANES)).T.astype(jnp.int32)
            across = jnp.concatenate([across] * halves, axis=1)
            table[j, pl.ds(c * LANES, LANES), :] = jnp.where(turned_index == across, 1.0, 0.0).astype(
                jnp.bfloat16
            )
        total = jnp.zeros((SUB, width), jnp.float32)
        for b in range(levels // block):
            blk = pl.ds(b * block * SUB, block * SUB)
            seen = jnp.dot(sums[0, blk, :], look, preferred_element_type=jnp.float32)
            seen += jnp.dot(sums[1, blk, :], look, preferred_element_type=jnp.float32)
            weight = arrived[j, pl.ds(b * block, block), :]
            for k in range(block):
                total += weight[k : k + 1, :] * seen[k * SUB : (k + 1) * SUB, :]
        modelled = jnp.sum(jnp.where(mask_of(j), total, 0.0), axis=0, keepdims=True)
        observed = arrived[j, pl.ds(levels + 1, 1), :]
        error = arrived[j, pl.ds(levels + 2, 1), :]
        residual = jnp.where(col >= 0, (modelled - observed) / error, 0.0)
        scaled[pl.ds(j, 1), :] = residual / error
        for i in range(senders):
            at = i * cap
            piece = residual[:, at // LANES * LANES : at // LANES * LANES + LANES]
            if at % LANES:
                piece = pltpu.roll(piece, LANES - at % LANES, 1)
            back[pl.ds(j * senders + i, 1), :] = piece

    zeros = jnp.zeros((SUB, LANES), jnp.float32)
    forcing[pl.ds(0, SUB), :] = zeros
    forcing[pl.ds(levels * rows + SUB, SUB), :] = zeros
    for b in range(levels // block):
        total = jnp.zeros((block * SUB, keys), jnp.float32)
        for j in range(parts):
            weight = arrived[j, pl.ds(b * block, block), :] * scaled[pl.ds(j, 1), :]
            top = weight.astype(jnp.bfloat16).astype(jnp.float32)
            mask = mask_of(j)
            for part in (top, weight - top):
                spread = jnp.concatenate(
                    [jnp.where(mask, part[k : k + 1, :], 0.0) for k in range(block)], axis=0
                ).astype(jnp.bfloat16)
                total += jnp.dot(spread, table[j, :, :], preferred_element_type=jnp.float32)
        for k in range(block):
            for h in range(halves):
                forcing[pl.ds((b * block + k) * rows + (h + 1) * SUB, SUB), :] = total[
                    k * SUB : (k + 1) * SUB, h * LANES : (h + 1) * LANES
                ]

    put_rims(forcing, SUB, levels, per_chunk, chunks, side_ref, 0, rows)
    put_rows(forcing, SUB, n_ref, s_ref, rows, levels)


def unpack_residual(cap, arrived, out):
    lane = lax.broadcasted_iota(jnp.int32, (1, LANES), 1)
    groups = LANES // cap
    for row in range(out.shape[0]):
        made = None
        for g in range(groups):
            piece = arrived[pl.ds(row * groups + g, 1), :]
            if g:
                piece = pltpu.roll(piece, g * cap, 1)
            made = piece if made is None else jnp.where(lane >= g * cap, piece, made)
        out[pl.ds(row, 1), :] = made


def shift(value, axis, by):
    count = lax.axis_size(axis)
    return lax.ppermute(value, axis, [(i, (i + by) % count) for i in range(count)])


def exchange(side_rim, south_rim, north_rim):
    return (
        shift(side_rim, "lon", 1),
        shift(side_rim, "lon", -1),
        shift(south_rim, "lat", -1),
        shift(north_rim, "lat", 1),
    )


def per_device(
    concentration, adjoint, wind_east, wind_north, mixing, sound_col, kernel, observed, obs_error
):
    levels, tracers, rows, cols = adjoint.shape
    bricks = lax.axis_size("lon") * lax.axis_size("lat")
    slots = sound_col.shape[2]
    cap = slots // bricks
    chunks, per_chunk = rim_chunks(levels)
    plane = tracers * rows
    per_level = slots // LANES
    groups = LANES // cap
    group_rows = -(-(levels + 3) // (groups * SUB)) * SUB
    field_bytes = levels * plane * cols * 4
    dma = pltpu.SemaphoreType.DMA

    def flat(x):
        return x.reshape(-1, LANES)

    packed = call(
        functools.partial(pack, levels, group_rows, cap),
        [ANY] * 4, f32(bricks, group_rows, LANES), VMEM,
        (
            vmem(levels * per_level, LANES), pltpu.VMEM((per_level, LANES), jnp.int32),
            vmem(per_level, LANES), vmem(per_level, LANES), vmem(groups * group_rows, LANES), dma((4,)),
        ),
        4, 10, 800000, "pack",
    )(flat(kernel), flat(sound_col), flat(observed), flat(obs_error))
    received = lax.all_to_all(packed, ("lon", "lat"), split_axis=0, concat_axis=0, tiled=True)

    field = adjoint.reshape(levels * tracers, rows, LANES)
    east, north, mix = flat(wind_east), flat(wind_north), flat(mixing)
    rims = call(
        functools.partial(first_rims, levels, tracers, rows, chunks, per_chunk),
        [ANY] * 3,
        (f32(chunks, plane + rows, LANES), f32(levels * tracers, LANES), f32(levels * tracers + levels, LANES)),
        (VMEM,) * 3,
        (vmem(levels * plane, LANES), vmem(levels * rows, LANES), vmem(levels * rows, LANES), dma((chunks * 2 + 2,))),
        10, field_bytes, 2 * field_bytes, "first_rims",
    )(flat(adjoint), east, north)
    start_rims = exchange(*rims)

    block = largest(levels, 24, 16, 8)
    sum_block = largest(levels, 12, 8)
    sums = call(
        functools.partial(tracer_sum, sum_block),
        [ANY], jax.ShapeDtypeStruct((2, levels * SUB, rows // SUB * cols), jnp.bfloat16), VMEM,
        (vmem(levels, tracers, rows, cols), dma((levels // sum_block,))),
        10, field_bytes // 4, field_bytes, "tracer_sum",
    )(concentration)

    width = largest(slots, 2 * LANES, LANES)
    parts = slots // width
    forcing, *rims, back = call(
        functools.partial(soundings, levels, rows, group_rows, cap, chunks, per_chunk, block),
        [VMEM] * 2,
        (
            f32(levels * rows + 2 * SUB, LANES), f32(chunks, rows, LANES), f32(levels, LANES), f32(levels, LANES),
            f32(bricks, LANES),
        ),
        (VMEM,) * 5,
        (
            vmem(parts, groups * group_rows, width),
            pltpu.VMEM((parts, width, rows // SUB * LANES), jnp.bfloat16),
            vmem(max(parts, SUB), width),
        ),
        16, field_bytes * 8, field_bytes, "soundings",
    )(received, sums)
    forcing_rims = exchange(*rims)

    unroll = largest(levels, 4, 3, 2, 1)

    def advance(value, first, *operands):
        outs, specs = (f32(*value.shape),), (ANY,)
        if first:
            outs += (f32(chunks, plane, LANES), f32(levels * tracers, LANES), f32(levels * tracers, LANES))
            specs += (VMEM,) * 3
        return call(
            functools.partial(step, levels, tracers, rows, chunks, per_chunk, unroll, first),
            [ANY] * 4 + [VMEM] * (2 + len(operands)), outs, specs,
            (
                vmem(levels * tracers + 2, rows, LANES), vmem(levels * rows, LANES), vmem(levels * rows, LANES),
                vmem(levels * rows, LANES), vmem(levels * rows, LANES), vmem(chunks, plane + rows, LANES),
                dma((levels // unroll + 3,)),
            ),
            12, field_bytes * 8, field_bytes * 2, "step",
        )(value, east, north, mix, start_rims[0], start_rims[3], *operands)

    stepped, *rims = advance(field, True, *start_rims, forcing, *forcing_rims)
    (result,) = advance(stepped, False, *exchange(*rims))

    returned = lax.all_to_all(
        back.reshape(bricks, 1, LANES), ("lon", "lat"), split_axis=0, concat_axis=0, tiled=True
    )
    residual = call(
        functools.partial(unpack_residual, cap), [VMEM], f32(per_level, LANES), VMEM, (), 2, 10, 10000, "residual",
    )(returned.reshape(bricks, LANES))
    return result.reshape(adjoint.shape), residual.reshape(sound_col.shape)


def solution(mesh):
    field = P(None, None, "lat", "lon")
    face = P(None, "lat", "lon")
    owned = P(None, ("lon", "lat"), None)
    return jax.shard_map(
        per_device,
        mesh=mesh,
        in_specs=(field, field, face, face, face, owned, owned, owned, owned),
        out_specs=(field, owned),
        check_vma=False,
    )
```

profile of v0, /device:TPU:0, one launch (start us, length us, event | category | flops | bytes accessed | tf_op | source)
XLA Modules:
  0.0 83.8 jit_solution(12973435283119472445)
XLA Ops:
  0.6 0.0 copy-start.8
  0.6 1.0 %copy-done.8 = f32[72,1,1024]{2,1,0:T(1,128)S(1)} copy-done((f32[72,1,1024]{2,1,0:T(1,128)S(1)}, f32[72,1,1024]{2,1,0:T(1,128)}, u32[]{:S(2)}) %copy-start.8) | copy-done | bytes 294936
  1.6 0.0 copy-start.9
  1.6 0.7 copy-done.9
  2.3 0.0 copy-start.10
  2.3 0.7 copy-done.10
  3.0 0.0 copy-start.11
  3.0 0.7 copy-done.11
  3.7 1.7 %pack.1 = f32[32,24,128]{2,1,0:T(8,128)} custom-call(f32[576,128]{1,0:T(8,128)S(1)} %bitcast.25, s32[8,128]{1,0:T(8,128)S(1)} %bitcast.28, f32[8,128]{1,0:T(8,128)S(1)} %bitcast.29, f32[8,128]{1,0:T(8,128)S(1)} %bitcast.30), custom_call_target="tpu_custom_call" | custom-call | flops 10 | bytes 800000 | tf_op jit(solution)/shard_map/pack/pallas_call | solution.py:481
  5.4 7.3 %all-to-all-start = ((f32[32,24,128]{2,1,0:T(8,128)}), f32[32,24,128]{2,1,0:T(8,128)S(1)}, u32[]{:S(2)}, u32[]{:S(2)}) async-start(f32[32,24,128]{2,1,0:T(8,128)} %pack.1), calls=%async_computation | async-start | bytes 786432 | tf_op jit(solution)/shard_map/all_to_all | solution.py:490
  12.7 0.0 copy-start
  12.7 2.3 %copy-done = f32[72,8,16,128]{3,2,1,0:T(8,128)S(1)} copy-done((f32[72,8,16,128]{3,2,1,0:T(8,128)S(1)}, f32[72,8,16,128]{3,2,1,0:T(8,128)}, u32[]{:S(2)}) %copy-start) | copy-done | bytes 4718616
  15.0 0.0 copy-start.2
  15.0 1.1 %copy-done.2 = f32[72,16,128]{2,1,0:T(8,128)S(1)} copy-done((f32[72,16,128]{2,1,0:T(8,128)S(1)}, f32[72,16,128]{2,1,0:T(8,128)}, u32[]{:S(2)}) %copy-start.2) | copy-done | bytes 589848
  16.1 0.0 copy-start.4
  16.1 1.1 %copy-done.4 = f32[72,16,128]{2,1,0:T(8,128)S(1)} copy-done((f32[72,16,128]{2,1,0:T(8,128)S(1)}, f32[72,16,128]{2,1,0:T(8,128)}, u32[]{:S(2)}) %copy-start.4) | copy-done | bytes 589848
  17.1 0.0 copy-start.6
  17.1 0.0 copy-start.3
  17.2 0.0 copy-start.5
  17.2 0.0 copy-start.7
  17.2 4.4 %first_rims.1 = (f32[2,144,128]{2,1,0:T(8,128)}, f32[576,128]{1,0:T(8,128)}, f32[648,128]{1,0:T(8,128)}) custom-call(f32[9216,128]{1,0:T(8,128)S(1)} %bitcast.15, f32[1152,128]{1,0:T(8,128)S(1)} %bitcast.17, f32[1152,128]{1,0:T(8,128)S(1)} %bitcast.20), custom_call_target="tpu_custom_call" | custom-call | flops 4718592 | bytes 9437184 | tf_op jit(solution)/shard_map/first_rims/pallas_call | solution.py:494
  21.5 1.8 %collective-permute-start.1 = (f32[648,128]{1,0:T(8,128)}, f32[648,128]{1,0:T(8,128)S(1)}, u32[]{:S(2)}, u32[]{:S(2)}) collective-permute-start(f32[648,128]{1,0:T(8,128)} %get-tuple-element.15), channel_id=1, source_target_pairs={{0,1},{1,2},{2,3},{3,0},{4,5},{5,6},{6,7},{7,4},{8,9},{9,10},{10,1... | collective-permute-start | bytes 995336 | tf_op jit(solution)/shard_map/ppermute | solution.py:451
  23.3 2.1 %collective-permute-start.3 = (f32[576,128]{1,0:T(8,128)}, f32[576,128]{1,0:T(8,128)S(1)}, u32[]{:S(2)}, u32[]{:S(2)}) collective-permute-start(f32[576,128]{1,0:T(8,128)} %get-tuple-element.16), channel_id=1, source_target_pairs={{0,3},{1,0},{2,1},{3,2},{4,7},{5,4},{6,5},{7,6},{8,11},{9,8},{10,9... | collective-permute-start | bytes 884744 | tf_op jit(solution)/shard_map/ppermute | solution.py:451
  25.4 1.9 %collective-permute-start.2 = (f32[2,144,128]{2,1,0:T(8,128)}, f32[2,144,128]{2,1,0:T(8,128)}, u32[]{:S(2)}, u32[]{:S(2)}) collective-permute-start(f32[2,144,128]{2,1,0:T(8,128)} %get-tuple-element.14), channel_id=1, source_target_pairs={{0,28},{4,0},{8,4},{12,8},{16,12},{20,16},{24,20},{28,24},{1,29},{... | collective-permute-start | bytes 442376 | tf_op jit(solution)/shard_map/ppermute | solution.py:451
  27.3 0.0 collective-permute-start
  27.3 0.0 copy-done.6
  27.3 0.7 tracer_sum.1.sums
  28.0 0.0 all-to-all-done.received
  28.0 2.7 %soundings.1 = (f32[1168,128]{1,0:T(8,128)S(1)}, f32[2,16,128]{2,1,0:T(8,128)S(1)}, f32[72,128]{1,0:T(8,128)S(1)}, f32[72,128]{1,0:T(8,128)S(1)}, f32[32,128]{1,0:T(8,128)S(1)}) custom-call(f32[32,24,128]{2,1,0:T(8,128)S(1)} %all-to-all-done.received, bf16[2,576,256]{2,1,0:T(8,128)(2,1)S(1)} %tracer_sum.1.sums), custom_call_target="tpu_custom_call" | custom-call | flops 37748736 | bytes 4718592 | tf_op jit(solution)/shard_map/soundings/pallas_call | solution.py:515
  30.7 1.6 %collective-permute-start.6 = (f32[72,128]{1,0:T(8,128)S(1)}, f32[72,128]{1,0:T(8,128)S(1)}, u32[]{:S(2)}, u32[]{:S(2)}) collective-permute-start(f32[72,128]{1,0:T(8,128)S(1)} %get-tuple-element.19), channel_id=1, source_target_pairs={{0,3},{1,0},{2,1},{3,2},{4,7},{5,4},{6,5},{7,6},{8,11},{9,8},{10,9... | collective-permute-start | bytes 110600 | tf_op jit(solution)/shard_map/ppermute | solution.py:451
  32.3 0.0 collective-permute-done.2.refs_7_
  32.3 0.5 collective-permute-start.7
  32.8 0.2 collective-permute-done.refs_4_.refs_6_
  33.0 1.9 %collective-permute-start.5 = (f32[2,16,128]{2,1,0:T(8,128)S(1)}, f32[2,16,128]{2,1,0:T(8,128)S(1)}, u32[]{:S(2)}, u32[]{:S(2)}) collective-permute-start(f32[2,16,128]{2,1,0:T(8,128)S(1)} %get-tuple-element.18), channel_id=1, source_target_pairs={{0,28},{4,0},{8,4},{12,8},{16,12},{20,16},{24,20},{28,24},{1,29},{... | collective-permute-start | bytes 49160 | tf_op jit(solution)/shard_map/ppermute | solution.py:451
  34.9 5.0 %collective-permute-done.3.refs_8_ = f32[576,128]{1,0:T(8,128)S(1)} collective-permute-done((f32[576,128]{1,0:T(8,128)}, f32[576,128]{1,0:T(8,128)S(1)}, u32[]{:S(2)}, u32[]{:S(2)}) %collective-permute-start.3) | collective-permute-done | bytes 294944 | tf_op jit(solution)/shard_map/ppermute | solution.py:451
  39.8 0.0 collective-permute-start.4
  39.9 0.0 collective-permute-done.1.refs_5_.refs_9_
  39.9 0.0 collective-permute-done.5.refs_12_
  39.9 4.1 %collective-permute-done.4.refs_11_ = f32[2,16,128]{2,1,0:T(8,128)S(1)} collective-permute-done((f32[2,16,128]{2,1,0:T(8,128)S(1)}, f32[2,16,128]{2,1,0:T(8,128)S(1)}, u32[]{:S(2)}, u32[]{:S(2)}) %collective-permute-start.4) | collective-permute-done | bytes 16416 | tf_op jit(solution)/shard_map/ppermute | solution.py:451
  43.9 0.0 collective-permute-done.6.refs_13_
  43.9 0.0 collective-permute-done.7.refs_14_
  43.9 0.0 copy-done.3
  43.9 0.0 copy-done.5
  43.9 0.0 copy-done.7
  43.9 0.0 copy-start.1
  44.0 2.3 %copy-done.1 = f32[72,8,16,128]{3,2,1,0:T(8,128)S(1)} copy-done((f32[72,8,16,128]{3,2,1,0:T(8,128)S(1)}, f32[72,8,16,128]{3,2,1,0:T(8,128)}, u32[]{:S(2)}) %copy-start.1) | copy-done | bytes 4718616
  46.3 11.6 %step.2 = (f32[576,16,128]{2,1,0:T(8,128)S(1)}, f32[2,128,128]{2,1,0:T(8,128)S(1)}, f32[576,128]{1,0:T(8,128)S(1)}, f32[576,128]{1,0:T(8,128)S(1)}) custom-call(f32[576,16,128]{2,1,0:T(8,128)S(1)} %bitcast.16, f32[1152,128]{1,0:T(8,128)S(1)} %bitcast.18, f32[1152,128]{1,0:T(8,128)S(1)} %bitcast.21, f32[1152,128]{1,0:T(8,128)S(1)} %bitcast.23, ...), custom_call_target="tpu_custom_call" | custom-call | flops 37748736 | bytes 9437184 | tf_op jit(solution)/shard_map/step/pallas_call | solution.py:539
  57.9 2.6 %collective-permute-start.10 = (f32[576,128]{1,0:T(8,128)S(1)}, f32[576,128]{1,0:T(8,128)S(1)}, u32[]{:S(2)}, u32[]{:S(2)}) collective-permute-start(f32[576,128]{1,0:T(8,128)S(1)} %get-tuple-element.23), channel_id=1, source_target_pairs={{0,3},{1,0},{2,1},{3,2},{4,7},{5,4},{6,5},{7,6},{8,11},{9,8},{10,9... | collective-permute-start | bytes 884744 | tf_op jit(solution)/shard_map/ppermute | solution.py:451
  60.4 0.0 collective-permute-start.11
  60.4 0.0 collective-permute-start.9
  60.4 0.5 collective-permute-start.8
  61.0 12.8 %all_to_all.10 = f32[32,1,128]{2,1,0:T(1,128)S(1)} all-to-all(f32[32,1,128]{2,1,0:T(1,128)S(1)} %bitcast.27), channel_id=1, replica_groups=mesh['lon'=8,'lat'=4] {'lon','lat'}, dimensions={0} | all-to-all | bytes 32768 | tf_op jit(solution)/shard_map/all_to_all | solution.py:553
  73.7 0.7 residual.1
  74.4 0.0 collective-permute-done.9.refs_7_
  74.4 0.0 collective-permute-done.8.refs_6_
  74.4 0.0 collective-permute-done.10.refs_8_
  74.4 0.0 collective-permute-done.11.refs_9_
  74.5 9.4 %step.3 = f32[576,16,128]{2,1,0:T(8,128)} custom-call(f32[576,16,128]{2,1,0:T(8,128)S(1)} %get-tuple-element.21.refs_0_, f32[1152,128]{1,0:T(8,128)S(1)} %bitcast.19, f32[1152,128]{1,0:T(8,128)S(1)} %bitcast.22, f32[1152,128]{1,0:T(8,128)S(1)} %bitcast.24, f32[2,144,128]{2,1,0:T(8,128)S(1)} %collective-permute-done.refs_4_.refs_6_, ...), custom_call_target="tpu_custom_call" | custom-call | flops 37748736 | bytes 9437184 | tf_op jit(solution)/shard_map/step/pallas_call | solution.py:539
Async XLA Ops:
  0.6 1.0 %copy-start.8 = (f32[72,1,1024]{2,1,0:T(1,128)S(1)}, f32[72,1,1024]{2,1,0:T(1,128)}, u32[]{:S(2)}) copy-start(f32[72,1,1024]{2,1,0:T(1,128)} %param.15) | copy-start | bytes 884740
  1.6 0.7 copy-start.9
  2.3 0.7 copy-start.10
  3.0 0.7 copy-start.11
  5.4 22.6 %all-to-all-start = ((f32[32,24,128]{2,1,0:T(8,128)}), f32[32,24,128]{2,1,0:T(8,128)S(1)}, u32[]{:S(2)}, u32[]{:S(2)}) async-start(f32[32,24,128]{2,1,0:T(8,128)} %pack.1), calls=%async_computation | async-start | bytes 786432 | tf_op jit(solution)/shard_map/all_to_all | solution.py:490
  12.7 2.3 %copy-start = (f32[72,8,16,128]{3,2,1,0:T(8,128)S(1)}, f32[72,8,16,128]{3,2,1,0:T(8,128)}, u32[]{:S(2)}) copy-start(f32[72,8,16,128]{3,2,1,0:T(8,128)} %param.10) | copy-start | bytes 14155780
  15.0 1.1 %copy-start.2 = (f32[72,16,128]{2,1,0:T(8,128)S(1)}, f32[72,16,128]{2,1,0:T(8,128)}, u32[]{:S(2)}) copy-start(f32[72,16,128]{2,1,0:T(8,128)} %param.11) | copy-start | bytes 1769476
  16.1 1.1 %copy-start.4 = (f32[72,16,128]{2,1,0:T(8,128)S(1)}, f32[72,16,128]{2,1,0:T(8,128)}, u32[]{:S(2)}) copy-start(f32[72,16,128]{2,1,0:T(8,128)} %param.12) | copy-start | bytes 1769476
  17.1 10.1 %copy-start.6 = (f32[72,8,16,128]{3,2,1,0:T(8,128)S(1)}, f32[72,8,16,128]{3,2,1,0:T(8,128)}, u32[]{:S(2)}) copy-start(f32[72,8,16,128]{3,2,1,0:T(8,128)} %concentration.1) | copy-start | bytes 14155780
  17.1 26.8 %copy-start.3 = (f32[72,16,128]{2,1,0:T(8,128)S(1)}, f32[72,16,128]{2,1,0:T(8,128)}, u32[]{:S(2)}) copy-start(f32[72,16,128]{2,1,0:T(8,128)} %param.11) | copy-start | bytes 1769476
  17.2 26.8 %copy-start.5 = (f32[72,16,128]{2,1,0:T(8,128)S(1)}, f32[72,16,128]{2,1,0:T(8,128)}, u32[]{:S(2)}) copy-start(f32[72,16,128]{2,1,0:T(8,128)} %param.12) | copy-start | bytes 1769476
  17.2 26.8 %copy-start.7 = (f32[72,16,128]{2,1,0:T(8,128)S(1)}, f32[72,16,128]{2,1,0:T(8,128)}, u32[]{:S(2)}) copy-start(f32[72,16,128]{2,1,0:T(8,128)} %param.13) | copy-start | bytes 1769476
  21.5 18.3 %collective-permute-start.1 = (f32[648,128]{1,0:T(8,128)}, f32[648,128]{1,0:T(8,128)S(1)}, u32[]{:S(2)}, u32[]{:S(2)}) collective-permute-start(f32[648,128]{1,0:T(8,128)} %get-tuple-element.15), channel_id=1, source_target_pairs={{0,1},{1,2},{2,3},{3,0},{4,5},{5,6},{6,7},{7,4},{8,9},{9,10},{10,1... | collective-permute-start | bytes 995336 | tf_op jit(solution)/shard_map/ppermute | solution.py:451
  23.3 16.5 %collective-permute-start.3 = (f32[576,128]{1,0:T(8,128)}, f32[576,128]{1,0:T(8,128)S(1)}, u32[]{:S(2)}, u32[]{:S(2)}) collective-permute-start(f32[576,128]{1,0:T(8,128)} %get-tuple-element.16), channel_id=1, source_target_pairs={{0,3},{1,0},{2,1},{3,2},{4,7},{5,4},{6,5},{7,6},{8,11},{9,8},{10,9... | collective-permute-start | bytes 884744 | tf_op jit(solution)/shard_map/ppermute | solution.py:451
  25.4 6.9 %collective-permute-start.2 = (f32[2,144,128]{2,1,0:T(8,128)}, f32[2,144,128]{2,1,0:T(8,128)}, u32[]{:S(2)}, u32[]{:S(2)}) collective-permute-start(f32[2,144,128]{2,1,0:T(8,128)} %get-tuple-element.14), channel_id=1, source_target_pairs={{0,28},{4,0},{8,4},{12,8},{16,12},{20,16},{24,20},{28,24},{1,29},{... | collective-permute-start | bytes 442376 | tf_op jit(solution)/shard_map/ppermute | solution.py:451
  27.3 5.7 %collective-permute-start = (f32[2,144,128]{2,1,0:T(8,128)}, f32[2,144,128]{2,1,0:T(8,128)S(1)}, u32[]{:S(2)}, u32[]{:S(2)}) collective-permute-start(f32[2,144,128]{2,1,0:T(8,128)} %get-tuple-element.14), channel_id=1, source_target_pairs={{0,4},{4,8},{8,12},{12,16},{16,20},{20,24},{24,28},{28,0},{1,5},{5... | collective-permute-start | bytes 442376 | tf_op jit(solution)/shard_map/ppermute | solution.py:451
  30.7 13.2 %collective-permute-start.6 = (f32[72,128]{1,0:T(8,128)S(1)}, f32[72,128]{1,0:T(8,128)S(1)}, u32[]{:S(2)}, u32[]{:S(2)}) collective-permute-start(f32[72,128]{1,0:T(8,128)S(1)} %get-tuple-element.19), channel_id=1, source_target_pairs={{0,3},{1,0},{2,1},{3,2},{4,7},{5,4},{6,5},{7,6},{8,11},{9,8},{10,9... | collective-permute-start | bytes 110600 | tf_op jit(solution)/shard_map/ppermute | solution.py:451
  32.3 11.6 %collective-permute-start.7 = (f32[72,128]{1,0:T(8,128)S(1)}, f32[72,128]{1,0:T(8,128)S(1)}, u32[]{:S(2)}, u32[]{:S(2)}) collective-permute-start(f32[72,128]{1,0:T(8,128)S(1)} %get-tuple-element.20), channel_id=1, source_target_pairs={{0,1},{1,2},{2,3},{3,0},{4,5},{5,6},{6,7},{7,4},{8,9},{9,10},{10,1... | collective-permute-start | bytes 110600 | tf_op jit(solution)/shard_map/ppermute | solution.py:451
  33.0 6.9 %collective-permute-start.5 = (f32[2,16,128]{2,1,0:T(8,128)S(1)}, f32[2,16,128]{2,1,0:T(8,128)S(1)}, u32[]{:S(2)}, u32[]{:S(2)}) collective-permute-start(f32[2,16,128]{2,1,0:T(8,128)S(1)} %get-tuple-element.18), channel_id=1, source_target_pairs={{0,28},{4,0},{8,4},{12,8},{16,12},{20,16},{24,20},{28,24},{1,29},{... | collective-permute-start | bytes 49160 | tf_op jit(solution)/shard_map/ppermute | solution.py:451
  39.8 4.1 %collective-permute-start.4 = (f32[2,16,128]{2,1,0:T(8,128)S(1)}, f32[2,16,128]{2,1,0:T(8,128)S(1)}, u32[]{:S(2)}, u32[]{:S(2)}) collective-permute-start(f32[2,16,128]{2,1,0:T(8,128)S(1)} %get-tuple-element.18), channel_id=1, source_target_pairs={{0,4},{4,8},{8,12},{12,16},{16,20},{20,24},{24,28},{28,0},{1,5},{5... | collective-permute-start | bytes 49160 | tf_op jit(solution)/shard_map/ppermute | solution.py:451
  43.9 2.3 %copy-start.1 = (f32[72,8,16,128]{3,2,1,0:T(8,128)S(1)}, f32[72,8,16,128]{3,2,1,0:T(8,128)}, u32[]{:S(2)}) copy-start(f32[72,8,16,128]{3,2,1,0:T(8,128)} %param.10) | copy-start | bytes 14155780
  57.9 16.6 %collective-permute-start.10 = (f32[576,128]{1,0:T(8,128)S(1)}, f32[576,128]{1,0:T(8,128)S(1)}, u32[]{:S(2)}, u32[]{:S(2)}) collective-permute-start(f32[576,128]{1,0:T(8,128)S(1)} %get-tuple-element.23), channel_id=1, source_target_pairs={{0,3},{1,0},{2,1},{3,2},{4,7},{5,4},{6,5},{7,6},{8,11},{9,8},{10,9... | collective-permute-start | bytes 884744 | tf_op jit(solution)/shard_map/ppermute | solution.py:451
  60.4 14.0 %collective-permute-start.11 = (f32[576,128]{1,0:T(8,128)S(1)}, f32[576,128]{1,0:T(8,128)S(1)}, u32[]{:S(2)}, u32[]{:S(2)}) collective-permute-start(f32[576,128]{1,0:T(8,128)S(1)} %get-tuple-element.24), channel_id=1, source_target_pairs={{0,1},{1,2},{2,3},{3,0},{4,5},{5,6},{6,7},{7,4},{8,9},{9,10},{10,1... | collective-permute-start | bytes 884744 | tf_op jit(solution)/shard_map/ppermute | solution.py:451
  60.4 14.0 %collective-permute-start.9 = (f32[2,128,128]{2,1,0:T(8,128)S(1)}, f32[2,128,128]{2,1,0:T(8,128)S(1)}, u32[]{:S(2)}, u32[]{:S(2)}) collective-permute-start(f32[2,128,128]{2,1,0:T(8,128)S(1)} %get-tuple-element.22), channel_id=1, source_target_pairs={{0,28},{4,0},{8,4},{12,8},{16,12},{20,16},{24,20},{28,24},{1,29},{... | collective-permute-start | bytes 393224 | tf_op jit(solution)/shard_map/ppermute | solution.py:451
  60.4 14.0 %collective-permute-start.8 = (f32[2,128,128]{2,1,0:T(8,128)S(1)}, f32[2,128,128]{2,1,0:T(8,128)S(1)}, u32[]{:S(2)}, u32[]{:S(2)}) collective-permute-start(f32[2,128,128]{2,1,0:T(8,128)S(1)} %get-tuple-element.22), channel_id=1, source_target_pairs={{0,4},{4,8},{8,12},{12,16},{16,20},{20,24},{24,28},{28,0},{1,5},{5... | collective-permute-start | bytes 393224 | tf_op jit(solution)/shard_map/ppermute | solution.py:451
where the time goes:
time: 84.4 us; the launch traced here: 83.8 us
  Pallas kernels  31.1 us (37%)
  starting transfers between devices  20.1 us (24%)
  blocking collectives  12.8 us (15%)
  local copies, waits for them, and re-layouts  9.82 us (12%)
  waiting for transfers between devices  9.24 us (11%)
    pallas_call x2, Pallas kernels, advance(): call(functools.partial(step, levels, tracers, rows, chunks, per_chunk, un...  21 us
    ppermute x12, starting transfers between devices, shift(): lax.ppermute(value, axis, [(i, (i + by) % count) for i in range(count)])  12.8 us
    all_to_all x1, blocking collectives, per_device(): lax.all_to_all(back.reshape(bricks, 1, LANES), ('lon', 'lat'), split_axis...  12.8 us
    unnamed x24, local copies, waits for them, and re-layouts  9.82 us
    ppermute x12, waiting for transfers between devices, shift(): lax.ppermute(value, axis, [(i, (i + by) % count) for i in range(count)])  9.24 us
    all_to_all x1, starting transfers between devices, per_device(): lax.all_to_all(packed, ('lon', 'lat'), split_axis=0, concat_axis=0, tiled...  7.3 us
    pallas_call x1, Pallas kernels, per_device(): call(functools.partial(first_rims, levels, tracers, rows, chunks, per_chu...  4.36 us
    pallas_call x1, Pallas kernels, per_device(): call(functools.partial(soundings, levels, rows, group_rows, cap, chunks,...  2.7 us
  transfers between devices with their start and end apart: 13, of which 3 were waited for; matrix products, arithmetic and copies ran while one was open for 0% of the time, Pallas kernels for 10%

commit v1 on v0

--- a/solution.py
+++ b/solution.py
@@ -10,7 +10,7 @@
 LANES = 128
 SUB = 8
 MIB = 1 << 20
-ANY = pl.BlockSpec(memory_space=pl.ANY)
+HBM = pl.BlockSpec(memory_space=pltpu.HBM)
 VMEM = pl.BlockSpec(memory_space=pltpu.VMEM)
 
 
@@ -52,88 +52,145 @@
     )
 
 
-def put_rims(field, offset, levels, per_chunk, chunks, out, first, plane):
+def put_rims(field, offset, levels, per_chunk, chunk, out, first, plane):
     lane = lane_iota()
     group = largest(plane // SUB, 4, 2, 1)
-    for chunk in range(chunks):
-        count = min(per_chunk, levels - chunk * per_chunk)
-
-        def body(i, carry, chunk=chunk, count=count):
-            r = pl.multiple_of(i * SUB * group, SUB * group)
-            made = [jnp.zeros((SUB, LANES), jnp.float32)] * group
-            for q in range(count):
-                for g in range(group):
-                    at = pl.multiple_of((chunk * per_chunk + q) * plane + offset + r + g * SUB, SUB)
-                    turned = pltpu.roll(field[pl.ds(at, SUB), :], 2 * q + 2, 1)
-                    made[g] = jnp.where(lane >= 2 * q + 1, turned, made[g])
+    count = min(per_chunk, levels - chunk * per_chunk)
+
+    def body(i, carry):
+        r = pl.multiple_of(i * SUB * group, SUB * group)
+        made = [jnp.zeros((SUB, LANES), jnp.float32)] * group
+        for q in range(count):
             for g in range(group):
-                out[chunk, pl.ds(pl.multiple_of(first + r + g * SUB, SUB), SUB), :] = made[g]
-            return carry
-
-        lax.fori_loop(0, plane // SUB // group, body, 0)
-
-
-def put_rows(field, offset, north, south, rows, count):
-    unroll = largest(count // SUB, 9, 8, 4, 2, 1)
+                at = pl.multiple_of((chunk * per_chunk + q) * plane + offset + r + g * SUB, SUB)
+                turned = pltpu.roll(field[pl.ds(at, SUB), :], 2 * q + 2, 1)
+                made[g] = jnp.where(lane >= 2 * q + 1, turned, made[g])
+        for g in range(group):
+            out[chunk, pl.ds(pl.multiple_of(first + r + g * SUB, SUB), SUB), :] = made[g]
+        return carry
+
+    lax.fori_loop(0, plane // SUB // group, body, 0)
+
+
+def put_rows(field, offset, a_ref, b_ref, rows, begin, end):
+    unroll = largest((end - begin) // SUB, 9, 8, 4, 2, 1)
+    odd = lax.axis_index("lat") % 2
+    in_a = (1 - odd) * (rows - 1)
+    in_b = odd * (rows - 1)
 
     def body(i, carry):
         for u in range(unroll):
-            start = pl.multiple_of((i * unroll + u) * SUB, SUB)
+            start = pl.multiple_of(begin + (i * unroll + u) * SUB, SUB)
             at = start * rows + offset
-            if south is not None:
-                south[pl.ds(start, SUB), :] = field[pl.ds(at, SUB, stride=rows), :]
-            north[pl.ds(start, SUB), :] = field[pl.ds(at + rows - 1, SUB, stride=rows), :]
-        return carry
-
-    lax.fori_loop(0, count // SUB // unroll, body, 0)
-
-
-def first_rims(levels, tracers, rows, chunks, per_chunk, field, east, north, side, s_ref, n_ref, f, e, n, sems):
+            a_ref[pl.ds(start, SUB), :] = field[pl.ds(at + in_a, SUB, stride=rows), :]
+            b_ref[pl.ds(start, SUB), :] = field[pl.ds(at + in_b, SUB, stride=rows), :]
+        return carry
+
+    lax.fori_loop(0, (end - begin) // SUB // unroll, body, 0)
+
+
+def first_rims(levels, tracers, rows, chunks, per_chunk, field, east, north, side, a_ref, b_ref, f, e, n, sems):
     plane = tracers * rows
-    half = chunks * 2
-    size = levels * plane // half
     wind_copies = [
-        pltpu.make_async_copy(east, e, sems.at[half]),
-        pltpu.make_async_copy(north, n, sems.at[half + 1]),
+        pltpu.make_async_copy(east, e, sems.at[chunks]),
+        pltpu.make_async_copy(north, n, sems.at[chunks + 1]),
     ]
-    copies = [
-        pltpu.make_async_copy(field.at[pl.ds(i * size, size)], f.at[pl.ds(i * size, size)], sems.at[i])
-        for i in range(half)
-    ]
+    copies = []
+    for i in range(chunks):
+        part = pl.ds(i * per_chunk * plane, min(per_chunk, levels - i * per_chunk) * plane)
+        copies.append(pltpu.make_async_copy(field.at[part], f.at[part], sems.at[i]))
     for copy in wind_copies + copies:
         copy.start()
     wind_copies[0].wait()
-    put_rims(e, 0, levels, per_chunk, chunks, side, plane, rows)
+    for i in range(chunks):
+        put_rims(e, 0, levels, per_chunk, i, side, plane, rows)
     wind_copies[1].wait()
-    put_rows(n, 0, n_ref.at[pl.ds(levels * tracers, levels)], None, rows, levels)
+    winds = pl.ds(levels * tracers, levels)
+    put_rows(n, 0, a_ref.at[winds], b_ref.at[winds], rows, 0, levels)
+    for i in range(chunks):
+        copies[i].wait()
+        put_rims(f, 0, levels, per_chunk, i, side, 0, plane)
+        put_rows(
+            f, 0, a_ref, b_ref, rows, i * per_chunk * tracers, min((i + 1) * per_chunk, levels) * tracers
+        )
+
+
+def coefficients(levels, tracers, rows, per_chunk, unroll, east, north, mixing, west0, a0, b0, *refs):
+    outs, (e_buf, n_buf, m_buf, sems) = refs[:7], refs[7:]
+    plane = tracers * rows
+    halves = rows // SUB
+    lane, sub = lane_iota(), sub_iota()
+    copies = [
+        pltpu.make_async_copy(source, target, sems.at[i])
+        for i, (source, target) in enumerate(((east, e_buf), (north, n_buf), (mixing, m_buf)))
+    ]
+    for copy in copies:
+        copy.start()
     for copy in copies:
         copy.wait()
-    put_rims(f, 0, levels, per_chunk, chunks, side, 0, plane)
-    put_rows(f, 0, n_ref.at[pl.ds(0, levels * tracers)], s_ref, rows, levels * tracers)
+    place = lax.axis_index("lat")
+    even = jnp.full((1, LANES), place, jnp.int32) % 2 == 0
+    south_flag = (place > 0).astype(jnp.float32)
+    north_flag = (place < lax.axis_size("lat") - 1).astype(jnp.float32)
+    north_mask = jnp.where(sub == SUB - 1, north_flag, 1.0)
+
+    def level(k, pivots):
+        chunk, q = k // per_chunk, k % per_chunk
+        has_up = (k < levels - 1).astype(jnp.float32)
+        new, edge = [], None
+        for h in range(halves):
+            blk = pl.ds(pl.multiple_of(k * rows + h * SUB, SUB), SUB)
+            down, factor = pivots[h]
+            up = m_buf[blk, :] * has_up
+            inv = 1.0 / (1.0 + up + down - down * factor)
+            factor = up * inv
+            new.append((up, factor))
+            e, n = e_buf[blk, :], n_buf[blk, :]
+            side = pltpu.roll(west0[chunk, pl.ds(plane + h * SUB, SUB), :], LANES - 1 - 2 * q, 1)
+            w_in = jnp.minimum(jnp.where(lane == 0, side, pltpu.roll(e, 1, 1)), 0.0)
+            if h == 0:
+                row = pl.ds(levels * tracers + k, 1)
+                edge = jnp.where(even, b0[row, :], a0[row, :]) * south_flag
+            s_in = jnp.minimum(jnp.where(sub == 0, edge, pltpu.roll(n, 1, 0)), 0.0)
+            edge = n[SUB - 1 : SUB, :]
+            e_out, n_out = jnp.maximum(e, 0.0), jnp.maximum(n, 0.0)
+            from_n = n_out * inv
+            if h == halves - 1:
+                from_n = from_n * north_mask
+            stay = (1.0 - e_out + w_in - n_out + s_in) * inv
+            values = (stay, e_out * inv, -(w_in * inv), from_n, -(s_in * inv), down * inv, factor)
+            for out, value in zip(outs, values):
+                out[blk, :] = value
+        return tuple(new)
+
+    def body(b, carry):
+        for u in range(unroll):
+            carry = level(b * unroll + u, carry)
+        return carry
+
+    zero = jnp.zeros((SUB, LANES), jnp.float32)
+    lax.fori_loop(0, levels // unroll, body, ((zero, zero),) * halves)
 
 
 def step(levels, tracers, rows, chunks, per_chunk, unroll, first, *refs):
     refs = list(refs)
-    field, east, north, mixing, west0, south0 = refs[:6]
-    west_in, east_in, north_in, south_in = refs[6:10]
-    refs = refs[10:]
+    field, weights, (west_in, east_in, a_in, b_in) = refs[0], refs[1:7], refs[8:12]
+    above = refs[7]
+    refs = refs[12:]
     if first:
-        forcing, f_west, f_east, f_north, f_south = refs[:5]
+        forcing, f_west, f_east, f_a, f_b = refs[:5]
         refs = refs[5:]
     out = refs.pop(0)
     if first:
-        side_ref, s_ref, n_ref = refs[:3]
+        side_ref, a_ref, b_ref = refs[:3]
         refs = refs[3:]
-    buf, e_buf, n_buf, m_buf, above, rim, sems = refs
+    buf, rim, edges, sems = refs
 
     plane = tracers * rows
     halves = rows // SUB
     lane, sub = lane_iota(), sub_iota()
     blocks = levels // unroll
     flat = buf.reshape((levels * tracers + 2) * rows, LANES)
-    south_flag = (lax.axis_index("lat") > 0).astype(jnp.float32)
-    north_flag = (lax.axis_index("lat") < lax.axis_size("lat") - 1).astype(jnp.float32)
-    north_mask = jnp.where(sub == SUB - 1, north_flag, 1.0)
 
     def load(b):
         at = b * unroll * tracers
@@ -147,27 +204,36 @@
             buf.at[pl.ds(at + 1, unroll * tracers)], out.at[pl.ds(at, unroll * tracers)], sems.at[b]
         )
 
-    winds = [
-        pltpu.make_async_copy(source, target, sems.at[blocks + i])
-        for i, (source, target) in enumerate(((east, e_buf), (north, n_buf), (mixing, m_buf)))
-    ]
-    for copy in winds:
-        copy.start()
     for b in range(blocks):
         load(b).start()
 
-    def meet(target, from_west, from_east, source, count):
+    def meet(target, from_west, from_east, count):
         for chunk in range(chunks):
             for r in range(0, count, SUB):
-                a, b = pl.ds(target + r, SUB), pl.ds(source + r, SUB)
+                a, b = pl.ds(target + r, SUB), pl.ds(r, SUB)
                 turned = pltpu.roll(from_east[chunk, b, :], LANES - 2, 1)
                 rim[chunk, a, :] = jnp.where(lane % 2 == 1, from_west[chunk, b, :], turned)
 
-    meet(0, west_in, east_in, 0, plane)
+    even = jnp.full((SUB, LANES), lax.axis_index("lat"), jnp.int32) % 2 == 0
+
+    def pair(target, from_a, from_b, count):
+        repeat = largest(count // SUB, 9, 8, 4, 2, 1)
+
+        def body(i, carry):
+            for u in range(repeat):
+                at = pl.multiple_of((i * repeat + u) * SUB, SUB)
+                a, b = from_a[pl.ds(at, SUB), :], from_b[pl.ds(at, SUB), :]
+                edges[0, pl.ds(target + at, SUB), :] = jnp.where(even, a, b)
+                edges[1, pl.ds(target + at, SUB), :] = jnp.where(even, b, a)
+            return carry
+
+        lax.fori_loop(0, count // SUB // repeat, body, 0)
+
+    meet(0, west_in, east_in, plane)
+    pair(0, a_in, b_in, levels * tracers)
     if first:
-        meet(plane, f_west, f_east, 0, rows)
-    for copy in winds:
-        copy.wait()
+        meet(plane, f_west, f_east, rows)
+        pair(levels * tracers, f_a, f_b, levels)
 
     def stencil(source, at, rim_row, chunk, turn, edge_n, edge_s, co):
         values = []
@@ -188,53 +254,34 @@
             values.append((c0 * cell + ce * e) + (cw * w + cn * n) + cs * s)
         return values
 
-    def forward(k, carry):
+    def edge(side, row):
+        return edges[side, pl.ds(row, 1), :]
+
+    def forward(k, solved):
         chunk, q = k // per_chunk, k % per_chunk
         turn = LANES - 1 - 2 * q
-        has_up = (k < levels - 1).astype(jnp.float32)
-        solved, pivots = carry
-        co, new_pivots, edge = [], [], None
+        co = []
         for h in range(halves):
             blk = pl.ds(pl.multiple_of(k * rows + h * SUB, SUB), SUB)
-            down, factor = pivots[h]
-            up = m_buf[blk, :] * has_up
-            inv = 1.0 / (1.0 + up + down - down * factor)
-            factor = up * inv
-            new_pivots.append((up, factor))
-            above[blk, :] = factor
-            e, n = e_buf[blk, :], n_buf[blk, :]
-            side = pltpu.roll(west0[chunk, pl.ds(plane + h * SUB, SUB), :], turn, 1)
-            w_in = jnp.minimum(jnp.where(lane == 0, side, pltpu.roll(e, 1, 1)), 0.0)
-            if h == 0:
-                edge = south0[pl.ds(levels * tracers + k, 1), :] * south_flag
-            s_in = jnp.minimum(jnp.where(sub == 0, edge, pltpu.roll(n, 1, 0)), 0.0)
-            edge = n[SUB - 1 : SUB, :]
-            e_out, n_out = jnp.maximum(e, 0.0), jnp.maximum(n, 0.0)
-            from_n = n_out * inv
-            if h == halves - 1:
-                from_n = from_n * north_mask
-            stay = (1.0 - e_out + w_in - n_out + s_in) * inv
-            co.append((stay, e_out * inv, -(w_in * inv), from_n, -(s_in * inv), down * inv))
-        extra = None
+            co.append([weight[blk, :] for weight in weights])
         if first:
+            row = levels * tracers + k
             extra = stencil(
-                forcing, k * rows + SUB, plane, chunk, turn,
-                f_north[pl.ds(k, 1), :], f_south[pl.ds(k, 1), :], co,
+                forcing, k * rows + SUB, plane, chunk, turn, edge(0, row), edge(1, row), co
             )
         new = []
         for t in range(tracers):
-            at = (k + 1) * plane - plane + (t + 1) * rows
-            values = stencil(
-                flat, at, t * rows, chunk, turn,
-                north_in[pl.ds(k * tracers + t, 1), :], south_in[pl.ds(k * tracers + t, 1), :], co,
-            )
+            at = k * plane + (t + 1) * rows
+            row = k * tracers + t
+            values = stencil(flat, at, t * rows, chunk, turn, edge(0, row), edge(1, row), co)
             for h in range(halves):
-                value = values[h] + co[h][5] * solved[t * halves + h]
+                value = values[h]
                 if first:
                     value = value + extra[h]
+                value = value + co[h][5] * solved[t * halves + h]
                 new.append(value)
                 flat[pl.ds(pl.multiple_of(at + h * SUB, SUB), SUB), :] = value
-        return tuple(new), tuple(new_pivots)
+        return tuple(new)
 
     def forward_block(b, carry):
         load(b).wait()
@@ -244,7 +291,7 @@
 
     zero = jnp.zeros((SUB, LANES), jnp.float32)
     zeros = (zero,) * (tracers * halves)
-    lax.fori_loop(0, blocks, forward_block, (zeros, ((zero, zero),) * halves))
+    lax.fori_loop(0, blocks, forward_block, zeros)
 
     def backward(k, carry):
         new = []
@@ -266,8 +313,9 @@
 
     lax.fori_loop(0, blocks, backward_block, zeros)
     if first:
-        put_rims(flat, rows, levels, per_chunk, chunks, side_ref, 0, plane)
-        put_rows(flat, rows, n_ref, s_ref, rows, levels * tracers)
+        for chunk in range(chunks):
+            put_rims(flat, rows, levels, per_chunk, chunk, side_ref, 0, plane)
+        put_rows(flat, rows, a_ref, b_ref, rows, 0, levels * tracers)
     for b in range(blocks):
         store(b).wait()
 
@@ -340,14 +388,13 @@
 
 def soundings(
     levels, rows, group_rows, cap, chunks, per_chunk, block,
-    received, sums, forcing, side_ref, s_ref, n_ref, back, arrived, table, scaled
+    received, sums, forcing, side_ref, a_ref, b_ref, back, arrived, table, scaled
 ):
     lane = lane_iota()
     parts, _, width = arrived.shape
     halves = rows // SUB
     keys = halves * LANES
     groups = LANES // cap
-    senders = width // cap
 
     def unpack(c, carry):
         part, col = c // (width // LANES), c % (width // LANES)
@@ -402,12 +449,8 @@
         error = arrived[j, pl.ds(levels + 2, 1), :]
         residual = jnp.where(col >= 0, (modelled - observed) / error, 0.0)
         scaled[pl.ds(j, 1), :] = residual / error
-        for i in range(senders):
-            at = i * cap
-            piece = residual[:, at // LANES * LANES : at // LANES * LANES + LANES]
-            if at % LANES:
-                piece = pltpu.roll(piece, LANES - at % LANES, 1)
-            back[pl.ds(j * senders + i, 1), :] = piece
+        for c in range(width // LANES):
+            back[pl.ds(j * (width // LANES) + c, 1), :] = residual[:, c * LANES : (c + 1) * LANES]
 
     zeros = jnp.zeros((SUB, LANES), jnp.float32)
     forcing[pl.ds(0, SUB), :] = zeros
@@ -429,34 +472,37 @@
                     k * SUB : (k + 1) * SUB, h * LANES : (h + 1) * LANES
                 ]
 
-    put_rims(forcing, SUB, levels, per_chunk, chunks, side_ref, 0, rows)
-    put_rows(forcing, SUB, n_ref, s_ref, rows, levels)
-
-
-def unpack_residual(cap, arrived, out):
+    for chunk in range(chunks):
+        put_rims(forcing, SUB, levels, per_chunk, chunk, side_ref, 0, rows)
+    put_rows(forcing, SUB, a_ref, b_ref, rows, 0, levels)
+
+
+def unpack_residual(cap, gathered, out):
     lane = lax.broadcasted_iota(jnp.int32, (1, LANES), 1)
     groups = LANES // cap
+    me = lax.axis_index("lon") * lax.axis_size("lat") + lax.axis_index("lat")
+    mine, place = me // groups, me % groups
     for row in range(out.shape[0]):
         made = None
         for g in range(groups):
-            piece = arrived[pl.ds(row * groups + g, 1), :]
-            if g:
-                piece = pltpu.roll(piece, g * cap, 1)
+            piece = gathered[row * groups + g, pl.ds(mine, 1), :]
+            piece = pltpu.roll(piece, (g - place + groups) % groups * cap, 1)
             made = piece if made is None else jnp.where(lane >= g * cap, piece, made)
         out[pl.ds(row, 1), :] = made
 
 
-def shift(value, axis, by):
-    count = lax.axis_size(axis)
-    return lax.ppermute(value, axis, [(i, (i + by) % count) for i in range(count)])
-
-
-def exchange(side_rim, south_rim, north_rim):
+def exchange(side_rim, a_rim, b_rim):
+    lons, lats = lax.axis_size("lon"), lax.axis_size("lat")
+
+    def partner(j, odd):
+        other = j + 1 if j % 2 == odd else j - 1
+        return other if 0 <= other < lats else j
+
     return (
-        shift(side_rim, "lon", 1),
-        shift(side_rim, "lon", -1),
-        shift(south_rim, "lat", -1),
-        shift(north_rim, "lat", 1),
+        lax.ppermute(side_rim, "lon", [(i, (i + 1) % lons) for i in range(lons)]),
+        lax.ppermute(side_rim, "lon", [((i + 1) % lons, i) for i in range(lons)]),
+        lax.ppermute(a_rim, "lat", [(j, partner(j, 0)) for j in range(lats)]),
+        lax.ppermute(b_rim, "lat", [(j, partner(j, 1)) for j in range(lats)]),
     )
 
 
@@ -480,7 +526,7 @@
 
     packed = call(
         functools.partial(pack, levels, group_rows, cap),
-        [ANY] * 4, f32(bricks, group_rows, LANES), VMEM,
+        [HBM] * 4, f32(bricks, group_rows, LANES), VMEM,
         (
             vmem(levels * per_level, LANES), pltpu.VMEM((per_level, LANES), jnp.int32),
             vmem(per_level, LANES), vmem(per_level, LANES), vmem(groups * group_rows, LANES), dma((4,)),
@@ -493,10 +539,10 @@
     east, north, mix = flat(wind_east), flat(wind_north), flat(mixing)
     rims = call(
         functools.partial(first_rims, levels, tracers, rows, chunks, per_chunk),
-        [ANY] * 3,
-        (f32(chunks, plane + rows, LANES), f32(levels * tracers, LANES), f32(levels * tracers + levels, LANES)),
+        [HBM] * 3,
+        (f32(chunks, plane + rows, LANES),) + (f32(levels * tracers + levels, LANES),) * 2,
         (VMEM,) * 3,
-        (vmem(levels * plane, LANES), vmem(levels * rows, LANES), vmem(levels * rows, LANES), dma((chunks * 2 + 2,))),
+        (vmem(levels * plane, LANES), vmem(levels * rows, LANES), vmem(levels * rows, LANES), dma((chunks + 2,))),
         10, field_bytes, 2 * field_bytes, "first_rims",
     )(flat(adjoint), east, north)
     start_rims = exchange(*rims)
@@ -505,7 +551,7 @@
     sum_block = largest(levels, 12, 8)
     sums = call(
         functools.partial(tracer_sum, sum_block),
-        [ANY], jax.ShapeDtypeStruct((2, levels * SUB, rows // SUB * cols), jnp.bfloat16), VMEM,
+        [HBM], jax.ShapeDtypeStruct((2, levels * SUB, rows // SUB * cols), jnp.bfloat16), VMEM,
         (vmem(levels, tracers, rows, cols), dma((levels // sum_block,))),
         10, field_bytes // 4, field_bytes, "tracer_sum",
     )(concentration)
@@ -517,7 +563,7 @@
         [VMEM] * 2,
         (
             f32(levels * rows + 2 * SUB, LANES), f32(chunks, rows, LANES), f32(levels, LANES), f32(levels, LANES),
-            f32(bricks, LANES),
+            f32(per_level, LANES),
         ),
         (VMEM,) * 5,
         (
@@ -525,37 +571,40 @@
             pltpu.VMEM((parts, width, rows // SUB * LANES), jnp.bfloat16),
             vmem(max(parts, SUB), width),
         ),
-        16, field_bytes * 8, field_bytes, "soundings",
+        6, field_bytes * 8, field_bytes, "soundings",
     )(received, sums)
     forcing_rims = exchange(*rims)
 
-    unroll = largest(levels, 4, 3, 2, 1)
+    unroll = largest(levels, 8, 4, 3, 2, 1)
+    weights = call(
+        functools.partial(coefficients, levels, tracers, rows, per_chunk, unroll),
+        [HBM] * 3 + [VMEM] * 3, (f32(levels * rows, LANES),) * 7, (VMEM,) * 7,
+        (vmem(levels * rows, LANES),) * 3 + (dma((3,)),),
+        4, field_bytes, field_bytes, "coefficients",
+    )(east, north, mix, start_rims[0], start_rims[2], start_rims[3])
 
     def advance(value, first, *operands):
-        outs, specs = (f32(*value.shape),), (ANY,)
+        outs, specs = (f32(*value.shape),), (HBM,)
         if first:
             outs += (f32(chunks, plane, LANES), f32(levels * tracers, LANES), f32(levels * tracers, LANES))
             specs += (VMEM,) * 3
         return call(
             functools.partial(step, levels, tracers, rows, chunks, per_chunk, unroll, first),
-            [ANY] * 4 + [VMEM] * (2 + len(operands)), outs, specs,
+            [HBM] + [VMEM] * (7 + len(operands)), outs, specs,
             (
-                vmem(levels * tracers + 2, rows, LANES), vmem(levels * rows, LANES), vmem(levels * rows, LANES),
-                vmem(levels * rows, LANES), vmem(levels * rows, LANES), vmem(chunks, plane + rows, LANES),
-                dma((levels // unroll + 3,)),
+                vmem(levels * tracers + 2, rows, LANES), vmem(chunks, plane + rows, LANES),
+                vmem(2, levels * tracers + levels, LANES), dma((levels // unroll,)),
             ),
-            12, field_bytes * 8, field_bytes * 2, "step",
-        )(value, east, north, mix, start_rims[0], start_rims[3], *operands)
+            8, field_bytes * 8, field_bytes * 2, "step",
+        )(value, *weights, *operands)
 
     stepped, *rims = advance(field, True, *start_rims, forcing, *forcing_rims)
     (result,) = advance(stepped, False, *exchange(*rims))
 
-    returned = lax.all_to_all(
-        back.reshape(bricks, 1, LANES), ("lon", "lat"), split_axis=0, concat_axis=0, tiled=True
-    )
+    gathered = lax.all_gather(back, ("lon", "lat"))
     residual = call(
         functools.partial(unpack_residual, cap), [VMEM], f32(per_level, LANES), VMEM, (), 2, 10, 10000, "residual",
-    )(returned.reshape(bricks, LANES))
+    )(gathered)
     return result.reshape(adjoint.shape), residual.reshape(sound_col.shape)
 
 

time: 84.4 us -> 133 us (1.58)
  blocking collectives: 12.8 us -> 69.3 us
  waiting for transfers between devices: 9.24 us -> 0.94 us
    all_gather x0 -> x1, blocking collectives: none -> 69.3 us  [per_device(): gathered = lax.all_gather(back, ('lon', 'lat'))]
    all_to_all x1 -> x0, blocking collectives: 12.8 us -> none  [per_device(): lax.all_to_all(back.reshape(bricks, 1, LANES), ('lon', 'lat'), split_axis...]
    ppermute x12, waiting for transfers between devices: 9.24 us -> 0.93 us  [the longest x3 0.91 us: exchange(): lax.ppermute(side_rim, 'lon', [(i, (i + 1) % lons) for i in range(lons)])]
    pallas_call x2 -> x3, Pallas kernels: 2.42 us -> 5.1 us  [the longest x1 2.68 us: per_device(): call(functools.partial(coefficients, levels, tracers, rows, per_chunk, un...]
    pallas_call x2, Pallas kernels: 21 us -> 18.3 us  [advance(): call(functools.partial(step, levels, tracers, rows, chunks, per_chunk, un...]
  transfers between devices with their start and end apart: 13 -> 13, of which waited for: 3 -> 1; matrix products, arithmetic and copies ran while one was open for 0% -> 0% of each run, Pallas kernels for 10% -> 8%
where the time goes in v1:
time: 133 us
  blocking collectives  69.3 us (52%)
  Pallas kernels  30.6 us (23%)
  starting transfers between devices  21.2 us (16%)
  local copies, waits for them, and re-layouts  9.82 us (7%)
    all_gather x1, blocking collectives, per_device(): gathered = lax.all_gather(back, ('lon', 'lat'))  69.3 us
    pallas_call x2, Pallas kernels, advance(): call(functools.partial(step, levels, tracers, rows, chunks, per_chunk, un...  18.3 us
    unnamed x24, local copies, waits for them, and re-layouts  9.82 us
    all_to_all x1, starting transfers between devices, per_device(): lax.all_to_all(packed, ('lon', 'lat'), split_axis=0, concat_axis=0, tiled...  7.3 us
    ppermute x3, starting transfers between devices, exchange(): lax.ppermute(a_rim, 'lat', [(j, partner(j, 0)) for j in range(lats)])  6.7 us
    pallas_call x1, Pallas kernels, per_device(): call(functools.partial(first_rims, levels, tracers, rows, chunks, per_chu...  3.85 us
    ppermute x3, starting transfers between devices, exchange(): lax.ppermute(side_rim, 'lon', [((i + 1) % lons, i) for i in range(lons)])  3.8 us
    ppermute x3, starting transfers between devices, exchange(): lax.ppermute(b_rim, 'lat', [(j, partner(j, 1)) for j in range(lats)])  2.94 us
  transfers between devices with their start and end apart: 13, of which 1 were waited for; matrix products, arithmetic and copies ran while one was open for 0% of the time, Pallas kernels for 8%

profile of v1, /device:TPU:0, one launch (start us, length us, event | category | flops | bytes accessed | tf_op | source)
XLA Modules:
  0.0 132.7 jit_solution(15094154030719399473)
XLA Ops:
  0.6 0.0 copy-start.8
  0.6 1.0 copy-done.8
  1.6 0.0 copy-start.9
  1.6 0.7 copy-done.9
  2.3 0.0 copy-start.10
  2.3 0.7 copy-done.10
  3.0 0.0 copy-start.11
  3.0 0.7 copy-done.11
  3.7 1.7 %pack.1 = f32[32,24,128]{2,1,0:T(8,128)} custom-call(f32[576,128]{1,0:T(8,128)S(1)} %bitcast.20, s32[8,128]{1,0:T(8,128)S(1)} %bitcast.21, f32[8,128]{1,0:T(8,128)S(1)} %bitcast.22, f32[8,128]{1,0:T(8,128)S(1)} %bitcast.23), custom_call_target="tpu_custom_call" | custom-call | flops 10 | bytes 800000 | tf_op jit(solution)/shard_map/pack/pallas_call | solution.py:527
  5.4 7.3 %all-to-all-start = ((f32[32,24,128]{2,1,0:T(8,128)}), f32[32,24,128]{2,1,0:T(8,128)S(1)}, u32[]{:S(2)}, u32[]{:S(2)}) async-start(f32[32,24,128]{2,1,0:T(8,128)} %pack.1), calls=%async_computation | async-start | bytes 786432 | tf_op jit(solution)/shard_map/all_to_all | solution.py:536
  12.7 0.0 copy-start
  12.7 2.3 %copy-done = f32[72,8,16,128]{3,2,1,0:T(8,128)S(1)} copy-done((f32[72,8,16,128]{3,2,1,0:T(8,128)S(1)}, f32[72,8,16,128]{3,2,1,0:T(8,128)}, u32[]{:S(2)}) %copy-start) | copy-done | bytes 4718616
  15.0 0.0 copy-start.3
  15.0 1.1 copy-done.3
  16.1 0.0 copy-start.5
  16.1 1.1 copy-done.5
  17.1 0.0 copy-start.2
  17.1 0.0 copy-start.4
  17.2 0.0 copy-start.6
  17.2 0.0 copy-start.7
  17.2 3.8 %first_rims.1 = (f32[2,144,128]{2,1,0:T(8,128)}, f32[648,128]{1,0:T(8,128)}, f32[648,128]{1,0:T(8,128)}) custom-call(f32[9216,128]{1,0:T(8,128)S(1)} %bitcast.12, f32[1152,128]{1,0:T(8,128)S(1)} %bitcast.14, f32[1152,128]{1,0:T(8,128)S(1)} %bitcast.16), custom_call_target="tpu_custom_call" | custom-call | flops 4718592 | bytes 9437184 | tf_op jit(solution)/shard_map/first_rims/pallas_call | solution.py:540
  21.0 1.8 %collective-permute-start.1 = (f32[648,128]{1,0:T(8,128)}, f32[648,128]{1,0:T(8,128)S(1)}, u32[]{:S(2)}, u32[]{:S(2)}) collective-permute-start(f32[648,128]{1,0:T(8,128)} %get-tuple-element.22), channel_id=1, source_target_pairs={{0,1},{1,0},{2,3},{3,2},{4,5},{5,4},{6,7},{7,6},{8,9},{9,8},{10,11... | collective-permute-start | bytes 995336 | tf_op jit(solution)/shard_map/ppermute | solution.py:504
  22.9 1.6 %collective-permute-start.2 = (f32[648,128]{1,0:T(8,128)}, f32[648,128]{1,0:T(8,128)S(1)}, u32[]{:S(2)}, u32[]{:S(2)}) collective-permute-start(f32[648,128]{1,0:T(8,128)} %get-tuple-element.23), channel_id=1, source_target_pairs={{0,0},{1,2},{2,1},{3,3},{4,4},{5,6},{6,5},{7,7},{8,8},{9,10},{10,9... | collective-permute-start | bytes 995336 | tf_op jit(solution)/shard_map/ppermute | solution.py:505
  24.5 0.0 collective-permute-start
  24.5 2.6 %collective-permute-start.3 = (f32[2,144,128]{2,1,0:T(8,128)}, f32[2,144,128]{2,1,0:T(8,128)}, u32[]{:S(2)}, u32[]{:S(2)}) collective-permute-start(f32[2,144,128]{2,1,0:T(8,128)} %get-tuple-element.21), channel_id=1, source_target_pairs={{4,0},{8,4},{12,8},{16,12},{20,16},{24,20},{28,24},{0,28},{5,1},{9... | collective-permute-start | bytes 442376 | tf_op jit(solution)/shard_map/ppermute | solution.py:503
  27.1 0.0 copy-done.2
  27.1 0.7 tracer_sum.1.sums
  27.8 0.0 all-to-all-done.received
  27.9 2.7 %soundings.1 = (f32[1168,128]{1,0:T(8,128)S(1)}, f32[2,16,128]{2,1,0:T(8,128)S(1)}, f32[72,128]{1,0:T(8,128)S(1)}, f32[72,128]{1,0:T(8,128)S(1)}, f32[8,128]{1,0:T(8,128)S(1)}) custom-call(f32[32,24,128]{2,1,0:T(8,128)S(1)} %all-to-all-done.received, bf16[2,576,256]{2,1,0:T(8,128)(2,1)S(1)} %tracer_sum.1.sums), custom_call_target="tpu_custom_call" | custom-call | flops 37748736 | bytes 4718592 | tf_op jit(solution)/shard_map/soundings/pallas_call | solution.py:561
  30.5 3.4 %collective-permute-start.6 = (f32[72,128]{1,0:T(8,128)S(1)}, f32[72,128]{1,0:T(8,128)S(1)}, u32[]{:S(2)}, u32[]{:S(2)}) collective-permute-start(f32[72,128]{1,0:T(8,128)S(1)} %get-tuple-element.33), channel_id=1, source_target_pairs={{0,1},{1,0},{2,3},{3,2},{4,5},{5,4},{6,7},{7,6},{8,9},{9,8},{10,11... | collective-permute-start | bytes 110600 | tf_op jit(solution)/shard_map/ppermute | solution.py:504
  33.9 0.0 collective-permute-done.west0.refs_8_
  33.9 0.7 collective-permute-start.7
  34.6 0.0 collective-permute-done.1.a0.refs_10_
  34.6 0.1 collective-permute-start.5
  34.7 0.0 collective-permute-done.2.b0.refs_11_
  34.7 0.5 collective-permute-start.4
  35.2 0.0 copy-done.4
  35.2 0.0 copy-done.6
  35.2 0.0 copy-done.7
  35.2 2.7 %coefficients.1 = (f32[1152,128]{1,0:T(8,128)S(1)}, f32[1152,128]{1,0:T(8,128)S(1)}, f32[1152,128]{1,0:T(8,128)S(1)}, f32[1152,128]{1,0:T(8,128)S(1)}, f32[1152,...) custom-call(f32[1152,128]{1,0:T(8,128)S(1)} %bitcast.15, f32[1152,128]{1,0:T(8,128)S(1)} %bitcast.17, ...), custom_call_target="tpu_custom_call" | custom-call | flops 4718592 | bytes 4718592 | tf_op jit(solution)/shard_map/coefficients/pallas_call | solution.py:579
  37.9 0.0 collective-permute-done.3.refs_9_
  37.9 0.0 collective-permute-done.5.refs_14_
  37.9 0.9 collective-permute-done.4.refs_13_
  38.8 0.0 collective-permute-done.6.refs_15_
  38.8 0.0 collective-permute-done.7.refs_16_
  38.8 0.0 copy-start.1
  38.8 2.3 %copy-done.1 = f32[72,8,16,128]{3,2,1,0:T(8,128)S(1)} copy-done((f32[72,8,16,128]{3,2,1,0:T(8,128)S(1)}, f32[72,8,16,128]{3,2,1,0:T(8,128)}, u32[]{:S(2)}) %copy-start.1) | copy-done | bytes 4718616
  41.1 10.3 %step.2 = (f32[576,16,128]{2,1,0:T(8,128)S(1)}, f32[2,128,128]{2,1,0:T(8,128)S(1)}, f32[576,128]{1,0:T(8,128)S(1)}, f32[576,128]{1,0:T(8,128)S(1)}) custom-call(f32[576,16,128]{2,1,0:T(8,128)S(1)} %bitcast.13, f32[1152,128]{1,0:T(8,128)S(1)} %get-tuple-element.24.refs_1_, f32[1152,128]{1,0:T(8,128)S(1)} %get-tuple-element.25.refs_2_, ...), custom_call_target="tpu_custom_call" | custom-call | flops 37748736 | bytes 9437184 | tf_op jit(solution)/shard_map/step/pallas_call | solution.py:591
  51.4 1.5 %collective-permute-start.10 = (f32[576,128]{1,0:T(8,128)S(1)}, f32[576,128]{1,0:T(8,128)S(1)}, u32[]{:S(2)}, u32[]{:S(2)}) collective-permute-start(f32[576,128]{1,0:T(8,128)S(1)} %get-tuple-element.37), channel_id=1, source_target_pairs={{0,1},{1,0},{2,3},{3,2},{4,5},{5,4},{6,7},{7,6},{8,9},{9,8},{10,11... | collective-permute-start | bytes 884744 | tf_op jit(solution)/shard_map/ppermute | solution.py:504
  52.9 0.7 collective-permute-start.11
  53.6 1.1 collective-permute-start.9
  54.7 0.0 collective-permute-start.8
  54.7 69.3 %all-gather = f32[256,128]{1,0:T(8,128)S(1)} all-gather(f32[8,128]{1,0:T(8,128)S(1)} %get-tuple-element.39), channel_id=2, replica_groups=mesh['lon'=8,'lat'=4] {'lon','lat'}, dimensions={0}, use_global_device_ids=true | all-gather | bytes 135168 | tf_op jit(solution)/shard_map/all_gather | solution.py:604
  124.0 0.7 residual.1
  124.7 0.0 collective-permute-done.9.refs_9_
  124.7 0.0 collective-permute-done.8.refs_8_
  124.7 0.0 collective-permute-done.10.refs_10_
  124.7 0.0 collective-permute-done.11.refs_11_
  124.7 8.0 %step.3 = f32[576,16,128]{2,1,0:T(8,128)} custom-call(f32[576,16,128]{2,1,0:T(8,128)S(1)} %get-tuple-element.35.refs_0_, f32[1152,128]{1,0:T(8,128)S(1)} %get-tuple-element.24.refs_1_, f32[1152,128]{1,0:T(8,128)S(1)} %get-tuple-element.25.refs_2_, f32[1152,128]{1,0:T(8,128)S(1)} %get-tuple-element.26.refs_3_, f32[1152,128]{1,0:T(8,128)S(1)} %get-tuple-element.27.refs_4_, ...), custom_call_target="tpu_custom_call" | custom-call | flops 37748736 | bytes 9437184 | tf_op jit(solution)/shard_map/step/pallas_call | solution.py:591
Async XLA Ops:
  0.6 1.0 copy-start.8
  1.6 0.7 copy-start.9
  2.3 0.7 copy-start.10
  3.0 0.7 copy-start.11
  5.4 22.5 %all-to-all-start = ((f32[32,24,128]{2,1,0:T(8,128)}), f32[32,24,128]{2,1,0:T(8,128)S(1)}, u32[]{:S(2)}, u32[]{:S(2)}) async-start(f32[32,24,128]{2,1,0:T(8,128)} %pack.1), calls=%async_computation | async-start | bytes 786432 | tf_op jit(solution)/shard_map/all_to_all | solution.py:536
  12.7 2.3 %copy-start = (f32[72,8,16,128]{3,2,1,0:T(8,128)S(1)}, f32[72,8,16,128]{3,2,1,0:T(8,128)}, u32[]{:S(2)}) copy-start(f32[72,8,16,128]{3,2,1,0:T(8,128)} %param.10) | copy-start | bytes 14155780
  15.0 1.1 copy-start.3
  16.1 1.1 copy-start.5
  17.1 10.0 %copy-start.2 = (f32[72,8,16,128]{3,2,1,0:T(8,128)S(1)}, f32[72,8,16,128]{3,2,1,0:T(8,128)}, u32[]{:S(2)}) copy-start(f32[72,8,16,128]{3,2,1,0:T(8,128)} %concentration.1) | copy-start | bytes 14155780
  17.1 18.0 %copy-start.4 = (f32[72,16,128]{2,1,0:T(8,128)S(1)}, f32[72,16,128]{2,1,0:T(8,128)}, u32[]{:S(2)}) copy-start(f32[72,16,128]{2,1,0:T(8,128)} %param.11) | copy-start | bytes 1769476
  17.2 18.0 %copy-start.6 = (f32[72,16,128]{2,1,0:T(8,128)S(1)}, f32[72,16,128]{2,1,0:T(8,128)}, u32[]{:S(2)}) copy-start(f32[72,16,128]{2,1,0:T(8,128)} %param.12) | copy-start | bytes 1769476
  17.2 18.0 %copy-start.7 = (f32[72,16,128]{2,1,0:T(8,128)S(1)}, f32[72,16,128]{2,1,0:T(8,128)}, u32[]{:S(2)}) copy-start(f32[72,16,128]{2,1,0:T(8,128)} %param.13) | copy-start | bytes 1769476
  21.0 13.6 %collective-permute-start.1 = (f32[648,128]{1,0:T(8,128)}, f32[648,128]{1,0:T(8,128)S(1)}, u32[]{:S(2)}, u32[]{:S(2)}) collective-permute-start(f32[648,128]{1,0:T(8,128)} %get-tuple-element.22), channel_id=1, source_target_pairs={{0,1},{1,0},{2,3},{3,2},{4,5},{5,4},{6,7},{7,6},{8,9},{9,8},{10,11... | collective-permute-start | bytes 995336 | tf_op jit(solution)/shard_map/ppermute | solution.py:504
  22.9 11.8 %collective-permute-start.2 = (f32[648,128]{1,0:T(8,128)}, f32[648,128]{1,0:T(8,128)S(1)}, u32[]{:S(2)}, u32[]{:S(2)}) collective-permute-start(f32[648,128]{1,0:T(8,128)} %get-tuple-element.23), channel_id=1, source_target_pairs={{0,0},{1,2},{2,1},{3,3},{4,4},{5,6},{6,5},{7,7},{8,8},{9,10},{10,9... | collective-permute-start | bytes 995336 | tf_op jit(solution)/shard_map/ppermute | solution.py:505
  24.5 9.4 %collective-permute-start = (f32[2,144,128]{2,1,0:T(8,128)}, f32[2,144,128]{2,1,0:T(8,128)}, u32[]{:S(2)}, u32[]{:S(2)}) collective-permute-start(f32[2,144,128]{2,1,0:T(8,128)} %get-tuple-element.21), channel_id=1, source_target_pairs={{0,4},{4,8},{8,12},{12,16},{16,20},{20,24},{24,28},{28,0},{1,5},{5... | collective-permute-start | bytes 442376 | tf_op jit(solution)/shard_map/ppermute | solution.py:502
  24.5 13.4 %collective-permute-start.3 = (f32[2,144,128]{2,1,0:T(8,128)}, f32[2,144,128]{2,1,0:T(8,128)}, u32[]{:S(2)}, u32[]{:S(2)}) collective-permute-start(f32[2,144,128]{2,1,0:T(8,128)} %get-tuple-element.21), channel_id=1, source_target_pairs={{4,0},{8,4},{12,8},{16,12},{20,16},{24,20},{28,24},{0,28},{5,1},{9... | collective-permute-start | bytes 442376 | tf_op jit(solution)/shard_map/ppermute | solution.py:503
  30.5 8.2 %collective-permute-start.6 = (f32[72,128]{1,0:T(8,128)S(1)}, f32[72,128]{1,0:T(8,128)S(1)}, u32[]{:S(2)}, u32[]{:S(2)}) collective-permute-start(f32[72,128]{1,0:T(8,128)S(1)} %get-tuple-element.33), channel_id=1, source_target_pairs={{0,1},{1,0},{2,3},{3,2},{4,5},{5,4},{6,7},{7,6},{8,9},{9,8},{10,11... | collective-permute-start | bytes 110600 | tf_op jit(solution)/shard_map/ppermute | solution.py:504
  33.9 4.9 %collective-permute-start.7 = (f32[72,128]{1,0:T(8,128)S(1)}, f32[72,128]{1,0:T(8,128)S(1)}, u32[]{:S(2)}, u32[]{:S(2)}) collective-permute-start(f32[72,128]{1,0:T(8,128)S(1)} %get-tuple-element.34), channel_id=1, source_target_pairs={{0,0},{1,2},{2,1},{3,3},{4,4},{5,6},{6,5},{7,7},{8,8},{9,10},{10,9... | collective-permute-start | bytes 110600 | tf_op jit(solution)/shard_map/ppermute | solution.py:505
  34.6 3.3 %collective-permute-start.5 = (f32[2,16,128]{2,1,0:T(8,128)S(1)}, f32[2,16,128]{2,1,0:T(8,128)S(1)}, u32[]{:S(2)}, u32[]{:S(2)}) collective-permute-start(f32[2,16,128]{2,1,0:T(8,128)S(1)} %get-tuple-element.32), channel_id=1, source_target_pairs={{4,0},{8,4},{12,8},{16,12},{20,16},{24,20},{28,24},{0,28},{5,1},{9... | collective-permute-start | bytes 49160 | tf_op jit(solution)/shard_map/ppermute | solution.py:503
  34.7 4.1 %collective-permute-start.4 = (f32[2,16,128]{2,1,0:T(8,128)S(1)}, f32[2,16,128]{2,1,0:T(8,128)S(1)}, u32[]{:S(2)}, u32[]{:S(2)}) collective-permute-start(f32[2,16,128]{2,1,0:T(8,128)S(1)} %get-tuple-element.32), channel_id=1, source_target_pairs={{0,4},{4,8},{8,12},{12,16},{16,20},{20,24},{24,28},{28,0},{1,5},{5... | collective-permute-start | bytes 49160 | tf_op jit(solution)/shard_map/ppermute | solution.py:502
  38.8 2.3 %copy-start.1 = (f32[72,8,16,128]{3,2,1,0:T(8,128)S(1)}, f32[72,8,16,128]{3,2,1,0:T(8,128)}, u32[]{:S(2)}) copy-start(f32[72,8,16,128]{3,2,1,0:T(8,128)} %param.10) | copy-start | bytes 14155780
  51.4 73.2 %collective-permute-start.10 = (f32[576,128]{1,0:T(8,128)S(1)}, f32[576,128]{1,0:T(8,128)S(1)}, u32[]{:S(2)}, u32[]{:S(2)}) collective-permute-start(f32[576,128]{1,0:T(8,128)S(1)} %get-tuple-element.37), channel_id=1, source_target_pairs={{0,1},{1,0},{2,3},{3,2},{4,5},{5,4},{6,7},{7,6},{8,9},{9,8},{10,11... | collective-permute-start | bytes 884744 | tf_op jit(solution)/shard_map/ppermute | solution.py:504
  52.9 71.7 %collective-permute-start.11 = (f32[576,128]{1,0:T(8,128)S(1)}, f32[576,128]{1,0:T(8,128)S(1)}, u32[]{:S(2)}, u32[]{:S(2)}) collective-permute-start(f32[576,128]{1,0:T(8,128)S(1)} %get-tuple-element.38), channel_id=1, source_target_pairs={{0,0},{1,2},{2,1},{3,3},{4,4},{5,6},{6,5},{7,7},{8,8},{9,10},{10,9... | collective-permute-start | bytes 884744 | tf_op jit(solution)/shard_map/ppermute | solution.py:505
  53.6 71.1 %collective-permute-start.9 = (f32[2,128,128]{2,1,0:T(8,128)S(1)}, f32[2,128,128]{2,1,0:T(8,128)S(1)}, u32[]{:S(2)}, u32[]{:S(2)}) collective-permute-start(f32[2,128,128]{2,1,0:T(8,128)S(1)} %get-tuple-element.36), channel_id=1, source_target_pairs={{4,0},{8,4},{12,8},{16,12},{20,16},{24,20},{28,24},{0,28},{5,1},{9... | collective-permute-start | bytes 393224 | tf_op jit(solution)/shard_map/ppermute | solution.py:503
  54.7 70.0 %collective-permute-start.8 = (f32[2,128,128]{2,1,0:T(8,128)S(1)}, f32[2,128,128]{2,1,0:T(8,128)S(1)}, u32[]{:S(2)}, u32[]{:S(2)}) collective-permute-start(f32[2,128,128]{2,1,0:T(8,128)S(1)} %get-tuple-element.36), channel_id=1, source_target_pairs={{0,4},{4,8},{8,12},{12,16},{16,20},{20,24},{24,28},{28,0},{1,5},{5... | collective-permute-start | bytes 393224 | tf_op jit(solution)/shard_map/ppermute | solution.py:502

commit v2 on v1

--- a/solution.py
+++ b/solution.py
@@ -29,6 +29,10 @@
 
 def largest(count, *choices):
     return next(u for u in choices if count % u == 0)
+
+
+def in_hbm(x):
+    return pltpu.with_memory_space_constraint(x, pltpu.HBM)
 
 
 def f32(*shape):
@@ -235,52 +239,43 @@
         meet(plane, f_west, f_east, rows)
         pair(levels * tracers, f_a, f_b, levels)
 
-    def stencil(source, at, rim_row, chunk, turn, edge_n, edge_s, co):
-        values = []
-        for h in range(halves):
-            here = at + h * SUB
-            cell = source[pl.ds(pl.multiple_of(here, SUB), SUB), :]
-            side = pltpu.roll(rim[chunk, pl.ds(rim_row + h * SUB, SUB), :], turn, 1)
-            e = jnp.where(lane == LANES - 1, side, pltpu.roll(cell, LANES - 1, 1))
-            w = jnp.where(lane == 0, side, pltpu.roll(cell, 1, 1))
-            if h == halves - 1:
-                n = jnp.where(sub == SUB - 1, edge_n, pltpu.roll(cell, SUB - 1, 0))
-            else:
-                n = source[pl.ds(here + 1, SUB), :]
+    def stencil(source, at, rim_row, chunk, turn, row, h, co):
+        here = at + h * SUB
+        cell = source[pl.ds(pl.multiple_of(here, SUB), SUB), :]
+        side = pltpu.roll(rim[chunk, pl.ds(rim_row + h * SUB, SUB), :], turn, 1)
+        e = jnp.where(lane == LANES - 1, side, pltpu.roll(cell, LANES - 1, 1))
+        w = jnp.where(lane == 0, side, pltpu.roll(cell, 1, 1))
+        if h == halves - 1:
+            n = jnp.where(sub == SUB - 1, edges[0, pl.ds(row, 1), :], pltpu.roll(cell, SUB - 1, 0))
+        else:
+            n = source[pl.ds(here + 1, SUB), :]
+        if h == 0:
+            s = jnp.where(sub == 0, edges[1, pl.ds(row, 1), :], pltpu.roll(cell, 1, 0))
+        else:
             s = source[pl.ds(here - 1, SUB), :]
-            if h == 0:
-                s = jnp.where(sub == 0, edge_s, s)
-            c0, ce, cw, cn, cs = co[h][:5]
-            values.append((c0 * cell + ce * e) + (cw * w + cn * n) + cs * s)
-        return values
-
-    def edge(side, row):
-        return edges[side, pl.ds(row, 1), :]
+        c0, ce, cw, cn, cs = co[:5]
+        return (c0 * cell + ce * e) + (cw * w + cn * n) + cs * s
 
     def forward(k, solved):
         chunk, q = k // per_chunk, k % per_chunk
         turn = LANES - 1 - 2 * q
-        co = []
+        new = []
         for h in range(halves):
             blk = pl.ds(pl.multiple_of(k * rows + h * SUB, SUB), SUB)
-            co.append([weight[blk, :] for weight in weights])
-        if first:
-            row = levels * tracers + k
-            extra = stencil(
-                forcing, k * rows + SUB, plane, chunk, turn, edge(0, row), edge(1, row), co
-            )
-        new = []
-        for t in range(tracers):
-            at = k * plane + (t + 1) * rows
-            row = k * tracers + t
-            values = stencil(flat, at, t * rows, chunk, turn, edge(0, row), edge(1, row), co)
-            for h in range(halves):
-                value = values[h]
+            co = [weight[blk, :] for weight in weights]
+            extra = None
+            if first:
+                extra = stencil(forcing, k * rows + SUB, plane, chunk, turn, levels * tracers + k, h, co)
+            for t in range(tracers):
+                at = k * plane + (t + 1) * rows
+                value = stencil(flat, at, t * rows, chunk, turn, k * tracers + t, h, co)
                 if first:
-                    value = value + extra[h]
-                value = value + co[h][5] * solved[t * halves + h]
-                new.append(value)
-                flat[pl.ds(pl.multiple_of(at + h * SUB, SUB), SUB), :] = value
+                    value = value + extra
+                new.append(value + co[5] * solved[h * tracers + t])
+        for h in range(halves):
+            for t in range(tracers):
+                at = k * plane + (t + 1) * rows + h * SUB
+                flat[pl.ds(pl.multiple_of(at, SUB), SUB), :] = new[h * tracers + t]
         return tuple(new)
 
     def forward_block(b, carry):
@@ -449,8 +444,12 @@
         error = arrived[j, pl.ds(levels + 2, 1), :]
         residual = jnp.where(col >= 0, (modelled - observed) / error, 0.0)
         scaled[pl.ds(j, 1), :] = residual / error
-        for c in range(width // LANES):
-            back[pl.ds(j * (width // LANES) + c, 1), :] = residual[:, c * LANES : (c + 1) * LANES]
+        for i in range(width // cap):
+            at = i * cap
+            piece = residual[:, at // LANES * LANES : at // LANES * LANES + LANES]
+            if at % LANES:
+                piece = pltpu.roll(piece, LANES - at % LANES, 1)
+            back[pl.ds(j * (width // cap) + i, 1), :] = piece
 
     zeros = jnp.zeros((SUB, LANES), jnp.float32)
     forcing[pl.ds(0, SUB), :] = zeros
@@ -477,16 +476,15 @@
     put_rows(forcing, SUB, a_ref, b_ref, rows, 0, levels)
 
 
-def unpack_residual(cap, gathered, out):
+def unpack_residual(cap, arrived, out):
     lane = lax.broadcasted_iota(jnp.int32, (1, LANES), 1)
     groups = LANES // cap
-    me = lax.axis_index("lon") * lax.axis_size("lat") + lax.axis_index("lat")
-    mine, place = me // groups, me % groups
     for row in range(out.shape[0]):
         made = None
         for g in range(groups):
-            piece = gathered[row * groups + g, pl.ds(mine, 1), :]
-            piece = pltpu.roll(piece, (g - place + groups) % groups * cap, 1)
+            piece = arrived[pl.ds(row * groups + g, 1), :]
+            if g:
+                piece = pltpu.roll(piece, g * cap, 1)
             made = piece if made is None else jnp.where(lane >= g * cap, piece, made)
         out[pl.ds(row, 1), :] = made
 
@@ -532,11 +530,11 @@
             vmem(per_level, LANES), vmem(per_level, LANES), vmem(groups * group_rows, LANES), dma((4,)),
         ),
         4, 10, 800000, "pack",
-    )(flat(kernel), flat(sound_col), flat(observed), flat(obs_error))
+    )(*(in_hbm(flat(x)) for x in (kernel, sound_col, observed, obs_error)))
     received = lax.all_to_all(packed, ("lon", "lat"), split_axis=0, concat_axis=0, tiled=True)
 
     field = adjoint.reshape(levels * tracers, rows, LANES)
-    east, north, mix = flat(wind_east), flat(wind_north), flat(mixing)
+    east, north, mix = (in_hbm(flat(x)) for x in (wind_east, wind_north, mixing))
     rims = call(
         functools.partial(first_rims, levels, tracers, rows, chunks, per_chunk),
         [HBM] * 3,
@@ -544,7 +542,7 @@
         (VMEM,) * 3,
         (vmem(levels * plane, LANES), vmem(levels * rows, LANES), vmem(levels * rows, LANES), dma((chunks + 2,))),
         10, field_bytes, 2 * field_bytes, "first_rims",
-    )(flat(adjoint), east, north)
+    )(in_hbm(flat(adjoint)), east, north)
     start_rims = exchange(*rims)
 
     block = largest(levels, 24, 16, 8)
@@ -563,7 +561,7 @@
         [VMEM] * 2,
         (
             f32(levels * rows + 2 * SUB, LANES), f32(chunks, rows, LANES), f32(levels, LANES), f32(levels, LANES),
-            f32(per_level, LANES),
+            f32(bricks, LANES),
         ),
         (VMEM,) * 5,
         (
@@ -571,7 +569,7 @@
             pltpu.VMEM((parts, width, rows // SUB * LANES), jnp.bfloat16),
             vmem(max(parts, SUB), width),
         ),
-        6, field_bytes * 8, field_bytes, "soundings",
+        10, field_bytes * 8, field_bytes, "soundings",
     )(received, sums)
     forcing_rims = exchange(*rims)
 
@@ -598,13 +596,16 @@
             8, field_bytes * 8, field_bytes * 2, "step",
         )(value, *weights, *operands)
 
-    stepped, *rims = advance(field, True, *start_rims, forcing, *forcing_rims)
+    stepped, *rims = advance(in_hbm(field), True, *start_rims, forcing, *forcing_rims)
     (result,) = advance(stepped, False, *exchange(*rims))
 
-    gathered = lax.all_gather(back, ("lon", "lat"))
+    returned = lax.all_to_all(
+        back.reshape(bricks, 1, LANES), ("lon", "lat"), split_axis=0, concat_axis=0, tiled=True
+    )
+    result, returned = lax.optimization_barrier((result, returned))
     residual = call(
         functools.partial(unpack_residual, cap), [VMEM], f32(per_level, LANES), VMEM, (), 2, 10, 10000, "residual",
-    )(gathered)
+    )(returned.reshape(bricks, LANES))
     return result.reshape(adjoint.shape), residual.reshape(sound_col.shape)
 
 

time: 133 us -> 80.5 us (0.61)
  blocking collectives: 69.3 us -> 0 us
  starting transfers between devices: 21.2 us -> 29.2 us
  local copies, waits for them, and re-layouts: 9.82 us -> 14.2 us
  Pallas kernels: 30.6 us -> 33.7 us
    all_gather x1 -> x0, blocking collectives: 69.3 us -> none  [per_device(): gathered = lax.all_gather(back, ('lon', 'lat'))]
    all_to_all x0 -> x1, starting transfers between devices: none -> 5.08 us  [per_device(): lax.all_to_all(back.reshape(bricks, 1, LANES), ('lon', 'lat'), split_axis...]
    unnamed x24 -> x30, local copies, waits for them, and re-layouts: 9.82 us -> 14.2 us
    ppermute x3, starting transfers between devices: 2.94 us -> 5.07 us  [exchange(): lax.ppermute(b_rim, 'lat', [(j, partner(j, 1)) for j in range(lats)])]
  transfers between devices with their start and end apart: 13 -> 14, of which waited for: 1 -> 2; matrix products, arithmetic and copies ran while one was open for 0% -> 0% of each run, Pallas kernels for 8% -> 25%
where the time goes in v2:
time: 80.5 us; the launch traced here: 79.8 us
  Pallas kernels  33.7 us (42%)
  starting transfers between devices  29.2 us (36%)
  local copies, waits for them, and re-layouts  14.2 us (18%)
  waiting for transfers between devices  1.85 us (2%)
  between operations  0.87 us (1%)
    pallas_call x2, Pallas kernels, advance(): call(functools.partial(step, levels, tracers, rows, chunks, per_chunk, un...  19.2 us
    unnamed x30, local copies, waits for them, and re-layouts  14.2 us
    all_to_all x1, starting transfers between devices, per_device(): lax.all_to_all(packed, ('lon', 'lat'), split_axis=0, concat_axis=0, tiled...  7.3 us
    ppermute x3, starting transfers between devices, exchange(): lax.ppermute(a_rim, 'lat', [(j, partner(j, 0)) for j in range(lats)])  6.42 us
    all_to_all x1, starting transfers between devices, per_device(): lax.all_to_all(back.reshape(bricks, 1, LANES), ('lon', 'lat'), split_axis...  5.08 us
    ppermute x3, starting transfers between devices, exchange(): lax.ppermute(b_rim, 'lat', [(j, partner(j, 1)) for j in range(lats)])  5.07 us
    pallas_call x1, Pallas kernels, per_device(): call(functools.partial(first_rims, levels, tracers, rows, chunks, per_chu...  4.94 us
    ppermute x3, starting transfers between devices, exchange(): lax.ppermute(side_rim, 'lon', [((i + 1) % lons, i) for i in range(lons)])  4.73 us
  transfers between devices with their start and end apart: 14, of which 2 were waited for; matrix products, arithmetic and copies ran while one was open for 0% of the time, Pallas kernels for 25%

profile of v2, /device:TPU:0, one launch (start us, length us, event | category | flops | bytes accessed | tf_op | source)
XLA Modules:
  0.0 79.8 jit_solution(10729086741966470537)
XLA Ops:
  0.6 2.6 %pack.1 = f32[32,24,128]{2,1,0:T(8,128)} custom-call(f32[576,128]{1,0:T(8,128)} %bitcast.25, s32[8,128]{1,0:T(8,128)} %bitcast.26, f32[8,128]{1,0:T(8,128)} %bitcast.27, f32[8,128]{1,0:T(8,128)} %bitcast.28), custom_call_target="tpu_custom_call" | custom-call | flops 10 | bytes 800000 | tf_op jit(solution)/shard_map/pack/pallas_call | solution.py:525
  3.3 7.3 %all-to-all-start = ((f32[32,24,128]{2,1,0:T(8,128)}), f32[32,24,128]{2,1,0:T(8,128)S(1)}, u32[]{:S(2)}, u32[]{:S(2)}) async-start(f32[32,24,128]{2,1,0:T(8,128)} %pack.1), calls=%async_computation | async-start | bytes 786432 | tf_op jit(solution)/shard_map/all_to_all | solution.py:534
  10.6 0.0 copy-start.2
  10.6 4.9 %first_rims.1 = (f32[2,144,128]{2,1,0:T(8,128)}, f32[648,128]{1,0:T(8,128)S(1)}, f32[648,128]{1,0:T(8,128)S(1)}) custom-call(f32[9216,128]{1,0:T(8,128)} %bitcast.17, f32[1152,128]{1,0:T(8,128)} %bitcast.20, f32[1152,128]{1,0:T(8,128)} %bitcast.22), custom_call_target="tpu_custom_call" | custom-call | flops 4718592 | bytes 9437184 | tf_op jit(solution)/shard_map/first_rims/pallas_call | solution.py:538
  15.6 1.8 %collective-permute-start.1 = (f32[648,128]{1,0:T(8,128)S(1)}, f32[648,128]{1,0:T(8,128)S(1)}, u32[]{:S(2)}, u32[]{:S(2)}) collective-permute-start(f32[648,128]{1,0:T(8,128)S(1)} %get-tuple-element.24), channel_id=1, source_target_pairs={{0,1},{1,0},{2,3},{3,2},{4,5},{5,4},{6,7},{7,6},{8,9},{9,8},{10,11... | collective-permute-start | bytes 995336 | tf_op jit(solution)/shard_map/ppermute | solution.py:502
  17.4 0.7 collective-permute-start.2
  18.1 0.1 collective-permute-start
  18.1 2.6 %collective-permute-start.3 = (f32[2,144,128]{2,1,0:T(8,128)}, f32[2,144,128]{2,1,0:T(8,128)}, u32[]{:S(2)}, u32[]{:S(2)}) collective-permute-start(f32[2,144,128]{2,1,0:T(8,128)} %get-tuple-element.23), channel_id=1, source_target_pairs={{4,0},{8,4},{12,8},{16,12},{20,16},{24,20},{28,24},{0,28},{5,1},{9... | collective-permute-start | bytes 442376 | tf_op jit(solution)/shard_map/ppermute | solution.py:501
  20.8 0.0 copy-done.2
  20.8 0.7 tracer_sum.1.sums
  21.5 1.3 %all-to-all-done.received = f32[32,24,128]{2,1,0:T(8,128)S(1)} async-done(((f32[32,24,128]{2,1,0:T(8,128)}), f32[32,24,128]{2,1,0:T(8,128)S(1)}, u32[]{:S(2)}, u32[]{:S(2)}) %all-to-all-start) | async-done | bytes 393248 | tf_op jit(solution)/shard_map/all_to_all | solution.py:534
  22.8 2.7 %soundings.1 = (f32[1168,128]{1,0:T(8,128)S(1)}, f32[2,16,128]{2,1,0:T(8,128)S(1)}, f32[72,128]{1,0:T(8,128)S(1)}, f32[72,128]{1,0:T(8,128)S(1)}, f32[32,128]{1,0:T(8,128)S(1)}) custom-call(f32[32,24,128]{2,1,0:T(8,128)S(1)} %all-to-all-done.received, bf16[2,576,256]{2,1,0:T(8,128)(2,1)S(1)} %tracer_sum.1.sums), custom_call_target="tpu_custom_call" | custom-call | flops 37748736 | bytes 4718592 | tf_op jit(solution)/shard_map/soundings/pallas_call | solution.py:559
  25.5 0.0 copy-start.14
  25.5 0.6 copy-done.14
  26.1 2.9 %collective-permute-start.6 = (f32[72,128]{1,0:T(8,128)S(1)}, f32[72,128]{1,0:T(8,128)S(1)}, u32[]{:S(2)}, u32[]{:S(2)}) collective-permute-start(f32[72,128]{1,0:T(8,128)S(1)} %get-tuple-element.35), channel_id=1, source_target_pairs={{0,1},{1,0},{2,3},{3,2},{4,5},{5,4},{6,7},{7,6},{8,9},{9,8},{10,11... | collective-permute-start | bytes 110600 | tf_op jit(solution)/shard_map/ppermute | solution.py:502
  29.0 0.0 collective-permute-done.west0.refs_8_
  29.0 0.7 copy-done.11
  29.7 0.7 collective-permute-start.7
  30.3 0.0 collective-permute-done.1.a0.refs_10_
  30.4 0.0 copy-start.5
  30.4 0.7 copy-done.5
  31.1 0.0 collective-permute-start.5
  31.1 0.0 collective-permute-done.2.b0.refs_11_
  31.1 0.0 copy-start.8
  31.1 0.7 copy-done.8
  31.8 0.5 collective-permute-start.4
  32.3 0.0 copy-start.6
  32.3 1.0 %copy-done.6 = f32[648,128]{1,0:T(8,128)S(1)} copy-done((f32[648,128]{1,0:T(8,128)S(1)}, f32[648,128]{1,0:T(8,128)}, u32[]{:S(2)}) %copy-start.6) | copy-done | bytes 331800
  33.3 0.0 copy-start.9
  33.3 1.0 %copy-done.9 = f32[648,128]{1,0:T(8,128)S(1)} copy-done((f32[648,128]{1,0:T(8,128)S(1)}, f32[648,128]{1,0:T(8,128)}, u32[]{:S(2)}) %copy-start.9) | copy-done | bytes 331800
  34.3 0.0 copy-start.12
  34.3 0.9 %copy-done.12 = f32[2,144,128]{2,1,0:T(8,128)S(1)} copy-done((f32[2,144,128]{2,1,0:T(8,128)S(1)}, f32[2,144,128]{2,1,0:T(8,128)}, u32[]{:S(2)}) %copy-start.12) | copy-done | bytes 147480
  35.2 2.8 %coefficients.1 = (f32[1152,128]{1,0:T(8,128)S(1)}, f32[1152,128]{1,0:T(8,128)S(1)}, f32[1152,128]{1,0:T(8,128)S(1)}, f32[1152,128]{1,0:T(8,128)S(1)}, f32[1152,...) custom-call(f32[1152,128]{1,0:T(8,128)} %bitcast.21, f32[1152,128]{1,0:T(8,128)} %bitcast.23, ...), custom_call_target="tpu_custom_call" | custom-call | flops 4718592 | bytes 4718592 | tf_op jit(solution)/shard_map/coefficients/pallas_call | solution.py:577
  38.0 0.0 copy-start.3
  38.0 0.0 collective-permute-done.3.refs_9_
  38.0 0.0 collective-permute-done.5.refs_14_
  38.1 0.0 collective-permute-done.4.refs_13_
  38.1 0.0 collective-permute-done.6.refs_15_
  38.1 0.0 collective-permute-done.7.refs_16_
  38.1 0.0 copy-start.7
  38.1 1.1 %copy-done.7 = f32[648,128]{1,0:T(8,128)S(1)} copy-done((f32[648,128]{1,0:T(8,128)S(1)}, f32[648,128]{1,0:T(8,128)}, u32[]{:S(2)}) %copy-start.7) | copy-done | bytes 331800
  39.2 0.0 copy-start.10
  39.2 1.0 %copy-done.10 = f32[648,128]{1,0:T(8,128)S(1)} copy-done((f32[648,128]{1,0:T(8,128)S(1)}, f32[648,128]{1,0:T(8,128)}, u32[]{:S(2)}) %copy-start.10) | copy-done | bytes 331800
  40.2 0.0 copy-start.13
  40.2 0.9 %copy-done.13 = f32[2,144,128]{2,1,0:T(8,128)S(1)} copy-done((f32[2,144,128]{2,1,0:T(8,128)S(1)}, f32[2,144,128]{2,1,0:T(8,128)}, u32[]{:S(2)}) %copy-start.13) | copy-done | bytes 147480
  41.1 10.8 %step.2 = (f32[576,16,128]{2,1,0:T(8,128)S(1)}, f32[2,128,128]{2,1,0:T(8,128)}, f32[576,128]{1,0:T(8,128)}, f32[576,128]{1,0:T(8,128)}) custom-call(f32[576,16,128]{2,1,0:T(8,128)} %bitcast.18, f32[1152,128]{1,0:T(8,128)S(1)} %get-tuple-element.26.refs_1_, f32[1152,128]{1,0:T(8,128)S(1)} %get-tuple-element.27.refs_2_, ...), custom_call_target="tpu_custom_call" | custom-call | flops 37748736 | bytes 9437184 | tf_op jit(solution)/shard_map/step/pallas_call | solution.py:589
  51.9 0.0 copy-done.3
  51.9 0.0 copy-start
  51.9 2.2 %copy-done = f32[576,16,128]{2,1,0:T(8,128)} copy-done((f32[576,16,128]{2,1,0:T(8,128)}, f32[576,16,128]{2,1,0:T(8,128)S(1)}, u32[]{:S(2)}) %copy-start) | copy-done | bytes 4718616
  54.1 1.7 %collective-permute-start.10 = (f32[576,128]{1,0:T(8,128)}, f32[576,128]{1,0:T(8,128)}, u32[]{:S(2)}, u32[]{:S(2)}) collective-permute-start(f32[576,128]{1,0:T(8,128)} %get-tuple-element.39), channel_id=1, source_target_pairs={{0,1},{1,0},{2,3},{3,2},{4,5},{5,4},{6,7},{7,6},{8,9},{9,8},{10,11... | collective-permute-start | bytes 884744 | tf_op jit(solution)/shard_map/ppermute | solution.py:502
  55.8 3.7 %collective-permute-start.11 = (f32[576,128]{1,0:T(8,128)}, f32[576,128]{1,0:T(8,128)}, u32[]{:S(2)}, u32[]{:S(2)}) collective-permute-start(f32[576,128]{1,0:T(8,128)} %get-tuple-element.40), channel_id=1, source_target_pairs={{0,0},{1,2},{2,1},{3,3},{4,4},{5,6},{6,5},{7,7},{8,8},{9,10},{10,9... | collective-permute-start | bytes 884744 | tf_op jit(solution)/shard_map/ppermute | solution.py:503
  59.5 2.1 %collective-permute-start.9 = (f32[2,128,128]{2,1,0:T(8,128)}, f32[2,128,128]{2,1,0:T(8,128)}, u32[]{:S(2)}, u32[]{:S(2)}) collective-permute-start(f32[2,128,128]{2,1,0:T(8,128)} %get-tuple-element.38), channel_id=1, source_target_pairs={{4,0},{8,4},{12,8},{16,12},{20,16},{24,20},{28,24},{0,28},{5,1},{9... | collective-permute-start | bytes 393224 | tf_op jit(solution)/shard_map/ppermute | solution.py:501
  61.6 0.0 collective-permute-start.8
  61.6 5.1 %all-to-all-start.1 = ((f32[32,1,128]{2,1,0:T(1,128)}), f32[32,1,128]{2,1,0:T(1,128)S(1)}, u32[]{:S(2)}, u32[]{:S(2)}) async-start(f32[32,1,128]{2,1,0:T(1,128)} %bitcast.16), calls=%async_computation.1 | async-start | bytes 32768 | tf_op jit(solution)/shard_map/all_to_all | solution.py:602
  66.7 0.0 collective-permute-done.9.refs_9_
  66.7 0.5 collective-permute-done.8.refs_8_
  67.2 0.0 collective-permute-done.10.refs_10_
  67.2 0.0 collective-permute-done.11.refs_11_
  67.3 0.0 copy-start.1
  67.3 2.3 %copy-done.1 = f32[576,16,128]{2,1,0:T(8,128)S(1)} copy-done((f32[576,16,128]{2,1,0:T(8,128)S(1)}, f32[576,16,128]{2,1,0:T(8,128)}, u32[]{:S(2)}) %copy-start.1) | copy-done | bytes 4718616
  69.6 1.1 %copy-done.4 = f32[1152,128]{1,0:T(8,128)S(1)} copy-done((f32[1152,128]{1,0:T(8,128)S(1)}, f32[1152,128]{1,0:T(8,128)}, u32[]{:S(2)}) %copy-start.4) | copy-done | bytes 589848
  70.7 8.4 %step.3 = f32[576,16,128]{2,1,0:T(8,128)} custom-call(f32[576,16,128]{2,1,0:T(8,128)S(1)} %copy-done.1, f32[1152,128]{1,0:T(8,128)S(1)} %get-tuple-element.26.refs_1_, f32[1152,128]{1,0:T(8,128)S(1)} %get-tuple-element.27.refs_2_, f32[1152,128]{1,0:T(8,128)S(1)} %get-tuple-element.28.refs_3_, f32[1152,128]{1,0:T(8,128)S(1)} %get-tuple-element.29.refs_4_, ...), custom_call_target="tpu_custom_call" | custom-call | flops 37748736 | bytes 9437184 | tf_op jit(solution)/shard_map/step/pallas_call | solution.py:589
  79.1 0.0 all-to-all-done.1
  79.1 0.7 residual.1
  (2 shorter events, 0.0 us)
Async XLA Ops:
  3.3 19.5 %all-to-all-start = ((f32[32,24,128]{2,1,0:T(8,128)}), f32[32,24,128]{2,1,0:T(8,128)S(1)}, u32[]{:S(2)}, u32[]{:S(2)}) async-start(f32[32,24,128]{2,1,0:T(8,128)} %pack.1), calls=%async_computation | async-start | bytes 786432 | tf_op jit(solution)/shard_map/all_to_all | solution.py:534
  10.6 10.2 %copy-start.2 = (f32[72,8,16,128]{3,2,1,0:T(8,128)S(1)}, f32[72,8,16,128]{3,2,1,0:T(8,128)}, u32[]{:S(2)}) copy-start(f32[72,8,16,128]{3,2,1,0:T(8,128)} %concentration.1) | copy-start | bytes 14155780
  15.6 14.8 %collective-permute-start.1 = (f32[648,128]{1,0:T(8,128)S(1)}, f32[648,128]{1,0:T(8,128)S(1)}, u32[]{:S(2)}, u32[]{:S(2)}) collective-permute-start(f32[648,128]{1,0:T(8,128)S(1)} %get-tuple-element.24), channel_id=1, source_target_pairs={{0,1},{1,0},{2,3},{3,2},{4,5},{5,4},{6,7},{7,6},{8,9},{9,8},{10,11... | collective-permute-start | bytes 995336 | tf_op jit(solution)/shard_map/ppermute | solution.py:502
  17.4 13.7 %collective-permute-start.2 = (f32[648,128]{1,0:T(8,128)S(1)}, f32[648,128]{1,0:T(8,128)S(1)}, u32[]{:S(2)}, u32[]{:S(2)}) collective-permute-start(f32[648,128]{1,0:T(8,128)S(1)} %get-tuple-element.25), channel_id=1, source_target_pairs={{0,0},{1,2},{2,1},{3,3},{4,4},{5,6},{6,5},{7,7},{8,8},{9,10},{10,9... | collective-permute-start | bytes 995336 | tf_op jit(solution)/shard_map/ppermute | solution.py:503
  18.1 11.0 %collective-permute-start = (f32[2,144,128]{2,1,0:T(8,128)}, f32[2,144,128]{2,1,0:T(8,128)S(1)}, u32[]{:S(2)}, u32[]{:S(2)}) collective-permute-start(f32[2,144,128]{2,1,0:T(8,128)} %get-tuple-element.23), channel_id=1, source_target_pairs={{0,4},{4,8},{8,12},{12,16},{16,20},{20,24},{24,28},{28,0},{1,5},{5... | collective-permute-start | bytes 442376 | tf_op jit(solution)/shard_map/ppermute | solution.py:500
  18.1 19.9 %collective-permute-start.3 = (f32[2,144,128]{2,1,0:T(8,128)}, f32[2,144,128]{2,1,0:T(8,128)}, u32[]{:S(2)}, u32[]{:S(2)}) collective-permute-start(f32[2,144,128]{2,1,0:T(8,128)} %get-tuple-element.23), channel_id=1, source_target_pairs={{4,0},{8,4},{12,8},{16,12},{20,16},{24,20},{28,24},{0,28},{5,1},{9... | collective-permute-start | bytes 442376 | tf_op jit(solution)/shard_map/ppermute | solution.py:501
  25.5 0.6 copy-start.14
  26.1 11.9 %collective-permute-start.6 = (f32[72,128]{1,0:T(8,128)S(1)}, f32[72,128]{1,0:T(8,128)S(1)}, u32[]{:S(2)}, u32[]{:S(2)}) collective-permute-start(f32[72,128]{1,0:T(8,128)S(1)} %get-tuple-element.35), channel_id=1, source_target_pairs={{0,1},{1,0},{2,3},{3,2},{4,5},{5,4},{6,7},{7,6},{8,9},{9,8},{10,11... | collective-permute-start | bytes 110600 | tf_op jit(solution)/shard_map/ppermute | solution.py:502
  29.0 0.7 copy-start.11
  29.7 8.4 %collective-permute-start.7 = (f32[72,128]{1,0:T(8,128)S(1)}, f32[72,128]{1,0:T(8,128)S(1)}, u32[]{:S(2)}, u32[]{:S(2)}) collective-permute-start(f32[72,128]{1,0:T(8,128)S(1)} %get-tuple-element.36), channel_id=1, source_target_pairs={{0,0},{1,2},{2,1},{3,3},{4,4},{5,6},{6,5},{7,7},{8,8},{9,10},{10,9... | collective-permute-start | bytes 110600 | tf_op jit(solution)/shard_map/ppermute | solution.py:503
  30.4 0.7 copy-start.5
  31.1 7.0 %collective-permute-start.5 = (f32[2,16,128]{2,1,0:T(8,128)S(1)}, f32[2,16,128]{2,1,0:T(8,128)S(1)}, u32[]{:S(2)}, u32[]{:S(2)}) collective-permute-start(f32[2,16,128]{2,1,0:T(8,128)S(1)} %get-tuple-element.34), channel_id=1, source_target_pairs={{4,0},{8,4},{12,8},{16,12},{20,16},{24,20},{28,24},{0,28},{5,1},{9... | collective-permute-start | bytes 49160 | tf_op jit(solution)/shard_map/ppermute | solution.py:501
  31.1 0.7 copy-start.8
  31.8 6.2 %collective-permute-start.4 = (f32[2,16,128]{2,1,0:T(8,128)S(1)}, f32[2,16,128]{2,1,0:T(8,128)S(1)}, u32[]{:S(2)}, u32[]{:S(2)}) collective-permute-start(f32[2,16,128]{2,1,0:T(8,128)S(1)} %get-tuple-element.34), channel_id=1, source_target_pairs={{0,4},{4,8},{8,12},{12,16},{16,20},{20,24},{24,28},{28,0},{1,5},{5... | collective-permute-start | bytes 49160 | tf_op jit(solution)/shard_map/ppermute | solution.py:500
  32.3 1.0 %copy-start.6 = (f32[648,128]{1,0:T(8,128)S(1)}, f32[648,128]{1,0:T(8,128)}, u32[]{:S(2)}) copy-start(f32[648,128]{1,0:T(8,128)} %copy-done.5) | copy-start | bytes 995332
  33.3 1.0 %copy-start.9 = (f32[648,128]{1,0:T(8,128)S(1)}, f32[648,128]{1,0:T(8,128)}, u32[]{:S(2)}) copy-start(f32[648,128]{1,0:T(8,128)} %copy-done.8) | copy-start | bytes 995332
  34.3 0.9 %copy-start.12 = (f32[2,144,128]{2,1,0:T(8,128)S(1)}, f32[2,144,128]{2,1,0:T(8,128)}, u32[]{:S(2)}) copy-start(f32[2,144,128]{2,1,0:T(8,128)} %copy-done.11) | copy-start | bytes 442372
  38.0 13.9 %copy-start.3 = (f32[1152,128]{1,0:T(8,128)}, f32[1152,128]{1,0:T(8,128)S(1)}, u32[]{:S(2)}) copy-start(f32[1152,128]{1,0:T(8,128)S(1)} %get-tuple-element.32.refs_7_) | copy-start | bytes 1769476
  38.1 1.1 %copy-start.7 = (f32[648,128]{1,0:T(8,128)S(1)}, f32[648,128]{1,0:T(8,128)}, u32[]{:S(2)}) copy-start(f32[648,128]{1,0:T(8,128)} %copy-done.5) | copy-start | bytes 995332
  39.2 1.0 %copy-start.10 = (f32[648,128]{1,0:T(8,128)S(1)}, f32[648,128]{1,0:T(8,128)}, u32[]{:S(2)}) copy-start(f32[648,128]{1,0:T(8,128)} %copy-done.8) | copy-start | bytes 995332
  40.2 0.9 %copy-start.13 = (f32[2,144,128]{2,1,0:T(8,128)S(1)}, f32[2,144,128]{2,1,0:T(8,128)}, u32[]{:S(2)}) copy-start(f32[2,144,128]{2,1,0:T(8,128)} %copy-done.11) | copy-start | bytes 442372
  51.9 2.2 %copy-start = (f32[576,16,128]{2,1,0:T(8,128)}, f32[576,16,128]{2,1,0:T(8,128)S(1)}, u32[]{:S(2)}) copy-start(f32[576,16,128]{2,1,0:T(8,128)S(1)} %get-tuple-element.37.refs_0_) | copy-start | bytes 14155780
  54.1 13.1 %collective-permute-start.10 = (f32[576,128]{1,0:T(8,128)}, f32[576,128]{1,0:T(8,128)}, u32[]{:S(2)}, u32[]{:S(2)}) collective-permute-start(f32[576,128]{1,0:T(8,128)} %get-tuple-element.39), channel_id=1, source_target_pairs={{0,1},{1,0},{2,3},{3,2},{4,5},{5,4},{6,7},{7,6},{8,9},{9,8},{10,11... | collective-permute-start | bytes 884744 | tf_op jit(solution)/shard_map/ppermute | solution.py:502
  55.8 11.5 %collective-permute-start.11 = (f32[576,128]{1,0:T(8,128)}, f32[576,128]{1,0:T(8,128)}, u32[]{:S(2)}, u32[]{:S(2)}) collective-permute-start(f32[576,128]{1,0:T(8,128)} %get-tuple-element.40), channel_id=1, source_target_pairs={{0,0},{1,2},{2,1},{3,3},{4,4},{5,6},{6,5},{7,7},{8,8},{9,10},{10,9... | collective-permute-start | bytes 884744 | tf_op jit(solution)/shard_map/ppermute | solution.py:503
  59.5 7.2 %collective-permute-start.9 = (f32[2,128,128]{2,1,0:T(8,128)}, f32[2,128,128]{2,1,0:T(8,128)}, u32[]{:S(2)}, u32[]{:S(2)}) collective-permute-start(f32[2,128,128]{2,1,0:T(8,128)} %get-tuple-element.38), channel_id=1, source_target_pairs={{4,0},{8,4},{12,8},{16,12},{20,16},{24,20},{28,24},{0,28},{5,1},{9... | collective-permute-start | bytes 393224 | tf_op jit(solution)/shard_map/ppermute | solution.py:501
  61.6 5.6 %collective-permute-start.8 = (f32[2,128,128]{2,1,0:T(8,128)}, f32[2,128,128]{2,1,0:T(8,128)}, u32[]{:S(2)}, u32[]{:S(2)}) collective-permute-start(f32[2,128,128]{2,1,0:T(8,128)} %get-tuple-element.38), channel_id=1, source_target_pairs={{0,4},{4,8},{8,12},{12,16},{16,20},{20,24},{24,28},{28,0},{1,5},{5... | collective-permute-start | bytes 393224 | tf_op jit(solution)/shard_map/ppermute | solution.py:500
  61.6 17.4 %all-to-all-start.1 = ((f32[32,1,128]{2,1,0:T(1,128)}), f32[32,1,128]{2,1,0:T(1,128)S(1)}, u32[]{:S(2)}, u32[]{:S(2)}) async-start(f32[32,1,128]{2,1,0:T(1,128)} %bitcast.16), calls=%async_computation.1 | async-start | bytes 32768 | tf_op jit(solution)/shard_map/all_to_all | solution.py:602
  67.3 2.3 %copy-start.1 = (f32[576,16,128]{2,1,0:T(8,128)S(1)}, f32[576,16,128]{2,1,0:T(8,128)}, u32[]{:S(2)}) copy-start(f32[576,16,128]{2,1,0:T(8,128)} %copy-done) | copy-start | bytes 14155780
  69.6 1.1 %copy-start.4 = (f32[1152,128]{1,0:T(8,128)S(1)}, f32[1152,128]{1,0:T(8,128)}, u32[]{:S(2)}) copy-start(f32[1152,128]{1,0:T(8,128)} %copy-done.3) | copy-start | bytes 1769476

commit v3 on v2

--- a/solution.py
+++ b/solution.py
@@ -10,13 +10,15 @@
 LANES = 128
 SUB = 8
 MIB = 1 << 20
+ANY = pl.BlockSpec(memory_space=pl.ANY)
 HBM = pl.BlockSpec(memory_space=pltpu.HBM)
 VMEM = pl.BlockSpec(memory_space=pltpu.VMEM)
 
 
-def rim_chunks(levels):
-    chunks = -(-levels // 63)
-    return chunks, -(-levels // chunks)
+def rim_chunks(levels, unroll):
+    per_chunk = 63 // unroll * unroll
+    chunks = -(-levels // per_chunk)
+    return chunks, -(-levels // (chunks * unroll)) * unroll
 
 
 def lane_iota():
@@ -33,6 +35,10 @@
 
 def in_hbm(x):
     return pltpu.with_memory_space_constraint(x, pltpu.HBM)
+
+
+def hbm(*shape):
+    return pltpu.HBM(shape, jnp.float32)
 
 
 def f32(*shape):
@@ -120,13 +126,18 @@
 
 
 def coefficients(levels, tracers, rows, per_chunk, unroll, east, north, mixing, west0, a0, b0, *refs):
-    outs, (e_buf, n_buf, m_buf, sems) = refs[:7], refs[7:]
+    outs, (e_buf, n_buf, m_buf, w_rim, a_rim, b_rim, sems) = refs[:7], refs[7:]
     plane = tracers * rows
     halves = rows // SUB
     lane, sub = lane_iota(), sub_iota()
     copies = [
         pltpu.make_async_copy(source, target, sems.at[i])
-        for i, (source, target) in enumerate(((east, e_buf), (north, n_buf), (mixing, m_buf)))
+        for i, (source, target) in enumerate(
+            (
+                (east, e_buf), (north, n_buf), (mixing, m_buf), (west0.at[:, pl.ds(plane, rows)], w_rim),
+                (a0.at[pl.ds(levels * tracers, levels)], a_rim), (b0.at[pl.ds(levels * tracers, levels)], b_rim),
+            )
+        )
     ]
     for copy in copies:
         copy.start()
@@ -150,11 +161,11 @@
             factor = up * inv
             new.append((up, factor))
             e, n = e_buf[blk, :], n_buf[blk, :]
-            side = pltpu.roll(west0[chunk, pl.ds(plane + h * SUB, SUB), :], LANES - 1 - 2 * q, 1)
+            side = pltpu.roll(w_rim[chunk, pl.ds(h * SUB, SUB), :], LANES - 1 - 2 * q, 1)
             w_in = jnp.minimum(jnp.where(lane == 0, side, pltpu.roll(e, 1, 1)), 0.0)
             if h == 0:
-                row = pl.ds(levels * tracers + k, 1)
-                edge = jnp.where(even, b0[row, :], a0[row, :]) * south_flag
+                row = pl.ds(k, 1)
+                edge = jnp.where(even, b_rim[row, :], a_rim[row, :]) * south_flag
             s_in = jnp.minimum(jnp.where(sub == 0, edge, pltpu.roll(n, 1, 0)), 0.0)
             edge = n[SUB - 1 : SUB, :]
             e_out, n_out = jnp.maximum(e, 0.0), jnp.maximum(n, 0.0)
@@ -178,8 +189,7 @@
 
 def step(levels, tracers, rows, chunks, per_chunk, unroll, first, *refs):
     refs = list(refs)
-    field, weights, (west_in, east_in, a_in, b_in) = refs[0], refs[1:7], refs[8:12]
-    above = refs[7]
+    weights, (field, above_in, *rims_in) = refs[:6], refs[6:12]
     refs = refs[12:]
     if first:
         forcing, f_west, f_east, f_a, f_b = refs[:5]
@@ -188,7 +198,7 @@
     if first:
         side_ref, a_ref, b_ref = refs[:3]
         refs = refs[3:]
-    buf, rim, edges, sems = refs
+    buf, above, west_buf, east_buf, a_buf, b_buf, rim, edges, sems = refs
 
     plane = tracers * rows
     halves = rows // SUB
@@ -208,8 +218,23 @@
             buf.at[pl.ds(at + 1, unroll * tracers)], out.at[pl.ds(at, unroll * tracers)], sems.at[b]
         )
 
-    for b in range(blocks):
+    columns, latitudes = pl.ds(0, plane), pl.ds(0, levels * tracers)
+    rim_copies = [
+        pltpu.make_async_copy(source, target, sems.at[blocks + i])
+        for i, (source, target) in enumerate(
+            (
+                (rims_in[0].at[:, columns], west_buf), (rims_in[1].at[:, columns], east_buf),
+                (rims_in[2].at[latitudes], a_buf), (rims_in[3].at[latitudes], b_buf),
+            )
+        )
+    ]
+    above_copy = pltpu.make_async_copy(above_in, above, sems.at[blocks + 4])
+    load(0).start()
+    for copy in rim_copies:
+        copy.start()
+    for b in range(1, blocks):
         load(b).start()
+    above_copy.start()
 
     def meet(target, from_west, from_east, count):
         for chunk in range(chunks):
@@ -233,11 +258,13 @@
 
         lax.fori_loop(0, count // SUB // repeat, body, 0)
 
-    meet(0, west_in, east_in, plane)
-    pair(0, a_in, b_in, levels * tracers)
     if first:
         meet(plane, f_west, f_east, rows)
         pair(levels * tracers, f_a, f_b, levels)
+    for copy in rim_copies:
+        copy.wait()
+    meet(0, west_buf, east_buf, plane)
+    pair(0, a_buf, b_buf, levels * tracers)
 
     def stencil(source, at, rim_row, chunk, turn, row, h, co):
         here = at + h * SUB
@@ -245,48 +272,51 @@
         side = pltpu.roll(rim[chunk, pl.ds(rim_row + h * SUB, SUB), :], turn, 1)
         e = jnp.where(lane == LANES - 1, side, pltpu.roll(cell, LANES - 1, 1))
         w = jnp.where(lane == 0, side, pltpu.roll(cell, 1, 1))
+        n = source[pl.ds(here + 1, SUB), :]
+        s = source[pl.ds(here - 1, SUB), :]
         if h == halves - 1:
-            n = jnp.where(sub == SUB - 1, edges[0, pl.ds(row, 1), :], pltpu.roll(cell, SUB - 1, 0))
-        else:
-            n = source[pl.ds(here + 1, SUB), :]
+            n = jnp.where(sub == SUB - 1, edges[0, pl.ds(row, 1), :], n)
         if h == 0:
-            s = jnp.where(sub == 0, edges[1, pl.ds(row, 1), :], pltpu.roll(cell, 1, 0))
-        else:
-            s = source[pl.ds(here - 1, SUB), :]
+            s = jnp.where(sub == 0, edges[1, pl.ds(row, 1), :], s)
         c0, ce, cw, cn, cs = co[:5]
         return (c0 * cell + ce * e) + (cw * w + cn * n) + cs * s
 
-    def forward(k, solved):
-        chunk, q = k // per_chunk, k % per_chunk
+    def forward(k, chunk, q, solved):
         turn = LANES - 1 - 2 * q
-        new = []
+        co, extra, new = [], [], []
         for h in range(halves):
             blk = pl.ds(pl.multiple_of(k * rows + h * SUB, SUB), SUB)
-            co = [weight[blk, :] for weight in weights]
-            extra = None
+            co.append([weight[blk, :] for weight in weights])
             if first:
-                extra = stencil(forcing, k * rows + SUB, plane, chunk, turn, levels * tracers + k, h, co)
-            for t in range(tracers):
-                at = k * plane + (t + 1) * rows
-                value = stencil(flat, at, t * rows, chunk, turn, k * tracers + t, h, co)
-                if first:
-                    value = value + extra
-                new.append(value + co[5] * solved[h * tracers + t])
-        for h in range(halves):
-            for t in range(tracers):
-                at = k * plane + (t + 1) * rows + h * SUB
-                flat[pl.ds(pl.multiple_of(at, SUB), SUB), :] = new[h * tracers + t]
+                row = levels * tracers + k
+                extra.append(stencil(forcing, k * rows + SUB, plane, chunk, turn, row, h, co[h]))
+        for t in range(tracers):
+            at = k * plane + (t + 1) * rows
+            values = [
+                stencil(flat, at, t * rows, chunk, turn, k * tracers + t, h, co[h]) for h in range(halves)
+            ]
+            for h in range(halves):
+                value = values[h] + extra[h] if first else values[h]
+                value = value + co[h][5] * solved[t * halves + h]
+                new.append(value)
+                flat[pl.ds(pl.multiple_of(at + h * SUB, SUB), SUB), :] = value
         return tuple(new)
 
     def forward_block(b, carry):
-        load(b).wait()
+        @pl.when(b < blocks - 1)
+        def _():
+            load(b + 1).wait()
+
+        chunk, q = b * unroll // per_chunk, b * unroll % per_chunk
         for u in range(unroll):
-            carry = forward(b * unroll + u, carry)
+            carry = forward(b * unroll + u, chunk, q + u, carry)
         return carry
 
     zero = jnp.zeros((SUB, LANES), jnp.float32)
     zeros = (zero,) * (tracers * halves)
+    load(0).wait()
     lax.fori_loop(0, blocks, forward_block, zeros)
+    above_copy.wait()
 
     def backward(k, carry):
         new = []
@@ -331,25 +361,31 @@
     groups = LANES // cap
     pad = groups * group_rows - levels - 3
 
-    def body(i, carry):
-        one = pl.ds(i, 1)
-        tail = [c_buf[one, :].astype(jnp.float32), o_buf[one, :], e_buf[one, :]]
-        wide[pl.ds(0, levels), :] = k_buf[pl.ds(i, levels, stride=per_level), :]
-        wide[pl.ds(levels, pad + 3), :] = jnp.concatenate(
-            tail + [jnp.zeros((pad, LANES), jnp.float32)], axis=0
-        )
-        for j in range(groups):
-            for m in range(group_rows // SUB):
-                made = None
-                for g in range(groups):
-                    piece = wide[pl.ds(g * group_rows + m * SUB, SUB), :]
-                    if g != j:
-                        piece = pltpu.roll(piece, (g - j) * cap % LANES, 1)
-                    made = piece if made is None else jnp.where(lane >= g * cap, piece, made)
-                out[i * groups + j, pl.ds(m * SUB, SUB), :] = made
-        return carry
-
-    lax.fori_loop(0, per_level, body, 0)
+    together = wide.shape[0]
+
+    def body(start, carry):
+        for n in range(together):
+            i = start * together + n
+            one = pl.ds(i, 1)
+            tail = [c_buf[one, :].astype(jnp.float32), o_buf[one, :], e_buf[one, :]]
+            wide[n, pl.ds(0, levels), :] = k_buf[pl.ds(i, levels, stride=per_level), :]
+            wide[n, pl.ds(levels, pad + 3), :] = jnp.concatenate(
+                tail + [jnp.zeros((pad, LANES), jnp.float32)], axis=0
+            )
+        for n in range(together):
+            i = start * together + n
+            for j in range(groups):
+                for m in range(group_rows // SUB):
+                    made = None
+                    for g in range(groups):
+                        piece = wide[n, pl.ds(g * group_rows + m * SUB, SUB), :]
+                        if g != j:
+                            piece = pltpu.roll(piece, (g - j) * cap % LANES, 1)
+                        made = piece if made is None else jnp.where(lane >= g * cap, piece, made)
+                    out[i * groups + j, pl.ds(m * SUB, SUB), :] = made
+        return carry
+
+    lax.fori_loop(0, per_level // together, body, 0)
 
 
 def tracer_sum(block, concentration, out, buf, sems):
@@ -511,7 +547,8 @@
     bricks = lax.axis_size("lon") * lax.axis_size("lat")
     slots = sound_col.shape[2]
     cap = slots // bricks
-    chunks, per_chunk = rim_chunks(levels)
+    unroll = largest(levels, 8, 4, 3, 2, 1)
+    chunks, per_chunk = rim_chunks(levels, unroll)
     plane = tracers * rows
     per_level = slots // LANES
     groups = LANES // cap
@@ -527,7 +564,8 @@
         [HBM] * 4, f32(bricks, group_rows, LANES), VMEM,
         (
             vmem(levels * per_level, LANES), pltpu.VMEM((per_level, LANES), jnp.int32),
-            vmem(per_level, LANES), vmem(per_level, LANES), vmem(groups * group_rows, LANES), dma((4,)),
+            vmem(per_level, LANES), vmem(per_level, LANES),
+            vmem(largest(per_level, 8, 4, 2, 1), groups * group_rows, LANES), dma((4,)),
         ),
         4, 10, 800000, "pack",
     )(*(in_hbm(flat(x)) for x in (kernel, sound_col, observed, obs_error)))
@@ -561,7 +599,7 @@
         [VMEM] * 2,
         (
             f32(levels * rows + 2 * SUB, LANES), f32(chunks, rows, LANES), f32(levels, LANES), f32(levels, LANES),
-            f32(bricks, LANES),
+            hbm(bricks, LANES),
         ),
         (VMEM,) * 5,
         (
@@ -573,31 +611,34 @@
     )(received, sums)
     forcing_rims = exchange(*rims)
 
-    unroll = largest(levels, 8, 4, 3, 2, 1)
-    weights = call(
+    *weights, above = call(
         functools.partial(coefficients, levels, tracers, rows, per_chunk, unroll),
-        [HBM] * 3 + [VMEM] * 3, (f32(levels * rows, LANES),) * 7, (VMEM,) * 7,
-        (vmem(levels * rows, LANES),) * 3 + (dma((3,)),),
+        [HBM] * 3 + [ANY] * 3, (f32(levels * rows, LANES),) * 6 + (hbm(levels * rows, LANES),), (VMEM,) * 7,
+        (vmem(levels * rows, LANES),) * 3
+        + (vmem(chunks, rows, LANES), vmem(levels, LANES), vmem(levels, LANES), dma((6,))),
         4, field_bytes, field_bytes, "coefficients",
     )(east, north, mix, start_rims[0], start_rims[2], start_rims[3])
 
-    def advance(value, first, *operands):
-        outs, specs = (f32(*value.shape),), (HBM,)
+    def advance(value, rims, first, *operands):
+        outs, specs = ((hbm if first else f32)(*value.shape),), (HBM,)
         if first:
             outs += (f32(chunks, plane, LANES), f32(levels * tracers, LANES), f32(levels * tracers, LANES))
             specs += (VMEM,) * 3
         return call(
             functools.partial(step, levels, tracers, rows, chunks, per_chunk, unroll, first),
-            [HBM] + [VMEM] * (7 + len(operands)), outs, specs,
+            [VMEM] * 6 + [HBM] * 2 + [ANY] * 4 + [VMEM] * len(operands), outs, specs,
             (
-                vmem(levels * tracers + 2, rows, LANES), vmem(chunks, plane + rows, LANES),
-                vmem(2, levels * tracers + levels, LANES), dma((levels // unroll,)),
+                vmem(levels * tracers + 2, rows, LANES), vmem(levels * rows, LANES),
+                vmem(chunks, plane, LANES), vmem(chunks, plane, LANES),
+                vmem(levels * tracers, LANES), vmem(levels * tracers, LANES),
+                vmem(chunks, plane + rows, LANES), vmem(2, levels * tracers + levels, LANES),
+                dma((levels // unroll + 5,)),
             ),
-            8, field_bytes * 8, field_bytes * 2, "step",
-        )(value, *weights, *operands)
-
-    stepped, *rims = advance(in_hbm(field), True, *start_rims, forcing, *forcing_rims)
-    (result,) = advance(stepped, False, *exchange(*rims))
+            10, field_bytes * 8, field_bytes * 2, "step",
+        )(*weights, in_hbm(value), in_hbm(above), *rims, *operands)
+
+    stepped, *rims = advance(field, start_rims, True, forcing, *forcing_rims)
+    (result,) = advance(stepped, exchange(*rims), False)
 
     returned = lax.all_to_all(
         back.reshape(bricks, 1, LANES), ("lon", "lat"), split_axis=0, concat_axis=0, tiled=True

time: 80.5 us -> 75 us (0.932)
  local copies, waits for them, and re-layouts: 14.2 us -> 7.82 us
  Pallas kernels: 33.7 us -> 34.8 us
    unnamed x30 -> x20, local copies, waits for them, and re-layouts: 14.2 us -> 7.82 us
    pallas_call x1, Pallas kernels: 2.82 us -> 3.64 us  [per_device(): call(functools.partial(coefficients, levels, tracers, rows, per_chunk, un...]
  transfers between devices with their start and end apart: 14 -> 14, of which waited for: 2 -> 2; matrix products, arithmetic and copies ran while one was open for 0% -> 0% of each run, Pallas kernels for 25% -> 29%
where the time goes in v3:
time: 75 us; the launch traced here: 74.3 us
  Pallas kernels  34.8 us (46%)
  starting transfers between devices  29.2 us (39%)
  local copies, waits for them, and re-layouts  7.82 us (10%)
  waiting for transfers between devices  1.73 us (2%)
  between operations  0.82 us (1%)
    pallas_call x2, Pallas kernels, advance(): call(functools.partial(step, levels, tracers, rows, chunks, per_chunk, un...  19.4 us
    unnamed x20, local copies, waits for them, and re-layouts  7.82 us
    all_to_all x1, starting transfers between devices, per_device(): lax.all_to_all(packed, ('lon', 'lat'), split_axis=0, concat_axis=0, tiled...  7.3 us
    ppermute x3, starting transfers between devices, exchange(): lax.ppermute(a_rim, 'lat', [(j, partner(j, 0)) for j in range(lats)])  6.59 us
    all_to_all x1, starting transfers between devices, per_device(): lax.all_to_all(back.reshape(bricks, 1, LANES), ('lon', 'lat'), split_axis...  5.09 us
    ppermute x3, starting transfers between devices, exchange(): lax.ppermute(b_rim, 'lat', [(j, partner(j, 1)) for j in range(lats)])  5.06 us
    pallas_call x1, Pallas kernels, per_device(): call(functools.partial(first_rims, levels, tracers, rows, chunks, per_chu...  5.05 us
    ppermute x3, starting transfers between devices, exchange(): lax.ppermute(side_rim, 'lon', [((i + 1) % lons, i) for i in range(lons)])  4.55 us
  transfers between devices with their start and end apart: 14, of which 2 were waited for; matrix products, arithmetic and copies ran while one was open for 0% of the time, Pallas kernels for 29%

profile of v3, /device:TPU:0, one launch (start us, length us, event | category | flops | bytes accessed | tf_op | source)
XLA Modules:
  0.0 74.3 jit_solution(12023775771714555129)
XLA Ops:
  0.6 2.1 %pack.1 = f32[32,24,128]{2,1,0:T(8,128)} custom-call(f32[576,128]{1,0:T(8,128)} %bitcast.24, s32[8,128]{1,0:T(8,128)} %bitcast.26, f32[8,128]{1,0:T(8,128)} %bitcast.27, f32[8,128]{1,0:T(8,128)} %bitcast.28), custom_call_target="tpu_custom_call" | custom-call | flops 10 | bytes 800000 | tf_op jit(solution)/shard_map/pack/pallas_call | solution.py:562
  2.8 7.3 %all-to-all-start = ((f32[32,24,128]{2,1,0:T(8,128)}), f32[32,24,128]{2,1,0:T(8,128)S(1)}, u32[]{:S(2)}, u32[]{:S(2)}) async-start(f32[32,24,128]{2,1,0:T(8,128)} %pack.1), calls=%async_computation | async-start | bytes 786432 | tf_op jit(solution)/shard_map/all_to_all | solution.py:572
  10.1 0.0 copy-start
  10.1 5.0 %first_rims.1 = (f32[2,144,128]{2,1,0:T(8,128)}, f32[648,128]{1,0:T(8,128)S(1)}, f32[648,128]{1,0:T(8,128)S(1)}) custom-call(f32[9216,128]{1,0:T(8,128)} %bitcast.16, f32[1152,128]{1,0:T(8,128)} %bitcast.19, f32[1152,128]{1,0:T(8,128)} %bitcast.21), custom_call_target="tpu_custom_call" | custom-call | flops 4718592 | bytes 9437184 | tf_op jit(solution)/shard_map/first_rims/pallas_call | solution.py:576
  15.2 1.8 %collective-permute-start.1 = (f32[648,128]{1,0:T(8,128)S(1)}, f32[648,128]{1,0:T(8,128)S(1)}, u32[]{:S(2)}, u32[]{:S(2)}) collective-permute-start(f32[648,128]{1,0:T(8,128)S(1)} %get-tuple-element.24), channel_id=1, source_target_pairs={{0,1},{1,0},{2,3},{3,2},{4,5},{5,4},{6,7},{7,6},{8,9},{9,8},{10,11... | collective-permute-start | bytes 995336 | tf_op jit(solution)/shard_map/ppermute | solution.py:538
  17.0 0.7 collective-permute-start.2
  17.7 0.1 collective-permute-start
  17.7 2.6 %collective-permute-start.3 = (f32[2,144,128]{2,1,0:T(8,128)}, f32[2,144,128]{2,1,0:T(8,128)}, u32[]{:S(2)}, u32[]{:S(2)}) collective-permute-start(f32[2,144,128]{2,1,0:T(8,128)} %get-tuple-element.23), channel_id=1, source_target_pairs={{4,0},{8,4},{12,8},{16,12},{20,16},{24,20},{28,24},{0,28},{5,1},{9... | collective-permute-start | bytes 442376 | tf_op jit(solution)/shard_map/ppermute | solution.py:537
  20.4 0.0 copy-done
  20.4 0.7 tracer_sum.1.sums
  21.1 1.2 %all-to-all-done.received = f32[32,24,128]{2,1,0:T(8,128)S(1)} async-done(((f32[32,24,128]{2,1,0:T(8,128)}), f32[32,24,128]{2,1,0:T(8,128)S(1)}, u32[]{:S(2)}, u32[]{:S(2)}) %all-to-all-start) | async-done | bytes 393248 | tf_op jit(solution)/shard_map/all_to_all | solution.py:572
  22.3 3.2 %soundings.1 = (f32[1168,128]{1,0:T(8,128)S(1)}, f32[2,16,128]{2,1,0:T(8,128)S(1)}, f32[72,128]{1,0:T(8,128)S(1)}, f32[72,128]{1,0:T(8,128)S(1)}, f32[32,128]{1,0:T(8,128)}) custom-call(f32[32,24,128]{2,1,0:T(8,128)S(1)} %all-to-all-done.received, bf16[2,576,256]{2,1,0:T(8,128)(2,1)S(1)} %tracer_sum.1.sums), custom_call_target="tpu_custom_call" | custom-call | flops 37748736 | bytes 4718592 | tf_op jit(solution)/shard_map/soundings/pallas_call | solution.py:597
  25.5 3.0 %collective-permute-start.6 = (f32[72,128]{1,0:T(8,128)S(1)}, f32[72,128]{1,0:T(8,128)S(1)}, u32[]{:S(2)}, u32[]{:S(2)}) collective-permute-start(f32[72,128]{1,0:T(8,128)S(1)} %get-tuple-element.35), channel_id=1, source_target_pairs={{0,1},{1,0},{2,3},{3,2},{4,5},{5,4},{6,7},{7,6},{8,9},{9,8},{10,11... | collective-permute-start | bytes 110600 | tf_op jit(solution)/shard_map/ppermute | solution.py:538
  28.5 0.0 collective-permute-done.west0.refs_8_
  28.5 0.0 copy-start.7
  28.5 0.7 copy-done.7
  29.2 0.7 collective-permute-start.7
  29.8 0.0 collective-permute-done.1.a0.refs_10_
  29.8 0.0 copy-start.1
  29.9 0.7 copy-done.1
  30.6 0.0 collective-permute-start.5
  30.6 0.0 collective-permute-done.2.b0.refs_11_
  30.6 0.0 copy-start.4
  30.6 0.7 copy-done.4
  31.3 0.5 collective-permute-start.4
  31.8 0.0 copy-start.2
  31.8 1.0 %copy-done.2 = f32[648,128]{1,0:T(8,128)S(1)} copy-done((f32[648,128]{1,0:T(8,128)S(1)}, f32[648,128]{1,0:T(8,128)}, u32[]{:S(2)}) %copy-start.2) | copy-done | bytes 331800
  32.8 0.0 copy-start.5
  32.8 1.0 %copy-done.5 = f32[648,128]{1,0:T(8,128)S(1)} copy-done((f32[648,128]{1,0:T(8,128)S(1)}, f32[648,128]{1,0:T(8,128)}, u32[]{:S(2)}) %copy-start.5) | copy-done | bytes 331800
  33.8 0.0 copy-start.8
  33.8 0.9 %copy-done.8 = f32[2,144,128]{2,1,0:T(8,128)S(1)} copy-done((f32[2,144,128]{2,1,0:T(8,128)S(1)}, f32[2,144,128]{2,1,0:T(8,128)}, u32[]{:S(2)}) %copy-start.8) | copy-done | bytes 147480
  34.7 3.6 %coefficients.1 = (f32[1152,128]{1,0:T(8,128)S(1)}, f32[1152,128]{1,0:T(8,128)S(1)}, f32[1152,128]{1,0:T(8,128)S(1)}, f32[1152,128]{1,0:T(8,128)S(1)}, f32[1152,...) custom-call(f32[1152,128]{1,0:T(8,128)} %bitcast.20, f32[1152,128]{1,0:T(8,128)} %bitcast.22, ...), custom_call_target="tpu_custom_call" | custom-call | flops 4718592 | bytes 4718592 | tf_op jit(solution)/shard_map/coefficients/pallas_call | solution.py:614
  38.3 0.0 collective-permute-done.3.refs_9_
  38.3 0.0 collective-permute-done.5.refs_14_
  38.3 0.0 collective-permute-done.4.refs_13_
  38.3 0.0 collective-permute-done.6.refs_15_
  38.4 0.0 collective-permute-done.7.refs_16_
  38.4 0.0 copy-start.3
  38.4 1.0 %copy-done.3 = f32[648,128]{1,0:T(8,128)S(1)} copy-done((f32[648,128]{1,0:T(8,128)S(1)}, f32[648,128]{1,0:T(8,128)}, u32[]{:S(2)}) %copy-start.3) | copy-done | bytes 331800
  39.3 0.0 copy-start.6
  39.3 1.0 %copy-done.6 = f32[648,128]{1,0:T(8,128)S(1)} copy-done((f32[648,128]{1,0:T(8,128)S(1)}, f32[648,128]{1,0:T(8,128)}, u32[]{:S(2)}) %copy-start.6) | copy-done | bytes 331800
  40.3 0.0 copy-start.9
  40.3 0.9 %copy-done.9 = f32[2,144,128]{2,1,0:T(8,128)S(1)} copy-done((f32[2,144,128]{2,1,0:T(8,128)S(1)}, f32[2,144,128]{2,1,0:T(8,128)}, u32[]{:S(2)}) %copy-start.9) | copy-done | bytes 147480
  41.2 10.4 %step.2 = (f32[576,16,128]{2,1,0:T(8,128)}, f32[2,128,128]{2,1,0:T(8,128)}, f32[576,128]{1,0:T(8,128)}, f32[576,128]{1,0:T(8,128)}) custom-call(f32[1152,128]{1,0:T(8,128)S(1)} %get-tuple-element.26.refs_0_, f32[1152,128]{1,0:T(8,128)S(1)} %get-tuple-element.27.refs_1_, f32[1152,128]{1,0:T(8,128)S(1)} %get-tuple-element.28.refs_2_, ...), custom_call_target="tpu_custom_call" | custom-call | flops 37748736 | bytes 9437184 | tf_op jit(solution)/shard_map/step/pallas_call | solution.py:627
  51.7 1.7 %collective-permute-start.10 = (f32[576,128]{1,0:T(8,128)}, f32[576,128]{1,0:T(8,128)}, u32[]{:S(2)}, u32[]{:S(2)}) collective-permute-start(f32[576,128]{1,0:T(8,128)} %get-tuple-element.39), channel_id=1, source_target_pairs={{0,1},{1,0},{2,3},{3,2},{4,5},{5,4},{6,7},{7,6},{8,9},{9,8},{10,11... | collective-permute-start | bytes 884744 | tf_op jit(solution)/shard_map/ppermute | solution.py:538
  53.4 3.7 %collective-permute-start.11 = (f32[576,128]{1,0:T(8,128)}, f32[576,128]{1,0:T(8,128)}, u32[]{:S(2)}, u32[]{:S(2)}) collective-permute-start(f32[576,128]{1,0:T(8,128)} %get-tuple-element.40), channel_id=1, source_target_pairs={{0,0},{1,2},{2,1},{3,3},{4,4},{5,6},{6,5},{7,7},{8,8},{9,10},{10,9... | collective-permute-start | bytes 884744 | tf_op jit(solution)/shard_map/ppermute | solution.py:539
  57.1 1.9 %collective-permute-start.9 = (f32[2,128,128]{2,1,0:T(8,128)}, f32[2,128,128]{2,1,0:T(8,128)}, u32[]{:S(2)}, u32[]{:S(2)}) collective-permute-start(f32[2,128,128]{2,1,0:T(8,128)} %get-tuple-element.38), channel_id=1, source_target_pairs={{4,0},{8,4},{12,8},{16,12},{20,16},{24,20},{28,24},{0,28},{5,1},{9... | collective-permute-start | bytes 393224 | tf_op jit(solution)/shard_map/ppermute | solution.py:537
  59.1 0.0 collective-permute-start.8
  59.1 5.1 %all-to-all-start.1 = ((f32[32,1,128]{2,1,0:T(1,128)}), f32[32,1,128]{2,1,0:T(1,128)S(1)}, u32[]{:S(2)}, u32[]{:S(2)}) async-start(f32[32,1,128]{2,1,0:T(1,128)} %bitcast.25), calls=%async_computation.1 | async-start | bytes 32768 | tf_op jit(solution)/shard_map/all_to_all | solution.py:643
  64.2 0.0 collective-permute-done.9.refs_9_
  64.2 0.5 collective-permute-done.8.refs_8_
  64.7 0.0 collective-permute-done.10.refs_10_
  64.7 0.0 collective-permute-done.11.refs_11_
  64.7 8.9 %step.3 = f32[576,16,128]{2,1,0:T(8,128)} custom-call(f32[1152,128]{1,0:T(8,128)S(1)} %get-tuple-element.26.refs_0_, f32[1152,128]{1,0:T(8,128)S(1)} %get-tuple-element.27.refs_1_, f32[1152,128]{1,0:T(8,128)S(1)} %get-tuple-element.28.refs_2_, f32[1152,128]{1,0:T(8,128)S(1)} %get-tuple-element.29.refs_3_, f32[1152,128]{1,0:T(8,128)S(1)} %get-tuple-element.30.refs_4_, ...), custom_call_target="tpu_custom_call" | custom-call | flops 37748736 | bytes 9437184 | tf_op jit(solution)/shard_map/step/pallas_call | solution.py:627
  73.6 0.0 all-to-all-done.1
  73.6 0.7 residual.1
Async XLA Ops:
  2.8 19.5 %all-to-all-start = ((f32[32,24,128]{2,1,0:T(8,128)}), f32[32,24,128]{2,1,0:T(8,128)S(1)}, u32[]{:S(2)}, u32[]{:S(2)}) async-start(f32[32,24,128]{2,1,0:T(8,128)} %pack.1), calls=%async_computation | async-start | bytes 786432 | tf_op jit(solution)/shard_map/all_to_all | solution.py:572
  10.1 10.3 %copy-start = (f32[72,8,16,128]{3,2,1,0:T(8,128)S(1)}, f32[72,8,16,128]{3,2,1,0:T(8,128)}, u32[]{:S(2)}) copy-start(f32[72,8,16,128]{3,2,1,0:T(8,128)} %concentration.1) | copy-start | bytes 14155780
  15.2 14.7 %collective-permute-start.1 = (f32[648,128]{1,0:T(8,128)S(1)}, f32[648,128]{1,0:T(8,128)S(1)}, u32[]{:S(2)}, u32[]{:S(2)}) collective-permute-start(f32[648,128]{1,0:T(8,128)S(1)} %get-tuple-element.24), channel_id=1, source_target_pairs={{0,1},{1,0},{2,3},{3,2},{4,5},{5,4},{6,7},{7,6},{8,9},{9,8},{10,11... | collective-permute-start | bytes 995336 | tf_op jit(solution)/shard_map/ppermute | solution.py:538
  17.0 13.6 %collective-permute-start.2 = (f32[648,128]{1,0:T(8,128)S(1)}, f32[648,128]{1,0:T(8,128)S(1)}, u32[]{:S(2)}, u32[]{:S(2)}) collective-permute-start(f32[648,128]{1,0:T(8,128)S(1)} %get-tuple-element.25), channel_id=1, source_target_pairs={{0,0},{1,2},{2,1},{3,3},{4,4},{5,6},{6,5},{7,7},{8,8},{9,10},{10,9... | collective-permute-start | bytes 995336 | tf_op jit(solution)/shard_map/ppermute | solution.py:539
  17.7 10.8 %collective-permute-start = (f32[2,144,128]{2,1,0:T(8,128)}, f32[2,144,128]{2,1,0:T(8,128)S(1)}, u32[]{:S(2)}, u32[]{:S(2)}) collective-permute-start(f32[2,144,128]{2,1,0:T(8,128)} %get-tuple-element.23), channel_id=1, source_target_pairs={{0,4},{4,8},{8,12},{12,16},{16,20},{20,24},{24,28},{28,0},{1,5},{5... | collective-permute-start | bytes 442376 | tf_op jit(solution)/shard_map/ppermute | solution.py:536
  17.7 20.6 %collective-permute-start.3 = (f32[2,144,128]{2,1,0:T(8,128)}, f32[2,144,128]{2,1,0:T(8,128)}, u32[]{:S(2)}, u32[]{:S(2)}) collective-permute-start(f32[2,144,128]{2,1,0:T(8,128)} %get-tuple-element.23), channel_id=1, source_target_pairs={{4,0},{8,4},{12,8},{16,12},{20,16},{24,20},{28,24},{0,28},{5,1},{9... | collective-permute-start | bytes 442376 | tf_op jit(solution)/shard_map/ppermute | solution.py:537
  25.5 12.9 %collective-permute-start.6 = (f32[72,128]{1,0:T(8,128)S(1)}, f32[72,128]{1,0:T(8,128)S(1)}, u32[]{:S(2)}, u32[]{:S(2)}) collective-permute-start(f32[72,128]{1,0:T(8,128)S(1)} %get-tuple-element.35), channel_id=1, source_target_pairs={{0,1},{1,0},{2,3},{3,2},{4,5},{5,4},{6,7},{7,6},{8,9},{9,8},{10,11... | collective-permute-start | bytes 110600 | tf_op jit(solution)/shard_map/ppermute | solution.py:538
  28.5 0.7 copy-start.7
  29.2 9.2 %collective-permute-start.7 = (f32[72,128]{1,0:T(8,128)S(1)}, f32[72,128]{1,0:T(8,128)S(1)}, u32[]{:S(2)}, u32[]{:S(2)}) collective-permute-start(f32[72,128]{1,0:T(8,128)S(1)} %get-tuple-element.36), channel_id=1, source_target_pairs={{0,0},{1,2},{2,1},{3,3},{4,4},{5,6},{6,5},{7,7},{8,8},{9,10},{10,9... | collective-permute-start | bytes 110600 | tf_op jit(solution)/shard_map/ppermute | solution.py:539
  29.8 0.7 copy-start.1
  30.6 7.8 %collective-permute-start.5 = (f32[2,16,128]{2,1,0:T(8,128)S(1)}, f32[2,16,128]{2,1,0:T(8,128)S(1)}, u32[]{:S(2)}, u32[]{:S(2)}) collective-permute-start(f32[2,16,128]{2,1,0:T(8,128)S(1)} %get-tuple-element.34), channel_id=1, source_target_pairs={{4,0},{8,4},{12,8},{16,12},{20,16},{24,20},{28,24},{0,28},{5,1},{9... | collective-permute-start | bytes 49160 | tf_op jit(solution)/shard_map/ppermute | solution.py:537
  30.6 0.7 copy-start.4
  31.3 7.0 %collective-permute-start.4 = (f32[2,16,128]{2,1,0:T(8,128)S(1)}, f32[2,16,128]{2,1,0:T(8,128)S(1)}, u32[]{:S(2)}, u32[]{:S(2)}) collective-permute-start(f32[2,16,128]{2,1,0:T(8,128)S(1)} %get-tuple-element.34), channel_id=1, source_target_pairs={{0,4},{4,8},{8,12},{12,16},{16,20},{20,24},{24,28},{28,0},{1,5},{5... | collective-permute-start | bytes 49160 | tf_op jit(solution)/shard_map/ppermute | solution.py:536
  31.8 1.0 %copy-start.2 = (f32[648,128]{1,0:T(8,128)S(1)}, f32[648,128]{1,0:T(8,128)}, u32[]{:S(2)}) copy-start(f32[648,128]{1,0:T(8,128)} %copy-done.1) | copy-start | bytes 995332
  32.8 1.0 %copy-start.5 = (f32[648,128]{1,0:T(8,128)S(1)}, f32[648,128]{1,0:T(8,128)}, u32[]{:S(2)}) copy-start(f32[648,128]{1,0:T(8,128)} %copy-done.4) | copy-start | bytes 995332
  33.8 0.9 %copy-start.8 = (f32[2,144,128]{2,1,0:T(8,128)S(1)}, f32[2,144,128]{2,1,0:T(8,128)}, u32[]{:S(2)}) copy-start(f32[2,144,128]{2,1,0:T(8,128)} %copy-done.7) | copy-start | bytes 442372
  38.4 1.0 %copy-start.3 = (f32[648,128]{1,0:T(8,128)S(1)}, f32[648,128]{1,0:T(8,128)}, u32[]{:S(2)}) copy-start(f32[648,128]{1,0:T(8,128)} %copy-done.1) | copy-start | bytes 995332
  39.3 1.0 %copy-start.6 = (f32[648,128]{1,0:T(8,128)S(1)}, f32[648,128]{1,0:T(8,128)}, u32[]{:S(2)}) copy-start(f32[648,128]{1,0:T(8,128)} %copy-done.4) | copy-start | bytes 995332
  40.3 0.9 %copy-start.9 = (f32[2,144,128]{2,1,0:T(8,128)S(1)}, f32[2,144,128]{2,1,0:T(8,128)}, u32[]{:S(2)}) copy-start(f32[2,144,128]{2,1,0:T(8,128)} %copy-done.7) | copy-start | bytes 442372
  51.7 13.0 %collective-permute-start.10 = (f32[576,128]{1,0:T(8,128)}, f32[576,128]{1,0:T(8,128)}, u32[]{:S(2)}, u32[]{:S(2)}) collective-permute-start(f32[576,128]{1,0:T(8,128)} %get-tuple-element.39), channel_id=1, source_target_pairs={{0,1},{1,0},{2,3},{3,2},{4,5},{5,4},{6,7},{7,6},{8,9},{9,8},{10,11... | collective-permute-start | bytes 884744 | tf_op jit(solution)/shard_map/ppermute | solution.py:538
  53.4 11.3 %collective-permute-start.11 = (f32[576,128]{1,0:T(8,128)}, f32[576,128]{1,0:T(8,128)}, u32[]{:S(2)}, u32[]{:S(2)}) collective-permute-start(f32[576,128]{1,0:T(8,128)} %get-tuple-element.40), channel_id=1, source_target_pairs={{0,0},{1,2},{2,1},{3,3},{4,4},{5,6},{6,5},{7,7},{8,8},{9,10},{10,9... | collective-permute-start | bytes 884744 | tf_op jit(solution)/shard_map/ppermute | solution.py:539
  57.1 7.0 %collective-permute-start.9 = (f32[2,128,128]{2,1,0:T(8,128)}, f32[2,128,128]{2,1,0:T(8,128)}, u32[]{:S(2)}, u32[]{:S(2)}) collective-permute-start(f32[2,128,128]{2,1,0:T(8,128)} %get-tuple-element.38), channel_id=1, source_target_pairs={{4,0},{8,4},{12,8},{16,12},{20,16},{24,20},{28,24},{0,28},{5,1},{9... | collective-permute-start | bytes 393224 | tf_op jit(solution)/shard_map/ppermute | solution.py:537
  59.1 5.6 %collective-permute-start.8 = (f32[2,128,128]{2,1,0:T(8,128)}, f32[2,128,128]{2,1,0:T(8,128)}, u32[]{:S(2)}, u32[]{:S(2)}) collective-permute-start(f32[2,128,128]{2,1,0:T(8,128)} %get-tuple-element.38), channel_id=1, source_target_pairs={{0,4},{4,8},{8,12},{12,16},{16,20},{20,24},{24,28},{28,0},{1,5},{5... | collective-permute-start | bytes 393224 | tf_op jit(solution)/shard_map/ppermute | solution.py:536
  59.1 14.6 %all-to-all-start.1 = ((f32[32,1,128]{2,1,0:T(1,128)}), f32[32,1,128]{2,1,0:T(1,128)S(1)}, u32[]{:S(2)}, u32[]{:S(2)}) async-start(f32[32,1,128]{2,1,0:T(1,128)} %bitcast.25), calls=%async_computation.1 | async-start | bytes 32768 | tf_op jit(solution)/shard_map/all_to_all | solution.py:643

commit v4 on v3

--- a/solution.py
+++ b/solution.py
@@ -125,22 +125,45 @@
         )
 
 
-def coefficients(levels, tracers, rows, per_chunk, unroll, east, north, mixing, west0, a0, b0, *refs):
-    outs, (e_buf, n_buf, m_buf, w_rim, a_rim, b_rim, sems) = refs[:7], refs[7:]
+def meet(rim, target, from_west, from_east, count):
+    lane = lane_iota()
+    for chunk in range(rim.shape[0]):
+        for r in range(0, count, SUB):
+            rows = pl.ds(r, SUB)
+            turned = pltpu.roll(from_east[chunk, rows, :], LANES - 2, 1)
+            rim[chunk, pl.ds(target + r, SUB), :] = jnp.where(lane % 2 == 1, from_west[chunk, rows, :], turned)
+
+
+def pair(edges, target, from_a, from_b, count):
+    even = jnp.full((SUB, LANES), lax.axis_index("lat"), jnp.int32) % 2 == 0
+    repeat = largest(count // SUB, 9, 8, 4, 2, 1)
+
+    def body(i, carry):
+        for u in range(repeat):
+            at = pl.multiple_of((i * repeat + u) * SUB, SUB)
+            a, b = from_a[pl.ds(at, SUB), :], from_b[pl.ds(at, SUB), :]
+            edges[0, pl.ds(target + at, SUB), :] = jnp.where(even, a, b)
+            edges[1, pl.ds(target + at, SUB), :] = jnp.where(even, b, a)
+        return carry
+
+    lax.fori_loop(0, count // SUB // repeat, body, 0)
+
+
+def coefficients(
+    levels, tracers, rows, per_chunk, unroll, east, north, mixing, west0, east0, a0, b0, *refs
+):
+    outs, (rim, edges), (e_buf, n_buf, m_buf, sems) = refs[:7], refs[7:9], refs[9:]
     plane = tracers * rows
     halves = rows // SUB
     lane, sub = lane_iota(), sub_iota()
     copies = [
         pltpu.make_async_copy(source, target, sems.at[i])
-        for i, (source, target) in enumerate(
-            (
-                (east, e_buf), (north, n_buf), (mixing, m_buf), (west0.at[:, pl.ds(plane, rows)], w_rim),
-                (a0.at[pl.ds(levels * tracers, levels)], a_rim), (b0.at[pl.ds(levels * tracers, levels)], b_rim),
-            )
-        )
+        for i, (source, target) in enumerate(((east, e_buf), (north, n_buf), (mixing, m_buf)))
     ]
     for copy in copies:
         copy.start()
+    meet(rim, 0, west0, east0, plane)
+    pair(edges, 0, a0, b0, levels * tracers)
     for copy in copies:
         copy.wait()
     place = lax.axis_index("lat")
@@ -161,11 +184,11 @@
             factor = up * inv
             new.append((up, factor))
             e, n = e_buf[blk, :], n_buf[blk, :]
-            side = pltpu.roll(w_rim[chunk, pl.ds(h * SUB, SUB), :], LANES - 1 - 2 * q, 1)
+            side = pltpu.roll(west0[chunk, pl.ds(plane + h * SUB, SUB), :], LANES - 1 - 2 * q, 1)
             w_in = jnp.minimum(jnp.where(lane == 0, side, pltpu.roll(e, 1, 1)), 0.0)
             if h == 0:
-                row = pl.ds(k, 1)
-                edge = jnp.where(even, b_rim[row, :], a_rim[row, :]) * south_flag
+                row = pl.ds(levels * tracers + k, 1)
+                edge = jnp.where(even, b0[row, :], a0[row, :]) * south_flag
             s_in = jnp.minimum(jnp.where(sub == 0, edge, pltpu.roll(n, 1, 0)), 0.0)
             edge = n[SUB - 1 : SUB, :]
             e_out, n_out = jnp.maximum(e, 0.0), jnp.maximum(n, 0.0)
@@ -189,16 +212,13 @@
 
 def step(levels, tracers, rows, chunks, per_chunk, unroll, first, *refs):
     refs = list(refs)
-    weights, (field, above_in, *rims_in) = refs[:6], refs[6:12]
-    refs = refs[12:]
+    weights, (field, above_in) = refs[:6], refs[6:8]
     if first:
-        forcing, f_west, f_east, f_a, f_b = refs[:5]
-        refs = refs[5:]
-    out = refs.pop(0)
-    if first:
-        side_ref, a_ref, b_ref = refs[:3]
-        refs = refs[3:]
-    buf, above, west_buf, east_buf, a_buf, b_buf, rim, edges, sems = refs
+        rim, edges, forcing, f_west, f_east, f_a, f_b, out, side_ref, a_ref, b_ref = refs[8:19]
+        buf, above, rim_now, f_rim, f_edges, sems = refs[19:]
+    else:
+        west_in, east_in, a_in, b_in, out = refs[8:13]
+        buf, above, rim_now, west_buf, east_buf, a_buf, b_buf, rim, edges, sems = refs[13:]
 
     plane = tracers * rows
     halves = rows // SUB
@@ -218,17 +238,15 @@
             buf.at[pl.ds(at + 1, unroll * tracers)], out.at[pl.ds(at, unroll * tracers)], sems.at[b]
         )
 
-    columns, latitudes = pl.ds(0, plane), pl.ds(0, levels * tracers)
-    rim_copies = [
-        pltpu.make_async_copy(source, target, sems.at[blocks + i])
-        for i, (source, target) in enumerate(
-            (
-                (rims_in[0].at[:, columns], west_buf), (rims_in[1].at[:, columns], east_buf),
-                (rims_in[2].at[latitudes], a_buf), (rims_in[3].at[latitudes], b_buf),
+    rim_copies = []
+    if not first:
+        rim_copies = [
+            pltpu.make_async_copy(source, target, sems.at[blocks + 1 + i])
+            for i, (source, target) in enumerate(
+                ((west_in, west_buf), (east_in, east_buf), (a_in, a_buf), (b_in, b_buf))
             )
-        )
-    ]
-    above_copy = pltpu.make_async_copy(above_in, above, sems.at[blocks + 4])
+        ]
+    above_copy = pltpu.make_async_copy(above_in, above, sems.at[blocks])
     load(0).start()
     for copy in rim_copies:
         copy.start()
@@ -236,81 +254,80 @@
         load(b).start()
     above_copy.start()
 
-    def meet(target, from_west, from_east, count):
-        for chunk in range(chunks):
-            for r in range(0, count, SUB):
-                a, b = pl.ds(target + r, SUB), pl.ds(r, SUB)
-                turned = pltpu.roll(from_east[chunk, b, :], LANES - 2, 1)
-                rim[chunk, a, :] = jnp.where(lane % 2 == 1, from_west[chunk, b, :], turned)
-
-    even = jnp.full((SUB, LANES), lax.axis_index("lat"), jnp.int32) % 2 == 0
-
-    def pair(target, from_a, from_b, count):
-        repeat = largest(count // SUB, 9, 8, 4, 2, 1)
-
-        def body(i, carry):
-            for u in range(repeat):
-                at = pl.multiple_of((i * repeat + u) * SUB, SUB)
-                a, b = from_a[pl.ds(at, SUB), :], from_b[pl.ds(at, SUB), :]
-                edges[0, pl.ds(target + at, SUB), :] = jnp.where(even, a, b)
-                edges[1, pl.ds(target + at, SUB), :] = jnp.where(even, b, a)
-            return carry
-
-        lax.fori_loop(0, count // SUB // repeat, body, 0)
-
     if first:
-        meet(plane, f_west, f_east, rows)
-        pair(levels * tracers, f_a, f_b, levels)
-    for copy in rim_copies:
-        copy.wait()
-    meet(0, west_buf, east_buf, plane)
-    pair(0, a_buf, b_buf, levels * tracers)
-
-    def stencil(source, at, rim_row, chunk, turn, row, h, co):
-        here = at + h * SUB
-        cell = source[pl.ds(pl.multiple_of(here, SUB), SUB), :]
-        side = pltpu.roll(rim[chunk, pl.ds(rim_row + h * SUB, SUB), :], turn, 1)
+        meet(f_rim, 0, f_west, f_east, rows)
+        pair(f_edges, 0, f_a, f_b, levels)
+    else:
+        for copy in rim_copies:
+            copy.wait()
+        meet(rim, 0, west_buf, east_buf, plane)
+        pair(edges, 0, a_buf, b_buf, levels * tracers)
+
+    def stencil(cells, near, here, side, edge, row, h, co):
+        at = here + h * SUB
+        cell = cells[pl.ds(at, SUB), :]
         e = jnp.where(lane == LANES - 1, side, pltpu.roll(cell, LANES - 1, 1))
         w = jnp.where(lane == 0, side, pltpu.roll(cell, 1, 1))
-        n = source[pl.ds(here + 1, SUB), :]
-        s = source[pl.ds(here - 1, SUB), :]
+        source, start = near
+        n = source[pl.ds(start + at + 1, SUB), :]
+        s = source[pl.ds(start + at - 1, SUB), :]
         if h == halves - 1:
-            n = jnp.where(sub == SUB - 1, edges[0, pl.ds(row, 1), :], n)
+            n = jnp.where(sub == SUB - 1, edge[0, pl.ds(row, 1), :], n)
         if h == 0:
-            s = jnp.where(sub == 0, edges[1, pl.ds(row, 1), :], s)
+            s = jnp.where(sub == 0, edge[1, pl.ds(row, 1), :], s)
         c0, ce, cw, cn, cs = co[:5]
         return (c0 * cell + ce * e) + (cw * w + cn * n) + cs * s
 
-    def forward(k, chunk, q, solved):
-        turn = LANES - 1 - 2 * q
-        co, extra, new = [], [], []
-        for h in range(halves):
-            blk = pl.ds(pl.multiple_of(k * rows + h * SUB, SUB), SUB)
-            co.append([weight[blk, :] for weight in weights])
-            if first:
-                row = levels * tracers + k
-                extra.append(stencil(forcing, k * rows + SUB, plane, chunk, turn, row, h, co[h]))
-        for t in range(tracers):
-            at = k * plane + (t + 1) * rows
-            values = [
-                stencil(flat, at, t * rows, chunk, turn, k * tracers + t, h, co[h]) for h in range(halves)
-            ]
-            for h in range(halves):
-                value = values[h] + extra[h] if first else values[h]
-                value = value + co[h][5] * solved[t * halves + h]
-                new.append(value)
-                flat[pl.ds(pl.multiple_of(at + h * SUB, SUB), SUB), :] = value
-        return tuple(new)
-
-    def forward_block(b, carry):
+    def part(ref, b, size, offset=0):
+        return ref.at[pl.ds(pl.multiple_of(b * unroll * size + offset, SUB), unroll * size)]
+
+    def forward_block(b, solved):
         @pl.when(b < blocks - 1)
         def _():
             load(b + 1).wait()
 
         chunk, q = b * unroll // per_chunk, b * unroll % per_chunk
+        turn = (LANES - 2 * q) % LANES
+        for r in range(0, plane, SUB):
+            rim_now[pl.ds(r, SUB), :] = pltpu.roll(rim[chunk, pl.ds(r, SUB), :], turn, 1)
+        if first:
+            for r in range(0, rows, SUB):
+                rim_now[pl.ds(plane + r, SUB), :] = pltpu.roll(f_rim[chunk, pl.ds(r, SUB), :], turn, 1)
+
+        def side(u, r):
+            return pltpu.roll(rim_now[pl.ds(r, SUB), :], LANES - 1 - 2 * u, 1)
+
+        cells = part(flat, b, plane, rows)
+        near = (flat, b * unroll * plane + rows)
+        edge = edges.at[:, pl.ds(pl.multiple_of(b * unroll * tracers, SUB), unroll * tracers)]
+        co_parts = [part(weight, b, rows) for weight in weights]
+        if first:
+            f_cells = part(forcing, b, rows, SUB)
+            f_near = (forcing, b * unroll * rows + SUB)
+            f_edge = f_edges.at[:, pl.ds(pl.multiple_of(b * unroll, SUB), unroll)]
         for u in range(unroll):
-            carry = forward(b * unroll + u, chunk, q + u, carry)
-        return carry
+            co, extra, new = [], [], []
+            for h in range(halves):
+                co.append([weight[pl.ds(u * rows + h * SUB, SUB), :] for weight in co_parts])
+                if first:
+                    extra.append(
+                        stencil(f_cells, f_near, u * rows, side(u, plane + h * SUB), f_edge, u, h, co[h])
+                    )
+            for t in range(tracers):
+                here = u * plane + t * rows
+                values = [
+                    stencil(
+                        cells, near, here, side(u, t * rows + h * SUB), edge, u * tracers + t, h, co[h]
+                    )
+                    for h in range(halves)
+                ]
+                for h in range(halves):
+                    value = values[h] + extra[h] if first else values[h]
+                    value = value + co[h][5] * solved[t * halves + h]
+                    new.append(value)
+                    cells[pl.ds(here + h * SUB, SUB), :] = value
+            solved = tuple(new)
+        return solved
 
     zero = jnp.zeros((SUB, LANES), jnp.float32)
     zeros = (zero,) * (tracers * halves)
@@ -318,23 +335,22 @@
     lax.fori_loop(0, blocks, forward_block, zeros)
     above_copy.wait()
 
-    def backward(k, carry):
-        new = []
-        for h in range(halves):
-            f = above[pl.ds(pl.multiple_of(k * rows + h * SUB, SUB), SUB), :]
-            for t in range(tracers):
-                blk = pl.ds(pl.multiple_of(k * plane + (t + 1) * rows + h * SUB, SUB), SUB)
-                value = flat[blk, :] + f * carry[h * tracers + t]
-                flat[blk, :] = value
-                new.append(value)
-        return tuple(new)
-
-    def backward_block(i, carry):
+    def backward_block(i, later):
         b = blocks - 1 - i
+        cells = part(flat, b, plane, rows)
+        factors = part(above, b, rows)
         for u in reversed(range(unroll)):
-            carry = backward(b * unroll + u, carry)
+            new = []
+            for h in range(halves):
+                factor = factors[pl.ds(u * rows + h * SUB, SUB), :]
+                for t in range(tracers):
+                    blk = pl.ds(u * plane + t * rows + h * SUB, SUB)
+                    value = cells[blk, :] + factor * later[h * tracers + t]
+                    cells[blk, :] = value
+                    new.append(value)
+            later = tuple(new)
         store(b).start()
-        return carry
+        return later
 
     lax.fori_loop(0, blocks, backward_block, zeros)
     if first:
@@ -611,34 +627,37 @@
     )(received, sums)
     forcing_rims = exchange(*rims)
 
-    *weights, above = call(
+    rim_shape, edge_shape = (chunks, plane, LANES), (2, levels * tracers, LANES)
+    *weights, above, rim0, edges0 = call(
         functools.partial(coefficients, levels, tracers, rows, per_chunk, unroll),
-        [HBM] * 3 + [ANY] * 3, (f32(levels * rows, LANES),) * 6 + (hbm(levels * rows, LANES),), (VMEM,) * 7,
-        (vmem(levels * rows, LANES),) * 3
-        + (vmem(chunks, rows, LANES), vmem(levels, LANES), vmem(levels, LANES), dma((6,))),
+        [HBM] * 3 + [VMEM] * 4,
+        (f32(levels * rows, LANES),) * 6 + (hbm(levels * rows, LANES), f32(*rim_shape), f32(*edge_shape)),
+        (VMEM,) * 9,
+        (vmem(levels * rows, LANES),) * 3 + (dma((3,)),),
         4, field_bytes, field_bytes, "coefficients",
-    )(east, north, mix, start_rims[0], start_rims[2], start_rims[3])
-
-    def advance(value, rims, first, *operands):
-        outs, specs = ((hbm if first else f32)(*value.shape),), (HBM,)
+    )(east, north, mix, *start_rims)
+
+    def advance(value, first, specs, operands, scratch):
+        outs, out_specs = ((hbm if first else f32)(*value.shape),), (HBM,)
         if first:
-            outs += (f32(chunks, plane, LANES), f32(levels * tracers, LANES), f32(levels * tracers, LANES))
-            specs += (VMEM,) * 3
+            outs += (f32(*rim_shape), f32(levels * tracers, LANES), f32(levels * tracers, LANES))
+            out_specs += (VMEM,) * 3
         return call(
             functools.partial(step, levels, tracers, rows, chunks, per_chunk, unroll, first),
-            [VMEM] * 6 + [HBM] * 2 + [ANY] * 4 + [VMEM] * len(operands), outs, specs,
-            (
-                vmem(levels * tracers + 2, rows, LANES), vmem(levels * rows, LANES),
-                vmem(chunks, plane, LANES), vmem(chunks, plane, LANES),
-                vmem(levels * tracers, LANES), vmem(levels * tracers, LANES),
-                vmem(chunks, plane + rows, LANES), vmem(2, levels * tracers + levels, LANES),
-                dma((levels // unroll + 5,)),
-            ),
+            [VMEM] * 6 + [HBM] * 2 + [specs] * len(operands), outs, out_specs,
+            (vmem(levels * tracers + 2, rows, LANES), vmem(levels * rows, LANES), vmem(plane + rows, LANES))
+            + scratch + (dma((levels // unroll + 5,)),),
             10, field_bytes * 8, field_bytes * 2, "step",
-        )(*weights, in_hbm(value), in_hbm(above), *rims, *operands)
-
-    stepped, *rims = advance(field, start_rims, True, forcing, *forcing_rims)
-    (result,) = advance(stepped, exchange(*rims), False)
+        )(*weights, in_hbm(value), in_hbm(above), *operands)
+
+    stepped, *rims = advance(
+        field, True, VMEM, (rim0, edges0, forcing, *forcing_rims),
+        (vmem(chunks, rows, LANES), vmem(2, levels, LANES)),
+    )
+    (result,) = advance(
+        stepped, False, ANY, exchange(*rims),
+        (vmem(*rim_shape),) * 2 + (vmem(levels * tracers, LANES),) * 2 + (vmem(*rim_shape), vmem(*edge_shape)),
+    )
 
     returned = lax.all_to_all(
         back.reshape(bricks, 1, LANES), ("lon", "lat"), split_axis=0, concat_axis=0, tiled=True

time: 75 us -> 74.6 us (level)
  waiting for transfers between devices: 1.73 us -> 3.19 us
  local copies, waits for them, and re-layouts: 7.82 us -> 6.53 us
    ppermute x3, starting transfers between devices: 4.55 us -> 6.02 us  [exchange(): lax.ppermute(side_rim, 'lon', [((i + 1) % lons, i) for i in range(lons)])]
    all_to_all x1, waiting for transfers between devices: 1.2 us -> 2.64 us  [per_device(): lax.all_to_all(packed, ('lon', 'lat'), split_axis=0, concat_axis=0, tiled...]
    unnamed x20 -> x18, local copies, waits for them, and re-layouts: 7.82 us -> 6.53 us
    ppermute x3, starting transfers between devices: 6.59 us -> 5.38 us  [exchange(): lax.ppermute(a_rim, 'lat', [(j, partner(j, 0)) for j in range(lats)])]
  transfers between devices with their start and end apart: 14 -> 14, of which waited for: 2 -> 2; matrix products, arithmetic and copies ran while one was open for 0% -> 0% of each run, Pallas kernels for 29% -> 28%
where the time goes in v4:
time: 74.6 us; the launch traced here: 74 us
  Pallas kernels  34.6 us (46%)
  starting transfers between devices  28.8 us (39%)
  local copies, waits for them, and re-layouts  6.53 us (9%)
  waiting for transfers between devices  3.19 us (4%)
  between operations  0.8 us (1%)
    pallas_call x2, Pallas kernels, advance(): call(functools.partial(step, levels, tracers, rows, chunks, per_chunk, un...  19.9 us
    all_to_all x1, starting transfers between devices, per_device(): lax.all_to_all(packed, ('lon', 'lat'), split_axis=0, concat_axis=0, tiled...  7.3 us
    unnamed x18, local copies, waits for them, and re-layouts  6.53 us
    ppermute x3, starting transfers between devices, exchange(): lax.ppermute(side_rim, 'lon', [((i + 1) % lons, i) for i in range(lons)])  6.02 us
    ppermute x3, starting transfers between devices, exchange(): lax.ppermute(a_rim, 'lat', [(j, partner(j, 0)) for j in range(lats)])  5.38 us
    all_to_all x1, starting transfers between devices, per_device(): lax.all_to_all(back.reshape(bricks, 1, LANES), ('lon', 'lat'), split_axis...  5.08 us
    ppermute x3, starting transfers between devices, exchange(): lax.ppermute(b_rim, 'lat', [(j, partner(j, 1)) for j in range(lats)])  5.07 us
    pallas_call x1, Pallas kernels, per_device(): call(functools.partial(first_rims, levels, tracers, rows, chunks, per_chu...  4.38 us
  transfers between devices with their start and end apart: 14, of which 2 were waited for; matrix products, arithmetic and copies ran while one was open for 0% of the time, Pallas kernels for 28%

profile of v4, /device:TPU:0, one launch (start us, length us, event | category | flops | bytes accessed | tf_op | source)
XLA Modules:
  0.0 74.0 jit_solution(11214829681479223517)
XLA Ops:
  0.6 2.1 %pack.1 = f32[32,24,128]{2,1,0:T(8,128)} custom-call(f32[576,128]{1,0:T(8,128)} %bitcast.24, s32[8,128]{1,0:T(8,128)} %bitcast.26, f32[8,128]{1,0:T(8,128)} %bitcast.27, f32[8,128]{1,0:T(8,128)} %bitcast.28), custom_call_target="tpu_custom_call" | custom-call | flops 10 | bytes 800000 | tf_op jit(solution)/shard_map/pack/pallas_call | solution.py:578
  2.8 7.3 %all-to-all-start = ((f32[32,24,128]{2,1,0:T(8,128)}), f32[32,24,128]{2,1,0:T(8,128)S(1)}, u32[]{:S(2)}, u32[]{:S(2)}) async-start(f32[32,24,128]{2,1,0:T(8,128)} %pack.1), calls=%async_computation | async-start | bytes 786432 | tf_op jit(solution)/shard_map/all_to_all | solution.py:588
  10.1 0.0 copy-start
  10.1 4.4 %first_rims.1 = (f32[2,144,128]{2,1,0:T(8,128)S(1)}, f32[648,128]{1,0:T(8,128)S(1)}, f32[648,128]{1,0:T(8,128)S(1)}) custom-call(f32[9216,128]{1,0:T(8,128)} %bitcast.16, f32[1152,128]{1,0:T(8,128)} %bitcast.19, f32[1152,128]{1,0:T(8,128)} %bitcast.21), custom_call_target="tpu_custom_call" | custom-call | flops 4718592 | bytes 9437184 | tf_op jit(solution)/shard_map/first_rims/pallas_call | solution.py:592
  14.5 1.8 %collective-permute-start.2 = (f32[648,128]{1,0:T(8,128)S(1)}, f32[648,128]{1,0:T(8,128)S(1)}, u32[]{:S(2)}, u32[]{:S(2)}) collective-permute-start(f32[648,128]{1,0:T(8,128)S(1)} %get-tuple-element.26), channel_id=1, source_target_pairs={{0,1},{1,0},{2,3},{3,2},{4,5},{5,4},{6,7},{7,6},{8,9},{9,8},{10,11... | collective-permute-start | bytes 995336 | tf_op jit(solution)/shard_map/ppermute | solution.py:554
  16.3 0.7 collective-permute-start.3
  17.0 1.9 %collective-permute-start.1 = (f32[2,144,128]{2,1,0:T(8,128)S(1)}, f32[2,144,128]{2,1,0:T(8,128)S(1)}, u32[]{:S(2)}, u32[]{:S(2)}) collective-permute-start(f32[2,144,128]{2,1,0:T(8,128)S(1)} %get-tuple-element.25), channel_id=1, source_target_pairs={{4,0},{8,4},{12,8},{16,12},{20,16},{24,20},{28,24},{0,28},{5,1},{9... | collective-permute-start | bytes 442376 | tf_op jit(solution)/shard_map/ppermute | solution.py:553
  18.9 0.0 collective-permute-start
  18.9 0.0 copy-done
  18.9 0.7 tracer_sum.1.sums
  19.6 2.6 %all-to-all-done.received = f32[32,24,128]{2,1,0:T(8,128)S(1)} async-done(((f32[32,24,128]{2,1,0:T(8,128)}), f32[32,24,128]{2,1,0:T(8,128)S(1)}, u32[]{:S(2)}, u32[]{:S(2)}) %all-to-all-start) | async-done | bytes 393248 | tf_op jit(solution)/shard_map/all_to_all | solution.py:588
  22.3 3.2 %soundings.1 = (f32[1168,128]{1,0:T(8,128)S(1)}, f32[2,16,128]{2,1,0:T(8,128)S(1)}, f32[72,128]{1,0:T(8,128)S(1)}, f32[72,128]{1,0:T(8,128)S(1)}, f32[32,128]{1,0:T(8,128)}) custom-call(f32[32,24,128]{2,1,0:T(8,128)S(1)} %all-to-all-done.received, bf16[2,576,256]{2,1,0:T(8,128)(2,1)S(1)} %tracer_sum.1.sums), custom_call_target="tpu_custom_call" | custom-call | flops 37748736 | bytes 4718592 | tf_op jit(solution)/shard_map/soundings/pallas_call | solution.py:613
  25.5 1.9 %collective-permute-start.6 = (f32[72,128]{1,0:T(8,128)S(1)}, f32[72,128]{1,0:T(8,128)S(1)}, u32[]{:S(2)}, u32[]{:S(2)}) collective-permute-start(f32[72,128]{1,0:T(8,128)S(1)} %get-tuple-element.39), channel_id=1, source_target_pairs={{0,1},{1,0},{2,3},{3,2},{4,5},{5,4},{6,7},{7,6},{8,9},{9,8},{10,11... | collective-permute-start | bytes 110600 | tf_op jit(solution)/shard_map/ppermute | solution.py:554
  27.4 0.0 collective-permute-done.1.east0
  27.4 0.0 copy-start.5
  27.4 0.7 copy-done.5
  28.1 0.7 collective-permute-start.7
  28.7 0.0 collective-permute-done.west0
  28.7 0.0 copy-start.7
  28.7 0.6 copy-done.7
  29.4 1.8 %collective-permute-start.5 = (f32[2,16,128]{2,1,0:T(8,128)S(1)}, f32[2,16,128]{2,1,0:T(8,128)S(1)}, u32[]{:S(2)}, u32[]{:S(2)}) collective-permute-start(f32[2,16,128]{2,1,0:T(8,128)S(1)} %get-tuple-element.38), channel_id=1, source_target_pairs={{4,0},{8,4},{12,8},{16,12},{20,16},{24,20},{28,24},{0,28},{5,1},{9... | collective-permute-start | bytes 49160 | tf_op jit(solution)/shard_map/ppermute | solution.py:553
  31.1 0.0 collective-permute-done.2.a0
  31.1 0.0 copy-start.1
  31.2 0.7 copy-done.1
  31.9 0.0 collective-permute-start.4
  31.9 0.0 collective-permute-done.3.b0
  31.9 0.0 copy-start.3
  31.9 0.7 copy-done.3
  32.6 0.0 copy-start.2
  32.6 1.0 %copy-done.2 = f32[648,128]{1,0:T(8,128)S(1)} copy-done((f32[648,128]{1,0:T(8,128)S(1)}, f32[648,128]{1,0:T(8,128)}, u32[]{:S(2)}) %copy-start.2) | copy-done | bytes 331800
  33.6 0.0 copy-start.4
  33.6 1.0 %copy-done.4 = f32[648,128]{1,0:T(8,128)S(1)} copy-done((f32[648,128]{1,0:T(8,128)S(1)}, f32[648,128]{1,0:T(8,128)}, u32[]{:S(2)}) %copy-start.4) | copy-done | bytes 331800
  34.6 0.0 copy-start.6
  34.6 0.9 %copy-done.6 = f32[2,144,128]{2,1,0:T(8,128)S(1)} copy-done((f32[2,144,128]{2,1,0:T(8,128)S(1)}, f32[2,144,128]{2,1,0:T(8,128)}, u32[]{:S(2)}) %copy-start.6) | copy-done | bytes 147480
  35.5 0.0 copy-start.8
  35.5 0.9 %copy-done.8 = f32[2,144,128]{2,1,0:T(8,128)S(1)} copy-done((f32[2,144,128]{2,1,0:T(8,128)S(1)}, f32[2,144,128]{2,1,0:T(8,128)}, u32[]{:S(2)}) %copy-start.8) | copy-done | bytes 147480
  36.4 3.6 %coefficients.1 = (f32[1152,128]{1,0:T(8,128)S(1)}, f32[1152,128]{1,0:T(8,128)S(1)}, f32[1152,128]{1,0:T(8,128)S(1)}, f32[1152,128]{1,0:T(8,128)S(1)}, f32[1152,...) custom-call(f32[1152,128]{1,0:T(8,128)} %bitcast.20, ...), custom_call_target="tpu_custom_call" | custom-call | flops 4718592 | bytes 4718592 | tf_op jit(solution)/shard_map/coefficients/pallas_call | solution.py:631
  40.0 0.0 collective-permute-done.5.refs_12_
  40.0 0.0 collective-permute-done.4.refs_11_
  40.0 0.0 collective-permute-done.6.refs_13_
  40.0 0.0 collective-permute-done.7.refs_14_
  40.0 10.7 %step.2 = (f32[576,16,128]{2,1,0:T(8,128)}, f32[2,128,128]{2,1,0:T(8,128)}, f32[576,128]{1,0:T(8,128)}, f32[576,128]{1,0:T(8,128)}) custom-call(f32[1152,128]{1,0:T(8,128)S(1)} %get-tuple-element.28.refs_0_, f32[1152,128]{1,0:T(8,128)S(1)} %get-tuple-element.29.refs_1_, f32[1152,128]{1,0:T(8,128)S(1)} %get-tuple-element.30.refs_2_, ...), custom_call_target="tpu_custom_call" | custom-call | flops 37748736 | bytes 9437184 | tf_op jit(solution)/shard_map/step/pallas_call | solution.py:645
  50.8 1.6 %collective-permute-start.10 = (f32[576,128]{1,0:T(8,128)}, f32[576,128]{1,0:T(8,128)}, u32[]{:S(2)}, u32[]{:S(2)}) collective-permute-start(f32[576,128]{1,0:T(8,128)} %get-tuple-element.43), channel_id=1, source_target_pairs={{0,1},{1,0},{2,3},{3,2},{4,5},{5,4},{6,7},{7,6},{8,9},{9,8},{10,11... | collective-permute-start | bytes 884744 | tf_op jit(solution)/shard_map/ppermute | solution.py:554
  52.4 3.7 %collective-permute-start.11 = (f32[576,128]{1,0:T(8,128)}, f32[576,128]{1,0:T(8,128)}, u32[]{:S(2)}, u32[]{:S(2)}) collective-permute-start(f32[576,128]{1,0:T(8,128)} %get-tuple-element.44), channel_id=1, source_target_pairs={{0,0},{1,2},{2,1},{3,3},{4,4},{5,6},{6,5},{7,7},{8,8},{9,10},{10,9... | collective-permute-start | bytes 884744 | tf_op jit(solution)/shard_map/ppermute | solution.py:555
  56.1 2.4 %collective-permute-start.9 = (f32[2,128,128]{2,1,0:T(8,128)}, f32[2,128,128]{2,1,0:T(8,128)}, u32[]{:S(2)}, u32[]{:S(2)}) collective-permute-start(f32[2,128,128]{2,1,0:T(8,128)} %get-tuple-element.42), channel_id=1, source_target_pairs={{4,0},{8,4},{12,8},{16,12},{20,16},{24,20},{28,24},{0,28},{5,1},{9... | collective-permute-start | bytes 393224 | tf_op jit(solution)/shard_map/ppermute | solution.py:553
  58.5 0.0 collective-permute-start.8
  58.5 5.1 %all-to-all-start.1 = ((f32[32,1,128]{2,1,0:T(1,128)}), f32[32,1,128]{2,1,0:T(1,128)S(1)}, u32[]{:S(2)}, u32[]{:S(2)}) async-start(f32[32,1,128]{2,1,0:T(1,128)} %bitcast.25), calls=%async_computation.1 | async-start | bytes 32768 | tf_op jit(solution)/shard_map/all_to_all | solution.py:662
  63.6 0.0 collective-permute-done.9.refs_9_
  63.6 0.5 collective-permute-done.8.refs_8_
  64.1 0.0 collective-permute-done.10.refs_10_
  64.1 0.0 collective-permute-done.11.refs_11_
  64.1 9.2 %step.3 = f32[576,16,128]{2,1,0:T(8,128)} custom-call(f32[1152,128]{1,0:T(8,128)S(1)} %get-tuple-element.28.refs_0_, f32[1152,128]{1,0:T(8,128)S(1)} %get-tuple-element.29.refs_1_, f32[1152,128]{1,0:T(8,128)S(1)} %get-tuple-element.30.refs_2_, f32[1152,128]{1,0:T(8,128)S(1)} %get-tuple-element.31.refs_3_, f32[1152,128]{1,0:T(8,128)S(1)} %get-tuple-element.32.refs_4_, ...), custom_call_target="tpu_custom_call" | custom-call | flops 37748736 | bytes 9437184 | tf_op jit(solution)/shard_map/step/pallas_call | solution.py:645
  73.3 0.0 all-to-all-done.1
  73.3 0.7 residual.1
Async XLA Ops:
  2.8 19.5 %all-to-all-start = ((f32[32,24,128]{2,1,0:T(8,128)}), f32[32,24,128]{2,1,0:T(8,128)S(1)}, u32[]{:S(2)}, u32[]{:S(2)}) async-start(f32[32,24,128]{2,1,0:T(8,128)} %pack.1), calls=%async_computation | async-start | bytes 786432 | tf_op jit(solution)/shard_map/all_to_all | solution.py:588
  10.1 8.8 %copy-start = (f32[72,8,16,128]{3,2,1,0:T(8,128)S(1)}, f32[72,8,16,128]{3,2,1,0:T(8,128)}, u32[]{:S(2)}) copy-start(f32[72,8,16,128]{3,2,1,0:T(8,128)} %concentration.1) | copy-start | bytes 14155780
  14.5 16.7 %collective-permute-start.2 = (f32[648,128]{1,0:T(8,128)S(1)}, f32[648,128]{1,0:T(8,128)S(1)}, u32[]{:S(2)}, u32[]{:S(2)}) collective-permute-start(f32[648,128]{1,0:T(8,128)S(1)} %get-tuple-element.26), channel_id=1, source_target_pairs={{0,1},{1,0},{2,3},{3,2},{4,5},{5,4},{6,7},{7,6},{8,9},{9,8},{10,11... | collective-permute-start | bytes 995336 | tf_op jit(solution)/shard_map/ppermute | solution.py:554
  16.3 15.6 %collective-permute-start.3 = (f32[648,128]{1,0:T(8,128)S(1)}, f32[648,128]{1,0:T(8,128)S(1)}, u32[]{:S(2)}, u32[]{:S(2)}) collective-permute-start(f32[648,128]{1,0:T(8,128)S(1)} %get-tuple-element.27), channel_id=1, source_target_pairs={{0,0},{1,2},{2,1},{3,3},{4,4},{5,6},{6,5},{7,7},{8,8},{9,10},{10,9... | collective-permute-start | bytes 995336 | tf_op jit(solution)/shard_map/ppermute | solution.py:555
  17.0 10.4 %collective-permute-start.1 = (f32[2,144,128]{2,1,0:T(8,128)S(1)}, f32[2,144,128]{2,1,0:T(8,128)S(1)}, u32[]{:S(2)}, u32[]{:S(2)}) collective-permute-start(f32[2,144,128]{2,1,0:T(8,128)S(1)} %get-tuple-element.25), channel_id=1, source_target_pairs={{4,0},{8,4},{12,8},{16,12},{20,16},{24,20},{28,24},{0,28},{5,1},{9... | collective-permute-start | bytes 442376 | tf_op jit(solution)/shard_map/ppermute | solution.py:553
  18.9 9.8 %collective-permute-start = (f32[2,144,128]{2,1,0:T(8,128)S(1)}, f32[2,144,128]{2,1,0:T(8,128)S(1)}, u32[]{:S(2)}, u32[]{:S(2)}) collective-permute-start(f32[2,144,128]{2,1,0:T(8,128)S(1)} %get-tuple-element.25), channel_id=1, source_target_pairs={{0,4},{4,8},{8,12},{12,16},{16,20},{20,24},{24,28},{28,0},{1,5},{5... | collective-permute-start | bytes 442376 | tf_op jit(solution)/shard_map/ppermute | solution.py:552
  25.5 14.6 %collective-permute-start.6 = (f32[72,128]{1,0:T(8,128)S(1)}, f32[72,128]{1,0:T(8,128)S(1)}, u32[]{:S(2)}, u32[]{:S(2)}) collective-permute-start(f32[72,128]{1,0:T(8,128)S(1)} %get-tuple-element.39), channel_id=1, source_target_pairs={{0,1},{1,0},{2,3},{3,2},{4,5},{5,4},{6,7},{7,6},{8,9},{9,8},{10,11... | collective-permute-start | bytes 110600 | tf_op jit(solution)/shard_map/ppermute | solution.py:554
  27.4 0.7 copy-start.5
  28.1 12.0 %collective-permute-start.7 = (f32[72,128]{1,0:T(8,128)S(1)}, f32[72,128]{1,0:T(8,128)S(1)}, u32[]{:S(2)}, u32[]{:S(2)}) collective-permute-start(f32[72,128]{1,0:T(8,128)S(1)} %get-tuple-element.40), channel_id=1, source_target_pairs={{0,0},{1,2},{2,1},{3,3},{4,4},{5,6},{6,5},{7,7},{8,8},{9,10},{10,9... | collective-permute-start | bytes 110600 | tf_op jit(solution)/shard_map/ppermute | solution.py:555
  28.7 0.7 copy-start.7
  29.4 10.6 %collective-permute-start.5 = (f32[2,16,128]{2,1,0:T(8,128)S(1)}, f32[2,16,128]{2,1,0:T(8,128)S(1)}, u32[]{:S(2)}, u32[]{:S(2)}) collective-permute-start(f32[2,16,128]{2,1,0:T(8,128)S(1)} %get-tuple-element.38), channel_id=1, source_target_pairs={{4,0},{8,4},{12,8},{16,12},{20,16},{24,20},{28,24},{0,28},{5,1},{9... | collective-permute-start | bytes 49160 | tf_op jit(solution)/shard_map/ppermute | solution.py:553
  31.1 0.7 copy-start.1
  31.9 8.1 %collective-permute-start.4 = (f32[2,16,128]{2,1,0:T(8,128)S(1)}, f32[2,16,128]{2,1,0:T(8,128)S(1)}, u32[]{:S(2)}, u32[]{:S(2)}) collective-permute-start(f32[2,16,128]{2,1,0:T(8,128)S(1)} %get-tuple-element.38), channel_id=1, source_target_pairs={{0,4},{4,8},{8,12},{12,16},{16,20},{20,24},{24,28},{28,0},{1,5},{5... | collective-permute-start | bytes 49160 | tf_op jit(solution)/shard_map/ppermute | solution.py:552
  31.9 0.7 copy-start.3
  32.6 1.0 %copy-start.2 = (f32[648,128]{1,0:T(8,128)S(1)}, f32[648,128]{1,0:T(8,128)}, u32[]{:S(2)}) copy-start(f32[648,128]{1,0:T(8,128)} %copy-done.1) | copy-start | bytes 995332
  33.6 1.0 %copy-start.4 = (f32[648,128]{1,0:T(8,128)S(1)}, f32[648,128]{1,0:T(8,128)}, u32[]{:S(2)}) copy-start(f32[648,128]{1,0:T(8,128)} %copy-done.3) | copy-start | bytes 995332
  34.6 0.9 %copy-start.6 = (f32[2,144,128]{2,1,0:T(8,128)S(1)}, f32[2,144,128]{2,1,0:T(8,128)}, u32[]{:S(2)}) copy-start(f32[2,144,128]{2,1,0:T(8,128)} %copy-done.5) | copy-start | bytes 442372
  35.5 0.9 %copy-start.8 = (f32[2,144,128]{2,1,0:T(8,128)S(1)}, f32[2,144,128]{2,1,0:T(8,128)}, u32[]{:S(2)}) copy-start(f32[2,144,128]{2,1,0:T(8,128)} %copy-done.7) | copy-start | bytes 442372
  50.8 13.3 %collective-permute-start.10 = (f32[576,128]{1,0:T(8,128)}, f32[576,128]{1,0:T(8,128)}, u32[]{:S(2)}, u32[]{:S(2)}) collective-permute-start(f32[576,128]{1,0:T(8,128)} %get-tuple-element.43), channel_id=1, source_target_pairs={{0,1},{1,0},{2,3},{3,2},{4,5},{5,4},{6,7},{7,6},{8,9},{9,8},{10,11... | collective-permute-start | bytes 884744 | tf_op jit(solution)/shard_map/ppermute | solution.py:554
  52.4 11.7 %collective-permute-start.11 = (f32[576,128]{1,0:T(8,128)}, f32[576,128]{1,0:T(8,128)}, u32[]{:S(2)}, u32[]{:S(2)}) collective-permute-start(f32[576,128]{1,0:T(8,128)} %get-tuple-element.44), channel_id=1, source_target_pairs={{0,0},{1,2},{2,1},{3,3},{4,4},{5,6},{6,5},{7,7},{8,8},{9,10},{10,9... | collective-permute-start | bytes 884744 | tf_op jit(solution)/shard_map/ppermute | solution.py:555
  56.1 7.5 %collective-permute-start.9 = (f32[2,128,128]{2,1,0:T(8,128)}, f32[2,128,128]{2,1,0:T(8,128)}, u32[]{:S(2)}, u32[]{:S(2)}) collective-permute-start(f32[2,128,128]{2,1,0:T(8,128)} %get-tuple-element.42), channel_id=1, source_target_pairs={{4,0},{8,4},{12,8},{16,12},{20,16},{24,20},{28,24},{0,28},{5,1},{9... | collective-permute-start | bytes 393224 | tf_op jit(solution)/shard_map/ppermute | solution.py:553
  58.5 5.6 %collective-permute-start.8 = (f32[2,128,128]{2,1,0:T(8,128)}, f32[2,128,128]{2,1,0:T(8,128)}, u32[]{:S(2)}, u32[]{:S(2)}) collective-permute-start(f32[2,128,128]{2,1,0:T(8,128)} %get-tuple-element.42), channel_id=1, source_target_pairs={{0,4},{4,8},{8,12},{12,16},{16,20},{20,24},{24,28},{28,0},{1,5},{5... | collective-permute-start | bytes 393224 | tf_op jit(solution)/shard_map/ppermute | solution.py:552
  58.5 14.8 %all-to-all-start.1 = ((f32[32,1,128]{2,1,0:T(1,128)}), f32[32,1,128]{2,1,0:T(1,128)S(1)}, u32[]{:S(2)}, u32[]{:S(2)}) async-start(f32[32,1,128]{2,1,0:T(1,128)} %bitcast.25), calls=%async_computation.1 | async-start | bytes 32768 | tf_op jit(solution)/shard_map/all_to_all | solution.py:662

commit v5 on v4

--- a/solution.py
+++ b/solution.py
@@ -152,7 +152,7 @@
 def coefficients(
     levels, tracers, rows, per_chunk, unroll, east, north, mixing, west0, east0, a0, b0, *refs
 ):
-    outs, (rim, edges), (e_buf, n_buf, m_buf, sems) = refs[:7], refs[7:9], refs[9:]
+    weights, rim, edges, e_buf, n_buf, m_buf, sems = refs
     plane = tracers * rows
     halves = rows // SUB
     lane, sub = lane_iota(), sub_iota()
@@ -196,9 +196,13 @@
             if h == halves - 1:
                 from_n = from_n * north_mask
             stay = (1.0 - e_out + w_in - n_out + s_in) * inv
-            values = (stay, e_out * inv, -(w_in * inv), from_n, -(s_in * inv), down * inv, factor)
-            for out, value in zip(outs, values):
-                out[blk, :] = value
+            from_e, from_w = e_out * inv, -(w_in * inv)
+            from_rim = jnp.where(lane == 0, from_w, jnp.where(lane == LANES - 1, from_e, 0.0))
+            from_e = jnp.where(lane == LANES - 1, 0.0, from_e)
+            from_w = jnp.where(lane == 0, 0.0, from_w)
+            values = (stay, from_e, from_w, from_n, -(s_in * inv), from_rim, down * inv, factor)
+            for i, value in enumerate(values):
+                weights[i, blk, :] = value
         return tuple(new)
 
     def body(b, carry):
@@ -211,14 +215,13 @@
 
 
 def step(levels, tracers, rows, chunks, per_chunk, unroll, first, *refs):
-    refs = list(refs)
-    weights, (field, above_in) = refs[:6], refs[6:8]
     if first:
-        rim, edges, forcing, f_west, f_east, f_a, f_b, out, side_ref, a_ref, b_ref = refs[8:19]
-        buf, above, rim_now, f_rim, f_edges, sems = refs[19:]
+        field, weights, rim, edges, forcing, f_west, f_east, f_a, f_b = refs[:9]
+        out, weights_out, side_ref, a_ref, b_ref = refs[9:14]
+        buf, rim_now, f_rim, f_edges, sems = refs[14:]
     else:
-        west_in, east_in, a_in, b_in, out = refs[8:13]
-        buf, above, rim_now, west_buf, east_buf, a_buf, b_buf, rim, edges, sems = refs[13:]
+        field, weights_in, west_in, east_in, a_in, b_in, out = refs[:7]
+        buf, rim_now, weights, west_buf, east_buf, a_buf, b_buf, rim, edges, sems = refs[7:]
 
     plane = tracers * rows
     halves = rows // SUB
@@ -238,53 +241,87 @@
             buf.at[pl.ds(at + 1, unroll * tracers)], out.at[pl.ds(at, unroll * tracers)], sems.at[b]
         )
 
-    rim_copies = []
-    if not first:
+    last = 2 * blocks
+    above = weights.at[weights.shape[0] - 1]
+    if first:
+        keep = pltpu.make_async_copy(weights, weights_out, sems.at[last])
+        for b in range(blocks):
+            load(b).start()
+        keep.start()
+        meet(f_rim, 0, f_west, f_east, rows)
+        pair(f_edges, 0, f_a, f_b, levels)
+    else:
         rim_copies = [
-            pltpu.make_async_copy(source, target, sems.at[blocks + 1 + i])
+            pltpu.make_async_copy(source, target, sems.at[last + 1 + i])
             for i, (source, target) in enumerate(
                 ((west_in, west_buf), (east_in, east_buf), (a_in, a_buf), (b_in, b_buf))
             )
         ]
-    above_copy = pltpu.make_async_copy(above_in, above, sems.at[blocks])
-    load(0).start()
-    for copy in rim_copies:
-        copy.start()
-    for b in range(1, blocks):
-        load(b).start()
-    above_copy.start()
-
-    if first:
-        meet(f_rim, 0, f_west, f_east, rows)
-        pair(f_edges, 0, f_a, f_b, levels)
-    else:
+        above_copy = pltpu.make_async_copy(weights_in.at[weights.shape[0] - 1], above, sems.at[last])
+        for copy in rim_copies:
+            copy.start()
+
+        def load_weights(b):
+            planes, levels_of = pl.ds(0, weights.shape[0] - 1), pl.ds(b * unroll * rows, unroll * rows)
+            return pltpu.make_async_copy(
+                weights_in.at[planes, levels_of], weights.at[planes, levels_of], sems.at[blocks + b]
+            )
+
+        for b in range(blocks):
+            load(b).start()
+            load_weights(b).start()
+        above_copy.start()
         for copy in rim_copies:
             copy.wait()
         meet(rim, 0, west_buf, east_buf, plane)
         pair(edges, 0, a_buf, b_buf, levels * tracers)
 
-    def stencil(cells, near, here, side, edge, row, h, co):
-        at = here + h * SUB
-        cell = cells[pl.ds(at, SUB), :]
-        e = jnp.where(lane == LANES - 1, side, pltpu.roll(cell, LANES - 1, 1))
-        w = jnp.where(lane == 0, side, pltpu.roll(cell, 1, 1))
+    def shifted(cells, near, here, edge, row):
+        norths, souths = [], []
+        if first:
+            halfs = [cells[pl.ds(here + h * SUB, SUB), :] for h in range(halves)]
+            ups = [pltpu.roll(half, SUB - 1, 0) for half in halfs] + [edge[0, pl.ds(row, 1), :]]
+            downs = [edge[1, pl.ds(row, 1), :]] + [pltpu.roll(half, 1, 0) for half in halfs]
+            for h in range(halves):
+                norths.append(jnp.where(sub == SUB - 1, ups[h + 1], ups[h]))
+                souths.append(jnp.where(sub == 0, downs[h], downs[h + 1]))
+            return norths, souths
         source, start = near
-        n = source[pl.ds(start + at + 1, SUB), :]
-        s = source[pl.ds(start + at - 1, SUB), :]
-        if h == halves - 1:
-            n = jnp.where(sub == SUB - 1, edge[0, pl.ds(row, 1), :], n)
-        if h == 0:
-            s = jnp.where(sub == 0, edge[1, pl.ds(row, 1), :], s)
-        c0, ce, cw, cn, cs = co[:5]
-        return (c0 * cell + ce * e) + (cw * w + cn * n) + cs * s
+        for h in range(halves):
+            n = source[pl.ds(start + here + h * SUB + 1, SUB), :]
+            s = source[pl.ds(start + here + h * SUB - 1, SUB), :]
+            if h == halves - 1:
+                n = jnp.where(sub == SUB - 1, edge[0, pl.ds(row, 1), :], n)
+            if h == 0:
+                s = jnp.where(sub == 0, edge[1, pl.ds(row, 1), :], s)
+            norths.append(n)
+            souths.append(s)
+        return norths, souths
+
+    def stencil(cells, near, here, side, edge, row, co):
+        norths, souths = shifted(cells, near, here, edge, row)
+        values = []
+        for h in range(halves):
+            cell = cells[pl.ds(here + h * SUB, SUB), :]
+            c0, ce, cw, cn, cs, rims = co[h][:6]
+            value = (c0 * cell + ce * pltpu.roll(cell, LANES - 1, 1)) + (
+                cw * pltpu.roll(cell, 1, 1) + cn * norths[h]
+            )
+            values.append(value + (cs * souths[h] + rims * side(h)))
+        return values
 
     def part(ref, b, size, offset=0):
         return ref.at[pl.ds(pl.multiple_of(b * unroll * size + offset, SUB), unroll * size)]
 
     def forward_block(b, solved):
-        @pl.when(b < blocks - 1)
-        def _():
-            load(b + 1).wait()
+        if first:
+            load(b).wait()
+        else:
+            load_weights(b).wait()
+
+            @pl.when(b < blocks - 1)
+            def _():
+                load(b + 1).wait()
 
         chunk, q = b * unroll // per_chunk, b * unroll % per_chunk
         turn = (LANES - 2 * q) % LANES
@@ -295,35 +332,30 @@
                 rim_now[pl.ds(plane + r, SUB), :] = pltpu.roll(f_rim[chunk, pl.ds(r, SUB), :], turn, 1)
 
         def side(u, r):
-            return pltpu.roll(rim_now[pl.ds(r, SUB), :], LANES - 1 - 2 * u, 1)
+            return lambda h: pltpu.roll(rim_now[pl.ds(r + h * SUB, SUB), :], LANES - 1 - 2 * u, 1)
 
         cells = part(flat, b, plane, rows)
         near = (flat, b * unroll * plane + rows)
         edge = edges.at[:, pl.ds(pl.multiple_of(b * unroll * tracers, SUB), unroll * tracers)]
-        co_parts = [part(weight, b, rows) for weight in weights]
+        co_part = weights.at[:, pl.ds(pl.multiple_of(b * unroll * rows, SUB), unroll * rows)]
         if first:
             f_cells = part(forcing, b, rows, SUB)
             f_near = (forcing, b * unroll * rows + SUB)
             f_edge = f_edges.at[:, pl.ds(pl.multiple_of(b * unroll, SUB), unroll)]
         for u in range(unroll):
-            co, extra, new = [], [], []
-            for h in range(halves):
-                co.append([weight[pl.ds(u * rows + h * SUB, SUB), :] for weight in co_parts])
-                if first:
-                    extra.append(
-                        stencil(f_cells, f_near, u * rows, side(u, plane + h * SUB), f_edge, u, h, co[h])
-                    )
+            co = [
+                [co_part[i, pl.ds(u * rows + h * SUB, SUB), :] for i in range(weights.shape[0] - 1)]
+                for h in range(halves)
+            ]
+            if first:
+                extra = stencil(f_cells, f_near, u * rows, side(u, plane), f_edge, u, co)
+            new = []
             for t in range(tracers):
                 here = u * plane + t * rows
-                values = [
-                    stencil(
-                        cells, near, here, side(u, t * rows + h * SUB), edge, u * tracers + t, h, co[h]
-                    )
-                    for h in range(halves)
-                ]
+                values = stencil(cells, near, here, side(u, t * rows), edge, u * tracers + t, co)
                 for h in range(halves):
                     value = values[h] + extra[h] if first else values[h]
-                    value = value + co[h][5] * solved[t * halves + h]
+                    value = value + co[h][6] * solved[t * halves + h]
                     new.append(value)
                     cells[pl.ds(here + h * SUB, SUB), :] = value
             solved = tuple(new)
@@ -331,9 +363,11 @@
 
     zero = jnp.zeros((SUB, LANES), jnp.float32)
     zeros = (zero,) * (tracers * halves)
-    load(0).wait()
+    if not first:
+        load(0).wait()
     lax.fori_loop(0, blocks, forward_block, zeros)
-    above_copy.wait()
+    if not first:
+        above_copy.wait()
 
     def backward_block(i, later):
         b = blocks - 1 - i
@@ -357,6 +391,7 @@
         for chunk in range(chunks):
             put_rims(flat, rows, levels, per_chunk, chunk, side_ref, 0, plane)
         put_rows(flat, rows, a_ref, b_ref, rows, 0, levels * tracers)
+        keep.wait()
     for b in range(blocks):
         store(b).wait()
 
@@ -628,35 +663,36 @@
     forcing_rims = exchange(*rims)
 
     rim_shape, edge_shape = (chunks, plane, LANES), (2, levels * tracers, LANES)
-    *weights, above, rim0, edges0 = call(
+    weight_shape = (8, levels * rows, LANES)
+    weights, rim0, edges0 = call(
         functools.partial(coefficients, levels, tracers, rows, per_chunk, unroll),
         [HBM] * 3 + [VMEM] * 4,
-        (f32(levels * rows, LANES),) * 6 + (hbm(levels * rows, LANES), f32(*rim_shape), f32(*edge_shape)),
-        (VMEM,) * 9,
+        (f32(*weight_shape), f32(*rim_shape), f32(*edge_shape)),
+        (VMEM,) * 3,
         (vmem(levels * rows, LANES),) * 3 + (dma((3,)),),
         4, field_bytes, field_bytes, "coefficients",
     )(east, north, mix, *start_rims)
 
-    def advance(value, first, specs, operands, scratch):
-        outs, out_specs = ((hbm if first else f32)(*value.shape),), (HBM,)
-        if first:
-            outs += (f32(*rim_shape), f32(levels * tracers, LANES), f32(levels * tracers, LANES))
-            out_specs += (VMEM,) * 3
+    def advance(first, specs, operands, outs, out_specs, scratch):
         return call(
             functools.partial(step, levels, tracers, rows, chunks, per_chunk, unroll, first),
-            [VMEM] * 6 + [HBM] * 2 + [specs] * len(operands), outs, out_specs,
-            (vmem(levels * tracers + 2, rows, LANES), vmem(levels * rows, LANES), vmem(plane + rows, LANES))
-            + scratch + (dma((levels // unroll + 5,)),),
-            10, field_bytes * 8, field_bytes * 2, "step",
-        )(*weights, in_hbm(value), in_hbm(above), *operands)
-
-    stepped, *rims = advance(
-        field, True, VMEM, (rim0, edges0, forcing, *forcing_rims),
+            specs, outs, out_specs,
+            (vmem(levels * tracers + 2, rows, LANES), vmem(plane + rows, LANES))
+            + scratch + (dma((2 * (levels // unroll) + 5,)),),
+            16, field_bytes * 8, field_bytes * 2, "step",
+        )(*operands)
+
+    edge_rows = f32(levels * tracers, LANES)
+    stepped, kept, *rims = advance(
+        True, [HBM] + [VMEM] * 8, (in_hbm(field), weights, rim0, edges0, forcing, *forcing_rims),
+        (hbm(*field.shape), hbm(*weight_shape), f32(*rim_shape), edge_rows, edge_rows), (HBM,) * 2 + (VMEM,) * 3,
         (vmem(chunks, rows, LANES), vmem(2, levels, LANES)),
     )
     (result,) = advance(
-        stepped, False, ANY, exchange(*rims),
-        (vmem(*rim_shape),) * 2 + (vmem(levels * tracers, LANES),) * 2 + (vmem(*rim_shape), vmem(*edge_shape)),
+        False, [HBM] * 2 + [ANY] * 4, (in_hbm(stepped), in_hbm(kept), *exchange(*rims)),
+        (f32(*field.shape),), (HBM,),
+        (vmem(*weight_shape),) + (vmem(*rim_shape),) * 2 + (vmem(levels * tracers, LANES),) * 2
+        + (vmem(*rim_shape), vmem(*edge_shape)),
     )
 
     returned = lax.all_to_all(

time: 74.6 us -> 63.3 us (0.85)
  local copies, waits for them, and re-layouts: 6.53 us -> 0.01 us
  starting transfers between devices: 28.8 us -> 25.1 us
  Pallas kernels: 34.6 us -> 33 us
    unnamed x18 -> x2, local copies, waits for them, and re-layouts: 6.53 us -> 0.01 us
    ppermute x3, starting transfers between devices: 5.07 us -> 1.99 us  [exchange(): lax.ppermute(b_rim, 'lat', [(j, partner(j, 1)) for j in range(lats)])]
    ppermute x3, starting transfers between devices: 6.02 us -> 4.96 us  [exchange(): lax.ppermute(side_rim, 'lon', [((i + 1) % lons, i) for i in range(lons)])]
    pallas_call x2, Pallas kernels: 19.9 us -> 19 us  [advance(): call(functools.partial(step, levels, tracers, rows, chunks, per_chunk, un...]
  transfers between devices with their start and end apart: 14 -> 14, of which waited for: 2 -> 2; matrix products, arithmetic and copies ran while one was open for 0% -> 0% of each run, Pallas kernels for 28% -> 33%
where the time goes in v5:
time: 63.3 us; the launch traced here: 62.7 us
  Pallas kernels  33 us (52%)
  starting transfers between devices  25.1 us (40%)
  waiting for transfers between devices  3.86 us (6%)
  between operations  0.79 us (1%)
    pallas_call x2, Pallas kernels, advance(): call(functools.partial(step, levels, tracers, rows, chunks, per_chunk, un...  19 us
    all_to_all x1, starting transfers between devices, per_device(): lax.all_to_all(packed, ('lon', 'lat'), split_axis=0, concat_axis=0, tiled...  7.3 us
    all_to_all x1, starting transfers between devices, per_device(): lax.all_to_all(back.reshape(bricks, 1, LANES), ('lon', 'lat'), split_axis...  5.43 us
    ppermute x3, starting transfers between devices, exchange(): lax.ppermute(a_rim, 'lat', [(j, partner(j, 0)) for j in range(lats)])  5.38 us
    ppermute x3, starting transfers between devices, exchange(): lax.ppermute(side_rim, 'lon', [((i + 1) % lons, i) for i in range(lons)])  4.96 us
    pallas_call x1, Pallas kernels, per_device(): call(functools.partial(first_rims, levels, tracers, rows, chunks, per_chu...  4.38 us
    pallas_call x1, Pallas kernels, per_device(): call(functools.partial(soundings, levels, rows, group_rows, cap, chunks,...  3.19 us
    pallas_call x1, Pallas kernels, per_device(): call(functools.partial(coefficients, levels, tracers, rows, per_chunk, un...  2.86 us
  transfers between devices with their start and end apart: 14, of which 2 were waited for; matrix products, arithmetic and copies ran while one was open for 0% of the time, Pallas kernels for 33%

profile of v5, /device:TPU:0, one launch (start us, length us, event | category | flops | bytes accessed | tf_op | source)
XLA Modules:
  0.0 62.7 jit_solution(77237381872065479)
XLA Ops:
  0.6 2.1 %pack.1 = f32[32,24,128]{2,1,0:T(8,128)} custom-call(f32[576,128]{1,0:T(8,128)} %bitcast.24, s32[8,128]{1,0:T(8,128)} %bitcast.25, f32[8,128]{1,0:T(8,128)} %bitcast.26, f32[8,128]{1,0:T(8,128)} %bitcast.27), custom_call_target="tpu_custom_call" | custom-call | flops 10 | bytes 800000 | tf_op jit(solution)/shard_map/pack/pallas_call | solution.py:613
  2.8 7.3 %all-to-all-start = ((f32[32,24,128]{2,1,0:T(8,128)}), f32[32,24,128]{2,1,0:T(8,128)S(1)}, u32[]{:S(2)}, u32[]{:S(2)}) async-start(f32[32,24,128]{2,1,0:T(8,128)} %pack.1), calls=%async_computation | async-start | bytes 786432 | tf_op jit(solution)/shard_map/all_to_all | solution.py:623
  10.1 0.0 copy-start
  10.1 4.4 %first_rims.1 = (f32[2,144,128]{2,1,0:T(8,128)S(1)}, f32[648,128]{1,0:T(8,128)S(1)}, f32[648,128]{1,0:T(8,128)S(1)}) custom-call(f32[9216,128]{1,0:T(8,128)} %bitcast.16, f32[1152,128]{1,0:T(8,128)} %bitcast.19, f32[1152,128]{1,0:T(8,128)} %bitcast.21), custom_call_target="tpu_custom_call" | custom-call | flops 4718592 | bytes 9437184 | tf_op jit(solution)/shard_map/first_rims/pallas_call | solution.py:627
  14.5 1.8 %collective-permute-start.2 = (f32[648,128]{1,0:T(8,128)S(1)}, f32[648,128]{1,0:T(8,128)S(1)}, u32[]{:S(2)}, u32[]{:S(2)}) collective-permute-start(f32[648,128]{1,0:T(8,128)S(1)} %get-tuple-element.21), channel_id=1, source_target_pairs={{0,1},{1,0},{2,3},{3,2},{4,5},{5,4},{6,7},{7,6},{8,9},{9,8},{10,11... | collective-permute-start | bytes 995336 | tf_op jit(solution)/shard_map/ppermute | solution.py:589
  16.3 0.7 %collective-permute-start.3 = (f32[648,128]{1,0:T(8,128)S(1)}, f32[648,128]{1,0:T(8,128)S(1)}, u32[]{:S(2)}, u32[]{:S(2)}) collective-permute-start(f32[648,128]{1,0:T(8,128)S(1)} %get-tuple-element.22), channel_id=1, source_target_pairs={{0,0},{1,2},{2,1},{3,3},{4,4},{5,6},{6,5},{7,7},{8,8},{9,10},{10,9... | collective-permute-start | bytes 995336 | tf_op jit(solution)/shard_map/ppermute | solution.py:590
  17.0 1.9 %collective-permute-start.1 = (f32[2,144,128]{2,1,0:T(8,128)S(1)}, f32[2,144,128]{2,1,0:T(8,128)S(1)}, u32[]{:S(2)}, u32[]{:S(2)}) collective-permute-start(f32[2,144,128]{2,1,0:T(8,128)S(1)} %get-tuple-element.20), channel_id=1, source_target_pairs={{4,0},{8,4},{12,8},{16,12},{20,16},{24,20},{28,24},{0,28},{5,1},{9... | collective-permute-start | bytes 442376 | tf_op jit(solution)/shard_map/ppermute | solution.py:588
  18.9 0.0 collective-permute-start
  18.9 0.0 copy-done
  18.9 0.7 %tracer_sum.1.sums = bf16[2,576,256]{2,1,0:T(8,128)(2,1)S(1)} custom-call(f32[72,8,16,128]{3,2,1,0:T(8,128)S(1)} %copy-done), custom_call_target="tpu_custom_call" | custom-call | flops 1179648 | bytes 4718592 | tf_op jit(solution)/shard_map/tracer_sum/pallas_call | solution.py:639
  19.6 2.6 %all-to-all-done.received = f32[32,24,128]{2,1,0:T(8,128)S(1)} async-done(((f32[32,24,128]{2,1,0:T(8,128)}), f32[32,24,128]{2,1,0:T(8,128)S(1)}, u32[]{:S(2)}, u32[]{:S(2)}) %all-to-all-start) | async-done | bytes 393248 | tf_op jit(solution)/shard_map/all_to_all | solution.py:623
  22.3 3.2 %soundings.1 = (f32[1168,128]{1,0:T(8,128)S(1)}, f32[2,16,128]{2,1,0:T(8,128)S(1)}, f32[72,128]{1,0:T(8,128)S(1)}, f32[72,128]{1,0:T(8,128)S(1)}, f32[32,128]{1,0:T(8,128)}) custom-call(f32[32,24,128]{2,1,0:T(8,128)S(1)} %all-to-all-done.received, bf16[2,576,256]{2,1,0:T(8,128)(2,1)S(1)} %tracer_sum.1.sums), custom_call_target="tpu_custom_call" | custom-call | flops 37748736 | bytes 4718592 | tf_op jit(solution)/shard_map/soundings/pallas_call | solution.py:648
  25.5 1.9 %collective-permute-start.6 = (f32[72,128]{1,0:T(8,128)S(1)}, f32[72,128]{1,0:T(8,128)S(1)}, u32[]{:S(2)}, u32[]{:S(2)}) collective-permute-start(f32[72,128]{1,0:T(8,128)S(1)} %get-tuple-element.28), channel_id=1, source_target_pairs={{0,1},{1,0},{2,3},{3,2},{4,5},{5,4},{6,7},{7,6},{8,9},{9,8},{10,11... | collective-permute-start | bytes 110600 | tf_op jit(solution)/shard_map/ppermute | solution.py:589
  27.4 0.0 collective-permute-done.1.east0
  27.4 0.7 %collective-permute-start.7 = (f32[72,128]{1,0:T(8,128)S(1)}, f32[72,128]{1,0:T(8,128)S(1)}, u32[]{:S(2)}, u32[]{:S(2)}) collective-permute-start(f32[72,128]{1,0:T(8,128)S(1)} %get-tuple-element.29), channel_id=1, source_target_pairs={{0,0},{1,2},{2,1},{3,3},{4,4},{5,6},{6,5},{7,7},{8,8},{9,10},{10,9... | collective-permute-start | bytes 110600 | tf_op jit(solution)/shard_map/ppermute | solution.py:590
  28.1 0.0 collective-permute-done.west0
  28.1 1.8 %collective-permute-start.5 = (f32[2,16,128]{2,1,0:T(8,128)S(1)}, f32[2,16,128]{2,1,0:T(8,128)S(1)}, u32[]{:S(2)}, u32[]{:S(2)}) collective-permute-start(f32[2,16,128]{2,1,0:T(8,128)S(1)} %get-tuple-element.27), channel_id=1, source_target_pairs={{4,0},{8,4},{12,8},{16,12},{20,16},{24,20},{28,24},{0,28},{5,1},{9... | collective-permute-start | bytes 49160 | tf_op jit(solution)/shard_map/ppermute | solution.py:588
  29.9 0.0 collective-permute-done.2.a0
  29.9 0.0 collective-permute-start.4
  29.9 0.0 collective-permute-done.3.b0
  29.9 2.9 %coefficients.1 = (f32[8,1152,128]{2,1,0:T(8,128)S(1)}, f32[2,128,128]{2,1,0:T(8,128)S(1)}, f32[2,576,128]{2,1,0:T(8,128)S(1)}) custom-call(f32[1152,128]{1,0:T(8,128)} %bitcast.20, f32[1152,128]{1,0:T(8,128)} %bitcast.22, f32[1152,128]{1,0:T(8,128)} %bitcast.23, f32[2,144,128]{2,1,0:T(8,128)S(1)} %collective-permute-done.west0, ...), custom_call_target="tpu_custom_call" | custom-call | flops 4718592 | bytes 4718592 | tf_op jit(solution)/shard_map/coefficients/pallas_call | solution.py:667
  32.8 0.0 collective-permute-done.5.refs_6_
  32.8 1.2 %collective-permute-done.4.refs_5_ = f32[2,16,128]{2,1,0:T(8,128)S(1)} collective-permute-done((f32[2,16,128]{2,1,0:T(8,128)S(1)}, f32[2,16,128]{2,1,0:T(8,128)S(1)}, u32[]{:S(2)}, u32[]{:S(2)}) %collective-permute-start.4) | collective-permute-done | bytes 16416 | tf_op jit(solution)/shard_map/ppermute | solution.py:587
  33.9 0.0 collective-permute-done.6.refs_7_
  34.0 0.0 collective-permute-done.7.refs_8_
  34.0 9.4 %step.2 = (f32[576,16,128]{2,1,0:T(8,128)}, f32[8,1152,128]{2,1,0:T(8,128)}, f32[2,128,128]{2,1,0:T(8,128)S(1)}, f32[576,128]{1,0:T(8,128)S(1)}, f32[576,128]{1,0:T(8,128)S(1)}) custom-call(f32[576,16,128]{2,1,0:T(8,128)} %bitcast.17, f32[8,1152,128]{2,1,0:T(8,128)S(1)} %get-tuple-element.23.refs_1_, f32[2,128,128]{2,1,0:T(8,128)S(1)} %get-tuple-element.24.refs_2_, ...), custom_call_target="tpu_custom_call" | custom-call | flops 37748736 | bytes 9437184 | tf_op jit(solution)/shard_map/step/pallas_call | solution.py:677
  43.3 1.6 %collective-permute-start.10 = (f32[576,128]{1,0:T(8,128)S(1)}, f32[576,128]{1,0:T(8,128)S(1)}, u32[]{:S(2)}, u32[]{:S(2)}) collective-permute-start(f32[576,128]{1,0:T(8,128)S(1)} %get-tuple-element.33), channel_id=1, source_target_pairs={{0,1},{1,0},{2,3},{3,2},{4,5},{5,4},{6,7},{7,6},{8,9},{9,8},{10,11... | collective-permute-start | bytes 884744 | tf_op jit(solution)/shard_map/ppermute | solution.py:589
  44.9 0.7 %collective-permute-start.11 = (f32[576,128]{1,0:T(8,128)S(1)}, f32[576,128]{1,0:T(8,128)S(1)}, u32[]{:S(2)}, u32[]{:S(2)}) collective-permute-start(f32[576,128]{1,0:T(8,128)S(1)} %get-tuple-element.34), channel_id=1, source_target_pairs={{0,0},{1,2},{2,1},{3,3},{4,4},{5,6},{6,5},{7,7},{8,8},{9,10},{10,9... | collective-permute-start | bytes 884744 | tf_op jit(solution)/shard_map/ppermute | solution.py:590
  45.6 1.3 %collective-permute-start.9 = (f32[2,128,128]{2,1,0:T(8,128)S(1)}, f32[2,128,128]{2,1,0:T(8,128)S(1)}, u32[]{:S(2)}, u32[]{:S(2)}) collective-permute-start(f32[2,128,128]{2,1,0:T(8,128)S(1)} %get-tuple-element.32), channel_id=1, source_target_pairs={{4,0},{8,4},{12,8},{16,12},{20,16},{24,20},{28,24},{0,28},{5,1},{9... | collective-permute-start | bytes 393224 | tf_op jit(solution)/shard_map/ppermute | solution.py:588
  46.9 0.0 collective-permute-start.8
  46.9 5.4 %all-to-all-start.1 = ((f32[32,1,128]{2,1,0:T(1,128)}), f32[32,1,128]{2,1,0:T(1,128)S(1)}, u32[]{:S(2)}, u32[]{:S(2)}) async-start(f32[32,1,128]{2,1,0:T(1,128)} %bitcast.10), calls=%async_computation.1 | async-start | bytes 32768 | tf_op jit(solution)/shard_map/all_to_all | solution.py:698
  52.3 0.0 collective-permute-done.9.refs_3_
  52.3 0.0 collective-permute-done.8.refs_2_
  52.3 0.0 collective-permute-done.10.refs_4_
  52.3 0.0 collective-permute-done.11.refs_5_
  52.4 9.6 %step.3 = f32[576,16,128]{2,1,0:T(8,128)} custom-call(f32[576,16,128]{2,1,0:T(8,128)} %get-tuple-element.30.refs_0_, f32[8,1152,128]{2,1,0:T(8,128)} %get-tuple-element.31.refs_1_, f32[2,128,128]{2,1,0:T(8,128)S(1)} %collective-permute-done.8.refs_2_, f32[2,128,128]{2,1,0:T(8,128)S(1)} %collective-permute-done.9.refs_3_, ...), custom_call_target="tpu_custom_call" | custom-call | flops 37748736 | bytes 9437184 | tf_op jit(solution)/shard_map/step/pallas_call | solution.py:677
  62.0 0.0 all-to-all-done.1
  62.0 0.7 %residual.1 = f32[8,128]{1,0:T(8,128)} custom-call(f32[32,128]{1,0:T(8,128)S(1)} %bitcast.15), custom_call_target="tpu_custom_call" | custom-call | flops 10 | bytes 10000 | tf_op jit(solution)/shard_map/residual/pallas_call | solution.py:702
Async XLA Ops:
  2.8 19.5 %all-to-all-start = ((f32[32,24,128]{2,1,0:T(8,128)}), f32[32,24,128]{2,1,0:T(8,128)S(1)}, u32[]{:S(2)}, u32[]{:S(2)}) async-start(f32[32,24,128]{2,1,0:T(8,128)} %pack.1), calls=%async_computation | async-start | bytes 786432 | tf_op jit(solution)/shard_map/all_to_all | solution.py:623
  10.1 8.8 %copy-start = (f32[72,8,16,128]{3,2,1,0:T(8,128)S(1)}, f32[72,8,16,128]{3,2,1,0:T(8,128)}, u32[]{:S(2)}) copy-start(f32[72,8,16,128]{3,2,1,0:T(8,128)} %concentration.1) | copy-start | bytes 14155780
  14.5 15.4 %collective-permute-start.2 = (f32[648,128]{1,0:T(8,128)S(1)}, f32[648,128]{1,0:T(8,128)S(1)}, u32[]{:S(2)}, u32[]{:S(2)}) collective-permute-start(f32[648,128]{1,0:T(8,128)S(1)} %get-tuple-element.21), channel_id=1, source_target_pairs={{0,1},{1,0},{2,3},{3,2},{4,5},{5,4},{6,7},{7,6},{8,9},{9,8},{10,11... | collective-permute-start | bytes 995336 | tf_op jit(solution)/shard_map/ppermute | solution.py:589
  16.3 13.6 %collective-permute-start.3 = (f32[648,128]{1,0:T(8,128)S(1)}, f32[648,128]{1,0:T(8,128)S(1)}, u32[]{:S(2)}, u32[]{:S(2)}) collective-permute-start(f32[648,128]{1,0:T(8,128)S(1)} %get-tuple-element.22), channel_id=1, source_target_pairs={{0,0},{1,2},{2,1},{3,3},{4,4},{5,6},{6,5},{7,7},{8,8},{9,10},{10,9... | collective-permute-start | bytes 995336 | tf_op jit(solution)/shard_map/ppermute | solution.py:590
  17.0 10.4 %collective-permute-start.1 = (f32[2,144,128]{2,1,0:T(8,128)S(1)}, f32[2,144,128]{2,1,0:T(8,128)S(1)}, u32[]{:S(2)}, u32[]{:S(2)}) collective-permute-start(f32[2,144,128]{2,1,0:T(8,128)S(1)} %get-tuple-element.20), channel_id=1, source_target_pairs={{4,0},{8,4},{12,8},{16,12},{20,16},{24,20},{28,24},{0,28},{5,1},{9... | collective-permute-start | bytes 442376 | tf_op jit(solution)/shard_map/ppermute | solution.py:588
  18.9 9.2 %collective-permute-start = (f32[2,144,128]{2,1,0:T(8,128)S(1)}, f32[2,144,128]{2,1,0:T(8,128)S(1)}, u32[]{:S(2)}, u32[]{:S(2)}) collective-permute-start(f32[2,144,128]{2,1,0:T(8,128)S(1)} %get-tuple-element.20), channel_id=1, source_target_pairs={{0,4},{4,8},{8,12},{12,16},{16,20},{20,24},{24,28},{28,0},{1,5},{5... | collective-permute-start | bytes 442376 | tf_op jit(solution)/shard_map/ppermute | solution.py:587
  25.5 8.5 %collective-permute-start.6 = (f32[72,128]{1,0:T(8,128)S(1)}, f32[72,128]{1,0:T(8,128)S(1)}, u32[]{:S(2)}, u32[]{:S(2)}) collective-permute-start(f32[72,128]{1,0:T(8,128)S(1)} %get-tuple-element.28), channel_id=1, source_target_pairs={{0,1},{1,0},{2,3},{3,2},{4,5},{5,4},{6,7},{7,6},{8,9},{9,8},{10,11... | collective-permute-start | bytes 110600 | tf_op jit(solution)/shard_map/ppermute | solution.py:589
  27.4 6.6 %collective-permute-start.7 = (f32[72,128]{1,0:T(8,128)S(1)}, f32[72,128]{1,0:T(8,128)S(1)}, u32[]{:S(2)}, u32[]{:S(2)}) collective-permute-start(f32[72,128]{1,0:T(8,128)S(1)} %get-tuple-element.29), channel_id=1, source_target_pairs={{0,0},{1,2},{2,1},{3,3},{4,4},{5,6},{6,5},{7,7},{8,8},{9,10},{10,9... | collective-permute-start | bytes 110600 | tf_op jit(solution)/shard_map/ppermute | solution.py:590
  28.1 4.7 %collective-permute-start.5 = (f32[2,16,128]{2,1,0:T(8,128)S(1)}, f32[2,16,128]{2,1,0:T(8,128)S(1)}, u32[]{:S(2)}, u32[]{:S(2)}) collective-permute-start(f32[2,16,128]{2,1,0:T(8,128)S(1)} %get-tuple-element.27), channel_id=1, source_target_pairs={{4,0},{8,4},{12,8},{16,12},{20,16},{24,20},{28,24},{0,28},{5,1},{9... | collective-permute-start | bytes 49160 | tf_op jit(solution)/shard_map/ppermute | solution.py:588
  29.9 4.1 %collective-permute-start.4 = (f32[2,16,128]{2,1,0:T(8,128)S(1)}, f32[2,16,128]{2,1,0:T(8,128)S(1)}, u32[]{:S(2)}, u32[]{:S(2)}) collective-permute-start(f32[2,16,128]{2,1,0:T(8,128)S(1)} %get-tuple-element.27), channel_id=1, source_target_pairs={{0,4},{4,8},{8,12},{12,16},{16,20},{20,24},{24,28},{28,0},{1,5},{5... | collective-permute-start | bytes 49160 | tf_op jit(solution)/shard_map/ppermute | solution.py:587
  43.3 9.0 %collective-permute-start.10 = (f32[576,128]{1,0:T(8,128)S(1)}, f32[576,128]{1,0:T(8,128)S(1)}, u32[]{:S(2)}, u32[]{:S(2)}) collective-permute-start(f32[576,128]{1,0:T(8,128)S(1)} %get-tuple-element.33), channel_id=1, source_target_pairs={{0,1},{1,0},{2,3},{3,2},{4,5},{5,4},{6,7},{7,6},{8,9},{9,8},{10,11... | collective-permute-start | bytes 884744 | tf_op jit(solution)/shard_map/ppermute | solution.py:589
  44.9 7.4 %collective-permute-start.11 = (f32[576,128]{1,0:T(8,128)S(1)}, f32[576,128]{1,0:T(8,128)S(1)}, u32[]{:S(2)}, u32[]{:S(2)}) collective-permute-start(f32[576,128]{1,0:T(8,128)S(1)} %get-tuple-element.34), channel_id=1, source_target_pairs={{0,0},{1,2},{2,1},{3,3},{4,4},{5,6},{6,5},{7,7},{8,8},{9,10},{10,9... | collective-permute-start | bytes 884744 | tf_op jit(solution)/shard_map/ppermute | solution.py:590
  45.6 6.7 %collective-permute-start.9 = (f32[2,128,128]{2,1,0:T(8,128)S(1)}, f32[2,128,128]{2,1,0:T(8,128)S(1)}, u32[]{:S(2)}, u32[]{:S(2)}) collective-permute-start(f32[2,128,128]{2,1,0:T(8,128)S(1)} %get-tuple-element.32), channel_id=1, source_target_pairs={{4,0},{8,4},{12,8},{16,12},{20,16},{24,20},{28,24},{0,28},{5,1},{9... | collective-permute-start | bytes 393224 | tf_op jit(solution)/shard_map/ppermute | solution.py:588
  46.9 5.5 %collective-permute-start.8 = (f32[2,128,128]{2,1,0:T(8,128)S(1)}, f32[2,128,128]{2,1,0:T(8,128)S(1)}, u32[]{:S(2)}, u32[]{:S(2)}) collective-permute-start(f32[2,128,128]{2,1,0:T(8,128)S(1)} %get-tuple-element.32), channel_id=1, source_target_pairs={{0,4},{4,8},{8,12},{12,16},{16,20},{20,24},{24,28},{28,0},{1,5},{5... | collective-permute-start | bytes 393224 | tf_op jit(solution)/shard_map/ppermute | solution.py:587
  46.9 15.1 %all-to-all-start.1 = ((f32[32,1,128]{2,1,0:T(1,128)}), f32[32,1,128]{2,1,0:T(1,128)S(1)}, u32[]{:S(2)}, u32[]{:S(2)}) async-start(f32[32,1,128]{2,1,0:T(1,128)} %bitcast.10), calls=%async_computation.1 | async-start | bytes 32768 | tf_op jit(solution)/shard_map/all_to_all | solution.py:698

commit v6 on v5

--- a/solution.py
+++ b/solution.py
@@ -276,52 +276,26 @@
         meet(rim, 0, west_buf, east_buf, plane)
         pair(edges, 0, a_buf, b_buf, levels * tracers)
 
-    def shifted(cells, near, here, edge, row):
-        norths, souths = [], []
-        if first:
-            halfs = [cells[pl.ds(here + h * SUB, SUB), :] for h in range(halves)]
-            ups = [pltpu.roll(half, SUB - 1, 0) for half in halfs] + [edge[0, pl.ds(row, 1), :]]
-            downs = [edge[1, pl.ds(row, 1), :]] + [pltpu.roll(half, 1, 0) for half in halfs]
-            for h in range(halves):
-                norths.append(jnp.where(sub == SUB - 1, ups[h + 1], ups[h]))
-                souths.append(jnp.where(sub == 0, downs[h], downs[h + 1]))
-            return norths, souths
-        source, start = near
-        for h in range(halves):
-            n = source[pl.ds(start + here + h * SUB + 1, SUB), :]
-            s = source[pl.ds(start + here + h * SUB - 1, SUB), :]
-            if h == halves - 1:
-                n = jnp.where(sub == SUB - 1, edge[0, pl.ds(row, 1), :], n)
-            if h == 0:
-                s = jnp.where(sub == 0, edge[1, pl.ds(row, 1), :], s)
-            norths.append(n)
-            souths.append(s)
-        return norths, souths
-
-    def stencil(cells, near, here, side, edge, row, co):
-        norths, souths = shifted(cells, near, here, edge, row)
+    def stencil(cells, here, side, edge, row, co):
+        halfs = [cells[pl.ds(here + h * SUB, SUB), :] for h in range(halves)]
+        ups = [pltpu.roll(half, SUB - 1, 0) for half in halfs] + [edge[0, pl.ds(row, 1), :]]
+        downs = [edge[1, pl.ds(row, 1), :]] + [pltpu.roll(half, 1, 0) for half in halfs]
         values = []
-        for h in range(halves):
-            cell = cells[pl.ds(here + h * SUB, SUB), :]
+        for h, cell in enumerate(halfs):
+            n = jnp.where(sub == SUB - 1, ups[h + 1], ups[h])
+            s = jnp.where(sub == 0, downs[h], downs[h + 1])
             c0, ce, cw, cn, cs, rims = co[h][:6]
-            value = (c0 * cell + ce * pltpu.roll(cell, LANES - 1, 1)) + (
-                cw * pltpu.roll(cell, 1, 1) + cn * norths[h]
-            )
-            values.append(value + (cs * souths[h] + rims * side(h)))
+            value = (c0 * cell + ce * pltpu.roll(cell, LANES - 1, 1)) + (cw * pltpu.roll(cell, 1, 1) + cn * n)
+            values.append(value + (cs * s + rims * side(h)))
         return values
 
     def part(ref, b, size, offset=0):
         return ref.at[pl.ds(pl.multiple_of(b * unroll * size + offset, SUB), unroll * size)]
 
     def forward_block(b, solved):
-        if first:
-            load(b).wait()
-        else:
+        load(b).wait()
+        if not first:
             load_weights(b).wait()
-
-            @pl.when(b < blocks - 1)
-            def _():
-                load(b + 1).wait()
 
         chunk, q = b * unroll // per_chunk, b * unroll % per_chunk
         turn = (LANES - 2 * q) % LANES
@@ -335,12 +309,10 @@
             return lambda h: pltpu.roll(rim_now[pl.ds(r + h * SUB, SUB), :], LANES - 1 - 2 * u, 1)
 
         cells = part(flat, b, plane, rows)
-        near = (flat, b * unroll * plane + rows)
         edge = edges.at[:, pl.ds(pl.multiple_of(b * unroll * tracers, SUB), unroll * tracers)]
         co_part = weights.at[:, pl.ds(pl.multiple_of(b * unroll * rows, SUB), unroll * rows)]
         if first:
             f_cells = part(forcing, b, rows, SUB)
-            f_near = (forcing, b * unroll * rows + SUB)
             f_edge = f_edges.at[:, pl.ds(pl.multiple_of(b * unroll, SUB), unroll)]
         for u in range(unroll):
             co = [
@@ -348,11 +320,11 @@
                 for h in range(halves)
             ]
             if first:
-                extra = stencil(f_cells, f_near, u * rows, side(u, plane), f_edge, u, co)
+                extra = stencil(f_cells, u * rows, side(u, plane), f_edge, u, co)
             new = []
             for t in range(tracers):
                 here = u * plane + t * rows
-                values = stencil(cells, near, here, side(u, t * rows), edge, u * tracers + t, co)
+                values = stencil(cells, here, side(u, t * rows), edge, u * tracers + t, co)
                 for h in range(halves):
                     value = values[h] + extra[h] if first else values[h]
                     value = value + co[h][6] * solved[t * halves + h]
@@ -363,8 +335,6 @@
 
     zero = jnp.zeros((SUB, LANES), jnp.float32)
     zeros = (zero,) * (tracers * halves)
-    if not first:
-        load(0).wait()
     lax.fori_loop(0, blocks, forward_block, zeros)
     if not first:
         above_copy.wait()
@@ -396,7 +366,11 @@
         store(b).wait()
 
 
-def pack(levels, group_rows, cap, kernel, columns, observed, errors, out, k_buf, c_buf, o_buf, e_buf, wide, sems):
+def row_offsets(count):
+    return list(range(0, count - SUB, SUB)) + [count - SUB]
+
+
+def pack(levels, group_rows, cap, kernel, columns, observed, errors, out, k_buf, c_buf, o_buf, e_buf, wide, out_buf, sems):
     lane = lane_iota()
     copies = [
         pltpu.make_async_copy(source, target, sems.at[i])
@@ -410,33 +384,45 @@
         copy.wait()
     per_level = columns.shape[0]
     groups = LANES // cap
-    pad = groups * group_rows - levels - 3
-
+    offsets = row_offsets(group_rows)
+    padded = wide.shape[1] // groups
     together = wide.shape[0]
 
     def body(start, carry):
         for n in range(together):
             i = start * together + n
             one = pl.ds(i, 1)
-            tail = [c_buf[one, :].astype(jnp.float32), o_buf[one, :], e_buf[one, :]]
-            wide[n, pl.ds(0, levels), :] = k_buf[pl.ds(i, levels, stride=per_level), :]
-            wide[n, pl.ds(levels, pad + 3), :] = jnp.concatenate(
-                tail + [jnp.zeros((pad, LANES), jnp.float32)], axis=0
-            )
+            for g in range(groups):
+                begin = g * group_rows
+                count = min(group_rows, levels - begin)
+                wide[n, pl.ds(g * padded, count), :] = k_buf[
+                    pl.ds(i + per_level * begin, count, stride=per_level), :
+                ]
+            end = (groups - 1) * padded + levels - (groups - 1) * group_rows
+            for m, row in enumerate((c_buf[one, :].astype(jnp.float32), o_buf[one, :], e_buf[one, :])):
+                wide[n, pl.ds(end + m, 1), :] = row
+            for m in range(end + 3, (groups - 1) * padded + group_rows):
+                wide[n, pl.ds(m, 1), :] = jnp.zeros((1, LANES), jnp.float32)
         for n in range(together):
             i = start * together + n
             for j in range(groups):
-                for m in range(group_rows // SUB):
+                for m in offsets:
                     made = None
                     for g in range(groups):
-                        piece = wide[n, pl.ds(g * group_rows + m * SUB, SUB), :]
+                        piece = wide[n, pl.ds(g * padded + m, SUB), :]
                         if g != j:
                             piece = pltpu.roll(piece, (g - j) * cap % LANES, 1)
                         made = piece if made is None else jnp.where(lane >= g * cap, piece, made)
-                    out[i * groups + j, pl.ds(m * SUB, SUB), :] = made
+                    out_buf[pl.ds((i * groups + j) * group_rows + m, SUB), :] = made
         return carry
 
-    lax.fori_loop(0, per_level // together, body, 0)
+    if per_level == together:
+        body(0, 0)
+    else:
+        lax.fori_loop(0, per_level // together, body, 0)
+    done = pltpu.make_async_copy(out_buf, out, sems.at[4])
+    done.start()
+    done.wait()
 
 
 def tracer_sum(block, concentration, out, buf, sems):
@@ -470,7 +456,7 @@
 
 def soundings(
     levels, rows, group_rows, cap, chunks, per_chunk, block,
-    received, sums, forcing, side_ref, a_ref, b_ref, back, arrived, table, scaled
+    received, sums, forcing, side_ref, a_ref, b_ref, back_out, arrived, table, scaled, back, sem
 ):
     lane = lane_iota()
     parts, _, width = arrived.shape
@@ -481,15 +467,15 @@
     def unpack(c, carry):
         part, col = c // (width // LANES), c % (width // LANES)
         for g in range(groups):
-            for m in range(group_rows // SUB):
+            for m in row_offsets(group_rows):
                 made = None
                 for p in range(groups):
-                    piece = received[c * groups + p, pl.ds(m * SUB, SUB), :]
+                    piece = received[pl.ds((c * groups + p) * group_rows + m, SUB), :]
                     if p != g:
                         piece = pltpu.roll(piece, (p - g) * cap % LANES, 1)
                     made = piece if made is None else jnp.where(lane >= p * cap, piece, made)
                 lanes = pl.ds(pl.multiple_of(col * LANES, LANES), LANES)
-                arrived[part, pl.ds(g * group_rows + m * SUB, SUB), lanes] = made
+                arrived[part, pl.ds(g * group_rows + m, SUB), lanes] = made
         return carry
 
     lax.fori_loop(0, parts * width // LANES, unpack, 0)
@@ -538,6 +524,8 @@
                 piece = pltpu.roll(piece, LANES - at % LANES, 1)
             back[pl.ds(j * (width // cap) + i, 1), :] = piece
 
+    leave = pltpu.make_async_copy(back, back_out, sem.at[0])
+    leave.start()
     zeros = jnp.zeros((SUB, LANES), jnp.float32)
     forcing[pl.ds(0, SUB), :] = zeros
     forcing[pl.ds(levels * rows + SUB, SUB), :] = zeros
@@ -561,6 +549,7 @@
     for chunk in range(chunks):
         put_rims(forcing, SUB, levels, per_chunk, chunk, side_ref, 0, rows)
     put_rows(forcing, SUB, a_ref, b_ref, rows, 0, levels)
+    leave.wait()
 
 
 def unpack_residual(cap, arrived, out):
@@ -603,7 +592,8 @@
     plane = tracers * rows
     per_level = slots // LANES
     groups = LANES // cap
-    group_rows = -(-(levels + 3) // (groups * SUB)) * SUB
+    group_rows = -(-(levels + 3) // groups)
+    padded_rows = -(-group_rows // SUB) * SUB
     field_bytes = levels * plane * cols * 4
     dma = pltpu.SemaphoreType.DMA
 
@@ -612,15 +602,18 @@
 
     packed = call(
         functools.partial(pack, levels, group_rows, cap),
-        [HBM] * 4, f32(bricks, group_rows, LANES), VMEM,
+        [HBM] * 4, f32(bricks * group_rows, LANES), HBM,
         (
             vmem(levels * per_level, LANES), pltpu.VMEM((per_level, LANES), jnp.int32),
             vmem(per_level, LANES), vmem(per_level, LANES),
-            vmem(largest(per_level, 8, 4, 2, 1), groups * group_rows, LANES), dma((4,)),
+            vmem(largest(per_level, 8, 4, 2, 1), groups * padded_rows, LANES),
+            vmem(bricks * group_rows, LANES), dma((5,)),
         ),
         4, 10, 800000, "pack",
     )(*(in_hbm(flat(x)) for x in (kernel, sound_col, observed, obs_error)))
-    received = lax.all_to_all(packed, ("lon", "lat"), split_axis=0, concat_axis=0, tiled=True)
+    received = lax.all_to_all(
+        packed.reshape(-1, 1, LANES), ("lon", "lat"), split_axis=0, concat_axis=0, tiled=True
+    ).reshape(-1, LANES)
 
     field = adjoint.reshape(levels * tracers, rows, LANES)
     east, north, mix = (in_hbm(flat(x)) for x in (wind_east, wind_north, mixing))
@@ -652,11 +645,11 @@
             f32(levels * rows + 2 * SUB, LANES), f32(chunks, rows, LANES), f32(levels, LANES), f32(levels, LANES),
             hbm(bricks, LANES),
         ),
-        (VMEM,) * 5,
+        (VMEM,) * 4 + (HBM,),
         (
-            vmem(parts, groups * group_rows, width),
+            vmem(parts, -(-groups * group_rows // SUB) * SUB, width),
             pltpu.VMEM((parts, width, rows // SUB * LANES), jnp.bfloat16),
-            vmem(max(parts, SUB), width),
+            vmem(max(parts, SUB), width), vmem(bricks, LANES), dma((1,)),
         ),
         10, field_bytes * 8, field_bytes, "soundings",
     )(received, sums)
@@ -673,23 +666,23 @@
         4, field_bytes, field_bytes, "coefficients",
     )(east, north, mix, *start_rims)
 
-    def advance(first, specs, operands, outs, out_specs, scratch):
+    def advance(first, together, specs, operands, outs, out_specs, scratch):
         return call(
-            functools.partial(step, levels, tracers, rows, chunks, per_chunk, unroll, first),
+            functools.partial(step, levels, tracers, rows, chunks, per_chunk, together, first),
             specs, outs, out_specs,
             (vmem(levels * tracers + 2, rows, LANES), vmem(plane + rows, LANES))
-            + scratch + (dma((2 * (levels // unroll) + 5,)),),
+            + scratch + (dma((2 * (levels // together) + 5,)),),
             16, field_bytes * 8, field_bytes * 2, "step",
         )(*operands)
 
     edge_rows = f32(levels * tracers, LANES)
     stepped, kept, *rims = advance(
-        True, [HBM] + [VMEM] * 8, (in_hbm(field), weights, rim0, edges0, forcing, *forcing_rims),
+        True, unroll, [HBM] + [VMEM] * 8, (in_hbm(field), weights, rim0, edges0, forcing, *forcing_rims),
         (hbm(*field.shape), hbm(*weight_shape), f32(*rim_shape), edge_rows, edge_rows), (HBM,) * 2 + (VMEM,) * 3,
         (vmem(chunks, rows, LANES), vmem(2, levels, LANES)),
     )
     (result,) = advance(
-        False, [HBM] * 2 + [ANY] * 4, (in_hbm(stepped), in_hbm(kept), *exchange(*rims)),
+        False, largest(unroll, 4, 3, 2, 1), [HBM] * 2 + [ANY] * 4, (in_hbm(stepped), in_hbm(kept), *exchange(*rims)),
         (f32(*field.shape),), (HBM,),
         (vmem(*weight_shape),) + (vmem(*rim_shape),) * 2 + (vmem(levels * tracers, LANES),) * 2
         + (vmem(*rim_shape), vmem(*edge_shape)),

time: 63.3 us -> 63.2 us (level)
  starting transfers between devices: 25.1 us -> 26.5 us
  waiting for transfers between devices: 3.86 us -> 2.51 us
    all_to_all x1, waiting for transfers between devices: 2.64 us -> 1.3 us  [per_device(): lax.all_to_all(packed.reshape(-1, 1, LANES), ('lon', 'lat'), split_axis=0...]
    ppermute x3, starting transfers between devices: 5.38 us -> 6.22 us  [exchange(): lax.ppermute(a_rim, 'lat', [(j, partner(j, 0)) for j in range(lats)])]
where the time goes in v6:
time: 63.2 us; the launch traced here: 62.9 us
  Pallas kernels  33.1 us (52%)
  starting transfers between devices  26.5 us (42%)
  waiting for transfers between devices  2.51 us (4%)
  between operations  0.8 us (1%)
    pallas_call x2, Pallas kernels, advance(): call(functools.partial(step, levels, tracers, rows, chunks, per_chunk, to...  19.1 us
    all_to_all x1, starting transfers between devices, per_device(): lax.all_to_all(packed.reshape(-1, 1, LANES), ('lon', 'lat'), split_axis=0...  7.3 us
    ppermute x3, starting transfers between devices, exchange(): lax.ppermute(a_rim, 'lat', [(j, partner(j, 0)) for j in range(lats)])  6.22 us
    ppermute x3, starting transfers between devices, exchange(): lax.ppermute(side_rim, 'lon', [((i + 1) % lons, i) for i in range(lons)])  5.56 us
    all_to_all x1, starting transfers between devices, per_device(): lax.all_to_all(back.reshape(bricks, 1, LANES), ('lon', 'lat'), split_axis...  5.43 us
    pallas_call x1, Pallas kernels, per_device(): call(functools.partial(first_rims, levels, tracers, rows, chunks, per_chu...  4.38 us
    pallas_call x1, Pallas kernels, per_device(): call(functools.partial(soundings, levels, rows, group_rows, cap, chunks,...  3.19 us
    pallas_call x1, Pallas kernels, per_device(): call(functools.partial(coefficients, levels, tracers, rows, per_chunk, un...  2.86 us
  transfers between devices with their start and end apart: 14, of which 2 were waited for; matrix products, arithmetic and copies ran while one was open for 0% of the time, Pallas kernels for 33%

profile of v6, /device:TPU:0, one launch (start us, length us, event | category | flops | bytes accessed | tf_op | source)
XLA Modules:
  0.0 62.9 jit_solution(17069268664271484316)
XLA Ops:
  0.6 2.2 %pack.1 = f32[608,128]{1,0:T(8,128)} custom-call(f32[576,128]{1,0:T(8,128)} %bitcast.29, s32[8,128]{1,0:T(8,128)} %bitcast.30, f32[8,128]{1,0:T(8,128)} %bitcast.31, f32[8,128]{1,0:T(8,128)} %bitcast.32), custom_call_target="tpu_custom_call" | custom-call | flops 10 | bytes 800000 | tf_op jit(solution)/shard_map/pack/pallas_call | solution.py:603
  2.8 7.3 %all-to-all-start = ((f32[608,1,128]{2,1,0:T(1,128)}), f32[608,1,128]{2,1,0:T(1,128)S(1)}, u32[]{:S(2)}, u32[]{:S(2)}) async-start(f32[608,1,128]{2,1,0:T(1,128)} %bitcast.10), calls=%async_computation | async-start | bytes 622592 | tf_op jit(solution)/shard_map/all_to_all | solution.py:614
  10.1 0.0 copy-start
  10.1 4.4 %first_rims.1 = (f32[2,144,128]{2,1,0:T(8,128)S(1)}, f32[648,128]{1,0:T(8,128)S(1)}, f32[648,128]{1,0:T(8,128)S(1)}) custom-call(f32[9216,128]{1,0:T(8,128)} %bitcast.21, f32[1152,128]{1,0:T(8,128)} %bitcast.24, f32[1152,128]{1,0:T(8,128)} %bitcast.26), custom_call_target="tpu_custom_call" | custom-call | flops 4718592 | bytes 9437184 | tf_op jit(solution)/shard_map/first_rims/pallas_call | solution.py:620
  14.5 1.8 %collective-permute-start.2 = (f32[648,128]{1,0:T(8,128)S(1)}, f32[648,128]{1,0:T(8,128)S(1)}, u32[]{:S(2)}, u32[]{:S(2)}) collective-permute-start(f32[648,128]{1,0:T(8,128)S(1)} %get-tuple-element.21), channel_id=1, source_target_pairs={{0,1},{1,0},{2,3},{3,2},{4,5},{5,4},{6,7},{7,6},{8,9},{9,8},{10,11... | collective-permute-start | bytes 995336 | tf_op jit(solution)/shard_map/ppermute | solution.py:578
  16.3 0.7 %collective-permute-start.3 = (f32[648,128]{1,0:T(8,128)S(1)}, f32[648,128]{1,0:T(8,128)S(1)}, u32[]{:S(2)}, u32[]{:S(2)}) collective-permute-start(f32[648,128]{1,0:T(8,128)S(1)} %get-tuple-element.22), channel_id=1, source_target_pairs={{0,0},{1,2},{2,1},{3,3},{4,4},{5,6},{6,5},{7,7},{8,8},{9,10},{10,9... | collective-permute-start | bytes 995336 | tf_op jit(solution)/shard_map/ppermute | solution.py:579
  17.0 1.9 %collective-permute-start.1 = (f32[2,144,128]{2,1,0:T(8,128)S(1)}, f32[2,144,128]{2,1,0:T(8,128)S(1)}, u32[]{:S(2)}, u32[]{:S(2)}) collective-permute-start(f32[2,144,128]{2,1,0:T(8,128)S(1)} %get-tuple-element.20), channel_id=1, source_target_pairs={{4,0},{8,4},{12,8},{16,12},{20,16},{24,20},{28,24},{0,28},{5,1},{9... | collective-permute-start | bytes 442376 | tf_op jit(solution)/shard_map/ppermute | solution.py:577
  18.9 0.0 collective-permute-start
  18.9 0.0 copy-done
  18.9 0.7 %tracer_sum.1.sums = bf16[2,576,256]{2,1,0:T(8,128)(2,1)S(1)} custom-call(f32[72,8,16,128]{3,2,1,0:T(8,128)S(1)} %copy-done), custom_call_target="tpu_custom_call" | custom-call | flops 1179648 | bytes 4718592 | tf_op jit(solution)/shard_map/tracer_sum/pallas_call | solution.py:632
  19.6 1.3 %all-to-all-done = f32[608,1,128]{2,1,0:T(1,128)S(1)} async-done(((f32[608,1,128]{2,1,0:T(1,128)}), f32[608,1,128]{2,1,0:T(1,128)S(1)}, u32[]{:S(2)}, u32[]{:S(2)}) %all-to-all-start) | async-done | bytes 311328 | tf_op jit(solution)/shard_map/all_to_all | solution.py:614
  20.9 3.2 %soundings.1 = (f32[1168,128]{1,0:T(8,128)S(1)}, f32[2,16,128]{2,1,0:T(8,128)S(1)}, f32[72,128]{1,0:T(8,128)S(1)}, f32[72,128]{1,0:T(8,128)S(1)}, f32[32,128]{1,0:T(8,128)}) custom-call(f32[608,128]{1,0:T(8,128)S(1)} %bitcast.19, bf16[2,576,256]{2,1,0:T(8,128)(2,1)S(1)} %tracer_sum.1.sums), custom_call_target="tpu_custom_call" | custom-call | flops 37748736 | bytes 4718592 | tf_op jit(solution)/shard_map/soundings/pallas_call | solution.py:641
  24.1 2.7 %collective-permute-start.6 = (f32[72,128]{1,0:T(8,128)S(1)}, f32[72,128]{1,0:T(8,128)S(1)}, u32[]{:S(2)}, u32[]{:S(2)}) collective-permute-start(f32[72,128]{1,0:T(8,128)S(1)} %get-tuple-element.28), channel_id=1, source_target_pairs={{0,1},{1,0},{2,3},{3,2},{4,5},{5,4},{6,7},{7,6},{8,9},{9,8},{10,11... | collective-permute-start | bytes 110600 | tf_op jit(solution)/shard_map/ppermute | solution.py:578
  26.9 0.0 collective-permute-done.1.east0
  26.9 0.7 %collective-permute-start.7 = (f32[72,128]{1,0:T(8,128)S(1)}, f32[72,128]{1,0:T(8,128)S(1)}, u32[]{:S(2)}, u32[]{:S(2)}) collective-permute-start(f32[72,128]{1,0:T(8,128)S(1)} %get-tuple-element.29), channel_id=1, source_target_pairs={{0,0},{1,2},{2,1},{3,3},{4,4},{5,6},{6,5},{7,7},{8,8},{9,10},{10,9... | collective-permute-start | bytes 110600 | tf_op jit(solution)/shard_map/ppermute | solution.py:579
  27.5 0.0 collective-permute-done.west0
  27.6 2.4 %collective-permute-start.5 = (f32[2,16,128]{2,1,0:T(8,128)S(1)}, f32[2,16,128]{2,1,0:T(8,128)S(1)}, u32[]{:S(2)}, u32[]{:S(2)}) collective-permute-start(f32[2,16,128]{2,1,0:T(8,128)S(1)} %get-tuple-element.27), channel_id=1, source_target_pairs={{4,0},{8,4},{12,8},{16,12},{20,16},{24,20},{28,24},{0,28},{5,1},{9... | collective-permute-start | bytes 49160 | tf_op jit(solution)/shard_map/ppermute | solution.py:577
  30.0 0.0 collective-permute-done.2.a0
  30.0 0.0 collective-permute-start.4
  30.0 0.0 collective-permute-done.3.b0
  30.0 2.9 %coefficients.1 = (f32[8,1152,128]{2,1,0:T(8,128)S(1)}, f32[2,128,128]{2,1,0:T(8,128)S(1)}, f32[2,576,128]{2,1,0:T(8,128)S(1)}) custom-call(f32[1152,128]{1,0:T(8,128)} %bitcast.25, f32[1152,128]{1,0:T(8,128)} %bitcast.27, f32[1152,128]{1,0:T(8,128)} %bitcast.28, f32[2,144,128]{2,1,0:T(8,128)S(1)} %collective-permute-done.west0, ...), custom_call_target="tpu_custom_call" | custom-call | flops 4718592 | bytes 4718592 | tf_op jit(solution)/shard_map/coefficients/pallas_call | solution.py:660
  32.8 0.0 collective-permute-done.5.refs_6_
  32.9 1.2 %collective-permute-done.4.refs_5_ = f32[2,16,128]{2,1,0:T(8,128)S(1)} collective-permute-done((f32[2,16,128]{2,1,0:T(8,128)S(1)}, f32[2,16,128]{2,1,0:T(8,128)S(1)}, u32[]{:S(2)}, u32[]{:S(2)}) %collective-permute-start.4) | collective-permute-done | bytes 16416 | tf_op jit(solution)/shard_map/ppermute | solution.py:576
  34.0 0.0 collective-permute-done.6.refs_7_
  34.0 0.0 collective-permute-done.7.refs_8_
  34.0 9.4 %step.2 = (f32[576,16,128]{2,1,0:T(8,128)}, f32[8,1152,128]{2,1,0:T(8,128)}, f32[2,128,128]{2,1,0:T(8,128)S(1)}, f32[576,128]{1,0:T(8,128)S(1)}, f32[576,128]{1,0:T(8,128)S(1)}) custom-call(f32[576,16,128]{2,1,0:T(8,128)} %bitcast.22, f32[8,1152,128]{2,1,0:T(8,128)S(1)} %get-tuple-element.23.refs_1_, f32[2,128,128]{2,1,0:T(8,128)S(1)} %get-tuple-element.24.refs_2_, ...), custom_call_target="tpu_custom_call" | custom-call | flops 37748736 | bytes 9437184 | tf_op jit(solution)/shard_map/step/pallas_call | solution.py:670
  43.4 1.6 %collective-permute-start.10 = (f32[576,128]{1,0:T(8,128)S(1)}, f32[576,128]{1,0:T(8,128)S(1)}, u32[]{:S(2)}, u32[]{:S(2)}) collective-permute-start(f32[576,128]{1,0:T(8,128)S(1)} %get-tuple-element.33), channel_id=1, source_target_pairs={{0,1},{1,0},{2,3},{3,2},{4,5},{5,4},{6,7},{7,6},{8,9},{9,8},{10,11... | collective-permute-start | bytes 884744 | tf_op jit(solution)/shard_map/ppermute | solution.py:578
  45.1 0.7 %collective-permute-start.11 = (f32[576,128]{1,0:T(8,128)S(1)}, f32[576,128]{1,0:T(8,128)S(1)}, u32[]{:S(2)}, u32[]{:S(2)}) collective-permute-start(f32[576,128]{1,0:T(8,128)S(1)} %get-tuple-element.34), channel_id=1, source_target_pairs={{0,0},{1,2},{2,1},{3,3},{4,4},{5,6},{6,5},{7,7},{8,8},{9,10},{10,9... | collective-permute-start | bytes 884744 | tf_op jit(solution)/shard_map/ppermute | solution.py:579
  45.7 1.3 %collective-permute-start.9 = (f32[2,128,128]{2,1,0:T(8,128)S(1)}, f32[2,128,128]{2,1,0:T(8,128)S(1)}, u32[]{:S(2)}, u32[]{:S(2)}) collective-permute-start(f32[2,128,128]{2,1,0:T(8,128)S(1)} %get-tuple-element.32), channel_id=1, source_target_pairs={{4,0},{8,4},{12,8},{16,12},{20,16},{24,20},{28,24},{0,28},{5,1},{9... | collective-permute-start | bytes 393224 | tf_op jit(solution)/shard_map/ppermute | solution.py:577
  47.0 0.0 collective-permute-start.8
  47.0 5.4 %all-to-all-start.1 = ((f32[32,1,128]{2,1,0:T(1,128)}), f32[32,1,128]{2,1,0:T(1,128)S(1)}, u32[]{:S(2)}, u32[]{:S(2)}) async-start(f32[32,1,128]{2,1,0:T(1,128)} %bitcast.13), calls=%async_computation.1 | async-start | bytes 32768 | tf_op jit(solution)/shard_map/all_to_all | solution.py:691
  52.4 0.0 collective-permute-done.9.refs_3_
  52.4 0.0 collective-permute-done.8.refs_2_
  52.5 0.0 collective-permute-done.10.refs_4_
  52.5 0.0 collective-permute-done.11.refs_5_
  52.5 9.7 %step.3 = f32[576,16,128]{2,1,0:T(8,128)} custom-call(f32[576,16,128]{2,1,0:T(8,128)} %get-tuple-element.30.refs_0_, f32[8,1152,128]{2,1,0:T(8,128)} %get-tuple-element.31.refs_1_, f32[2,128,128]{2,1,0:T(8,128)S(1)} %collective-permute-done.8.refs_2_, f32[2,128,128]{2,1,0:T(8,128)S(1)} %collective-permute-done.9.refs_3_, ...), custom_call_target="tpu_custom_call" | custom-call | flops 37748736 | bytes 9437184 | tf_op jit(solution)/shard_map/step/pallas_call | solution.py:670
  62.2 0.0 all-to-all-done.1
  62.2 0.7 %residual.1 = f32[8,128]{1,0:T(8,128)} custom-call(f32[32,128]{1,0:T(8,128)S(1)} %bitcast.20), custom_call_target="tpu_custom_call" | custom-call | flops 10 | bytes 10000 | tf_op jit(solution)/shard_map/residual/pallas_call | solution.py:695
Async XLA Ops:
  2.8 18.1 %all-to-all-start = ((f32[608,1,128]{2,1,0:T(1,128)}), f32[608,1,128]{2,1,0:T(1,128)S(1)}, u32[]{:S(2)}, u32[]{:S(2)}) async-start(f32[608,1,128]{2,1,0:T(1,128)} %bitcast.10), calls=%async_computation | async-start | bytes 622592 | tf_op jit(solution)/shard_map/all_to_all | solution.py:614
  10.1 8.8 %copy-start = (f32[72,8,16,128]{3,2,1,0:T(8,128)S(1)}, f32[72,8,16,128]{3,2,1,0:T(8,128)}, u32[]{:S(2)}) copy-start(f32[72,8,16,128]{3,2,1,0:T(8,128)} %concentration.1) | copy-start | bytes 14155780
  14.5 15.5 %collective-permute-start.2 = (f32[648,128]{1,0:T(8,128)S(1)}, f32[648,128]{1,0:T(8,128)S(1)}, u32[]{:S(2)}, u32[]{:S(2)}) collective-permute-start(f32[648,128]{1,0:T(8,128)S(1)} %get-tuple-element.21), channel_id=1, source_target_pairs={{0,1},{1,0},{2,3},{3,2},{4,5},{5,4},{6,7},{7,6},{8,9},{9,8},{10,11... | collective-permute-start | bytes 995336 | tf_op jit(solution)/shard_map/ppermute | solution.py:578
  16.3 13.6 %collective-permute-start.3 = (f32[648,128]{1,0:T(8,128)S(1)}, f32[648,128]{1,0:T(8,128)S(1)}, u32[]{:S(2)}, u32[]{:S(2)}) collective-permute-start(f32[648,128]{1,0:T(8,128)S(1)} %get-tuple-element.22), channel_id=1, source_target_pairs={{0,0},{1,2},{2,1},{3,3},{4,4},{5,6},{6,5},{7,7},{8,8},{9,10},{10,9... | collective-permute-start | bytes 995336 | tf_op jit(solution)/shard_map/ppermute | solution.py:579
  17.0 9.9 %collective-permute-start.1 = (f32[2,144,128]{2,1,0:T(8,128)S(1)}, f32[2,144,128]{2,1,0:T(8,128)S(1)}, u32[]{:S(2)}, u32[]{:S(2)}) collective-permute-start(f32[2,144,128]{2,1,0:T(8,128)S(1)} %get-tuple-element.20), channel_id=1, source_target_pairs={{4,0},{8,4},{12,8},{16,12},{20,16},{24,20},{28,24},{0,28},{5,1},{9... | collective-permute-start | bytes 442376 | tf_op jit(solution)/shard_map/ppermute | solution.py:577
  18.9 8.6 %collective-permute-start = (f32[2,144,128]{2,1,0:T(8,128)S(1)}, f32[2,144,128]{2,1,0:T(8,128)S(1)}, u32[]{:S(2)}, u32[]{:S(2)}) collective-permute-start(f32[2,144,128]{2,1,0:T(8,128)S(1)} %get-tuple-element.20), channel_id=1, source_target_pairs={{0,4},{4,8},{8,12},{12,16},{16,20},{20,24},{24,28},{28,0},{1,5},{5... | collective-permute-start | bytes 442376 | tf_op jit(solution)/shard_map/ppermute | solution.py:576
  24.1 9.9 %collective-permute-start.6 = (f32[72,128]{1,0:T(8,128)S(1)}, f32[72,128]{1,0:T(8,128)S(1)}, u32[]{:S(2)}, u32[]{:S(2)}) collective-permute-start(f32[72,128]{1,0:T(8,128)S(1)} %get-tuple-element.28), channel_id=1, source_target_pairs={{0,1},{1,0},{2,3},{3,2},{4,5},{5,4},{6,7},{7,6},{8,9},{9,8},{10,11... | collective-permute-start | bytes 110600 | tf_op jit(solution)/shard_map/ppermute | solution.py:578
  26.9 7.2 %collective-permute-start.7 = (f32[72,128]{1,0:T(8,128)S(1)}, f32[72,128]{1,0:T(8,128)S(1)}, u32[]{:S(2)}, u32[]{:S(2)}) collective-permute-start(f32[72,128]{1,0:T(8,128)S(1)} %get-tuple-element.29), channel_id=1, source_target_pairs={{0,0},{1,2},{2,1},{3,3},{4,4},{5,6},{6,5},{7,7},{8,8},{9,10},{10,9... | collective-permute-start | bytes 110600 | tf_op jit(solution)/shard_map/ppermute | solution.py:579
  27.6 5.3 %collective-permute-start.5 = (f32[2,16,128]{2,1,0:T(8,128)S(1)}, f32[2,16,128]{2,1,0:T(8,128)S(1)}, u32[]{:S(2)}, u32[]{:S(2)}) collective-permute-start(f32[2,16,128]{2,1,0:T(8,128)S(1)} %get-tuple-element.27), channel_id=1, source_target_pairs={{4,0},{8,4},{12,8},{16,12},{20,16},{24,20},{28,24},{0,28},{5,1},{9... | collective-permute-start | bytes 49160 | tf_op jit(solution)/shard_map/ppermute | solution.py:577
  30.0 4.1 %collective-permute-start.4 = (f32[2,16,128]{2,1,0:T(8,128)S(1)}, f32[2,16,128]{2,1,0:T(8,128)S(1)}, u32[]{:S(2)}, u32[]{:S(2)}) collective-permute-start(f32[2,16,128]{2,1,0:T(8,128)S(1)} %get-tuple-element.27), channel_id=1, source_target_pairs={{0,4},{4,8},{8,12},{12,16},{16,20},{20,24},{24,28},{28,0},{1,5},{5... | collective-permute-start | bytes 49160 | tf_op jit(solution)/shard_map/ppermute | solution.py:576
  43.4 9.0 %collective-permute-start.10 = (f32[576,128]{1,0:T(8,128)S(1)}, f32[576,128]{1,0:T(8,128)S(1)}, u32[]{:S(2)}, u32[]{:S(2)}) collective-permute-start(f32[576,128]{1,0:T(8,128)S(1)} %get-tuple-element.33), channel_id=1, source_target_pairs={{0,1},{1,0},{2,3},{3,2},{4,5},{5,4},{6,7},{7,6},{8,9},{9,8},{10,11... | collective-permute-start | bytes 884744 | tf_op jit(solution)/shard_map/ppermute | solution.py:578
  45.1 7.4 %collective-permute-start.11 = (f32[576,128]{1,0:T(8,128)S(1)}, f32[576,128]{1,0:T(8,128)S(1)}, u32[]{:S(2)}, u32[]{:S(2)}) collective-permute-start(f32[576,128]{1,0:T(8,128)S(1)} %get-tuple-element.34), channel_id=1, source_target_pairs={{0,0},{1,2},{2,1},{3,3},{4,4},{5,6},{6,5},{7,7},{8,8},{9,10},{10,9... | collective-permute-start | bytes 884744 | tf_op jit(solution)/shard_map/ppermute | solution.py:579
  45.7 6.7 %collective-permute-start.9 = (f32[2,128,128]{2,1,0:T(8,128)S(1)}, f32[2,128,128]{2,1,0:T(8,128)S(1)}, u32[]{:S(2)}, u32[]{:S(2)}) collective-permute-start(f32[2,128,128]{2,1,0:T(8,128)S(1)} %get-tuple-element.32), channel_id=1, source_target_pairs={{4,0},{8,4},{12,8},{16,12},{20,16},{24,20},{28,24},{0,28},{5,1},{9... | collective-permute-start | bytes 393224 | tf_op jit(solution)/shard_map/ppermute | solution.py:577
  47.0 5.5 %collective-permute-start.8 = (f32[2,128,128]{2,1,0:T(8,128)S(1)}, f32[2,128,128]{2,1,0:T(8,128)S(1)}, u32[]{:S(2)}, u32[]{:S(2)}) collective-permute-start(f32[2,128,128]{2,1,0:T(8,128)S(1)} %get-tuple-element.32), channel_id=1, source_target_pairs={{0,4},{4,8},{8,12},{12,16},{16,20},{20,24},{24,28},{28,0},{1,5},{5... | collective-permute-start | bytes 393224 | tf_op jit(solution)/shard_map/ppermute | solution.py:576
  47.0 15.2 %all-to-all-start.1 = ((f32[32,1,128]{2,1,0:T(1,128)}), f32[32,1,128]{2,1,0:T(1,128)S(1)}, u32[]{:S(2)}, u32[]{:S(2)}) async-start(f32[32,1,128]{2,1,0:T(1,128)} %bitcast.13), calls=%async_computation.1 | async-start | bytes 32768 | tf_op jit(solution)/shard_map/all_to_all | solution.py:691

commit v7 on v6

--- a/solution.py
+++ b/solution.py
@@ -216,65 +216,35 @@
 
 def step(levels, tracers, rows, chunks, per_chunk, unroll, first, *refs):
     if first:
-        field, weights, rim, edges, forcing, f_west, f_east, f_a, f_b = refs[:9]
-        out, weights_out, side_ref, a_ref, b_ref = refs[9:14]
-        buf, rim_now, f_rim, f_edges, sems = refs[14:]
+        field_in, weights, rim, edges, forcing, f_west, f_east, f_a, f_b = refs[:9]
+        solved_ref, side_ref, a_ref, b_ref, rim_now, f_rim, f_edges, sems = refs[9:]
+        field = solved_ref
     else:
-        field, weights_in, west_in, east_in, a_in, b_in, out = refs[:7]
-        buf, rim_now, weights, west_buf, east_buf, a_buf, b_buf, rim, edges, sems = refs[7:]
+        field, weights, west_in, east_in, a_in, b_in, out = refs[:7]
+        solved_ref, rim_now, rim, edges, sems = refs[7:]
 
     plane = tracers * rows
     halves = rows // SUB
     lane, sub = lane_iota(), sub_iota()
     blocks = levels // unroll
-    flat = buf.reshape((levels * tracers + 2) * rows, LANES)
+    above = weights.at[weights.shape[0] - 1]
 
     def load(b):
-        at = b * unroll * tracers
-        return pltpu.make_async_copy(
-            field.at[pl.ds(at, unroll * tracers)], buf.at[pl.ds(at + 1, unroll * tracers)], sems.at[b]
-        )
+        at = pl.ds(pl.multiple_of(b * unroll * plane, SUB), unroll * plane)
+        return pltpu.make_async_copy(field_in.at[at], field.at[at], sems.at[b])
 
     def store(b):
-        at = b * unroll * tracers
-        return pltpu.make_async_copy(
-            buf.at[pl.ds(at + 1, unroll * tracers)], out.at[pl.ds(at, unroll * tracers)], sems.at[b]
-        )
-
-    last = 2 * blocks
-    above = weights.at[weights.shape[0] - 1]
+        at = pl.ds(pl.multiple_of(b * unroll * plane, SUB), unroll * plane)
+        return pltpu.make_async_copy(solved_ref.at[at], out.at[at], sems.at[b])
+
     if first:
-        keep = pltpu.make_async_copy(weights, weights_out, sems.at[last])
         for b in range(blocks):
             load(b).start()
-        keep.start()
         meet(f_rim, 0, f_west, f_east, rows)
         pair(f_edges, 0, f_a, f_b, levels)
     else:
-        rim_copies = [
-            pltpu.make_async_copy(source, target, sems.at[last + 1 + i])
-            for i, (source, target) in enumerate(
-                ((west_in, west_buf), (east_in, east_buf), (a_in, a_buf), (b_in, b_buf))
-            )
-        ]
-        above_copy = pltpu.make_async_copy(weights_in.at[weights.shape[0] - 1], above, sems.at[last])
-        for copy in rim_copies:
-            copy.start()
-
-        def load_weights(b):
-            planes, levels_of = pl.ds(0, weights.shape[0] - 1), pl.ds(b * unroll * rows, unroll * rows)
-            return pltpu.make_async_copy(
-                weights_in.at[planes, levels_of], weights.at[planes, levels_of], sems.at[blocks + b]
-            )
-
-        for b in range(blocks):
-            load(b).start()
-            load_weights(b).start()
-        above_copy.start()
-        for copy in rim_copies:
-            copy.wait()
-        meet(rim, 0, west_buf, east_buf, plane)
-        pair(edges, 0, a_buf, b_buf, levels * tracers)
+        meet(rim, 0, west_in, east_in, plane)
+        pair(edges, 0, a_in, b_in, levels * tracers)
 
     def stencil(cells, here, side, edge, row, co):
         halfs = [cells[pl.ds(here + h * SUB, SUB), :] for h in range(halves)]
@@ -293,9 +263,8 @@
         return ref.at[pl.ds(pl.multiple_of(b * unroll * size + offset, SUB), unroll * size)]
 
     def forward_block(b, solved):
-        load(b).wait()
-        if not first:
-            load_weights(b).wait()
+        if first:
+            load(b).wait()
 
         chunk, q = b * unroll // per_chunk, b * unroll % per_chunk
         turn = (LANES - 2 * q) % LANES
@@ -308,7 +277,7 @@
         def side(u, r):
             return lambda h: pltpu.roll(rim_now[pl.ds(r + h * SUB, SUB), :], LANES - 1 - 2 * u, 1)
 
-        cells = part(flat, b, plane, rows)
+        cells, solves = part(field, b, plane), part(solved_ref, b, plane)
         edge = edges.at[:, pl.ds(pl.multiple_of(b * unroll * tracers, SUB), unroll * tracers)]
         co_part = weights.at[:, pl.ds(pl.multiple_of(b * unroll * rows, SUB), unroll * rows)]
         if first:
@@ -329,19 +298,17 @@
                     value = values[h] + extra[h] if first else values[h]
                     value = value + co[h][6] * solved[t * halves + h]
                     new.append(value)
-                    cells[pl.ds(here + h * SUB, SUB), :] = value
+                    solves[pl.ds(here + h * SUB, SUB), :] = value
             solved = tuple(new)
         return solved
 
     zero = jnp.zeros((SUB, LANES), jnp.float32)
     zeros = (zero,) * (tracers * halves)
     lax.fori_loop(0, blocks, forward_block, zeros)
-    if not first:
-        above_copy.wait()
 
     def backward_block(i, later):
         b = blocks - 1 - i
-        cells = part(flat, b, plane, rows)
+        cells = part(solved_ref, b, plane)
         factors = part(above, b, rows)
         for u in reversed(range(unroll)):
             new = []
@@ -353,17 +320,18 @@
                     cells[blk, :] = value
                     new.append(value)
             later = tuple(new)
-        store(b).start()
+        if not first:
+            store(b).start()
         return later
 
     lax.fori_loop(0, blocks, backward_block, zeros)
     if first:
         for chunk in range(chunks):
-            put_rims(flat, rows, levels, per_chunk, chunk, side_ref, 0, plane)
-        put_rows(flat, rows, a_ref, b_ref, rows, 0, levels * tracers)
-        keep.wait()
-    for b in range(blocks):
-        store(b).wait()
+            put_rims(solved_ref, 0, levels, per_chunk, chunk, side_ref, 0, plane)
+        put_rows(solved_ref, 0, a_ref, b_ref, rows, 0, levels * tracers)
+    else:
+        for b in range(blocks):
+            store(b).wait()
 
 
 def row_offsets(count):
@@ -615,7 +583,6 @@
         packed.reshape(-1, 1, LANES), ("lon", "lat"), split_axis=0, concat_axis=0, tiled=True
     ).reshape(-1, LANES)
 
-    field = adjoint.reshape(levels * tracers, rows, LANES)
     east, north, mix = (in_hbm(flat(x)) for x in (wind_east, wind_north, mixing))
     rims = call(
         functools.partial(first_rims, levels, tracers, rows, chunks, per_chunk),
@@ -663,29 +630,24 @@
         (f32(*weight_shape), f32(*rim_shape), f32(*edge_shape)),
         (VMEM,) * 3,
         (vmem(levels * rows, LANES),) * 3 + (dma((3,)),),
-        4, field_bytes, field_bytes, "coefficients",
+        4, field_bytes, 8 * field_bytes, "coefficients",
     )(east, north, mix, *start_rims)
 
-    def advance(first, together, specs, operands, outs, out_specs, scratch):
+    def advance(first, specs, operands, outs, out_specs, scratch):
         return call(
-            functools.partial(step, levels, tracers, rows, chunks, per_chunk, together, first),
-            specs, outs, out_specs,
-            (vmem(levels * tracers + 2, rows, LANES), vmem(plane + rows, LANES))
-            + scratch + (dma((2 * (levels // together) + 5,)),),
-            16, field_bytes * 8, field_bytes * 2, "step",
+            functools.partial(step, levels, tracers, rows, chunks, per_chunk, unroll, first),
+            specs, outs, out_specs, scratch + (dma((levels // unroll,)),), 10, 1, 1, "step",
         )(*operands)
 
-    edge_rows = f32(levels * tracers, LANES)
-    stepped, kept, *rims = advance(
-        True, unroll, [HBM] + [VMEM] * 8, (in_hbm(field), weights, rim0, edges0, forcing, *forcing_rims),
-        (hbm(*field.shape), hbm(*weight_shape), f32(*rim_shape), edge_rows, edge_rows), (HBM,) * 2 + (VMEM,) * 3,
-        (vmem(chunks, rows, LANES), vmem(2, levels, LANES)),
+    edge_rows, whole = f32(levels * tracers, LANES), (levels * plane, LANES)
+    stepped, *rims = advance(
+        True, [HBM] + [VMEM] * 8, (in_hbm(flat(adjoint)), weights, rim0, edges0, forcing, *forcing_rims),
+        (f32(*whole), f32(*rim_shape), edge_rows, edge_rows), (VMEM,) * 4,
+        (vmem(plane + rows, LANES), vmem(chunks, rows, LANES), vmem(2, levels, LANES)),
     )
     (result,) = advance(
-        False, largest(unroll, 4, 3, 2, 1), [HBM] * 2 + [ANY] * 4, (in_hbm(stepped), in_hbm(kept), *exchange(*rims)),
-        (f32(*field.shape),), (HBM,),
-        (vmem(*weight_shape),) + (vmem(*rim_shape),) * 2 + (vmem(levels * tracers, LANES),) * 2
-        + (vmem(*rim_shape), vmem(*edge_shape)),
+        False, [VMEM] * 6, (stepped, weights, *exchange(*rims)), (f32(*whole),), (HBM,),
+        (vmem(*whole), vmem(plane, LANES), vmem(*rim_shape), vmem(*edge_shape)),
     )
 
     returned = lax.all_to_all(

time: 63.2 us -> 67.3 us (1.065)
  local copies, waits for them, and re-layouts: 0.01 us -> 6.86 us
  Pallas kernels: 33.1 us -> 30.3 us
    unnamed x2 -> x10, local copies, waits for them, and re-layouts: 0.01 us -> 6.86 us
    pallas_call x2, Pallas kernels: 19.1 us -> 16.4 us  [advance(): call(functools.partial(step, levels, tracers, rows, chunks, per_chunk, un...]
  transfers between devices with their start and end apart: 14 -> 14, of which waited for: 2 -> 2; matrix products, arithmetic and copies ran while one was open for 0% -> 0% of each run, Pallas kernels for 33% -> 27%
where the time goes in v7:
time: 67.3 us; the launch traced here: 67 us
  Pallas kernels  30.3 us (45%)
  starting transfers between devices  26.4 us (39%)
  local copies, waits for them, and re-layouts  6.86 us (10%)
  waiting for transfers between devices  2.5 us (4%)
  between operations  0.83 us (1%)
    pallas_call x2, Pallas kernels, advance(): call(functools.partial(step, levels, tracers, rows, chunks, per_chunk, un...  16.4 us
    all_to_all x1, starting transfers between devices, per_device(): lax.all_to_all(packed.reshape(-1, 1, LANES), ('lon', 'lat'), split_axis=0...  7.3 us
    unnamed x10, local copies, waits for them, and re-layouts  6.86 us
    ppermute x3, starting transfers between devices, exchange(): lax.ppermute(a_rim, 'lat', [(j, partner(j, 0)) for j in range(lats)])  6.15 us
    ppermute x3, starting transfers between devices, exchange(): lax.ppermute(side_rim, 'lon', [((i + 1) % lons, i) for i in range(lons)])  5.57 us
    all_to_all x1, starting transfers between devices, per_device(): lax.all_to_all(back.reshape(bricks, 1, LANES), ('lon', 'lat'), split_axis...  5.41 us
    pallas_call x1, Pallas kernels, per_device(): call(functools.partial(first_rims, levels, tracers, rows, chunks, per_chu...  4.38 us
    pallas_call x1, Pallas kernels, per_device(): call(functools.partial(soundings, levels, rows, group_rows, cap, chunks,...  3.19 us
  transfers between devices with their start and end apart: 14, of which 2 were waited for; matrix products, arithmetic and copies ran while one was open for 0% of the time, Pallas kernels for 27%

profile of v7, /device:TPU:0, one launch (start us, length us, event | category | flops | bytes accessed | tf_op | source)
XLA Modules:
  0.0 67.0 jit_solution(11956970693205958809)
XLA Ops:
  0.6 2.2 %pack.1 = f32[608,128]{1,0:T(8,128)} custom-call(f32[576,128]{1,0:T(8,128)} %bitcast.28, s32[8,128]{1,0:T(8,128)} %bitcast.29, f32[8,128]{1,0:T(8,128)} %bitcast.30, f32[8,128]{1,0:T(8,128)} %bitcast.31), custom_call_target="tpu_custom_call" | custom-call | flops 10 | bytes 800000 | tf_op jit(solution)/shard_map/pack/pallas_call | solution.py:571
  2.8 7.3 %all-to-all-start = ((f32[608,1,128]{2,1,0:T(1,128)}), f32[608,1,128]{2,1,0:T(1,128)S(1)}, u32[]{:S(2)}, u32[]{:S(2)}) async-start(f32[608,1,128]{2,1,0:T(1,128)} %bitcast.9), calls=%async_computation | async-start | bytes 622592 | tf_op jit(solution)/shard_map/all_to_all | solution.py:582
  10.1 0.0 copy-start.4
  10.1 4.4 %first_rims.1 = (f32[2,144,128]{2,1,0:T(8,128)S(1)}, f32[648,128]{1,0:T(8,128)S(1)}, f32[648,128]{1,0:T(8,128)S(1)}) custom-call(f32[9216,128]{1,0:T(8,128)} %bitcast.20, f32[1152,128]{1,0:T(8,128)} %bitcast.23, f32[1152,128]{1,0:T(8,128)} %bitcast.25), custom_call_target="tpu_custom_call" | custom-call | flops 4718592 | bytes 9437184 | tf_op jit(solution)/shard_map/first_rims/pallas_call | solution.py:587
  14.5 1.8 %collective-permute-start.2 = (f32[648,128]{1,0:T(8,128)S(1)}, f32[648,128]{1,0:T(8,128)S(1)}, u32[]{:S(2)}, u32[]{:S(2)}) collective-permute-start(f32[648,128]{1,0:T(8,128)S(1)} %get-tuple-element.20), channel_id=1, source_target_pairs={{0,1},{1,0},{2,3},{3,2},{4,5},{5,4},{6,7},{7,6},{8,9},{9,8},{10,11... | collective-permute-start | bytes 995336 | tf_op jit(solution)/shard_map/ppermute | solution.py:546
  16.3 0.7 %collective-permute-start.3 = (f32[648,128]{1,0:T(8,128)S(1)}, f32[648,128]{1,0:T(8,128)S(1)}, u32[]{:S(2)}, u32[]{:S(2)}) collective-permute-start(f32[648,128]{1,0:T(8,128)S(1)} %get-tuple-element.21), channel_id=1, source_target_pairs={{0,0},{1,2},{2,1},{3,3},{4,4},{5,6},{6,5},{7,7},{8,8},{9,10},{10,9... | collective-permute-start | bytes 995336 | tf_op jit(solution)/shard_map/ppermute | solution.py:547
  17.0 1.9 %collective-permute-start.1 = (f32[2,144,128]{2,1,0:T(8,128)S(1)}, f32[2,144,128]{2,1,0:T(8,128)S(1)}, u32[]{:S(2)}, u32[]{:S(2)}) collective-permute-start(f32[2,144,128]{2,1,0:T(8,128)S(1)} %get-tuple-element.19), channel_id=1, source_target_pairs={{4,0},{8,4},{12,8},{16,12},{20,16},{24,20},{28,24},{0,28},{5,1},{9... | collective-permute-start | bytes 442376 | tf_op jit(solution)/shard_map/ppermute | solution.py:545
  18.9 0.0 collective-permute-start
  18.9 0.0 copy-done.4
  18.9 0.7 %tracer_sum.1.sums = bf16[2,576,256]{2,1,0:T(8,128)(2,1)S(1)} custom-call(f32[72,8,16,128]{3,2,1,0:T(8,128)S(1)} %copy-done.4), custom_call_target="tpu_custom_call" | custom-call | flops 1179648 | bytes 4718592 | tf_op jit(solution)/shard_map/tracer_sum/pallas_call | solution.py:599
  19.6 1.3 %all-to-all-done = f32[608,1,128]{2,1,0:T(1,128)S(1)} async-done(((f32[608,1,128]{2,1,0:T(1,128)}), f32[608,1,128]{2,1,0:T(1,128)S(1)}, u32[]{:S(2)}, u32[]{:S(2)}) %all-to-all-start) | async-done | bytes 311328 | tf_op jit(solution)/shard_map/all_to_all | solution.py:582
  20.9 3.2 %soundings.1 = (f32[1168,128]{1,0:T(8,128)S(1)}, f32[2,16,128]{2,1,0:T(8,128)S(1)}, f32[72,128]{1,0:T(8,128)S(1)}, f32[72,128]{1,0:T(8,128)S(1)}, f32[32,128]{1,0:T(8,128)}) custom-call(f32[608,128]{1,0:T(8,128)S(1)} %bitcast.18, bf16[2,576,256]{2,1,0:T(8,128)(2,1)S(1)} %tracer_sum.1.sums), custom_call_target="tpu_custom_call" | custom-call | flops 37748736 | bytes 4718592 | tf_op jit(solution)/shard_map/soundings/pallas_call | solution.py:608
  24.1 2.7 %collective-permute-start.6 = (f32[72,128]{1,0:T(8,128)S(1)}, f32[72,128]{1,0:T(8,128)S(1)}, u32[]{:S(2)}, u32[]{:S(2)}) collective-permute-start(f32[72,128]{1,0:T(8,128)S(1)} %get-tuple-element.27), channel_id=1, source_target_pairs={{0,1},{1,0},{2,3},{3,2},{4,5},{5,4},{6,7},{7,6},{8,9},{9,8},{10,11... | collective-permute-start | bytes 110600 | tf_op jit(solution)/shard_map/ppermute | solution.py:546
  26.9 0.0 collective-permute-done.1.east0
  26.9 0.7 collective-permute-start.7
  27.5 0.0 collective-permute-done.west0
  27.5 2.4 %collective-permute-start.5 = (f32[2,16,128]{2,1,0:T(8,128)S(1)}, f32[2,16,128]{2,1,0:T(8,128)S(1)}, u32[]{:S(2)}, u32[]{:S(2)}) collective-permute-start(f32[2,16,128]{2,1,0:T(8,128)S(1)} %get-tuple-element.26), channel_id=1, source_target_pairs={{4,0},{8,4},{12,8},{16,12},{20,16},{24,20},{28,24},{0,28},{5,1},{9... | collective-permute-start | bytes 49160 | tf_op jit(solution)/shard_map/ppermute | solution.py:545
  30.0 0.0 collective-permute-done.2.a0
  30.0 0.0 collective-permute-start.4
  30.0 0.0 collective-permute-done.3.b0
  30.0 2.9 %coefficients.1 = (f32[8,1152,128]{2,1,0:T(8,128)S(1)}, f32[2,128,128]{2,1,0:T(8,128)S(1)}, f32[2,576,128]{2,1,0:T(8,128)S(1)}) custom-call(f32[1152,128]{1,0:T(8,128)} %bitcast.24, f32[1152,128]{1,0:T(8,128)} %bitcast.26, f32[1152,128]{1,0:T(8,128)} %bitcast.27, f32[2,144,128]{2,1,0:T(8,128)S(1)} %collective-permute-done.west0, ...), custom_call_target="tpu_custom_call" | custom-call | flops 4718592 | bytes 37748736 | tf_op jit(solution)/shard_map/coefficients/pallas_call | solution.py:627
  32.8 0.0 copy-start
  32.8 0.0 collective-permute-done.5.refs_6_
  32.9 1.2 %collective-permute-done.4.refs_5_ = f32[2,16,128]{2,1,0:T(8,128)S(1)} collective-permute-done((f32[2,16,128]{2,1,0:T(8,128)S(1)}, f32[2,16,128]{2,1,0:T(8,128)S(1)}, u32[]{:S(2)}, u32[]{:S(2)}) %collective-permute-start.4) | collective-permute-done | bytes 16416 | tf_op jit(solution)/shard_map/ppermute | solution.py:544
  34.0 0.0 collective-permute-done.6.refs_7_
  34.0 0.0 collective-permute-done.7.refs_8_
  34.0 9.3 %step.2 = (f32[9216,128]{1,0:T(8,128)S(1)}, f32[2,128,128]{2,1,0:T(8,128)S(1)}, f32[576,128]{1,0:T(8,128)S(1)}, f32[576,128]{1,0:T(8,128)S(1)}) custom-call(f32[9216,128]{1,0:T(8,128)} %bitcast.21, f32[8,1152,128]{2,1,0:T(8,128)S(1)} %get-tuple-element.22.refs_1_, f32[2,128,128]{2,1,0:T(8,128)S(1)} %get-tuple-element.23.refs_2_, ...), custom_call_target="tpu_custom_call" | custom-call | flops 1 | bytes 1 | tf_op jit(solution)/shard_map/step/pallas_call | solution.py:637
  43.3 0.0 copy-done
  43.3 0.0 copy-start.2
  43.3 2.2 %copy-done.2 = f32[9216,128]{1,0:T(8,128)} copy-done((f32[9216,128]{1,0:T(8,128)}, f32[9216,128]{1,0:T(8,128)S(1)}, u32[]{:S(2)}) %copy-start.2) | copy-done | bytes 4718616
  45.5 1.6 %collective-permute-start.10 = (f32[576,128]{1,0:T(8,128)S(1)}, f32[576,128]{1,0:T(8,128)S(1)}, u32[]{:S(2)}, u32[]{:S(2)}) collective-permute-start(f32[576,128]{1,0:T(8,128)S(1)} %get-tuple-element.31), channel_id=1, source_target_pairs={{0,1},{1,0},{2,3},{3,2},{4,5},{5,4},{6,7},{7,6},{8,9},{9,8},{10,11... | collective-permute-start | bytes 884744 | tf_op jit(solution)/shard_map/ppermute | solution.py:546
  47.1 0.7 collective-permute-start.11
  47.8 1.3 %collective-permute-start.9 = (f32[2,128,128]{2,1,0:T(8,128)S(1)}, f32[2,128,128]{2,1,0:T(8,128)S(1)}, u32[]{:S(2)}, u32[]{:S(2)}) collective-permute-start(f32[2,128,128]{2,1,0:T(8,128)S(1)} %get-tuple-element.30), channel_id=1, source_target_pairs={{4,0},{8,4},{12,8},{16,12},{20,16},{24,20},{28,24},{0,28},{5,1},{9... | collective-permute-start | bytes 393224 | tf_op jit(solution)/shard_map/ppermute | solution.py:545
  49.0 0.0 collective-permute-start.8
  49.0 5.4 %all-to-all-start.1 = ((f32[32,1,128]{2,1,0:T(1,128)}), f32[32,1,128]{2,1,0:T(1,128)S(1)}, u32[]{:S(2)}, u32[]{:S(2)}) async-start(f32[32,1,128]{2,1,0:T(1,128)} %bitcast.12), calls=%async_computation.1 | async-start | bytes 32768 | tf_op jit(solution)/shard_map/all_to_all | solution.py:653
  54.4 0.0 collective-permute-done.9.refs_3_
  54.5 0.0 collective-permute-done.8.refs_2_
  54.5 0.0 collective-permute-done.10.refs_4_
  54.5 0.0 collective-permute-done.11.refs_5_
  54.5 0.0 copy-start.1
  54.5 2.3 %copy-done.1 = f32[8,1152,128]{2,1,0:T(8,128)S(1)} copy-done((f32[8,1152,128]{2,1,0:T(8,128)S(1)}, f32[8,1152,128]{2,1,0:T(8,128)}, u32[]{:S(2)}) %copy-start.1) | copy-done | bytes 4718616
  56.8 0.0 copy-start.3
  56.8 2.3 %copy-done.3 = f32[9216,128]{1,0:T(8,128)S(1)} copy-done((f32[9216,128]{1,0:T(8,128)S(1)}, f32[9216,128]{1,0:T(8,128)}, u32[]{:S(2)}) %copy-start.3) | copy-done | bytes 4718616
  59.2 7.1 %step.3 = f32[9216,128]{1,0:T(8,128)} custom-call(f32[9216,128]{1,0:T(8,128)S(1)} %copy-done.3, f32[8,1152,128]{2,1,0:T(8,128)S(1)} %copy-done.1, f32[2,128,128]{2,1,0:T(8,128)S(1)} %collective-permute-done.8.refs_2_, f32[2,128,128]{2,1,0:T(8,128)S(1)} %collective-permute-done.9.refs_3_, f32[576,128]{1,0:T(8,128)S(1)} %collective-permute-done.10.refs_4_, ...), custom_call_target="tpu_custom_call" | custom-call | flops 1 | bytes 1 | tf_op jit(solution)/shard_map/step/pallas_call | solution.py:637
  66.3 0.0 all-to-all-done.1
  66.3 0.7 %residual.1 = f32[8,128]{1,0:T(8,128)} custom-call(f32[32,128]{1,0:T(8,128)S(1)} %bitcast.19), custom_call_target="tpu_custom_call" | custom-call | flops 10 | bytes 10000 | tf_op jit(solution)/shard_map/residual/pallas_call | solution.py:657
Async XLA Ops:
  2.8 18.1 %all-to-all-start = ((f32[608,1,128]{2,1,0:T(1,128)}), f32[608,1,128]{2,1,0:T(1,128)S(1)}, u32[]{:S(2)}, u32[]{:S(2)}) async-start(f32[608,1,128]{2,1,0:T(1,128)} %bitcast.9), calls=%async_computation | async-start | bytes 622592 | tf_op jit(solution)/shard_map/all_to_all | solution.py:582
  10.1 8.8 %copy-start.4 = (f32[72,8,16,128]{3,2,1,0:T(8,128)S(1)}, f32[72,8,16,128]{3,2,1,0:T(8,128)}, u32[]{:S(2)}) copy-start(f32[72,8,16,128]{3,2,1,0:T(8,128)} %concentration.1) | copy-start | bytes 14155780
  14.5 15.5 %collective-permute-start.2 = (f32[648,128]{1,0:T(8,128)S(1)}, f32[648,128]{1,0:T(8,128)S(1)}, u32[]{:S(2)}, u32[]{:S(2)}) collective-permute-start(f32[648,128]{1,0:T(8,128)S(1)} %get-tuple-element.20), channel_id=1, source_target_pairs={{0,1},{1,0},{2,3},{3,2},{4,5},{5,4},{6,7},{7,6},{8,9},{9,8},{10,11... | collective-permute-start | bytes 995336 | tf_op jit(solution)/shard_map/ppermute | solution.py:546
  16.3 13.6 %collective-permute-start.3 = (f32[648,128]{1,0:T(8,128)S(1)}, f32[648,128]{1,0:T(8,128)S(1)}, u32[]{:S(2)}, u32[]{:S(2)}) collective-permute-start(f32[648,128]{1,0:T(8,128)S(1)} %get-tuple-element.21), channel_id=1, source_target_pairs={{0,0},{1,2},{2,1},{3,3},{4,4},{5,6},{6,5},{7,7},{8,8},{9,10},{10,9... | collective-permute-start | bytes 995336 | tf_op jit(solution)/shard_map/ppermute | solution.py:547
  17.0 9.9 %collective-permute-start.1 = (f32[2,144,128]{2,1,0:T(8,128)S(1)}, f32[2,144,128]{2,1,0:T(8,128)S(1)}, u32[]{:S(2)}, u32[]{:S(2)}) collective-permute-start(f32[2,144,128]{2,1,0:T(8,128)S(1)} %get-tuple-element.19), channel_id=1, source_target_pairs={{4,0},{8,4},{12,8},{16,12},{20,16},{24,20},{28,24},{0,28},{5,1},{9... | collective-permute-start | bytes 442376 | tf_op jit(solution)/shard_map/ppermute | solution.py:545
  18.9 8.6 %collective-permute-start = (f32[2,144,128]{2,1,0:T(8,128)S(1)}, f32[2,144,128]{2,1,0:T(8,128)S(1)}, u32[]{:S(2)}, u32[]{:S(2)}) collective-permute-start(f32[2,144,128]{2,1,0:T(8,128)S(1)} %get-tuple-element.19), channel_id=1, source_target_pairs={{0,4},{4,8},{8,12},{12,16},{16,20},{20,24},{24,28},{28,0},{1,5},{5... | collective-permute-start | bytes 442376 | tf_op jit(solution)/shard_map/ppermute | solution.py:544
  24.1 9.9 %collective-permute-start.6 = (f32[72,128]{1,0:T(8,128)S(1)}, f32[72,128]{1,0:T(8,128)S(1)}, u32[]{:S(2)}, u32[]{:S(2)}) collective-permute-start(f32[72,128]{1,0:T(8,128)S(1)} %get-tuple-element.27), channel_id=1, source_target_pairs={{0,1},{1,0},{2,3},{3,2},{4,5},{5,4},{6,7},{7,6},{8,9},{9,8},{10,11... | collective-permute-start | bytes 110600 | tf_op jit(solution)/shard_map/ppermute | solution.py:546
  26.9 7.2 %collective-permute-start.7 = (f32[72,128]{1,0:T(8,128)S(1)}, f32[72,128]{1,0:T(8,128)S(1)}, u32[]{:S(2)}, u32[]{:S(2)}) collective-permute-start(f32[72,128]{1,0:T(8,128)S(1)} %get-tuple-element.28), channel_id=1, source_target_pairs={{0,0},{1,2},{2,1},{3,3},{4,4},{5,6},{6,5},{7,7},{8,8},{9,10},{10,9... | collective-permute-start | bytes 110600 | tf_op jit(solution)/shard_map/ppermute | solution.py:547
  27.5 5.3 %collective-permute-start.5 = (f32[2,16,128]{2,1,0:T(8,128)S(1)}, f32[2,16,128]{2,1,0:T(8,128)S(1)}, u32[]{:S(2)}, u32[]{:S(2)}) collective-permute-start(f32[2,16,128]{2,1,0:T(8,128)S(1)} %get-tuple-element.26), channel_id=1, source_target_pairs={{4,0},{8,4},{12,8},{16,12},{20,16},{24,20},{28,24},{0,28},{5,1},{9... | collective-permute-start | bytes 49160 | tf_op jit(solution)/shard_map/ppermute | solution.py:545
  30.0 4.1 %collective-permute-start.4 = (f32[2,16,128]{2,1,0:T(8,128)S(1)}, f32[2,16,128]{2,1,0:T(8,128)S(1)}, u32[]{:S(2)}, u32[]{:S(2)}) collective-permute-start(f32[2,16,128]{2,1,0:T(8,128)S(1)} %get-tuple-element.26), channel_id=1, source_target_pairs={{0,4},{4,8},{8,12},{12,16},{16,20},{20,24},{24,28},{28,0},{1,5},{5... | collective-permute-start | bytes 49160 | tf_op jit(solution)/shard_map/ppermute | solution.py:544
  32.8 10.5 %copy-start = (f32[8,1152,128]{2,1,0:T(8,128)}, f32[8,1152,128]{2,1,0:T(8,128)S(1)}, u32[]{:S(2)}) copy-start(f32[8,1152,128]{2,1,0:T(8,128)S(1)} %get-tuple-element.22.refs_1_) | copy-start | bytes 14155780
  43.3 2.2 %copy-start.2 = (f32[9216,128]{1,0:T(8,128)}, f32[9216,128]{1,0:T(8,128)S(1)}, u32[]{:S(2)}) copy-start(f32[9216,128]{1,0:T(8,128)S(1)} %get-tuple-element.29.refs_0_) | copy-start | bytes 14155780
  45.5 9.0 %collective-permute-start.10 = (f32[576,128]{1,0:T(8,128)S(1)}, f32[576,128]{1,0:T(8,128)S(1)}, u32[]{:S(2)}, u32[]{:S(2)}) collective-permute-start(f32[576,128]{1,0:T(8,128)S(1)} %get-tuple-element.31), channel_id=1, source_target_pairs={{0,1},{1,0},{2,3},{3,2},{4,5},{5,4},{6,7},{7,6},{8,9},{9,8},{10,11... | collective-permute-start | bytes 884744 | tf_op jit(solution)/shard_map/ppermute | solution.py:546
  47.1 7.4 %collective-permute-start.11 = (f32[576,128]{1,0:T(8,128)S(1)}, f32[576,128]{1,0:T(8,128)S(1)}, u32[]{:S(2)}, u32[]{:S(2)}) collective-permute-start(f32[576,128]{1,0:T(8,128)S(1)} %get-tuple-element.32), channel_id=1, source_target_pairs={{0,0},{1,2},{2,1},{3,3},{4,4},{5,6},{6,5},{7,7},{8,8},{9,10},{10,9... | collective-permute-start | bytes 884744 | tf_op jit(solution)/shard_map/ppermute | solution.py:547
  47.8 6.7 %collective-permute-start.9 = (f32[2,128,128]{2,1,0:T(8,128)S(1)}, f32[2,128,128]{2,1,0:T(8,128)S(1)}, u32[]{:S(2)}, u32[]{:S(2)}) collective-permute-start(f32[2,128,128]{2,1,0:T(8,128)S(1)} %get-tuple-element.30), channel_id=1, source_target_pairs={{4,0},{8,4},{12,8},{16,12},{20,16},{24,20},{28,24},{0,28},{5,1},{9... | collective-permute-start | bytes 393224 | tf_op jit(solution)/shard_map/ppermute | solution.py:545
  49.0 5.4 %collective-permute-start.8 = (f32[2,128,128]{2,1,0:T(8,128)S(1)}, f32[2,128,128]{2,1,0:T(8,128)S(1)}, u32[]{:S(2)}, u32[]{:S(2)}) collective-permute-start(f32[2,128,128]{2,1,0:T(8,128)S(1)} %get-tuple-element.30), channel_id=1, source_target_pairs={{0,4},{4,8},{8,12},{12,16},{16,20},{20,24},{24,28},{28,0},{1,5},{5... | collective-permute-start | bytes 393224 | tf_op jit(solution)/shard_map/ppermute | solution.py:544
  49.0 17.2 %all-to-all-start.1 = ((f32[32,1,128]{2,1,0:T(1,128)}), f32[32,1,128]{2,1,0:T(1,128)S(1)}, u32[]{:S(2)}, u32[]{:S(2)}) async-start(f32[32,1,128]{2,1,0:T(1,128)} %bitcast.12), calls=%async_computation.1 | async-start | bytes 32768 | tf_op jit(solution)/shard_map/all_to_all | solution.py:653
  54.5 2.3 %copy-start.1 = (f32[8,1152,128]{2,1,0:T(8,128)S(1)}, f32[8,1152,128]{2,1,0:T(8,128)}, u32[]{:S(2)}) copy-start(f32[8,1152,128]{2,1,0:T(8,128)} %copy-done) | copy-start | bytes 14155780
  56.8 2.3 %copy-start.3 = (f32[9216,128]{1,0:T(8,128)S(1)}, f32[9216,128]{1,0:T(8,128)}, u32[]{:S(2)}) copy-start(f32[9216,128]{1,0:T(8,128)} %copy-done.2) | copy-start | bytes 14155780

commit v8 on v6

--- a/solution.py
+++ b/solution.py
@@ -82,11 +82,14 @@
     lax.fori_loop(0, plane // SUB // group, body, 0)
 
 
+def row_places(rows):
+    odd = lax.axis_index("lat") % 2
+    return (1 - odd) * (rows - 1), odd * (rows - 1)
+
+
 def put_rows(field, offset, a_ref, b_ref, rows, begin, end):
     unroll = largest((end - begin) // SUB, 9, 8, 4, 2, 1)
-    odd = lax.axis_index("lat") % 2
-    in_a = (1 - odd) * (rows - 1)
-    in_b = odd * (rows - 1)
+    in_a, in_b = row_places(rows)
 
     def body(i, carry):
         for u in range(unroll):
@@ -218,10 +221,10 @@
     if first:
         field, weights, rim, edges, forcing, f_west, f_east, f_a, f_b = refs[:9]
         out, weights_out, side_ref, a_ref, b_ref = refs[9:14]
-        buf, rim_now, f_rim, f_edges, sems = refs[14:]
+        buf, rim_now, f_rim, f_edges, f_part, sems = refs[14:]
     else:
         field, weights_in, west_in, east_in, a_in, b_in, out = refs[:7]
-        buf, rim_now, weights, west_buf, east_buf, a_buf, b_buf, rim, edges, sems = refs[7:]
+        buf, rim_now, weights, rim, edges, sems = refs[7:]
 
     plane = tracers * rows
     halves = rows // SUB
@@ -251,16 +254,7 @@
         meet(f_rim, 0, f_west, f_east, rows)
         pair(f_edges, 0, f_a, f_b, levels)
     else:
-        rim_copies = [
-            pltpu.make_async_copy(source, target, sems.at[last + 1 + i])
-            for i, (source, target) in enumerate(
-                ((west_in, west_buf), (east_in, east_buf), (a_in, a_buf), (b_in, b_buf))
-            )
-        ]
         above_copy = pltpu.make_async_copy(weights_in.at[weights.shape[0] - 1], above, sems.at[last])
-        for copy in rim_copies:
-            copy.start()
-
         def load_weights(b):
             planes, levels_of = pl.ds(0, weights.shape[0] - 1), pl.ds(b * unroll * rows, unroll * rows)
             return pltpu.make_async_copy(
@@ -271,10 +265,8 @@
             load(b).start()
             load_weights(b).start()
         above_copy.start()
-        for copy in rim_copies:
-            copy.wait()
-        meet(rim, 0, west_buf, east_buf, plane)
-        pair(edges, 0, a_buf, b_buf, levels * tracers)
+        meet(rim, 0, west_in, east_in, plane)
+        pair(edges, 0, a_in, b_in, levels * tracers)
 
     def stencil(cells, here, side, edge, row, co):
         halfs = [cells[pl.ds(here + h * SUB, SUB), :] for h in range(halves)]
@@ -292,41 +284,53 @@
     def part(ref, b, size, offset=0):
         return ref.at[pl.ds(pl.multiple_of(b * unroll * size + offset, SUB), unroll * size)]
 
+    def turned_rims(b, source, count):
+        chunk, q = b * unroll // per_chunk, b * unroll % per_chunk
+        for r in range(0, count, SUB):
+            rim_now[pl.ds(r, SUB), :] = pltpu.roll(source[chunk, pl.ds(r, SUB), :], (LANES - 2 * q) % LANES, 1)
+
+    def side(u, r):
+        return lambda h: pltpu.roll(rim_now[pl.ds(r + h * SUB, SUB), :], LANES - 1 - 2 * u, 1)
+
+    def weights_of(b):
+        co_part = weights.at[:, pl.ds(pl.multiple_of(b * unroll * rows, SUB), unroll * rows)]
+        return lambda u: [
+            [co_part[i, pl.ds(u * rows + h * SUB, SUB), :] for i in range(weights.shape[0] - 1)]
+            for h in range(halves)
+        ]
+
+    def forcing_block(b, carry):
+        turned_rims(b, f_rim, rows)
+        cells, co, parts = part(forcing, b, rows, SUB), weights_of(b), part(f_part, b, rows)
+        edge = f_edges.at[:, pl.ds(pl.multiple_of(b * unroll, SUB), unroll)]
+        for u in range(unroll):
+            values = stencil(cells, u * rows, side(u, 0), edge, u, co(u))
+            for h in range(halves):
+                parts[pl.ds(u * rows + h * SUB, SUB), :] = values[h]
+        return carry
+
+    if first:
+        lax.fori_loop(0, blocks, forcing_block, 0)
+
     def forward_block(b, solved):
         load(b).wait()
         if not first:
             load_weights(b).wait()
-
-        chunk, q = b * unroll // per_chunk, b * unroll % per_chunk
-        turn = (LANES - 2 * q) % LANES
-        for r in range(0, plane, SUB):
-            rim_now[pl.ds(r, SUB), :] = pltpu.roll(rim[chunk, pl.ds(r, SUB), :], turn, 1)
+        turned_rims(b, rim, plane)
+        cells, co_of = part(flat, b, plane, rows), weights_of(b)
+        edge = edges.at[:, pl.ds(pl.multiple_of(b * unroll * tracers, SUB), unroll * tracers)]
         if first:
-            for r in range(0, rows, SUB):
-                rim_now[pl.ds(plane + r, SUB), :] = pltpu.roll(f_rim[chunk, pl.ds(r, SUB), :], turn, 1)
-
-        def side(u, r):
-            return lambda h: pltpu.roll(rim_now[pl.ds(r + h * SUB, SUB), :], LANES - 1 - 2 * u, 1)
-
-        cells = part(flat, b, plane, rows)
-        edge = edges.at[:, pl.ds(pl.multiple_of(b * unroll * tracers, SUB), unroll * tracers)]
-        co_part = weights.at[:, pl.ds(pl.multiple_of(b * unroll * rows, SUB), unroll * rows)]
-        if first:
-            f_cells = part(forcing, b, rows, SUB)
-            f_edge = f_edges.at[:, pl.ds(pl.multiple_of(b * unroll, SUB), unroll)]
+            extra = part(f_part, b, rows)
         for u in range(unroll):
-            co = [
-                [co_part[i, pl.ds(u * rows + h * SUB, SUB), :] for i in range(weights.shape[0] - 1)]
-                for h in range(halves)
-            ]
-            if first:
-                extra = stencil(f_cells, u * rows, side(u, plane), f_edge, u, co)
+            co = co_of(u)
             new = []
             for t in range(tracers):
                 here = u * plane + t * rows
                 values = stencil(cells, here, side(u, t * rows), edge, u * tracers + t, co)
                 for h in range(halves):
-                    value = values[h] + extra[h] if first else values[h]
+                    value = values[h]
+                    if first:
+                        value = value + extra[pl.ds(u * rows + h * SUB, SUB), :]
                     value = value + co[h][6] * solved[t * halves + h]
                     new.append(value)
                     cells[pl.ds(here + h * SUB, SUB), :] = value
@@ -339,8 +343,29 @@
     if not first:
         above_copy.wait()
 
+    def rims_of(b):
+        cells = part(flat, b, plane, rows)
+        chunk, q = b * unroll // per_chunk, b * unroll % per_chunk
+        for r in range(0, plane, SUB):
+            made = jnp.zeros((SUB, LANES), jnp.float32)
+            for u in range(unroll):
+                turned = pltpu.roll(cells[pl.ds(u * plane + r, SUB), :], 2 * u + 2, 1)
+                made = jnp.where(lane >= 2 * u + 1, turned, made)
+            made = pltpu.roll(made, 2 * q, 1)
+            side_ref[chunk, pl.ds(r, SUB), :] = jnp.where(
+                lane <= 2 * (q + unroll), made, side_ref[chunk, pl.ds(r, SUB), :]
+            )
+        begin = b * unroll * tracers
+        for m in range(0, unroll * tracers, SUB):
+            for target, at in zip((a_ref, b_ref), row_places(rows)):
+                target[pl.ds(pl.multiple_of(begin + m, SUB), SUB), :] = flat[
+                    pl.ds((begin + m + 1) * rows + at, SUB, stride=rows), :
+                ]
+
     def backward_block(i, later):
         b = blocks - 1 - i
+        if first:
+            rims_of(jnp.minimum(b + 1, blocks - 1))
         cells = part(flat, b, plane, rows)
         factors = part(above, b, rows)
         for u in reversed(range(unroll)):
@@ -356,11 +381,11 @@
         store(b).start()
         return later
 
+    if first:
+        side_ref[...] = jnp.zeros(side_ref.shape, jnp.float32)
     lax.fori_loop(0, blocks, backward_block, zeros)
     if first:
-        for chunk in range(chunks):
-            put_rims(flat, rows, levels, per_chunk, chunk, side_ref, 0, plane)
-        put_rows(flat, rows, a_ref, b_ref, rows, 0, levels * tracers)
+        rims_of(0)
         keep.wait()
     for b in range(blocks):
         store(b).wait()
@@ -679,13 +704,12 @@
     stepped, kept, *rims = advance(
         True, unroll, [HBM] + [VMEM] * 8, (in_hbm(field), weights, rim0, edges0, forcing, *forcing_rims),
         (hbm(*field.shape), hbm(*weight_shape), f32(*rim_shape), edge_rows, edge_rows), (HBM,) * 2 + (VMEM,) * 3,
-        (vmem(chunks, rows, LANES), vmem(2, levels, LANES)),
+        (vmem(chunks, rows, LANES), vmem(2, levels, LANES), vmem(levels * rows, LANES)),
     )
     (result,) = advance(
-        False, largest(unroll, 4, 3, 2, 1), [HBM] * 2 + [ANY] * 4, (in_hbm(stepped), in_hbm(kept), *exchange(*rims)),
+        False, unroll, [HBM] * 2 + [VMEM] * 4, (in_hbm(stepped), in_hbm(kept), *exchange(*rims)),
         (f32(*field.shape),), (HBM,),
-        (vmem(*weight_shape),) + (vmem(*rim_shape),) * 2 + (vmem(levels * tracers, LANES),) * 2
-        + (vmem(*rim_shape), vmem(*edge_shape)),
+        (vmem(*weight_shape), vmem(*rim_shape), vmem(*edge_shape)),
     )
 
     returned = lax.all_to_all(

time: 63.2 us -> 62.8 us (level)
  transfers between devices with their start and end apart: 14 -> 14, of which waited for: 2 -> 2; matrix products, arithmetic and copies ran while one was open for 0% -> 0% of each run, Pallas kernels for 33% -> 31%
where the time goes in v8:
time: 62.8 us; the launch traced here: 62.5 us
  Pallas kernels  32.7 us (52%)
  starting transfers between devices  26.5 us (42%)
  waiting for transfers between devices  2.51 us (4%)
  between operations  0.8 us (1%)
    pallas_call x2, Pallas kernels, advance(): call(functools.partial(step, levels, tracers, rows, chunks, per_chunk, to...  18.7 us
    all_to_all x1, starting transfers between devices, per_device(): lax.all_to_all(packed.reshape(-1, 1, LANES), ('lon', 'lat'), split_axis=0...  7.3 us
    ppermute x3, starting transfers between devices, exchange(): lax.ppermute(a_rim, 'lat', [(j, partner(j, 0)) for j in range(lats)])  6.26 us
    ppermute x3, starting transfers between devices, exchange(): lax.ppermute(side_rim, 'lon', [((i + 1) % lons, i) for i in range(lons)])  5.56 us
    all_to_all x1, starting transfers between devices, per_device(): lax.all_to_all(back.reshape(bricks, 1, LANES), ('lon', 'lat'), split_axis...  5.39 us
    pallas_call x1, Pallas kernels, per_device(): call(functools.partial(first_rims, levels, tracers, rows, chunks, per_chu...  4.38 us
    pallas_call x1, Pallas kernels, per_device(): call(functools.partial(soundings, levels, rows, group_rows, cap, chunks,...  3.19 us
    pallas_call x1, Pallas kernels, per_device(): call(functools.partial(coefficients, levels, tracers, rows, per_chunk, un...  2.86 us
  transfers between devices with their start and end apart: 14, of which 2 were waited for; matrix products, arithmetic and copies ran while one was open for 0% of the time, Pallas kernels for 31%

profile of v8, /device:TPU:0, one launch (start us, length us, event | category | flops | bytes accessed | tf_op | source)
XLA Modules:
  0.0 62.5 jit_solution(3507723915024083653)
XLA Ops:
  0.6 2.2 %pack.1 = f32[608,128]{1,0:T(8,128)} custom-call(f32[576,128]{1,0:T(8,128)} %bitcast.29, s32[8,128]{1,0:T(8,128)} %bitcast.30, f32[8,128]{1,0:T(8,128)} %bitcast.31, f32[8,128]{1,0:T(8,128)} %bitcast.32), custom_call_target="tpu_custom_call" | custom-call | flops 10 | bytes 800000 | tf_op jit(solution)/shard_map/pack/pallas_call | solution.py:628
  2.8 7.3 %all-to-all-start = ((f32[608,1,128]{2,1,0:T(1,128)}), f32[608,1,128]{2,1,0:T(1,128)S(1)}, u32[]{:S(2)}, u32[]{:S(2)}) async-start(f32[608,1,128]{2,1,0:T(1,128)} %bitcast.10), calls=%async_computation | async-start | bytes 622592 | tf_op jit(solution)/shard_map/all_to_all | solution.py:639
  10.1 0.0 copy-start
  10.1 4.4 %first_rims.1 = (f32[2,144,128]{2,1,0:T(8,128)S(1)}, f32[648,128]{1,0:T(8,128)S(1)}, f32[648,128]{1,0:T(8,128)S(1)}) custom-call(f32[9216,128]{1,0:T(8,128)} %bitcast.21, f32[1152,128]{1,0:T(8,128)} %bitcast.24, f32[1152,128]{1,0:T(8,128)} %bitcast.26), custom_call_target="tpu_custom_call" | custom-call | flops 4718592 | bytes 9437184 | tf_op jit(solution)/shard_map/first_rims/pallas_call | solution.py:645
  14.5 1.8 %collective-permute-start.2 = (f32[648,128]{1,0:T(8,128)S(1)}, f32[648,128]{1,0:T(8,128)S(1)}, u32[]{:S(2)}, u32[]{:S(2)}) collective-permute-start(f32[648,128]{1,0:T(8,128)S(1)} %get-tuple-element.21), channel_id=1, source_target_pairs={{0,1},{1,0},{2,3},{3,2},{4,5},{5,4},{6,7},{7,6},{8,9},{9,8},{10,11... | collective-permute-start | bytes 995336 | tf_op jit(solution)/shard_map/ppermute | solution.py:603
  16.3 0.7 %collective-permute-start.3 = (f32[648,128]{1,0:T(8,128)S(1)}, f32[648,128]{1,0:T(8,128)S(1)}, u32[]{:S(2)}, u32[]{:S(2)}) collective-permute-start(f32[648,128]{1,0:T(8,128)S(1)} %get-tuple-element.22), channel_id=1, source_target_pairs={{0,0},{1,2},{2,1},{3,3},{4,4},{5,6},{6,5},{7,7},{8,8},{9,10},{10,9... | collective-permute-start | bytes 995336 | tf_op jit(solution)/shard_map/ppermute | solution.py:604
  17.0 1.9 %collective-permute-start.1 = (f32[2,144,128]{2,1,0:T(8,128)S(1)}, f32[2,144,128]{2,1,0:T(8,128)S(1)}, u32[]{:S(2)}, u32[]{:S(2)}) collective-permute-start(f32[2,144,128]{2,1,0:T(8,128)S(1)} %get-tuple-element.20), channel_id=1, source_target_pairs={{4,0},{8,4},{12,8},{16,12},{20,16},{24,20},{28,24},{0,28},{5,1},{9... | collective-permute-start | bytes 442376 | tf_op jit(solution)/shard_map/ppermute | solution.py:602
  18.9 0.0 collective-permute-start
  18.9 0.0 copy-done
  18.9 0.7 %tracer_sum.1.sums = bf16[2,576,256]{2,1,0:T(8,128)(2,1)S(1)} custom-call(f32[72,8,16,128]{3,2,1,0:T(8,128)S(1)} %copy-done), custom_call_target="tpu_custom_call" | custom-call | flops 1179648 | bytes 4718592 | tf_op jit(solution)/shard_map/tracer_sum/pallas_call | solution.py:657
  19.6 1.3 %all-to-all-done = f32[608,1,128]{2,1,0:T(1,128)S(1)} async-done(((f32[608,1,128]{2,1,0:T(1,128)}), f32[608,1,128]{2,1,0:T(1,128)S(1)}, u32[]{:S(2)}, u32[]{:S(2)}) %all-to-all-start) | async-done | bytes 311328 | tf_op jit(solution)/shard_map/all_to_all | solution.py:639
  20.9 3.2 %soundings.1 = (f32[1168,128]{1,0:T(8,128)S(1)}, f32[2,16,128]{2,1,0:T(8,128)S(1)}, f32[72,128]{1,0:T(8,128)S(1)}, f32[72,128]{1,0:T(8,128)S(1)}, f32[32,128]{1,0:T(8,128)}) custom-call(f32[608,128]{1,0:T(8,128)S(1)} %bitcast.19, bf16[2,576,256]{2,1,0:T(8,128)(2,1)S(1)} %tracer_sum.1.sums), custom_call_target="tpu_custom_call" | custom-call | flops 37748736 | bytes 4718592 | tf_op jit(solution)/shard_map/soundings/pallas_call | solution.py:666
  24.1 2.7 %collective-permute-start.6 = (f32[72,128]{1,0:T(8,128)S(1)}, f32[72,128]{1,0:T(8,128)S(1)}, u32[]{:S(2)}, u32[]{:S(2)}) collective-permute-start(f32[72,128]{1,0:T(8,128)S(1)} %get-tuple-element.28), channel_id=1, source_target_pairs={{0,1},{1,0},{2,3},{3,2},{4,5},{5,4},{6,7},{7,6},{8,9},{9,8},{10,11... | collective-permute-start | bytes 110600 | tf_op jit(solution)/shard_map/ppermute | solution.py:603
  26.9 0.0 collective-permute-done.1.east0
  26.9 0.7 %collective-permute-start.7 = (f32[72,128]{1,0:T(8,128)S(1)}, f32[72,128]{1,0:T(8,128)S(1)}, u32[]{:S(2)}, u32[]{:S(2)}) collective-permute-start(f32[72,128]{1,0:T(8,128)S(1)} %get-tuple-element.29), channel_id=1, source_target_pairs={{0,0},{1,2},{2,1},{3,3},{4,4},{5,6},{6,5},{7,7},{8,8},{9,10},{10,9... | collective-permute-start | bytes 110600 | tf_op jit(solution)/shard_map/ppermute | solution.py:604
  27.5 0.0 collective-permute-done.west0
  27.6 2.4 %collective-permute-start.5 = (f32[2,16,128]{2,1,0:T(8,128)S(1)}, f32[2,16,128]{2,1,0:T(8,128)S(1)}, u32[]{:S(2)}, u32[]{:S(2)}) collective-permute-start(f32[2,16,128]{2,1,0:T(8,128)S(1)} %get-tuple-element.27), channel_id=1, source_target_pairs={{4,0},{8,4},{12,8},{16,12},{20,16},{24,20},{28,24},{0,28},{5,1},{9... | collective-permute-start | bytes 49160 | tf_op jit(solution)/shard_map/ppermute | solution.py:602
  30.0 0.0 collective-permute-done.2.a0
  30.0 0.0 collective-permute-start.4
  30.0 0.0 collective-permute-done.3.b0
  30.0 2.9 %coefficients.1 = (f32[8,1152,128]{2,1,0:T(8,128)S(1)}, f32[2,128,128]{2,1,0:T(8,128)S(1)}, f32[2,576,128]{2,1,0:T(8,128)S(1)}) custom-call(f32[1152,128]{1,0:T(8,128)} %bitcast.25, f32[1152,128]{1,0:T(8,128)} %bitcast.27, f32[1152,128]{1,0:T(8,128)} %bitcast.28, f32[2,144,128]{2,1,0:T(8,128)S(1)} %collective-permute-done.west0, ...), custom_call_target="tpu_custom_call" | custom-call | flops 4718592 | bytes 4718592 | tf_op jit(solution)/shard_map/coefficients/pallas_call | solution.py:685
  32.8 0.0 collective-permute-done.5.refs_6_
  32.9 1.2 %collective-permute-done.4.refs_5_ = f32[2,16,128]{2,1,0:T(8,128)S(1)} collective-permute-done((f32[2,16,128]{2,1,0:T(8,128)S(1)}, f32[2,16,128]{2,1,0:T(8,128)S(1)}, u32[]{:S(2)}, u32[]{:S(2)}) %collective-permute-start.4) | collective-permute-done | bytes 16416 | tf_op jit(solution)/shard_map/ppermute | solution.py:601
  34.0 0.0 collective-permute-done.6.refs_7_
  34.0 0.0 collective-permute-done.7.refs_8_
  34.0 10.4 %step.2 = (f32[576,16,128]{2,1,0:T(8,128)}, f32[8,1152,128]{2,1,0:T(8,128)}, f32[2,128,128]{2,1,0:T(8,128)S(1)}, f32[576,128]{1,0:T(8,128)S(1)}, f32[576,128]{1,0:T(8,128)S(1)}) custom-call(f32[576,16,128]{2,1,0:T(8,128)} %bitcast.22, f32[8,1152,128]{2,1,0:T(8,128)S(1)} %get-tuple-element.23.refs_1_, f32[2,128,128]{2,1,0:T(8,128)S(1)} %get-tuple-element.24.refs_2_, ...), custom_call_target="tpu_custom_call" | custom-call | flops 37748736 | bytes 9437184 | tf_op jit(solution)/shard_map/step/pallas_call | solution.py:695
  44.5 1.7 %collective-permute-start.10 = (f32[576,128]{1,0:T(8,128)S(1)}, f32[576,128]{1,0:T(8,128)S(1)}, u32[]{:S(2)}, u32[]{:S(2)}) collective-permute-start(f32[576,128]{1,0:T(8,128)S(1)} %get-tuple-element.33), channel_id=1, source_target_pairs={{0,1},{1,0},{2,3},{3,2},{4,5},{5,4},{6,7},{7,6},{8,9},{9,8},{10,11... | collective-permute-start | bytes 884744 | tf_op jit(solution)/shard_map/ppermute | solution.py:603
  46.2 0.7 %collective-permute-start.11 = (f32[576,128]{1,0:T(8,128)S(1)}, f32[576,128]{1,0:T(8,128)S(1)}, u32[]{:S(2)}, u32[]{:S(2)}) collective-permute-start(f32[576,128]{1,0:T(8,128)S(1)} %get-tuple-element.34), channel_id=1, source_target_pairs={{0,0},{1,2},{2,1},{3,3},{4,4},{5,6},{6,5},{7,7},{8,8},{9,10},{10,9... | collective-permute-start | bytes 884744 | tf_op jit(solution)/shard_map/ppermute | solution.py:604
  46.8 1.3 %collective-permute-start.9 = (f32[2,128,128]{2,1,0:T(8,128)S(1)}, f32[2,128,128]{2,1,0:T(8,128)S(1)}, u32[]{:S(2)}, u32[]{:S(2)}) collective-permute-start(f32[2,128,128]{2,1,0:T(8,128)S(1)} %get-tuple-element.32), channel_id=1, source_target_pairs={{4,0},{8,4},{12,8},{16,12},{20,16},{24,20},{28,24},{0,28},{5,1},{9... | collective-permute-start | bytes 393224 | tf_op jit(solution)/shard_map/ppermute | solution.py:602
  48.1 0.0 collective-permute-start.8
  48.1 5.4 %all-to-all-start.1 = ((f32[32,1,128]{2,1,0:T(1,128)}), f32[32,1,128]{2,1,0:T(1,128)S(1)}, u32[]{:S(2)}, u32[]{:S(2)}) async-start(f32[32,1,128]{2,1,0:T(1,128)} %bitcast.13), calls=%async_computation.1 | async-start | bytes 32768 | tf_op jit(solution)/shard_map/all_to_all | solution.py:715
  53.5 0.0 collective-permute-done.9.refs_3_
  53.5 0.0 collective-permute-done.8.refs_2_
  53.5 0.0 collective-permute-done.10.refs_4_
  53.5 0.0 collective-permute-done.11.refs_5_
  53.5 8.3 %step.3 = f32[576,16,128]{2,1,0:T(8,128)} custom-call(f32[576,16,128]{2,1,0:T(8,128)} %get-tuple-element.30.refs_0_, f32[8,1152,128]{2,1,0:T(8,128)} %get-tuple-element.31.refs_1_, f32[2,128,128]{2,1,0:T(8,128)S(1)} %collective-permute-done.8.refs_2_, f32[2,128,128]{2,1,0:T(8,128)S(1)} %collective-permute-done.9.refs_3_, ...), custom_call_target="tpu_custom_call" | custom-call | flops 37748736 | bytes 9437184 | tf_op jit(solution)/shard_map/step/pallas_call | solution.py:695
  61.8 0.0 all-to-all-done.1
  61.8 0.7 %residual.1 = f32[8,128]{1,0:T(8,128)} custom-call(f32[32,128]{1,0:T(8,128)S(1)} %bitcast.20), custom_call_target="tpu_custom_call" | custom-call | flops 10 | bytes 10000 | tf_op jit(solution)/shard_map/residual/pallas_call | solution.py:719
Async XLA Ops:
  2.8 18.1 %all-to-all-start = ((f32[608,1,128]{2,1,0:T(1,128)}), f32[608,1,128]{2,1,0:T(1,128)S(1)}, u32[]{:S(2)}, u32[]{:S(2)}) async-start(f32[608,1,128]{2,1,0:T(1,128)} %bitcast.10), calls=%async_computation | async-start | bytes 622592 | tf_op jit(solution)/shard_map/all_to_all | solution.py:639
  10.1 8.8 %copy-start = (f32[72,8,16,128]{3,2,1,0:T(8,128)S(1)}, f32[72,8,16,128]{3,2,1,0:T(8,128)}, u32[]{:S(2)}) copy-start(f32[72,8,16,128]{3,2,1,0:T(8,128)} %concentration.1) | copy-start | bytes 14155780
  14.5 15.5 %collective-permute-start.2 = (f32[648,128]{1,0:T(8,128)S(1)}, f32[648,128]{1,0:T(8,128)S(1)}, u32[]{:S(2)}, u32[]{:S(2)}) collective-permute-start(f32[648,128]{1,0:T(8,128)S(1)} %get-tuple-element.21), channel_id=1, source_target_pairs={{0,1},{1,0},{2,3},{3,2},{4,5},{5,4},{6,7},{7,6},{8,9},{9,8},{10,11... | collective-permute-start | bytes 995336 | tf_op jit(solution)/shard_map/ppermute | solution.py:603
  16.3 13.6 %collective-permute-start.3 = (f32[648,128]{1,0:T(8,128)S(1)}, f32[648,128]{1,0:T(8,128)S(1)}, u32[]{:S(2)}, u32[]{:S(2)}) collective-permute-start(f32[648,128]{1,0:T(8,128)S(1)} %get-tuple-element.22), channel_id=1, source_target_pairs={{0,0},{1,2},{2,1},{3,3},{4,4},{5,6},{6,5},{7,7},{8,8},{9,10},{10,9... | collective-permute-start | bytes 995336 | tf_op jit(solution)/shard_map/ppermute | solution.py:604
  17.0 9.9 %collective-permute-start.1 = (f32[2,144,128]{2,1,0:T(8,128)S(1)}, f32[2,144,128]{2,1,0:T(8,128)S(1)}, u32[]{:S(2)}, u32[]{:S(2)}) collective-permute-start(f32[2,144,128]{2,1,0:T(8,128)S(1)} %get-tuple-element.20), channel_id=1, source_target_pairs={{4,0},{8,4},{12,8},{16,12},{20,16},{24,20},{28,24},{0,28},{5,1},{9... | collective-permute-start | bytes 442376 | tf_op jit(solution)/shard_map/ppermute | solution.py:602
  18.9 8.6 %collective-permute-start = (f32[2,144,128]{2,1,0:T(8,128)S(1)}, f32[2,144,128]{2,1,0:T(8,128)S(1)}, u32[]{:S(2)}, u32[]{:S(2)}) collective-permute-start(f32[2,144,128]{2,1,0:T(8,128)S(1)} %get-tuple-element.20), channel_id=1, source_target_pairs={{0,4},{4,8},{8,12},{12,16},{16,20},{20,24},{24,28},{28,0},{1,5},{5... | collective-permute-start | bytes 442376 | tf_op jit(solution)/shard_map/ppermute | solution.py:601
  24.1 9.9 %collective-permute-start.6 = (f32[72,128]{1,0:T(8,128)S(1)}, f32[72,128]{1,0:T(8,128)S(1)}, u32[]{:S(2)}, u32[]{:S(2)}) collective-permute-start(f32[72,128]{1,0:T(8,128)S(1)} %get-tuple-element.28), channel_id=1, source_target_pairs={{0,1},{1,0},{2,3},{3,2},{4,5},{5,4},{6,7},{7,6},{8,9},{9,8},{10,11... | collective-permute-start | bytes 110600 | tf_op jit(solution)/shard_map/ppermute | solution.py:603
  26.9 7.2 %collective-permute-start.7 = (f32[72,128]{1,0:T(8,128)S(1)}, f32[72,128]{1,0:T(8,128)S(1)}, u32[]{:S(2)}, u32[]{:S(2)}) collective-permute-start(f32[72,128]{1,0:T(8,128)S(1)} %get-tuple-element.29), channel_id=1, source_target_pairs={{0,0},{1,2},{2,1},{3,3},{4,4},{5,6},{6,5},{7,7},{8,8},{9,10},{10,9... | collective-permute-start | bytes 110600 | tf_op jit(solution)/shard_map/ppermute | solution.py:604
  27.6 5.3 %collective-permute-start.5 = (f32[2,16,128]{2,1,0:T(8,128)S(1)}, f32[2,16,128]{2,1,0:T(8,128)S(1)}, u32[]{:S(2)}, u32[]{:S(2)}) collective-permute-start(f32[2,16,128]{2,1,0:T(8,128)S(1)} %get-tuple-element.27), channel_id=1, source_target_pairs={{4,0},{8,4},{12,8},{16,12},{20,16},{24,20},{28,24},{0,28},{5,1},{9... | collective-permute-start | bytes 49160 | tf_op jit(solution)/shard_map/ppermute | solution.py:602
  30.0 4.1 %collective-permute-start.4 = (f32[2,16,128]{2,1,0:T(8,128)S(1)}, f32[2,16,128]{2,1,0:T(8,128)S(1)}, u32[]{:S(2)}, u32[]{:S(2)}) collective-permute-start(f32[2,16,128]{2,1,0:T(8,128)S(1)} %get-tuple-element.27), channel_id=1, source_target_pairs={{0,4},{4,8},{8,12},{12,16},{16,20},{20,24},{24,28},{28,0},{1,5},{5... | collective-permute-start | bytes 49160 | tf_op jit(solution)/shard_map/ppermute | solution.py:601
  44.5 9.0 %collective-permute-start.10 = (f32[576,128]{1,0:T(8,128)S(1)}, f32[576,128]{1,0:T(8,128)S(1)}, u32[]{:S(2)}, u32[]{:S(2)}) collective-permute-start(f32[576,128]{1,0:T(8,128)S(1)} %get-tuple-element.33), channel_id=1, source_target_pairs={{0,1},{1,0},{2,3},{3,2},{4,5},{5,4},{6,7},{7,6},{8,9},{9,8},{10,11... | collective-permute-start | bytes 884744 | tf_op jit(solution)/shard_map/ppermute | solution.py:603
  46.2 7.4 %collective-permute-start.11 = (f32[576,128]{1,0:T(8,128)S(1)}, f32[576,128]{1,0:T(8,128)S(1)}, u32[]{:S(2)}, u32[]{:S(2)}) collective-permute-start(f32[576,128]{1,0:T(8,128)S(1)} %get-tuple-element.34), channel_id=1, source_target_pairs={{0,0},{1,2},{2,1},{3,3},{4,4},{5,6},{6,5},{7,7},{8,8},{9,10},{10,9... | collective-permute-start | bytes 884744 | tf_op jit(solution)/shard_map/ppermute | solution.py:604
  46.8 6.7 %collective-permute-start.9 = (f32[2,128,128]{2,1,0:T(8,128)S(1)}, f32[2,128,128]{2,1,0:T(8,128)S(1)}, u32[]{:S(2)}, u32[]{:S(2)}) collective-permute-start(f32[2,128,128]{2,1,0:T(8,128)S(1)} %get-tuple-element.32), channel_id=1, source_target_pairs={{4,0},{8,4},{12,8},{16,12},{20,16},{24,20},{28,24},{0,28},{5,1},{9... | collective-permute-start | bytes 393224 | tf_op jit(solution)/shard_map/ppermute | solution.py:602
  48.1 5.4 %collective-permute-start.8 = (f32[2,128,128]{2,1,0:T(8,128)S(1)}, f32[2,128,128]{2,1,0:T(8,128)S(1)}, u32[]{:S(2)}, u32[]{:S(2)}) collective-permute-start(f32[2,128,128]{2,1,0:T(8,128)S(1)} %get-tuple-element.32), channel_id=1, source_target_pairs={{0,4},{4,8},{8,12},{12,16},{16,20},{20,24},{24,28},{28,0},{1,5},{5... | collective-permute-start | bytes 393224 | tf_op jit(solution)/shard_map/ppermute | solution.py:601
  48.1 13.7 %all-to-all-start.1 = ((f32[32,1,128]{2,1,0:T(1,128)}), f32[32,1,128]{2,1,0:T(1,128)S(1)}, u32[]{:S(2)}, u32[]{:S(2)}) async-start(f32[32,1,128]{2,1,0:T(1,128)} %bitcast.13), calls=%async_computation.1 | async-start | bytes 32768 | tf_op jit(solution)/shard_map/all_to_all | solution.py:715

commit v9 on v8

--- a/solution.py
+++ b/solution.py
@@ -62,7 +62,7 @@
     )
 
 
-def put_rims(field, offset, levels, per_chunk, chunk, out, first, plane):
+def put_rims(field, offset, levels, per_chunk, chunk, out, first, plane, begin=0, end=None):
     lane = lane_iota()
     group = largest(plane // SUB, 4, 2, 1)
     count = min(per_chunk, levels - chunk * per_chunk)
@@ -70,7 +70,11 @@
     def body(i, carry):
         r = pl.multiple_of(i * SUB * group, SUB * group)
         made = [jnp.zeros((SUB, LANES), jnp.float32)] * group
-        for q in range(count):
+        if begin:
+            made = [
+                out[chunk, pl.ds(pl.multiple_of(first + r + g * SUB, SUB), SUB), :] for g in range(group)
+            ]
+        for q in range(begin, count if end is None else end):
             for g in range(group):
                 at = pl.multiple_of((chunk * per_chunk + q) * plane + offset + r + g * SUB, SUB)
                 turned = pltpu.roll(field[pl.ds(at, SUB), :], 2 * q + 2, 1)
@@ -105,13 +109,16 @@
 def first_rims(levels, tracers, rows, chunks, per_chunk, field, east, north, side, a_ref, b_ref, f, e, n, sems):
     plane = tracers * rows
     wind_copies = [
-        pltpu.make_async_copy(east, e, sems.at[chunks]),
-        pltpu.make_async_copy(north, n, sems.at[chunks + 1]),
+        pltpu.make_async_copy(east, e, sems.at[2 * chunks]),
+        pltpu.make_async_copy(north, n, sems.at[2 * chunks + 1]),
     ]
-    copies = []
+    pieces, copies = [], []
     for i in range(chunks):
-        part = pl.ds(i * per_chunk * plane, min(per_chunk, levels - i * per_chunk) * plane)
-        copies.append(pltpu.make_async_copy(field.at[part], f.at[part], sems.at[i]))
+        count = min(per_chunk, levels - i * per_chunk)
+        for begin, end in ((0, count // 2), (count // 2, count)):
+            pieces.append((i, begin, end))
+            part = pl.ds((i * per_chunk + begin) * plane, (end - begin) * plane)
+            copies.append(pltpu.make_async_copy(field.at[part], f.at[part], sems.at[len(copies)]))
     for copy in wind_copies + copies:
         copy.start()
     wind_copies[0].wait()
@@ -120,12 +127,11 @@
     wind_copies[1].wait()
     winds = pl.ds(levels * tracers, levels)
     put_rows(n, 0, a_ref.at[winds], b_ref.at[winds], rows, 0, levels)
-    for i in range(chunks):
-        copies[i].wait()
-        put_rims(f, 0, levels, per_chunk, i, side, 0, plane)
-        put_rows(
-            f, 0, a_ref, b_ref, rows, i * per_chunk * tracers, min((i + 1) * per_chunk, levels) * tracers
-        )
+    for copy, (i, begin, end) in zip(copies, pieces):
+        copy.wait()
+        put_rims(f, 0, levels, per_chunk, i, side, 0, plane, begin, end)
+        at = i * per_chunk * tracers
+        put_rows(f, 0, a_ref, b_ref, rows, at + begin * tracers, at + end * tracers)
 
 
 def meet(rim, target, from_west, from_east, count):
@@ -221,10 +227,10 @@
     if first:
         field, weights, rim, edges, forcing, f_west, f_east, f_a, f_b = refs[:9]
         out, weights_out, side_ref, a_ref, b_ref = refs[9:14]
-        buf, rim_now, f_rim, f_edges, f_part, sems = refs[14:]
+        buf, rim_now, f_rim, f_edges, sems = refs[14:]
     else:
         field, weights_in, west_in, east_in, a_in, b_in, out = refs[:7]
-        buf, rim_now, weights, rim, edges, sems = refs[7:]
+        buf, rim_now, weights, rim, edges, solved_buf, sems = refs[7:]
 
     plane = tracers * rows
     halves = rows // SUB
@@ -238,10 +244,17 @@
             field.at[pl.ds(at, unroll * tracers)], buf.at[pl.ds(at + 1, unroll * tracers)], sems.at[b]
         )
 
+    if first:
+        solved_buf, solved_at = buf, 1
+        solved_ref = flat
+    else:
+        solved_at = 0
+        solved_ref = solved_buf.reshape(levels * tracers * rows, LANES)
+
     def store(b):
         at = b * unroll * tracers
         return pltpu.make_async_copy(
-            buf.at[pl.ds(at + 1, unroll * tracers)], out.at[pl.ds(at, unroll * tracers)], sems.at[b]
+            solved_buf.at[pl.ds(at + solved_at, unroll * tracers)], out.at[pl.ds(at, unroll * tracers)], sems.at[b]
         )
 
     last = 2 * blocks
@@ -268,14 +281,23 @@
         meet(rim, 0, west_in, east_in, plane)
         pair(edges, 0, a_in, b_in, levels * tracers)
 
-    def stencil(cells, here, side, edge, row, co):
+    def stencil(near, cells, here, side, edge, row, co, wanted=range(rows // SUB)):
         halfs = [cells[pl.ds(here + h * SUB, SUB), :] for h in range(halves)]
-        ups = [pltpu.roll(half, SUB - 1, 0) for half in halfs] + [edge[0, pl.ds(row, 1), :]]
-        downs = [edge[1, pl.ds(row, 1), :]] + [pltpu.roll(half, 1, 0) for half in halfs]
         values = []
-        for h, cell in enumerate(halfs):
-            n = jnp.where(sub == SUB - 1, ups[h + 1], ups[h])
-            s = jnp.where(sub == 0, downs[h], downs[h + 1])
+        for h in wanted:
+            cell = halfs[h]
+            if h == halves - 1:
+                n = jnp.where(sub == SUB - 1, edge[0, pl.ds(row, 1), :], pltpu.roll(cell, SUB - 1, 0))
+            elif near is not None:
+                n = near[0][pl.ds(near[1] + here + h * SUB + 1, SUB), :]
+            else:
+                n = jnp.where(sub == SUB - 1, pltpu.roll(halfs[h + 1], SUB - 1, 0), pltpu.roll(cell, SUB - 1, 0))
+            if h == 0:
+                s = jnp.where(sub == 0, edge[1, pl.ds(row, 1), :], pltpu.roll(cell, 1, 0))
+            elif near is not None:
+                s = near[0][pl.ds(near[1] + here + h * SUB - 1, SUB), :]
+            else:
+                s = jnp.where(sub == 0, pltpu.roll(halfs[h - 1], 1, 0), pltpu.roll(cell, 1, 0))
             c0, ce, cw, cn, cs, rims = co[h][:6]
             value = (c0 * cell + ce * pltpu.roll(cell, LANES - 1, 1)) + (cw * pltpu.roll(cell, 1, 1) + cn * n)
             values.append(value + (cs * s + rims * side(h)))
@@ -284,10 +306,11 @@
     def part(ref, b, size, offset=0):
         return ref.at[pl.ds(pl.multiple_of(b * unroll * size + offset, SUB), unroll * size)]
 
-    def turned_rims(b, source, count):
+    def turned_rims(b, source, count, first_row):
         chunk, q = b * unroll // per_chunk, b * unroll % per_chunk
         for r in range(0, count, SUB):
-            rim_now[pl.ds(r, SUB), :] = pltpu.roll(source[chunk, pl.ds(r, SUB), :], (LANES - 2 * q) % LANES, 1)
+            turned = pltpu.roll(source[chunk, pl.ds(r, SUB), :], (LANES - 2 * q) % LANES, 1)
+            rim_now[pl.ds(first_row + r, SUB), :] = turned
 
     def side(u, r):
         return lambda h: pltpu.roll(rim_now[pl.ds(r + h * SUB, SUB), :], LANES - 1 - 2 * u, 1)
@@ -299,42 +322,44 @@
             for h in range(halves)
         ]
 
-    def forcing_block(b, carry):
-        turned_rims(b, f_rim, rows)
-        cells, co, parts = part(forcing, b, rows, SUB), weights_of(b), part(f_part, b, rows)
-        edge = f_edges.at[:, pl.ds(pl.multiple_of(b * unroll, SUB), unroll)]
-        for u in range(unroll):
-            values = stencil(cells, u * rows, side(u, 0), edge, u, co(u))
-            for h in range(halves):
-                parts[pl.ds(u * rows + h * SUB, SUB), :] = values[h]
-        return carry
-
-    if first:
-        lax.fori_loop(0, blocks, forcing_block, 0)
-
     def forward_block(b, solved):
         load(b).wait()
         if not first:
             load_weights(b).wait()
-        turned_rims(b, rim, plane)
+        turned_rims(b, rim, plane, 0)
         cells, co_of = part(flat, b, plane, rows), weights_of(b)
         edge = edges.at[:, pl.ds(pl.multiple_of(b * unroll * tracers, SUB), unroll * tracers)]
         if first:
-            extra = part(f_part, b, rows)
+            turned_rims(b, f_rim, rows, plane)
+            f_cells = part(forcing, b, rows, SUB)
+            f_edge = f_edges.at[:, pl.ds(pl.multiple_of(b * unroll, SUB), unroll)]
+        else:
+            solves = part(solved_ref, b, plane)
         for u in range(unroll):
             co = co_of(u)
             new = []
-            for t in range(tracers):
-                here = u * plane + t * rows
-                values = stencil(cells, here, side(u, t * rows), edge, u * tracers + t, co)
+            if first:
+                extra = stencil((forcing, b * unroll * rows + SUB), f_cells, u * rows, side(u, plane), f_edge, u, co)
+                for t in range(tracers):
+                    here = u * plane + t * rows
+                    near = (flat, b * unroll * plane + rows)
+                    values = stencil(near, cells, here, side(u, t * rows), edge, u * tracers + t, co)
+                    for h in range(halves):
+                        value = values[h] + extra[h] + co[h][6] * solved[h * tracers + t]
+                        new.append(value)
+                        cells[pl.ds(here + h * SUB, SUB), :] = value
+                solved = tuple(new[t * halves + h] for h in range(halves) for t in range(tracers))
+            else:
                 for h in range(halves):
-                    value = values[h]
-                    if first:
-                        value = value + extra[pl.ds(u * rows + h * SUB, SUB), :]
-                    value = value + co[h][6] * solved[t * halves + h]
-                    new.append(value)
-                    cells[pl.ds(here + h * SUB, SUB), :] = value
-            solved = tuple(new)
+                    for t in range(tracers):
+                        here = u * plane + t * rows
+                        (value,) = stencil(
+                            None, cells, here, side(u, t * rows), edge, u * tracers + t, co, (h,)
+                        )
+                        value = value + co[h][6] * solved[h * tracers + t]
+                        new.append(value)
+                        solves[pl.ds(here + h * SUB, SUB), :] = value
+                solved = tuple(new)
         return solved
 
     zero = jnp.zeros((SUB, LANES), jnp.float32)
@@ -343,30 +368,9 @@
     if not first:
         above_copy.wait()
 
-    def rims_of(b):
-        cells = part(flat, b, plane, rows)
-        chunk, q = b * unroll // per_chunk, b * unroll % per_chunk
-        for r in range(0, plane, SUB):
-            made = jnp.zeros((SUB, LANES), jnp.float32)
-            for u in range(unroll):
-                turned = pltpu.roll(cells[pl.ds(u * plane + r, SUB), :], 2 * u + 2, 1)
-                made = jnp.where(lane >= 2 * u + 1, turned, made)
-            made = pltpu.roll(made, 2 * q, 1)
-            side_ref[chunk, pl.ds(r, SUB), :] = jnp.where(
-                lane <= 2 * (q + unroll), made, side_ref[chunk, pl.ds(r, SUB), :]
-            )
-        begin = b * unroll * tracers
-        for m in range(0, unroll * tracers, SUB):
-            for target, at in zip((a_ref, b_ref), row_places(rows)):
-                target[pl.ds(pl.multiple_of(begin + m, SUB), SUB), :] = flat[
-                    pl.ds((begin + m + 1) * rows + at, SUB, stride=rows), :
-                ]
-
     def backward_block(i, later):
         b = blocks - 1 - i
-        if first:
-            rims_of(jnp.minimum(b + 1, blocks - 1))
-        cells = part(flat, b, plane, rows)
+        cells = part(solved_ref, b, plane, solved_at * rows)
         factors = part(above, b, rows)
         for u in reversed(range(unroll)):
             new = []
@@ -381,11 +385,11 @@
         store(b).start()
         return later
 
-    if first:
-        side_ref[...] = jnp.zeros(side_ref.shape, jnp.float32)
     lax.fori_loop(0, blocks, backward_block, zeros)
     if first:
-        rims_of(0)
+        for chunk in range(chunks):
+            put_rims(flat, rows, levels, per_chunk, chunk, side_ref, 0, plane)
+        put_rows(flat, rows, a_ref, b_ref, rows, 0, levels * tracers)
         keep.wait()
     for b in range(blocks):
         store(b).wait()
@@ -489,7 +493,7 @@
     keys = halves * LANES
     groups = LANES // cap
 
-    def unpack(c, carry):
+    def unpack_one(c):
         part, col = c // (width // LANES), c % (width // LANES)
         for g in range(groups):
             for m in row_offsets(group_rows):
@@ -501,9 +505,15 @@
                     made = piece if made is None else jnp.where(lane >= p * cap, piece, made)
                 lanes = pl.ds(pl.multiple_of(col * LANES, LANES), LANES)
                 arrived[part, pl.ds(g * group_rows + m, SUB), lanes] = made
+
+    at_once = largest(parts * width // LANES, 4, 2, 1)
+
+    def unpack(i, carry):
+        for n in range(at_once):
+            unpack_one(i * at_once + n)
         return carry
 
-    lax.fori_loop(0, parts * width // LANES, unpack, 0)
+    lax.fori_loop(0, parts * width // LANES // at_once, unpack, 0)
 
     sub_index = lax.broadcasted_iota(jnp.int32, (SUB, width), 0)
     key_index = lax.broadcasted_iota(jnp.int32, (keys, width), 0)
@@ -647,7 +657,7 @@
         [HBM] * 3,
         (f32(chunks, plane + rows, LANES),) + (f32(levels * tracers + levels, LANES),) * 2,
         (VMEM,) * 3,
-        (vmem(levels * plane, LANES), vmem(levels * rows, LANES), vmem(levels * rows, LANES), dma((chunks + 2,))),
+        (vmem(levels * plane, LANES), vmem(levels * rows, LANES), vmem(levels * rows, LANES), dma((2 * chunks + 2,))),
         10, field_bytes, 2 * field_bytes, "first_rims",
     )(in_hbm(flat(adjoint)), east, north)
     start_rims = exchange(*rims)
@@ -697,19 +707,19 @@
             specs, outs, out_specs,
             (vmem(levels * tracers + 2, rows, LANES), vmem(plane + rows, LANES))
             + scratch + (dma((2 * (levels // together) + 5,)),),
-            16, field_bytes * 8, field_bytes * 2, "step",
+            22, field_bytes * 8, field_bytes * 2, "step",
         )(*operands)
 
     edge_rows = f32(levels * tracers, LANES)
     stepped, kept, *rims = advance(
         True, unroll, [HBM] + [VMEM] * 8, (in_hbm(field), weights, rim0, edges0, forcing, *forcing_rims),
         (hbm(*field.shape), hbm(*weight_shape), f32(*rim_shape), edge_rows, edge_rows), (HBM,) * 2 + (VMEM,) * 3,
-        (vmem(chunks, rows, LANES), vmem(2, levels, LANES), vmem(levels * rows, LANES)),
+        (vmem(chunks, rows, LANES), vmem(2, levels, LANES)),
     )
     (result,) = advance(
         False, unroll, [HBM] * 2 + [VMEM] * 4, (in_hbm(stepped), in_hbm(kept), *exchange(*rims)),
         (f32(*field.shape),), (HBM,),
-        (vmem(*weight_shape), vmem(*rim_shape), vmem(*edge_shape)),
+        (vmem(*weight_shape), vmem(*rim_shape), vmem(*edge_shape), vmem(levels * tracers, rows, LANES)),
     )
 
     returned = lax.all_to_all(

time: 62.8 us -> 61.7 us (0.982)
  Pallas kernels: 32.7 us -> 31.4 us
    pallas_call x2, Pallas kernels: 18.7 us -> 17.7 us  [advance(): call(functools.partial(step, levels, tracers, rows, chunks, per_chunk, to...]
where the time goes in v9:
time: 61.7 us; the launch traced here: 61.4 us
  Pallas kernels  31.4 us (51%)
  starting transfers between devices  26.8 us (43%)
  waiting for transfers between devices  2.33 us (4%)
  between operations  0.8 us (1%)
    pallas_call x2, Pallas kernels, advance(): call(functools.partial(step, levels, tracers, rows, chunks, per_chunk, to...  17.7 us
    all_to_all x1, starting transfers between devices, per_device(): lax.all_to_all(packed.reshape(-1, 1, LANES), ('lon', 'lat'), split_axis=0...  7.3 us
    ppermute x3, starting transfers between devices, exchange(): lax.ppermute(a_rim, 'lat', [(j, partner(j, 0)) for j in range(lats)])  6.52 us
    ppermute x3, starting transfers between devices, exchange(): lax.ppermute(side_rim, 'lon', [((i + 1) % lons, i) for i in range(lons)])  5.56 us
    all_to_all x1, starting transfers between devices, per_device(): lax.all_to_all(back.reshape(bricks, 1, LANES), ('lon', 'lat'), split_axis...  5.43 us
    pallas_call x1, Pallas kernels, per_device(): call(functools.partial(first_rims, levels, tracers, rows, chunks, per_chu...  4.53 us
    pallas_call x1, Pallas kernels, per_device(): call(functools.partial(coefficients, levels, tracers, rows, per_chunk, un...  2.86 us
    pallas_call x1, Pallas kernels, per_device(): call(functools.partial(soundings, levels, rows, group_rows, cap, chunks,...  2.79 us
  transfers between devices with their start and end apart: 14, of which 2 were waited for; matrix products, arithmetic and copies ran while one was open for 0% of the time, Pallas kernels for 31%

profile of v9, /device:TPU:0, one launch (start us, length us, event | category | flops | bytes accessed | tf_op | source)
XLA Modules:
  0.0 61.4 jit_solution(5203929683479123054)
XLA Ops:
  0.6 2.2 %pack.1 = f32[608,128]{1,0:T(8,128)} custom-call(f32[576,128]{1,0:T(8,128)} %bitcast.29, s32[8,128]{1,0:T(8,128)} %bitcast.30, f32[8,128]{1,0:T(8,128)} %bitcast.31, f32[8,128]{1,0:T(8,128)} %bitcast.32), custom_call_target="tpu_custom_call" | custom-call | flops 10 | bytes 800000 | tf_op jit(solution)/shard_map/pack/pallas_call | solution.py:638
  2.8 7.3 %all-to-all-start = ((f32[608,1,128]{2,1,0:T(1,128)}), f32[608,1,128]{2,1,0:T(1,128)S(1)}, u32[]{:S(2)}, u32[]{:S(2)}) async-start(f32[608,1,128]{2,1,0:T(1,128)} %bitcast.10), calls=%async_computation | async-start | bytes 622592 | tf_op jit(solution)/shard_map/all_to_all | solution.py:649
  10.1 0.0 copy-start
  10.1 4.5 %first_rims.1 = (f32[2,144,128]{2,1,0:T(8,128)S(1)}, f32[648,128]{1,0:T(8,128)S(1)}, f32[648,128]{1,0:T(8,128)S(1)}) custom-call(f32[9216,128]{1,0:T(8,128)} %bitcast.21, f32[1152,128]{1,0:T(8,128)} %bitcast.24, f32[1152,128]{1,0:T(8,128)} %bitcast.26), custom_call_target="tpu_custom_call" | custom-call | flops 4718592 | bytes 9437184 | tf_op jit(solution)/shard_map/first_rims/pallas_call | solution.py:655
  14.6 1.8 %collective-permute-start.2 = (f32[648,128]{1,0:T(8,128)S(1)}, f32[648,128]{1,0:T(8,128)S(1)}, u32[]{:S(2)}, u32[]{:S(2)}) collective-permute-start(f32[648,128]{1,0:T(8,128)S(1)} %get-tuple-element.21), channel_id=1, source_target_pairs={{0,1},{1,0},{2,3},{3,2},{4,5},{5,4},{6,7},{7,6},{8,9},{9,8},{10,11... | collective-permute-start | bytes 995336 | tf_op jit(solution)/shard_map/ppermute | solution.py:613
  16.5 0.7 %collective-permute-start.3 = (f32[648,128]{1,0:T(8,128)S(1)}, f32[648,128]{1,0:T(8,128)S(1)}, u32[]{:S(2)}, u32[]{:S(2)}) collective-permute-start(f32[648,128]{1,0:T(8,128)S(1)} %get-tuple-element.22), channel_id=1, source_target_pairs={{0,0},{1,2},{2,1},{3,3},{4,4},{5,6},{6,5},{7,7},{8,8},{9,10},{10,9... | collective-permute-start | bytes 995336 | tf_op jit(solution)/shard_map/ppermute | solution.py:614
  17.2 1.9 %collective-permute-start.1 = (f32[2,144,128]{2,1,0:T(8,128)S(1)}, f32[2,144,128]{2,1,0:T(8,128)S(1)}, u32[]{:S(2)}, u32[]{:S(2)}) collective-permute-start(f32[2,144,128]{2,1,0:T(8,128)S(1)} %get-tuple-element.20), channel_id=1, source_target_pairs={{4,0},{8,4},{12,8},{16,12},{20,16},{24,20},{28,24},{0,28},{5,1},{9... | collective-permute-start | bytes 442376 | tf_op jit(solution)/shard_map/ppermute | solution.py:612
  19.1 0.0 collective-permute-start
  19.1 0.0 copy-done
  19.1 0.7 %tracer_sum.1.sums = bf16[2,576,256]{2,1,0:T(8,128)(2,1)S(1)} custom-call(f32[72,8,16,128]{3,2,1,0:T(8,128)S(1)} %copy-done), custom_call_target="tpu_custom_call" | custom-call | flops 1179648 | bytes 4718592 | tf_op jit(solution)/shard_map/tracer_sum/pallas_call | solution.py:667
  19.8 1.1 %all-to-all-done = f32[608,1,128]{2,1,0:T(1,128)S(1)} async-done(((f32[608,1,128]{2,1,0:T(1,128)}), f32[608,1,128]{2,1,0:T(1,128)S(1)}, u32[]{:S(2)}, u32[]{:S(2)}) %all-to-all-start) | async-done | bytes 311328 | tf_op jit(solution)/shard_map/all_to_all | solution.py:649
  20.9 2.8 %soundings.1 = (f32[1168,128]{1,0:T(8,128)S(1)}, f32[2,16,128]{2,1,0:T(8,128)S(1)}, f32[72,128]{1,0:T(8,128)S(1)}, f32[72,128]{1,0:T(8,128)S(1)}, f32[32,128]{1,0:T(8,128)}) custom-call(f32[608,128]{1,0:T(8,128)S(1)} %bitcast.19, bf16[2,576,256]{2,1,0:T(8,128)(2,1)S(1)} %tracer_sum.1.sums), custom_call_target="tpu_custom_call" | custom-call | flops 37748736 | bytes 4718592 | tf_op jit(solution)/shard_map/soundings/pallas_call | solution.py:676
  23.7 2.9 %collective-permute-start.6 = (f32[72,128]{1,0:T(8,128)S(1)}, f32[72,128]{1,0:T(8,128)S(1)}, u32[]{:S(2)}, u32[]{:S(2)}) collective-permute-start(f32[72,128]{1,0:T(8,128)S(1)} %get-tuple-element.28), channel_id=1, source_target_pairs={{0,1},{1,0},{2,3},{3,2},{4,5},{5,4},{6,7},{7,6},{8,9},{9,8},{10,11... | collective-permute-start | bytes 110600 | tf_op jit(solution)/shard_map/ppermute | solution.py:613
  26.6 0.0 collective-permute-done.1.east0
  26.6 0.7 %collective-permute-start.7 = (f32[72,128]{1,0:T(8,128)S(1)}, f32[72,128]{1,0:T(8,128)S(1)}, u32[]{:S(2)}, u32[]{:S(2)}) collective-permute-start(f32[72,128]{1,0:T(8,128)S(1)} %get-tuple-element.29), channel_id=1, source_target_pairs={{0,0},{1,2},{2,1},{3,3},{4,4},{5,6},{6,5},{7,7},{8,8},{9,10},{10,9... | collective-permute-start | bytes 110600 | tf_op jit(solution)/shard_map/ppermute | solution.py:614
  27.3 0.0 collective-permute-done.west0
  27.3 2.4 %collective-permute-start.5 = (f32[2,16,128]{2,1,0:T(8,128)S(1)}, f32[2,16,128]{2,1,0:T(8,128)S(1)}, u32[]{:S(2)}, u32[]{:S(2)}) collective-permute-start(f32[2,16,128]{2,1,0:T(8,128)S(1)} %get-tuple-element.27), channel_id=1, source_target_pairs={{4,0},{8,4},{12,8},{16,12},{20,16},{24,20},{28,24},{0,28},{5,1},{9... | collective-permute-start | bytes 49160 | tf_op jit(solution)/shard_map/ppermute | solution.py:612
  29.7 0.0 collective-permute-done.2.a0
  29.7 0.0 collective-permute-start.4
  29.7 0.0 collective-permute-done.3.b0
  29.7 2.9 %coefficients.1 = (f32[8,1152,128]{2,1,0:T(8,128)S(1)}, f32[2,128,128]{2,1,0:T(8,128)S(1)}, f32[2,576,128]{2,1,0:T(8,128)S(1)}) custom-call(f32[1152,128]{1,0:T(8,128)} %bitcast.25, f32[1152,128]{1,0:T(8,128)} %bitcast.27, f32[1152,128]{1,0:T(8,128)} %bitcast.28, f32[2,144,128]{2,1,0:T(8,128)S(1)} %collective-permute-done.west0, ...), custom_call_target="tpu_custom_call" | custom-call | flops 4718592 | bytes 4718592 | tf_op jit(solution)/shard_map/coefficients/pallas_call | solution.py:695
  32.6 0.0 collective-permute-done.5.refs_6_
  32.6 1.2 %collective-permute-done.4.refs_5_ = f32[2,16,128]{2,1,0:T(8,128)S(1)} collective-permute-done((f32[2,16,128]{2,1,0:T(8,128)S(1)}, f32[2,16,128]{2,1,0:T(8,128)S(1)}, u32[]{:S(2)}, u32[]{:S(2)}) %collective-permute-start.4) | collective-permute-done | bytes 16416 | tf_op jit(solution)/shard_map/ppermute | solution.py:611
  33.8 0.0 collective-permute-done.6.refs_7_
  33.8 0.0 collective-permute-done.7.refs_8_
  33.8 9.4 %step.2 = (f32[576,16,128]{2,1,0:T(8,128)}, f32[8,1152,128]{2,1,0:T(8,128)}, f32[2,128,128]{2,1,0:T(8,128)S(1)}, f32[576,128]{1,0:T(8,128)S(1)}, f32[576,128]{1,0:T(8,128)S(1)}) custom-call(f32[576,16,128]{2,1,0:T(8,128)} %bitcast.22, f32[8,1152,128]{2,1,0:T(8,128)S(1)} %get-tuple-element.23.refs_1_, f32[2,128,128]{2,1,0:T(8,128)S(1)} %get-tuple-element.24.refs_2_, ...), custom_call_target="tpu_custom_call" | custom-call | flops 37748736 | bytes 9437184 | tf_op jit(solution)/shard_map/step/pallas_call | solution.py:705
  43.2 1.8 %collective-permute-start.10 = (f32[576,128]{1,0:T(8,128)S(1)}, f32[576,128]{1,0:T(8,128)S(1)}, u32[]{:S(2)}, u32[]{:S(2)}) collective-permute-start(f32[576,128]{1,0:T(8,128)S(1)} %get-tuple-element.33), channel_id=1, source_target_pairs={{0,1},{1,0},{2,3},{3,2},{4,5},{5,4},{6,7},{7,6},{8,9},{9,8},{10,11... | collective-permute-start | bytes 884744 | tf_op jit(solution)/shard_map/ppermute | solution.py:613
  44.9 0.7 %collective-permute-start.11 = (f32[576,128]{1,0:T(8,128)S(1)}, f32[576,128]{1,0:T(8,128)S(1)}, u32[]{:S(2)}, u32[]{:S(2)}) collective-permute-start(f32[576,128]{1,0:T(8,128)S(1)} %get-tuple-element.34), channel_id=1, source_target_pairs={{0,0},{1,2},{2,1},{3,3},{4,4},{5,6},{6,5},{7,7},{8,8},{9,10},{10,9... | collective-permute-start | bytes 884744 | tf_op jit(solution)/shard_map/ppermute | solution.py:614
  45.6 1.3 %collective-permute-start.9 = (f32[2,128,128]{2,1,0:T(8,128)S(1)}, f32[2,128,128]{2,1,0:T(8,128)S(1)}, u32[]{:S(2)}, u32[]{:S(2)}) collective-permute-start(f32[2,128,128]{2,1,0:T(8,128)S(1)} %get-tuple-element.32), channel_id=1, source_target_pairs={{4,0},{8,4},{12,8},{16,12},{20,16},{24,20},{28,24},{0,28},{5,1},{9... | collective-permute-start | bytes 393224 | tf_op jit(solution)/shard_map/ppermute | solution.py:612
  46.9 0.0 collective-permute-start.8
  46.9 5.4 %all-to-all-start.1 = ((f32[32,1,128]{2,1,0:T(1,128)}), f32[32,1,128]{2,1,0:T(1,128)S(1)}, u32[]{:S(2)}, u32[]{:S(2)}) async-start(f32[32,1,128]{2,1,0:T(1,128)} %bitcast.13), calls=%async_computation.1 | async-start | bytes 32768 | tf_op jit(solution)/shard_map/all_to_all | solution.py:725
  52.3 0.0 collective-permute-done.9.refs_3_
  52.3 0.0 collective-permute-done.8.refs_2_
  52.3 0.0 collective-permute-done.10.refs_4_
  52.3 0.0 collective-permute-done.11.refs_5_
  52.3 8.3 %step.3 = f32[576,16,128]{2,1,0:T(8,128)} custom-call(f32[576,16,128]{2,1,0:T(8,128)} %get-tuple-element.30.refs_0_, f32[8,1152,128]{2,1,0:T(8,128)} %get-tuple-element.31.refs_1_, f32[2,128,128]{2,1,0:T(8,128)S(1)} %collective-permute-done.8.refs_2_, f32[2,128,128]{2,1,0:T(8,128)S(1)} %collective-permute-done.9.refs_3_, ...), custom_call_target="tpu_custom_call" | custom-call | flops 37748736 | bytes 9437184 | tf_op jit(solution)/shard_map/step/pallas_call | solution.py:705
  60.7 0.0 all-to-all-done.1
  60.7 0.7 %residual.1 = f32[8,128]{1,0:T(8,128)} custom-call(f32[32,128]{1,0:T(8,128)S(1)} %bitcast.20), custom_call_target="tpu_custom_call" | custom-call | flops 10 | bytes 10000 | tf_op jit(solution)/shard_map/residual/pallas_call | solution.py:729
Async XLA Ops:
  2.8 18.1 %all-to-all-start = ((f32[608,1,128]{2,1,0:T(1,128)}), f32[608,1,128]{2,1,0:T(1,128)S(1)}, u32[]{:S(2)}, u32[]{:S(2)}) async-start(f32[608,1,128]{2,1,0:T(1,128)} %bitcast.10), calls=%async_computation | async-start | bytes 622592 | tf_op jit(solution)/shard_map/all_to_all | solution.py:649
  10.1 9.0 %copy-start = (f32[72,8,16,128]{3,2,1,0:T(8,128)S(1)}, f32[72,8,16,128]{3,2,1,0:T(8,128)}, u32[]{:S(2)}) copy-start(f32[72,8,16,128]{3,2,1,0:T(8,128)} %concentration.1) | copy-start | bytes 14155780
  14.6 15.1 %collective-permute-start.2 = (f32[648,128]{1,0:T(8,128)S(1)}, f32[648,128]{1,0:T(8,128)S(1)}, u32[]{:S(2)}, u32[]{:S(2)}) collective-permute-start(f32[648,128]{1,0:T(8,128)S(1)} %get-tuple-element.21), channel_id=1, source_target_pairs={{0,1},{1,0},{2,3},{3,2},{4,5},{5,4},{6,7},{7,6},{8,9},{9,8},{10,11... | collective-permute-start | bytes 995336 | tf_op jit(solution)/shard_map/ppermute | solution.py:613
  16.5 13.2 %collective-permute-start.3 = (f32[648,128]{1,0:T(8,128)S(1)}, f32[648,128]{1,0:T(8,128)S(1)}, u32[]{:S(2)}, u32[]{:S(2)}) collective-permute-start(f32[648,128]{1,0:T(8,128)S(1)} %get-tuple-element.22), channel_id=1, source_target_pairs={{0,0},{1,2},{2,1},{3,3},{4,4},{5,6},{6,5},{7,7},{8,8},{9,10},{10,9... | collective-permute-start | bytes 995336 | tf_op jit(solution)/shard_map/ppermute | solution.py:614
  17.2 9.5 %collective-permute-start.1 = (f32[2,144,128]{2,1,0:T(8,128)S(1)}, f32[2,144,128]{2,1,0:T(8,128)S(1)}, u32[]{:S(2)}, u32[]{:S(2)}) collective-permute-start(f32[2,144,128]{2,1,0:T(8,128)S(1)} %get-tuple-element.20), channel_id=1, source_target_pairs={{4,0},{8,4},{12,8},{16,12},{20,16},{24,20},{28,24},{0,28},{5,1},{9... | collective-permute-start | bytes 442376 | tf_op jit(solution)/shard_map/ppermute | solution.py:612
  19.1 8.2 %collective-permute-start = (f32[2,144,128]{2,1,0:T(8,128)S(1)}, f32[2,144,128]{2,1,0:T(8,128)S(1)}, u32[]{:S(2)}, u32[]{:S(2)}) collective-permute-start(f32[2,144,128]{2,1,0:T(8,128)S(1)} %get-tuple-element.20), channel_id=1, source_target_pairs={{0,4},{4,8},{8,12},{12,16},{16,20},{20,24},{24,28},{28,0},{1,5},{5... | collective-permute-start | bytes 442376 | tf_op jit(solution)/shard_map/ppermute | solution.py:611
  23.7 10.1 %collective-permute-start.6 = (f32[72,128]{1,0:T(8,128)S(1)}, f32[72,128]{1,0:T(8,128)S(1)}, u32[]{:S(2)}, u32[]{:S(2)}) collective-permute-start(f32[72,128]{1,0:T(8,128)S(1)} %get-tuple-element.28), channel_id=1, source_target_pairs={{0,1},{1,0},{2,3},{3,2},{4,5},{5,4},{6,7},{7,6},{8,9},{9,8},{10,11... | collective-permute-start | bytes 110600 | tf_op jit(solution)/shard_map/ppermute | solution.py:613
  26.6 7.2 %collective-permute-start.7 = (f32[72,128]{1,0:T(8,128)S(1)}, f32[72,128]{1,0:T(8,128)S(1)}, u32[]{:S(2)}, u32[]{:S(2)}) collective-permute-start(f32[72,128]{1,0:T(8,128)S(1)} %get-tuple-element.29), channel_id=1, source_target_pairs={{0,0},{1,2},{2,1},{3,3},{4,4},{5,6},{6,5},{7,7},{8,8},{9,10},{10,9... | collective-permute-start | bytes 110600 | tf_op jit(solution)/shard_map/ppermute | solution.py:614
  27.3 5.3 %collective-permute-start.5 = (f32[2,16,128]{2,1,0:T(8,128)S(1)}, f32[2,16,128]{2,1,0:T(8,128)S(1)}, u32[]{:S(2)}, u32[]{:S(2)}) collective-permute-start(f32[2,16,128]{2,1,0:T(8,128)S(1)} %get-tuple-element.27), channel_id=1, source_target_pairs={{4,0},{8,4},{12,8},{16,12},{20,16},{24,20},{28,24},{0,28},{5,1},{9... | collective-permute-start | bytes 49160 | tf_op jit(solution)/shard_map/ppermute | solution.py:612
  29.7 4.1 %collective-permute-start.4 = (f32[2,16,128]{2,1,0:T(8,128)S(1)}, f32[2,16,128]{2,1,0:T(8,128)S(1)}, u32[]{:S(2)}, u32[]{:S(2)}) collective-permute-start(f32[2,16,128]{2,1,0:T(8,128)S(1)} %get-tuple-element.27), channel_id=1, source_target_pairs={{0,4},{4,8},{8,12},{12,16},{16,20},{20,24},{24,28},{28,0},{1,5},{5... | collective-permute-start | bytes 49160 | tf_op jit(solution)/shard_map/ppermute | solution.py:611
  43.2 9.2 %collective-permute-start.10 = (f32[576,128]{1,0:T(8,128)S(1)}, f32[576,128]{1,0:T(8,128)S(1)}, u32[]{:S(2)}, u32[]{:S(2)}) collective-permute-start(f32[576,128]{1,0:T(8,128)S(1)} %get-tuple-element.33), channel_id=1, source_target_pairs={{0,1},{1,0},{2,3},{3,2},{4,5},{5,4},{6,7},{7,6},{8,9},{9,8},{10,11... | collective-permute-start | bytes 884744 | tf_op jit(solution)/shard_map/ppermute | solution.py:613
  44.9 7.4 %collective-permute-start.11 = (f32[576,128]{1,0:T(8,128)S(1)}, f32[576,128]{1,0:T(8,128)S(1)}, u32[]{:S(2)}, u32[]{:S(2)}) collective-permute-start(f32[576,128]{1,0:T(8,128)S(1)} %get-tuple-element.34), channel_id=1, source_target_pairs={{0,0},{1,2},{2,1},{3,3},{4,4},{5,6},{6,5},{7,7},{8,8},{9,10},{10,9... | collective-permute-start | bytes 884744 | tf_op jit(solution)/shard_map/ppermute | solution.py:614
  45.6 6.7 %collective-permute-start.9 = (f32[2,128,128]{2,1,0:T(8,128)S(1)}, f32[2,128,128]{2,1,0:T(8,128)S(1)}, u32[]{:S(2)}, u32[]{:S(2)}) collective-permute-start(f32[2,128,128]{2,1,0:T(8,128)S(1)} %get-tuple-element.32), channel_id=1, source_target_pairs={{4,0},{8,4},{12,8},{16,12},{20,16},{24,20},{28,24},{0,28},{5,1},{9... | collective-permute-start | bytes 393224 | tf_op jit(solution)/shard_map/ppermute | solution.py:612
  46.9 5.5 %collective-permute-start.8 = (f32[2,128,128]{2,1,0:T(8,128)S(1)}, f32[2,128,128]{2,1,0:T(8,128)S(1)}, u32[]{:S(2)}, u32[]{:S(2)}) collective-permute-start(f32[2,128,128]{2,1,0:T(8,128)S(1)} %get-tuple-element.32), channel_id=1, source_target_pairs={{0,4},{4,8},{8,12},{12,16},{16,20},{20,24},{24,28},{28,0},{1,5},{5... | collective-permute-start | bytes 393224 | tf_op jit(solution)/shard_map/ppermute | solution.py:611
  46.9 13.8 %all-to-all-start.1 = ((f32[32,1,128]{2,1,0:T(1,128)}), f32[32,1,128]{2,1,0:T(1,128)S(1)}, u32[]{:S(2)}, u32[]{:S(2)}) async-start(f32[32,1,128]{2,1,0:T(1,128)} %bitcast.13), calls=%async_computation.1 | async-start | bytes 32768 | tf_op jit(solution)/shard_map/all_to_all | solution.py:725

commit v10 on v9

--- a/solution.py
+++ b/solution.py
@@ -165,16 +165,20 @@
     plane = tracers * rows
     halves = rows // SUB
     lane, sub = lane_iota(), sub_iota()
-    copies = [
-        pltpu.make_async_copy(source, target, sems.at[i])
-        for i, (source, target) in enumerate(((east, e_buf), (north, n_buf), (mixing, m_buf)))
-    ]
-    for copy in copies:
-        copy.start()
+    blocks = levels // unroll
+
+    def load(b):
+        at = pl.ds(pl.multiple_of(b * unroll * rows, SUB), unroll * rows)
+        return [
+            pltpu.make_async_copy(source.at[at], target.at[at], sems.at[i, b])
+            for i, (source, target) in enumerate(((mixing, m_buf), (east, e_buf), (north, n_buf)))
+        ]
+
+    for b in range(blocks):
+        for copy in load(b):
+            copy.start()
     meet(rim, 0, west0, east0, plane)
     pair(edges, 0, a0, b0, levels * tracers)
-    for copy in copies:
-        copy.wait()
     place = lax.axis_index("lat")
     even = jnp.full((1, LANES), place, jnp.int32) % 2 == 0
     south_flag = (place > 0).astype(jnp.float32)
@@ -206,21 +210,20 @@
                 from_n = from_n * north_mask
             stay = (1.0 - e_out + w_in - n_out + s_in) * inv
             from_e, from_w = e_out * inv, -(w_in * inv)
-            from_rim = jnp.where(lane == 0, from_w, jnp.where(lane == LANES - 1, from_e, 0.0))
-            from_e = jnp.where(lane == LANES - 1, 0.0, from_e)
-            from_w = jnp.where(lane == 0, 0.0, from_w)
-            values = (stay, from_e, from_w, from_n, -(s_in * inv), from_rim, down * inv, factor)
+            values = (stay, from_e, from_w, from_n, -(s_in * inv), down * inv, factor)
             for i, value in enumerate(values):
                 weights[i, blk, :] = value
         return tuple(new)
 
     def body(b, carry):
+        for copy in load(b):
+            copy.wait()
         for u in range(unroll):
             carry = level(b * unroll + u, carry)
         return carry
 
     zero = jnp.zeros((SUB, LANES), jnp.float32)
-    lax.fori_loop(0, levels // unroll, body, ((zero, zero),) * halves)
+    lax.fori_loop(0, blocks, body, ((zero, zero),) * halves)
 
 
 def step(levels, tracers, rows, chunks, per_chunk, unroll, first, *refs):
@@ -317,10 +320,16 @@
 
     def weights_of(b):
         co_part = weights.at[:, pl.ds(pl.multiple_of(b * unroll * rows, SUB), unroll * rows)]
-        return lambda u: [
-            [co_part[i, pl.ds(u * rows + h * SUB, SUB), :] for i in range(weights.shape[0] - 1)]
-            for h in range(halves)
-        ]
+
+        def one(u, h):
+            c0, ce, cw, cn, cs, a = (
+                co_part[i, pl.ds(u * rows + h * SUB, SUB), :] for i in range(weights.shape[0] - 1)
+            )
+            first_col, last_col = lane == 0, lane == LANES - 1
+            rims = jnp.where(first_col, cw, jnp.where(last_col, ce, 0.0))
+            return c0, jnp.where(last_col, 0.0, ce), jnp.where(first_col, 0.0, cw), cn, cs, rims, a
+
+        return lambda u: [one(u, h) for h in range(halves)]
 
     def forward_block(b, solved):
         load(b).wait()
@@ -691,13 +700,13 @@
     forcing_rims = exchange(*rims)
 
     rim_shape, edge_shape = (chunks, plane, LANES), (2, levels * tracers, LANES)
-    weight_shape = (8, levels * rows, LANES)
+    weight_shape = (7, levels * rows, LANES)
     weights, rim0, edges0 = call(
         functools.partial(coefficients, levels, tracers, rows, per_chunk, unroll),
         [HBM] * 3 + [VMEM] * 4,
         (f32(*weight_shape), f32(*rim_shape), f32(*edge_shape)),
         (VMEM,) * 3,
-        (vmem(levels * rows, LANES),) * 3 + (dma((3,)),),
+        (vmem(levels * rows, LANES),) * 3 + (dma((3, levels // unroll)),),
         4, field_bytes, field_bytes, "coefficients",
     )(east, north, mix, *start_rims)
 

time: 61.7 us -> 61.3 us (level)
  no operation moved by 1% of the time
where the time goes in v10:
time: 61.3 us; the launch traced here: 61 us
  Pallas kernels  31.1 us (51%)
  starting transfers between devices  26.5 us (43%)
  waiting for transfers between devices  2.67 us (4%)
  between operations  0.8 us (1%)
    pallas_call x2, Pallas kernels, advance(): call(functools.partial(step, levels, tracers, rows, chunks, per_chunk, to...  17.7 us
    all_to_all x1, starting transfers between devices, per_device(): lax.all_to_all(packed.reshape(-1, 1, LANES), ('lon', 'lat'), split_axis=0...  7.3 us
    ppermute x3, starting transfers between devices, exchange(): lax.ppermute(a_rim, 'lat', [(j, partner(j, 0)) for j in range(lats)])  6.53 us
    all_to_all x1, starting transfers between devices, per_device(): lax.all_to_all(back.reshape(bricks, 1, LANES), ('lon', 'lat'), split_axis...  5.43 us
    ppermute x3, starting transfers between devices, exchange(): lax.ppermute(side_rim, 'lon', [((i + 1) % lons, i) for i in range(lons)])  5.22 us
    pallas_call x1, Pallas kernels, per_device(): call(functools.partial(first_rims, levels, tracers, rows, chunks, per_chu...  4.53 us
    pallas_call x1, Pallas kernels, per_device(): call(functools.partial(soundings, levels, rows, group_rows, cap, chunks,...  2.79 us
    pallas_call x1, Pallas kernels, per_device(): call(functools.partial(coefficients, levels, tracers, rows, per_chunk, un...  2.52 us
  transfers between devices with their start and end apart: 14, of which 2 were waited for; matrix products, arithmetic and copies ran while one was open for 0% of the time, Pallas kernels for 31%

profile of v10, /device:TPU:0, one launch (start us, length us, event | category | flops | bytes accessed | tf_op | source)
XLA Modules:
  0.0 61.0 jit_solution(14020216007002194631)
XLA Ops:
  0.6 2.2 %pack.1 = f32[608,128]{1,0:T(8,128)} custom-call(f32[576,128]{1,0:T(8,128)} %bitcast.29, s32[8,128]{1,0:T(8,128)} %bitcast.30, f32[8,128]{1,0:T(8,128)} %bitcast.31, f32[8,128]{1,0:T(8,128)} %bitcast.32), custom_call_target="tpu_custom_call" | custom-call | flops 10 | bytes 800000 | tf_op jit(solution)/shard_map/pack/pallas_call | solution.py:647
  2.8 7.3 %all-to-all-start = ((f32[608,1,128]{2,1,0:T(1,128)}), f32[608,1,128]{2,1,0:T(1,128)S(1)}, u32[]{:S(2)}, u32[]{:S(2)}) async-start(f32[608,1,128]{2,1,0:T(1,128)} %bitcast.10), calls=%async_computation | async-start | bytes 622592 | tf_op jit(solution)/shard_map/all_to_all | solution.py:658
  10.1 0.0 copy-start
  10.1 4.5 %first_rims.1 = (f32[2,144,128]{2,1,0:T(8,128)S(1)}, f32[648,128]{1,0:T(8,128)S(1)}, f32[648,128]{1,0:T(8,128)S(1)}) custom-call(f32[9216,128]{1,0:T(8,128)} %bitcast.21, f32[1152,128]{1,0:T(8,128)} %bitcast.24, f32[1152,128]{1,0:T(8,128)} %bitcast.26), custom_call_target="tpu_custom_call" | custom-call | flops 4718592 | bytes 9437184 | tf_op jit(solution)/shard_map/first_rims/pallas_call | solution.py:664
  14.6 1.8 %collective-permute-start.2 = (f32[648,128]{1,0:T(8,128)S(1)}, f32[648,128]{1,0:T(8,128)S(1)}, u32[]{:S(2)}, u32[]{:S(2)}) collective-permute-start(f32[648,128]{1,0:T(8,128)S(1)} %get-tuple-element.21), channel_id=1, source_target_pairs={{0,1},{1,0},{2,3},{3,2},{4,5},{5,4},{6,7},{7,6},{8,9},{9,8},{10,11... | collective-permute-start | bytes 995336 | tf_op jit(solution)/shard_map/ppermute | solution.py:622
  16.5 0.7 %collective-permute-start.3 = (f32[648,128]{1,0:T(8,128)S(1)}, f32[648,128]{1,0:T(8,128)S(1)}, u32[]{:S(2)}, u32[]{:S(2)}) collective-permute-start(f32[648,128]{1,0:T(8,128)S(1)} %get-tuple-element.22), channel_id=1, source_target_pairs={{0,0},{1,2},{2,1},{3,3},{4,4},{5,6},{6,5},{7,7},{8,8},{9,10},{10,9... | collective-permute-start | bytes 995336 | tf_op jit(solution)/shard_map/ppermute | solution.py:623
  17.2 1.9 %collective-permute-start.1 = (f32[2,144,128]{2,1,0:T(8,128)S(1)}, f32[2,144,128]{2,1,0:T(8,128)S(1)}, u32[]{:S(2)}, u32[]{:S(2)}) collective-permute-start(f32[2,144,128]{2,1,0:T(8,128)S(1)} %get-tuple-element.20), channel_id=1, source_target_pairs={{4,0},{8,4},{12,8},{16,12},{20,16},{24,20},{28,24},{0,28},{5,1},{9... | collective-permute-start | bytes 442376 | tf_op jit(solution)/shard_map/ppermute | solution.py:621
  19.1 0.0 collective-permute-start
  19.1 0.0 copy-done
  19.1 0.7 %tracer_sum.1.sums = bf16[2,576,256]{2,1,0:T(8,128)(2,1)S(1)} custom-call(f32[72,8,16,128]{3,2,1,0:T(8,128)S(1)} %copy-done), custom_call_target="tpu_custom_call" | custom-call | flops 1179648 | bytes 4718592 | tf_op jit(solution)/shard_map/tracer_sum/pallas_call | solution.py:676
  19.8 1.1 %all-to-all-done = f32[608,1,128]{2,1,0:T(1,128)S(1)} async-done(((f32[608,1,128]{2,1,0:T(1,128)}), f32[608,1,128]{2,1,0:T(1,128)S(1)}, u32[]{:S(2)}, u32[]{:S(2)}) %all-to-all-start) | async-done | bytes 311328 | tf_op jit(solution)/shard_map/all_to_all | solution.py:658
  20.9 2.8 %soundings.1 = (f32[1168,128]{1,0:T(8,128)S(1)}, f32[2,16,128]{2,1,0:T(8,128)S(1)}, f32[72,128]{1,0:T(8,128)S(1)}, f32[72,128]{1,0:T(8,128)S(1)}, f32[32,128]{1,0:T(8,128)}) custom-call(f32[608,128]{1,0:T(8,128)S(1)} %bitcast.19, bf16[2,576,256]{2,1,0:T(8,128)(2,1)S(1)} %tracer_sum.1.sums), custom_call_target="tpu_custom_call" | custom-call | flops 37748736 | bytes 4718592 | tf_op jit(solution)/shard_map/soundings/pallas_call | solution.py:685
  23.7 2.9 %collective-permute-start.6 = (f32[72,128]{1,0:T(8,128)S(1)}, f32[72,128]{1,0:T(8,128)S(1)}, u32[]{:S(2)}, u32[]{:S(2)}) collective-permute-start(f32[72,128]{1,0:T(8,128)S(1)} %get-tuple-element.28), channel_id=1, source_target_pairs={{0,1},{1,0},{2,3},{3,2},{4,5},{5,4},{6,7},{7,6},{8,9},{9,8},{10,11... | collective-permute-start | bytes 110600 | tf_op jit(solution)/shard_map/ppermute | solution.py:622
  26.6 0.0 collective-permute-done.1.east0
  26.6 0.7 %collective-permute-start.7 = (f32[72,128]{1,0:T(8,128)S(1)}, f32[72,128]{1,0:T(8,128)S(1)}, u32[]{:S(2)}, u32[]{:S(2)}) collective-permute-start(f32[72,128]{1,0:T(8,128)S(1)} %get-tuple-element.29), channel_id=1, source_target_pairs={{0,0},{1,2},{2,1},{3,3},{4,4},{5,6},{6,5},{7,7},{8,8},{9,10},{10,9... | collective-permute-start | bytes 110600 | tf_op jit(solution)/shard_map/ppermute | solution.py:623
  27.3 0.0 collective-permute-done.west0
  27.3 2.4 %collective-permute-start.5 = (f32[2,16,128]{2,1,0:T(8,128)S(1)}, f32[2,16,128]{2,1,0:T(8,128)S(1)}, u32[]{:S(2)}, u32[]{:S(2)}) collective-permute-start(f32[2,16,128]{2,1,0:T(8,128)S(1)} %get-tuple-element.27), channel_id=1, source_target_pairs={{4,0},{8,4},{12,8},{16,12},{20,16},{24,20},{28,24},{0,28},{5,1},{9... | collective-permute-start | bytes 49160 | tf_op jit(solution)/shard_map/ppermute | solution.py:621
  29.7 0.0 collective-permute-done.2.a0
  29.7 0.0 collective-permute-start.4
  29.7 0.0 collective-permute-done.3.b0
  29.7 2.5 %coefficients.1 = (f32[7,1152,128]{2,1,0:T(8,128)S(1)}, f32[2,128,128]{2,1,0:T(8,128)S(1)}, f32[2,576,128]{2,1,0:T(8,128)S(1)}) custom-call(f32[1152,128]{1,0:T(8,128)} %bitcast.25, f32[1152,128]{1,0:T(8,128)} %bitcast.27, f32[1152,128]{1,0:T(8,128)} %bitcast.28, f32[2,144,128]{2,1,0:T(8,128)S(1)} %collective-permute-done.west0, ...), custom_call_target="tpu_custom_call" | custom-call | flops 4718592 | bytes 4718592 | tf_op jit(solution)/shard_map/coefficients/pallas_call | solution.py:704
  32.2 0.0 collective-permute-done.5.refs_6_
  32.3 1.5 %collective-permute-done.4.refs_5_ = f32[2,16,128]{2,1,0:T(8,128)S(1)} collective-permute-done((f32[2,16,128]{2,1,0:T(8,128)S(1)}, f32[2,16,128]{2,1,0:T(8,128)S(1)}, u32[]{:S(2)}, u32[]{:S(2)}) %collective-permute-start.4) | collective-permute-done | bytes 16416 | tf_op jit(solution)/shard_map/ppermute | solution.py:620
  33.8 0.0 collective-permute-done.6.refs_7_
  33.8 0.0 collective-permute-done.7.refs_8_
  33.8 9.4 %step.2 = (f32[576,16,128]{2,1,0:T(8,128)}, f32[7,1152,128]{2,1,0:T(8,128)}, f32[2,128,128]{2,1,0:T(8,128)S(1)}, f32[576,128]{1,0:T(8,128)S(1)}, f32[576,128]{1,0:T(8,128)S(1)}) custom-call(f32[576,16,128]{2,1,0:T(8,128)} %bitcast.22, f32[7,1152,128]{2,1,0:T(8,128)S(1)} %get-tuple-element.23.refs_1_, f32[2,128,128]{2,1,0:T(8,128)S(1)} %get-tuple-element.24.refs_2_, ...), custom_call_target="tpu_custom_call" | custom-call | flops 37748736 | bytes 9437184 | tf_op jit(solution)/shard_map/step/pallas_call | solution.py:714
  43.2 1.8 %collective-permute-start.10 = (f32[576,128]{1,0:T(8,128)S(1)}, f32[576,128]{1,0:T(8,128)S(1)}, u32[]{:S(2)}, u32[]{:S(2)}) collective-permute-start(f32[576,128]{1,0:T(8,128)S(1)} %get-tuple-element.33), channel_id=1, source_target_pairs={{0,1},{1,0},{2,3},{3,2},{4,5},{5,4},{6,7},{7,6},{8,9},{9,8},{10,11... | collective-permute-start | bytes 884744 | tf_op jit(solution)/shard_map/ppermute | solution.py:622
  44.9 0.7 %collective-permute-start.11 = (f32[576,128]{1,0:T(8,128)S(1)}, f32[576,128]{1,0:T(8,128)S(1)}, u32[]{:S(2)}, u32[]{:S(2)}) collective-permute-start(f32[576,128]{1,0:T(8,128)S(1)} %get-tuple-element.34), channel_id=1, source_target_pairs={{0,0},{1,2},{2,1},{3,3},{4,4},{5,6},{6,5},{7,7},{8,8},{9,10},{10,9... | collective-permute-start | bytes 884744 | tf_op jit(solution)/shard_map/ppermute | solution.py:623
  45.6 0.9 %collective-permute-start.9 = (f32[2,128,128]{2,1,0:T(8,128)S(1)}, f32[2,128,128]{2,1,0:T(8,128)S(1)}, u32[]{:S(2)}, u32[]{:S(2)}) collective-permute-start(f32[2,128,128]{2,1,0:T(8,128)S(1)} %get-tuple-element.32), channel_id=1, source_target_pairs={{4,0},{8,4},{12,8},{16,12},{20,16},{24,20},{28,24},{0,28},{5,1},{9... | collective-permute-start | bytes 393224 | tf_op jit(solution)/shard_map/ppermute | solution.py:621
  46.5 0.0 collective-permute-start.8
  46.5 5.4 %all-to-all-start.1 = ((f32[32,1,128]{2,1,0:T(1,128)}), f32[32,1,128]{2,1,0:T(1,128)S(1)}, u32[]{:S(2)}, u32[]{:S(2)}) async-start(f32[32,1,128]{2,1,0:T(1,128)} %bitcast.13), calls=%async_computation.1 | async-start | bytes 32768 | tf_op jit(solution)/shard_map/all_to_all | solution.py:734
  52.0 0.0 collective-permute-done.9.refs_3_
  52.0 0.0 collective-permute-done.8.refs_2_
  52.0 0.0 collective-permute-done.10.refs_4_
  52.0 0.0 collective-permute-done.11.refs_5_
  52.0 8.3 %step.3 = f32[576,16,128]{2,1,0:T(8,128)} custom-call(f32[576,16,128]{2,1,0:T(8,128)} %get-tuple-element.30.refs_0_, f32[7,1152,128]{2,1,0:T(8,128)} %get-tuple-element.31.refs_1_, f32[2,128,128]{2,1,0:T(8,128)S(1)} %collective-permute-done.8.refs_2_, f32[2,128,128]{2,1,0:T(8,128)S(1)} %collective-permute-done.9.refs_3_, ...), custom_call_target="tpu_custom_call" | custom-call | flops 37748736 | bytes 9437184 | tf_op jit(solution)/shard_map/step/pallas_call | solution.py:714
  60.3 0.0 all-to-all-done.1
  60.3 0.7 %residual.1 = f32[8,128]{1,0:T(8,128)} custom-call(f32[32,128]{1,0:T(8,128)S(1)} %bitcast.20), custom_call_target="tpu_custom_call" | custom-call | flops 10 | bytes 10000 | tf_op jit(solution)/shard_map/residual/pallas_call | solution.py:738
Async XLA Ops:
  2.8 18.1 %all-to-all-start = ((f32[608,1,128]{2,1,0:T(1,128)}), f32[608,1,128]{2,1,0:T(1,128)S(1)}, u32[]{:S(2)}, u32[]{:S(2)}) async-start(f32[608,1,128]{2,1,0:T(1,128)} %bitcast.10), calls=%async_computation | async-start | bytes 622592 | tf_op jit(solution)/shard_map/all_to_all | solution.py:658
  10.1 9.0 %copy-start = (f32[72,8,16,128]{3,2,1,0:T(8,128)S(1)}, f32[72,8,16,128]{3,2,1,0:T(8,128)}, u32[]{:S(2)}) copy-start(f32[72,8,16,128]{3,2,1,0:T(8,128)} %concentration.1) | copy-start | bytes 14155780
  14.6 15.1 %collective-permute-start.2 = (f32[648,128]{1,0:T(8,128)S(1)}, f32[648,128]{1,0:T(8,128)S(1)}, u32[]{:S(2)}, u32[]{:S(2)}) collective-permute-start(f32[648,128]{1,0:T(8,128)S(1)} %get-tuple-element.21), channel_id=1, source_target_pairs={{0,1},{1,0},{2,3},{3,2},{4,5},{5,4},{6,7},{7,6},{8,9},{9,8},{10,11... | collective-permute-start | bytes 995336 | tf_op jit(solution)/shard_map/ppermute | solution.py:622
  16.5 13.2 %collective-permute-start.3 = (f32[648,128]{1,0:T(8,128)S(1)}, f32[648,128]{1,0:T(8,128)S(1)}, u32[]{:S(2)}, u32[]{:S(2)}) collective-permute-start(f32[648,128]{1,0:T(8,128)S(1)} %get-tuple-element.22), channel_id=1, source_target_pairs={{0,0},{1,2},{2,1},{3,3},{4,4},{5,6},{6,5},{7,7},{8,8},{9,10},{10,9... | collective-permute-start | bytes 995336 | tf_op jit(solution)/shard_map/ppermute | solution.py:623
  17.2 9.5 %collective-permute-start.1 = (f32[2,144,128]{2,1,0:T(8,128)S(1)}, f32[2,144,128]{2,1,0:T(8,128)S(1)}, u32[]{:S(2)}, u32[]{:S(2)}) collective-permute-start(f32[2,144,128]{2,1,0:T(8,128)S(1)} %get-tuple-element.20), channel_id=1, source_target_pairs={{4,0},{8,4},{12,8},{16,12},{20,16},{24,20},{28,24},{0,28},{5,1},{9... | collective-permute-start | bytes 442376 | tf_op jit(solution)/shard_map/ppermute | solution.py:621
  19.1 8.2 %collective-permute-start = (f32[2,144,128]{2,1,0:T(8,128)S(1)}, f32[2,144,128]{2,1,0:T(8,128)S(1)}, u32[]{:S(2)}, u32[]{:S(2)}) collective-permute-start(f32[2,144,128]{2,1,0:T(8,128)S(1)} %get-tuple-element.20), channel_id=1, source_target_pairs={{0,4},{4,8},{8,12},{12,16},{16,20},{20,24},{24,28},{28,0},{1,5},{5... | collective-permute-start | bytes 442376 | tf_op jit(solution)/shard_map/ppermute | solution.py:620
  23.7 10.1 %collective-permute-start.6 = (f32[72,128]{1,0:T(8,128)S(1)}, f32[72,128]{1,0:T(8,128)S(1)}, u32[]{:S(2)}, u32[]{:S(2)}) collective-permute-start(f32[72,128]{1,0:T(8,128)S(1)} %get-tuple-element.28), channel_id=1, source_target_pairs={{0,1},{1,0},{2,3},{3,2},{4,5},{5,4},{6,7},{7,6},{8,9},{9,8},{10,11... | collective-permute-start | bytes 110600 | tf_op jit(solution)/shard_map/ppermute | solution.py:622
  26.6 7.2 %collective-permute-start.7 = (f32[72,128]{1,0:T(8,128)S(1)}, f32[72,128]{1,0:T(8,128)S(1)}, u32[]{:S(2)}, u32[]{:S(2)}) collective-permute-start(f32[72,128]{1,0:T(8,128)S(1)} %get-tuple-element.29), channel_id=1, source_target_pairs={{0,0},{1,2},{2,1},{3,3},{4,4},{5,6},{6,5},{7,7},{8,8},{9,10},{10,9... | collective-permute-start | bytes 110600 | tf_op jit(solution)/shard_map/ppermute | solution.py:623
  27.3 5.0 %collective-permute-start.5 = (f32[2,16,128]{2,1,0:T(8,128)S(1)}, f32[2,16,128]{2,1,0:T(8,128)S(1)}, u32[]{:S(2)}, u32[]{:S(2)}) collective-permute-start(f32[2,16,128]{2,1,0:T(8,128)S(1)} %get-tuple-element.27), channel_id=1, source_target_pairs={{4,0},{8,4},{12,8},{16,12},{20,16},{24,20},{28,24},{0,28},{5,1},{9... | collective-permute-start | bytes 49160 | tf_op jit(solution)/shard_map/ppermute | solution.py:621
  29.7 4.1 %collective-permute-start.4 = (f32[2,16,128]{2,1,0:T(8,128)S(1)}, f32[2,16,128]{2,1,0:T(8,128)S(1)}, u32[]{:S(2)}, u32[]{:S(2)}) collective-permute-start(f32[2,16,128]{2,1,0:T(8,128)S(1)} %get-tuple-element.27), channel_id=1, source_target_pairs={{0,4},{4,8},{8,12},{12,16},{16,20},{20,24},{24,28},{28,0},{1,5},{5... | collective-permute-start | bytes 49160 | tf_op jit(solution)/shard_map/ppermute | solution.py:620
  43.2 8.8 %collective-permute-start.10 = (f32[576,128]{1,0:T(8,128)S(1)}, f32[576,128]{1,0:T(8,128)S(1)}, u32[]{:S(2)}, u32[]{:S(2)}) collective-permute-start(f32[576,128]{1,0:T(8,128)S(1)} %get-tuple-element.33), channel_id=1, source_target_pairs={{0,1},{1,0},{2,3},{3,2},{4,5},{5,4},{6,7},{7,6},{8,9},{9,8},{10,11... | collective-permute-start | bytes 884744 | tf_op jit(solution)/shard_map/ppermute | solution.py:622
  44.9 7.1 %collective-permute-start.11 = (f32[576,128]{1,0:T(8,128)S(1)}, f32[576,128]{1,0:T(8,128)S(1)}, u32[]{:S(2)}, u32[]{:S(2)}) collective-permute-start(f32[576,128]{1,0:T(8,128)S(1)} %get-tuple-element.34), channel_id=1, source_target_pairs={{0,0},{1,2},{2,1},{3,3},{4,4},{5,6},{6,5},{7,7},{8,8},{9,10},{10,9... | collective-permute-start | bytes 884744 | tf_op jit(solution)/shard_map/ppermute | solution.py:623
  45.6 6.4 %collective-permute-start.9 = (f32[2,128,128]{2,1,0:T(8,128)S(1)}, f32[2,128,128]{2,1,0:T(8,128)S(1)}, u32[]{:S(2)}, u32[]{:S(2)}) collective-permute-start(f32[2,128,128]{2,1,0:T(8,128)S(1)} %get-tuple-element.32), channel_id=1, source_target_pairs={{4,0},{8,4},{12,8},{16,12},{20,16},{24,20},{28,24},{0,28},{5,1},{9... | collective-permute-start | bytes 393224 | tf_op jit(solution)/shard_map/ppermute | solution.py:621
  46.5 5.5 %collective-permute-start.8 = (f32[2,128,128]{2,1,0:T(8,128)S(1)}, f32[2,128,128]{2,1,0:T(8,128)S(1)}, u32[]{:S(2)}, u32[]{:S(2)}) collective-permute-start(f32[2,128,128]{2,1,0:T(8,128)S(1)} %get-tuple-element.32), channel_id=1, source_target_pairs={{0,4},{4,8},{8,12},{12,16},{16,20},{20,24},{24,28},{28,0},{1,5},{5... | collective-permute-start | bytes 393224 | tf_op jit(solution)/shard_map/ppermute | solution.py:620
  46.5 13.8 %all-to-all-start.1 = ((f32[32,1,128]{2,1,0:T(1,128)}), f32[32,1,128]{2,1,0:T(1,128)S(1)}, u32[]{:S(2)}, u32[]{:S(2)}) async-start(f32[32,1,128]{2,1,0:T(1,128)} %bitcast.13), calls=%async_computation.1 | async-start | bytes 32768 | tf_op jit(solution)/shard_map/all_to_all | solution.py:734

commit v11 on v10

--- a/solution.py
+++ b/solution.py
@@ -64,7 +64,7 @@
 
 def put_rims(field, offset, levels, per_chunk, chunk, out, first, plane, begin=0, end=None):
     lane = lane_iota()
-    group = largest(plane // SUB, 4, 2, 1)
+    group = largest(plane // SUB, 16, 8, 4, 2, 1)
     count = min(per_chunk, levels - chunk * per_chunk)
 
     def body(i, carry):
@@ -91,9 +91,9 @@
     return (1 - odd) * (rows - 1), odd * (rows - 1)
 
 
-def put_rows(field, offset, a_ref, b_ref, rows, begin, end):
+def put_rows(field, offset, a_ref, b_ref, rows, begin, end, places=None):
     unroll = largest((end - begin) // SUB, 9, 8, 4, 2, 1)
-    in_a, in_b = row_places(rows)
+    in_a, in_b = places or row_places(rows)
 
     def body(i, carry):
         for u in range(unroll):
@@ -228,7 +228,7 @@
 
 def step(levels, tracers, rows, chunks, per_chunk, unroll, first, *refs):
     if first:
-        field, weights, rim, edges, forcing, f_west, f_east, f_a, f_b = refs[:9]
+        field, weights, rim, edges, forcing, f_west, f_east, f_north, f_south = refs[:9]
         out, weights_out, side_ref, a_ref, b_ref = refs[9:14]
         buf, rim_now, f_rim, f_edges, sems = refs[14:]
     else:
@@ -268,7 +268,8 @@
             load(b).start()
         keep.start()
         meet(f_rim, 0, f_west, f_east, rows)
-        pair(f_edges, 0, f_a, f_b, levels)
+        f_edges[0] = f_north[...]
+        f_edges[1] = f_south[...]
     else:
         above_copy = pltpu.make_async_copy(weights_in.at[weights.shape[0] - 1], above, sems.at[last])
         def load_weights(b):
@@ -592,7 +593,7 @@
 
     for chunk in range(chunks):
         put_rims(forcing, SUB, levels, per_chunk, chunk, side_ref, 0, rows)
-    put_rows(forcing, SUB, a_ref, b_ref, rows, 0, levels)
+    put_rows(forcing, SUB, a_ref, b_ref, rows, 0, levels, (0, rows - 1))
     leave.wait()
 
 
@@ -609,18 +610,32 @@
         out[pl.ds(row, 1), :] = made
 
 
+def turn(value, axis, by):
+    count = lax.axis_size(axis)
+    return lax.ppermute(value, axis, [(i, (i + by) % count) for i in range(count)])
+
+
 def exchange(side_rim, a_rim, b_rim):
-    lons, lats = lax.axis_size("lon"), lax.axis_size("lat")
+    lats = lax.axis_size("lat")
 
     def partner(j, odd):
         other = j + 1 if j % 2 == odd else j - 1
         return other if 0 <= other < lats else j
 
     return (
-        lax.ppermute(side_rim, "lon", [(i, (i + 1) % lons) for i in range(lons)]),
-        lax.ppermute(side_rim, "lon", [((i + 1) % lons, i) for i in range(lons)]),
+        turn(side_rim, "lon", 1),
+        turn(side_rim, "lon", -1),
         lax.ppermute(a_rim, "lat", [(j, partner(j, 0)) for j in range(lats)]),
         lax.ppermute(b_rim, "lat", [(j, partner(j, 1)) for j in range(lats)]),
+    )
+
+
+def exchange_small(side_rim, first_rows, last_rows):
+    return (
+        turn(side_rim, "lon", 1),
+        turn(side_rim, "lon", -1),
+        turn(first_rows, "lat", -1),
+        turn(last_rows, "lat", 1),
     )
 
 
@@ -697,7 +712,7 @@
         ),
         10, field_bytes * 8, field_bytes, "soundings",
     )(received, sums)
-    forcing_rims = exchange(*rims)
+    forcing_rims = exchange_small(*rims)
 
     rim_shape, edge_shape = (chunks, plane, LANES), (2, levels * tracers, LANES)
     weight_shape = (7, levels * rows, LANES)

time: 61.3 us -> 59.9 us (0.977)
  starting transfers between devices: 26.5 us -> 24.9 us
  Pallas kernels: 31.1 us -> 30 us
  waiting for transfers between devices: 2.67 us -> 3.49 us
    ppermute x3 -> x2, starting transfers between devices: 6.53 us -> 3.42 us  [exchange(): lax.ppermute(a_rim, 'lat', [(j, partner(j, 0)) for j in range(lats)])]
    ppermute x6 -> x8, starting transfers between devices: 5.23 us -> 7.5 us  [turn(): lax.ppermute(value, axis, [(i, (i + by) % count) for i in range(count)])]
    all_to_all x1, waiting for transfers between devices: 1.12 us -> 1.94 us  [per_device(): lax.all_to_all(packed.reshape(-1, 1, LANES), ('lon', 'lat'), split_axis=0...]
    pallas_call x1, Pallas kernels: 4.53 us -> 3.81 us  [per_device(): call(functools.partial(first_rims, levels, tracers, rows, chunks, per_chu...]
    ppermute x3 -> x2, starting transfers between devices: 1.99 us -> 1.34 us  [exchange(): lax.ppermute(b_rim, 'lat', [(j, partner(j, 1)) for j in range(lats)])]
    ppermute x6 -> x8, waiting for transfers between devices: 1.53 us -> 1.54 us  [turn(): lax.ppermute(value, axis, [(i, (i + by) % count) for i in range(count)])]
where the time goes in v11:
time: 59.9 us; the launch traced here: 59.2 us
  Pallas kernels  30 us (50%)
  starting transfers between devices  24.9 us (42%)
  waiting for transfers between devices  3.49 us (6%)
  between operations  0.79 us (1%)
    pallas_call x2, Pallas kernels, advance(): call(functools.partial(step, levels, tracers, rows, chunks, per_chunk, to...  17.4 us
    ppermute x8, starting transfers between devices, turn(): lax.ppermute(value, axis, [(i, (i + by) % count) for i in range(count)])  7.5 us
    all_to_all x1, starting transfers between devices, per_device(): lax.all_to_all(packed.reshape(-1, 1, LANES), ('lon', 'lat'), split_axis=0...  7.3 us
    all_to_all x1, starting transfers between devices, per_device(): lax.all_to_all(back.reshape(bricks, 1, LANES), ('lon', 'lat'), split_axis...  5.36 us
    pallas_call x1, Pallas kernels, per_device(): call(functools.partial(first_rims, levels, tracers, rows, chunks, per_chu...  3.81 us
    ppermute x2, starting transfers between devices, exchange(): lax.ppermute(a_rim, 'lat', [(j, partner(j, 0)) for j in range(lats)])  3.42 us
    pallas_call x1, Pallas kernels, per_device(): call(functools.partial(soundings, levels, rows, group_rows, cap, chunks,...  2.74 us
    pallas_call x1, Pallas kernels, per_device(): call(functools.partial(coefficients, levels, tracers, rows, per_chunk, un...  2.52 us
  transfers between devices with their start and end apart: 14, of which 2 were waited for; matrix products, arithmetic and copies ran while one was open for 0% of the time, Pallas kernels for 31%

profile of v11, /device:TPU:0, one launch (start us, length us, event | category | flops | bytes accessed | tf_op | source)
XLA Modules:
  0.0 59.2 jit_solution(14661003778990311269)
XLA Ops:
  0.6 2.2 %pack.1 = f32[608,128]{1,0:T(8,128)} custom-call(f32[576,128]{1,0:T(8,128)} %bitcast.29, s32[8,128]{1,0:T(8,128)} %bitcast.30, f32[8,128]{1,0:T(8,128)} %bitcast.31, f32[8,128]{1,0:T(8,128)} %bitcast.32), custom_call_target="tpu_custom_call" | custom-call | flops 10 | bytes 800000 | tf_op jit(solution)/shard_map/pack/pallas_call | solution.py:662
  2.8 7.3 %all-to-all-start = ((f32[608,1,128]{2,1,0:T(1,128)}), f32[608,1,128]{2,1,0:T(1,128)S(1)}, u32[]{:S(2)}, u32[]{:S(2)}) async-start(f32[608,1,128]{2,1,0:T(1,128)} %bitcast.10), calls=%async_computation | async-start | bytes 622592 | tf_op jit(solution)/shard_map/all_to_all | solution.py:673
  10.1 0.0 copy-start
  10.1 3.8 %first_rims.1 = (f32[2,144,128]{2,1,0:T(8,128)S(1)}, f32[648,128]{1,0:T(8,128)S(1)}, f32[648,128]{1,0:T(8,128)S(1)}) custom-call(f32[9216,128]{1,0:T(8,128)} %bitcast.21, f32[1152,128]{1,0:T(8,128)} %bitcast.24, f32[1152,128]{1,0:T(8,128)} %bitcast.26), custom_call_target="tpu_custom_call" | custom-call | flops 4718592 | bytes 9437184 | tf_op jit(solution)/shard_map/first_rims/pallas_call | solution.py:679
  13.9 1.8 %collective-permute-start.2 = (f32[648,128]{1,0:T(8,128)S(1)}, f32[648,128]{1,0:T(8,128)S(1)}, u32[]{:S(2)}, u32[]{:S(2)}) collective-permute-start(f32[648,128]{1,0:T(8,128)S(1)} %get-tuple-element.21), channel_id=1, source_target_pairs={{0,1},{1,0},{2,3},{3,2},{4,5},{5,4},{6,7},{7,6},{8,9},{9,8},{10,11... | collective-permute-start | bytes 995336 | tf_op jit(solution)/shard_map/ppermute | solution.py:628
  15.8 0.7 %collective-permute-start.3 = (f32[648,128]{1,0:T(8,128)S(1)}, f32[648,128]{1,0:T(8,128)S(1)}, u32[]{:S(2)}, u32[]{:S(2)}) collective-permute-start(f32[648,128]{1,0:T(8,128)S(1)} %get-tuple-element.22), channel_id=1, source_target_pairs={{0,0},{1,2},{2,1},{3,3},{4,4},{5,6},{6,5},{7,7},{8,8},{9,10},{10,9... | collective-permute-start | bytes 995336 | tf_op jit(solution)/shard_map/ppermute | solution.py:629
  16.4 1.9 %collective-permute-start.1 = (f32[2,144,128]{2,1,0:T(8,128)S(1)}, f32[2,144,128]{2,1,0:T(8,128)S(1)}, u32[]{:S(2)}, u32[]{:S(2)}) collective-permute-start(f32[2,144,128]{2,1,0:T(8,128)S(1)} %get-tuple-element.20), channel_id=1, source_target_pairs={{0,28},{4,0},{8,4},{12,8},{16,12},{20,16},{24,20},{28,24},{1,29},{... | collective-permute-start | bytes 442376 | tf_op jit(solution)/shard_map/ppermute | solution.py:615
  18.3 0.0 collective-permute-start
  18.3 0.0 copy-done
  18.3 0.7 %tracer_sum.1.sums = bf16[2,576,256]{2,1,0:T(8,128)(2,1)S(1)} custom-call(f32[72,8,16,128]{3,2,1,0:T(8,128)S(1)} %copy-done), custom_call_target="tpu_custom_call" | custom-call | flops 1179648 | bytes 4718592 | tf_op jit(solution)/shard_map/tracer_sum/pallas_call | solution.py:691
  19.1 1.9 %all-to-all-done = f32[608,1,128]{2,1,0:T(1,128)S(1)} async-done(((f32[608,1,128]{2,1,0:T(1,128)}), f32[608,1,128]{2,1,0:T(1,128)S(1)}, u32[]{:S(2)}, u32[]{:S(2)}) %all-to-all-start) | async-done | bytes 311328 | tf_op jit(solution)/shard_map/all_to_all | solution.py:673
  21.0 2.7 %soundings.1 = (f32[1168,128]{1,0:T(8,128)S(1)}, f32[2,16,128]{2,1,0:T(8,128)S(1)}, f32[72,128]{1,0:T(8,128)S(1)}, f32[72,128]{1,0:T(8,128)S(1)}, f32[32,128]{1,0:T(8,128)}) custom-call(f32[608,128]{1,0:T(8,128)S(1)} %bitcast.19, bf16[2,576,256]{2,1,0:T(8,128)(2,1)S(1)} %tracer_sum.1.sums), custom_call_target="tpu_custom_call" | custom-call | flops 37748736 | bytes 4718592 | tf_op jit(solution)/shard_map/soundings/pallas_call | solution.py:700
  23.8 2.0 %collective-permute-start.6 = (f32[72,128]{1,0:T(8,128)S(1)}, f32[72,128]{1,0:T(8,128)S(1)}, u32[]{:S(2)}, u32[]{:S(2)}) collective-permute-start(f32[72,128]{1,0:T(8,128)S(1)} %get-tuple-element.28), channel_id=1, source_target_pairs={{0,3},{1,0},{2,1},{3,2},{4,7},{5,4},{6,5},{7,6},{8,11},{9,8},{10,9... | collective-permute-start | bytes 110600 | tf_op jit(solution)/shard_map/ppermute | solution.py:615
  25.8 0.0 collective-permute-done.1.east0
  25.8 0.1 collective-permute-start.7
  25.9 0.0 collective-permute-done.west0
  25.9 2.5 %collective-permute-start.5 = (f32[2,16,128]{2,1,0:T(8,128)S(1)}, f32[2,16,128]{2,1,0:T(8,128)S(1)}, u32[]{:S(2)}, u32[]{:S(2)}) collective-permute-start(f32[2,16,128]{2,1,0:T(8,128)S(1)} %get-tuple-element.27), channel_id=1, source_target_pairs={{0,28},{4,0},{8,4},{12,8},{16,12},{20,16},{24,20},{28,24},{1,29},{... | collective-permute-start | bytes 49160 | tf_op jit(solution)/shard_map/ppermute | solution.py:615
  28.4 0.0 collective-permute-done.2.a0
  28.4 0.0 collective-permute-start.4
  28.5 0.0 collective-permute-done.3.b0
  28.5 2.5 %coefficients.1 = (f32[7,1152,128]{2,1,0:T(8,128)S(1)}, f32[2,128,128]{2,1,0:T(8,128)S(1)}, f32[2,576,128]{2,1,0:T(8,128)S(1)}) custom-call(f32[1152,128]{1,0:T(8,128)} %bitcast.25, f32[1152,128]{1,0:T(8,128)} %bitcast.27, f32[1152,128]{1,0:T(8,128)} %bitcast.28, f32[2,144,128]{2,1,0:T(8,128)S(1)} %collective-permute-done.west0, ...), custom_call_target="tpu_custom_call" | custom-call | flops 4718592 | bytes 4718592 | tf_op jit(solution)/shard_map/coefficients/pallas_call | solution.py:719
  31.0 0.0 collective-permute-done.5.refs_6_
  31.0 1.5 %collective-permute-done.4.refs_5_ = f32[2,16,128]{2,1,0:T(8,128)S(1)} collective-permute-done((f32[2,16,128]{2,1,0:T(8,128)S(1)}, f32[2,16,128]{2,1,0:T(8,128)S(1)}, u32[]{:S(2)}, u32[]{:S(2)}) %collective-permute-start.4) | collective-permute-done | bytes 16416 | tf_op jit(solution)/shard_map/ppermute | solution.py:615
  32.5 0.0 collective-permute-done.6.refs_7_
  32.5 0.0 collective-permute-done.7.refs_8_
  32.5 9.1 %step.2 = (f32[576,16,128]{2,1,0:T(8,128)}, f32[7,1152,128]{2,1,0:T(8,128)}, f32[2,128,128]{2,1,0:T(8,128)S(1)}, f32[576,128]{1,0:T(8,128)S(1)}, f32[576,128]{1,0:T(8,128)S(1)}) custom-call(f32[576,16,128]{2,1,0:T(8,128)} %bitcast.22, f32[7,1152,128]{2,1,0:T(8,128)S(1)} %get-tuple-element.23.refs_1_, f32[2,128,128]{2,1,0:T(8,128)S(1)} %get-tuple-element.24.refs_2_, ...), custom_call_target="tpu_custom_call" | custom-call | flops 37748736 | bytes 9437184 | tf_op jit(solution)/shard_map/step/pallas_call | solution.py:729
  41.6 1.6 %collective-permute-start.10 = (f32[576,128]{1,0:T(8,128)S(1)}, f32[576,128]{1,0:T(8,128)S(1)}, u32[]{:S(2)}, u32[]{:S(2)}) collective-permute-start(f32[576,128]{1,0:T(8,128)S(1)} %get-tuple-element.33), channel_id=1, source_target_pairs={{0,1},{1,0},{2,3},{3,2},{4,5},{5,4},{6,7},{7,6},{8,9},{9,8},{10,11... | collective-permute-start | bytes 884744 | tf_op jit(solution)/shard_map/ppermute | solution.py:628
  43.2 0.7 %collective-permute-start.11 = (f32[576,128]{1,0:T(8,128)S(1)}, f32[576,128]{1,0:T(8,128)S(1)}, u32[]{:S(2)}, u32[]{:S(2)}) collective-permute-start(f32[576,128]{1,0:T(8,128)S(1)} %get-tuple-element.34), channel_id=1, source_target_pairs={{0,0},{1,2},{2,1},{3,3},{4,4},{5,6},{6,5},{7,7},{8,8},{9,10},{10,9... | collective-permute-start | bytes 884744 | tf_op jit(solution)/shard_map/ppermute | solution.py:629
  43.9 0.9 %collective-permute-start.9 = (f32[2,128,128]{2,1,0:T(8,128)S(1)}, f32[2,128,128]{2,1,0:T(8,128)S(1)}, u32[]{:S(2)}, u32[]{:S(2)}) collective-permute-start(f32[2,128,128]{2,1,0:T(8,128)S(1)} %get-tuple-element.32), channel_id=1, source_target_pairs={{0,28},{4,0},{8,4},{12,8},{16,12},{20,16},{24,20},{28,24},{1,29},{... | collective-permute-start | bytes 393224 | tf_op jit(solution)/shard_map/ppermute | solution.py:615
  44.8 0.0 collective-permute-start.8
  44.8 5.4 %all-to-all-start.1 = ((f32[32,1,128]{2,1,0:T(1,128)}), f32[32,1,128]{2,1,0:T(1,128)S(1)}, u32[]{:S(2)}, u32[]{:S(2)}) async-start(f32[32,1,128]{2,1,0:T(1,128)} %bitcast.13), calls=%async_computation.1 | async-start | bytes 32768 | tf_op jit(solution)/shard_map/all_to_all | solution.py:749
  50.1 0.0 collective-permute-done.9.refs_3_
  50.2 0.0 collective-permute-done.8.refs_2_
  50.2 0.0 collective-permute-done.10.refs_4_
  50.2 0.0 collective-permute-done.11.refs_5_
  50.2 8.3 %step.3 = f32[576,16,128]{2,1,0:T(8,128)} custom-call(f32[576,16,128]{2,1,0:T(8,128)} %get-tuple-element.30.refs_0_, f32[7,1152,128]{2,1,0:T(8,128)} %get-tuple-element.31.refs_1_, f32[2,128,128]{2,1,0:T(8,128)S(1)} %collective-permute-done.8.refs_2_, f32[2,128,128]{2,1,0:T(8,128)S(1)} %collective-permute-done.9.refs_3_, ...), custom_call_target="tpu_custom_call" | custom-call | flops 37748736 | bytes 9437184 | tf_op jit(solution)/shard_map/step/pallas_call | solution.py:729
  58.5 0.0 all-to-all-done.1
  58.5 0.7 %residual.1 = f32[8,128]{1,0:T(8,128)} custom-call(f32[32,128]{1,0:T(8,128)S(1)} %bitcast.20), custom_call_target="tpu_custom_call" | custom-call | flops 10 | bytes 10000 | tf_op jit(solution)/shard_map/residual/pallas_call | solution.py:753
Async XLA Ops:
  2.8 18.2 %all-to-all-start = ((f32[608,1,128]{2,1,0:T(1,128)}), f32[608,1,128]{2,1,0:T(1,128)S(1)}, u32[]{:S(2)}, u32[]{:S(2)}) async-start(f32[608,1,128]{2,1,0:T(1,128)} %bitcast.10), calls=%async_computation | async-start | bytes 622592 | tf_op jit(solution)/shard_map/all_to_all | solution.py:673
  10.1 8.2 %copy-start = (f32[72,8,16,128]{3,2,1,0:T(8,128)S(1)}, f32[72,8,16,128]{3,2,1,0:T(8,128)}, u32[]{:S(2)}) copy-start(f32[72,8,16,128]{3,2,1,0:T(8,128)} %concentration.1) | copy-start | bytes 14155780
  13.9 14.5 %collective-permute-start.2 = (f32[648,128]{1,0:T(8,128)S(1)}, f32[648,128]{1,0:T(8,128)S(1)}, u32[]{:S(2)}, u32[]{:S(2)}) collective-permute-start(f32[648,128]{1,0:T(8,128)S(1)} %get-tuple-element.21), channel_id=1, source_target_pairs={{0,1},{1,0},{2,3},{3,2},{4,5},{5,4},{6,7},{7,6},{8,9},{9,8},{10,11... | collective-permute-start | bytes 995336 | tf_op jit(solution)/shard_map/ppermute | solution.py:628
  15.8 12.7 %collective-permute-start.3 = (f32[648,128]{1,0:T(8,128)S(1)}, f32[648,128]{1,0:T(8,128)S(1)}, u32[]{:S(2)}, u32[]{:S(2)}) collective-permute-start(f32[648,128]{1,0:T(8,128)S(1)} %get-tuple-element.22), channel_id=1, source_target_pairs={{0,0},{1,2},{2,1},{3,3},{4,4},{5,6},{6,5},{7,7},{8,8},{9,10},{10,9... | collective-permute-start | bytes 995336 | tf_op jit(solution)/shard_map/ppermute | solution.py:629
  16.4 9.3 %collective-permute-start.1 = (f32[2,144,128]{2,1,0:T(8,128)S(1)}, f32[2,144,128]{2,1,0:T(8,128)S(1)}, u32[]{:S(2)}, u32[]{:S(2)}) collective-permute-start(f32[2,144,128]{2,1,0:T(8,128)S(1)} %get-tuple-element.20), channel_id=1, source_target_pairs={{0,28},{4,0},{8,4},{12,8},{16,12},{20,16},{24,20},{28,24},{1,29},{... | collective-permute-start | bytes 442376 | tf_op jit(solution)/shard_map/ppermute | solution.py:615
  18.3 7.6 %collective-permute-start = (f32[2,144,128]{2,1,0:T(8,128)S(1)}, f32[2,144,128]{2,1,0:T(8,128)S(1)}, u32[]{:S(2)}, u32[]{:S(2)}) collective-permute-start(f32[2,144,128]{2,1,0:T(8,128)S(1)} %get-tuple-element.20), channel_id=1, source_target_pairs={{0,4},{4,8},{8,12},{12,16},{16,20},{20,24},{24,28},{28,0},{1,5},{5... | collective-permute-start | bytes 442376 | tf_op jit(solution)/shard_map/ppermute | solution.py:615
  23.8 8.8 %collective-permute-start.6 = (f32[72,128]{1,0:T(8,128)S(1)}, f32[72,128]{1,0:T(8,128)S(1)}, u32[]{:S(2)}, u32[]{:S(2)}) collective-permute-start(f32[72,128]{1,0:T(8,128)S(1)} %get-tuple-element.28), channel_id=1, source_target_pairs={{0,3},{1,0},{2,1},{3,2},{4,7},{5,4},{6,5},{7,6},{8,11},{9,8},{10,9... | collective-permute-start | bytes 110600 | tf_op jit(solution)/shard_map/ppermute | solution.py:615
  25.8 6.7 %collective-permute-start.7 = (f32[72,128]{1,0:T(8,128)S(1)}, f32[72,128]{1,0:T(8,128)S(1)}, u32[]{:S(2)}, u32[]{:S(2)}) collective-permute-start(f32[72,128]{1,0:T(8,128)S(1)} %get-tuple-element.29), channel_id=1, source_target_pairs={{0,1},{1,2},{2,3},{3,0},{4,5},{5,6},{6,7},{7,4},{8,9},{9,10},{10,1... | collective-permute-start | bytes 110600 | tf_op jit(solution)/shard_map/ppermute | solution.py:615
  25.9 5.1 %collective-permute-start.5 = (f32[2,16,128]{2,1,0:T(8,128)S(1)}, f32[2,16,128]{2,1,0:T(8,128)S(1)}, u32[]{:S(2)}, u32[]{:S(2)}) collective-permute-start(f32[2,16,128]{2,1,0:T(8,128)S(1)} %get-tuple-element.27), channel_id=1, source_target_pairs={{0,28},{4,0},{8,4},{12,8},{16,12},{20,16},{24,20},{28,24},{1,29},{... | collective-permute-start | bytes 49160 | tf_op jit(solution)/shard_map/ppermute | solution.py:615
  28.4 4.1 %collective-permute-start.4 = (f32[2,16,128]{2,1,0:T(8,128)S(1)}, f32[2,16,128]{2,1,0:T(8,128)S(1)}, u32[]{:S(2)}, u32[]{:S(2)}) collective-permute-start(f32[2,16,128]{2,1,0:T(8,128)S(1)} %get-tuple-element.27), channel_id=1, source_target_pairs={{0,4},{4,8},{8,12},{12,16},{16,20},{20,24},{24,28},{28,0},{1,5},{5... | collective-permute-start | bytes 49160 | tf_op jit(solution)/shard_map/ppermute | solution.py:615
  41.6 8.6 %collective-permute-start.10 = (f32[576,128]{1,0:T(8,128)S(1)}, f32[576,128]{1,0:T(8,128)S(1)}, u32[]{:S(2)}, u32[]{:S(2)}) collective-permute-start(f32[576,128]{1,0:T(8,128)S(1)} %get-tuple-element.33), channel_id=1, source_target_pairs={{0,1},{1,0},{2,3},{3,2},{4,5},{5,4},{6,7},{7,6},{8,9},{9,8},{10,11... | collective-permute-start | bytes 884744 | tf_op jit(solution)/shard_map/ppermute | solution.py:628
  43.2 7.0 %collective-permute-start.11 = (f32[576,128]{1,0:T(8,128)S(1)}, f32[576,128]{1,0:T(8,128)S(1)}, u32[]{:S(2)}, u32[]{:S(2)}) collective-permute-start(f32[576,128]{1,0:T(8,128)S(1)} %get-tuple-element.34), channel_id=1, source_target_pairs={{0,0},{1,2},{2,1},{3,3},{4,4},{5,6},{6,5},{7,7},{8,8},{9,10},{10,9... | collective-permute-start | bytes 884744 | tf_op jit(solution)/shard_map/ppermute | solution.py:629
  43.9 6.3 %collective-permute-start.9 = (f32[2,128,128]{2,1,0:T(8,128)S(1)}, f32[2,128,128]{2,1,0:T(8,128)S(1)}, u32[]{:S(2)}, u32[]{:S(2)}) collective-permute-start(f32[2,128,128]{2,1,0:T(8,128)S(1)} %get-tuple-element.32), channel_id=1, source_target_pairs={{0,28},{4,0},{8,4},{12,8},{16,12},{20,16},{24,20},{28,24},{1,29},{... | collective-permute-start | bytes 393224 | tf_op jit(solution)/shard_map/ppermute | solution.py:615
  44.8 5.4 %collective-permute-start.8 = (f32[2,128,128]{2,1,0:T(8,128)S(1)}, f32[2,128,128]{2,1,0:T(8,128)S(1)}, u32[]{:S(2)}, u32[]{:S(2)}) collective-permute-start(f32[2,128,128]{2,1,0:T(8,128)S(1)} %get-tuple-element.32), channel_id=1, source_target_pairs={{0,4},{4,8},{8,12},{12,16},{16,20},{20,24},{24,28},{28,0},{1,5},{5... | collective-permute-start | bytes 393224 | tf_op jit(solution)/shard_map/ppermute | solution.py:615
  44.8 13.7 %all-to-all-start.1 = ((f32[32,1,128]{2,1,0:T(1,128)}), f32[32,1,128]{2,1,0:T(1,128)S(1)}, u32[]{:S(2)}, u32[]{:S(2)}) async-start(f32[32,1,128]{2,1,0:T(1,128)} %bitcast.13), calls=%async_computation.1 | async-start | bytes 32768 | tf_op jit(solution)/shard_map/all_to_all | solution.py:749

commit v12 on v11

--- a/solution.py
+++ b/solution.py
@@ -484,10 +484,11 @@
                 top = part.astype(jnp.bfloat16).astype(jnp.float32)
                 tops.append(top)
                 rests.append(part - top)
-            at = pl.ds(pl.multiple_of(b * block * SUB, block * SUB), block * SUB)
+            at = pl.ds(pl.multiple_of(b * block * SUB, 2 * SUB), block * SUB)
+            rest_at = pl.ds(pl.multiple_of((levels + b * block) * SUB, 2 * SUB), block * SUB)
             lanes = pl.ds(h * cols, cols)
-            out[0, at, lanes] = jnp.concatenate(tops, axis=0).astype(jnp.bfloat16)
-            out[1, at, lanes] = jnp.concatenate(rests, axis=0).astype(jnp.bfloat16)
+            out[at, lanes] = jnp.concatenate(tops, axis=0).astype(jnp.bfloat16)
+            out[rest_at, lanes] = jnp.concatenate(rests, axis=0).astype(jnp.bfloat16)
         return carry
 
     lax.fori_loop(0, levels // block, body, 0)
@@ -495,7 +496,8 @@
 
 def soundings(
     levels, rows, group_rows, cap, chunks, per_chunk, block,
-    received, sums, forcing, side_ref, a_ref, b_ref, back_out, arrived, table, scaled, back, sem
+    received, sums, forcing, side_ref, a_ref, b_ref, back_out,
+    arrived, table, scaled, back, seen, spread, gathered, sem
 ):
     lane = lane_iota()
     parts, _, width = arrived.shape
@@ -550,13 +552,11 @@
                 jnp.bfloat16
             )
         total = jnp.zeros((SUB, width), jnp.float32)
-        for b in range(levels // block):
-            blk = pl.ds(b * block * SUB, block * SUB)
-            seen = jnp.dot(sums[0, blk, :], look, preferred_element_type=jnp.float32)
-            seen += jnp.dot(sums[1, blk, :], look, preferred_element_type=jnp.float32)
-            weight = arrived[j, pl.ds(b * block, block), :]
-            for k in range(block):
-                total += weight[k : k + 1, :] * seen[k * SUB : (k + 1) * SUB, :]
+        seen[...] = jnp.dot(sums[...], look, preferred_element_type=jnp.float32)
+        for k in range(levels):
+            at = k * SUB
+            both = seen[pl.ds(at, SUB), :] + seen[pl.ds(levels * SUB + at, SUB), :]
+            total += arrived[j, pl.ds(k, 1), :] * both
         modelled = jnp.sum(jnp.where(mask_of(j), total, 0.0), axis=0, keepdims=True)
         observed = arrived[j, pl.ds(levels + 1, 1), :]
         error = arrived[j, pl.ds(levels + 2, 1), :]
@@ -574,22 +574,23 @@
     zeros = jnp.zeros((SUB, LANES), jnp.float32)
     forcing[pl.ds(0, SUB), :] = zeros
     forcing[pl.ds(levels * rows + SUB, SUB), :] = zeros
-    for b in range(levels // block):
-        total = jnp.zeros((block * SUB, keys), jnp.float32)
-        for j in range(parts):
+    for j in range(parts):
+        mask = mask_of(j)
+        for b in range(levels // block):
             weight = arrived[j, pl.ds(b * block, block), :] * scaled[pl.ds(j, 1), :]
             top = weight.astype(jnp.bfloat16).astype(jnp.float32)
-            mask = mask_of(j)
-            for part in (top, weight - top):
-                spread = jnp.concatenate(
+            for first_row, part in ((0, top), (levels * SUB, weight - top)):
+                spread[pl.ds(first_row + b * block * SUB, block * SUB), :] = jnp.concatenate(
                     [jnp.where(mask, part[k : k + 1, :], 0.0) for k in range(block)], axis=0
                 ).astype(jnp.bfloat16)
-                total += jnp.dot(spread, table[j, :, :], preferred_element_type=jnp.float32)
-        for k in range(block):
-            for h in range(halves):
-                forcing[pl.ds((b * block + k) * rows + (h + 1) * SUB, SUB), :] = total[
-                    k * SUB : (k + 1) * SUB, h * LANES : (h + 1) * LANES
-                ]
+        made = jnp.dot(spread[...], table[j, :, :], preferred_element_type=jnp.float32)
+        made = made[: levels * SUB, :] + made[levels * SUB :, :]
+        gathered[...] = made if j == 0 else gathered[...] + made
+    for k in range(levels):
+        for h in range(halves):
+            forcing[pl.ds(k * rows + (h + 1) * SUB, SUB), :] = gathered[
+                pl.ds(k * SUB, SUB), pl.ds(h * LANES, LANES)
+            ]
 
     for chunk in range(chunks):
         put_rims(forcing, SUB, levels, per_chunk, chunk, side_ref, 0, rows)
@@ -690,7 +691,7 @@
     sum_block = largest(levels, 12, 8)
     sums = call(
         functools.partial(tracer_sum, sum_block),
-        [HBM], jax.ShapeDtypeStruct((2, levels * SUB, rows // SUB * cols), jnp.bfloat16), VMEM,
+        [HBM], jax.ShapeDtypeStruct((2 * levels * SUB, rows // SUB * cols), jnp.bfloat16), VMEM,
         (vmem(levels, tracers, rows, cols), dma((levels // sum_block,))),
         10, field_bytes // 4, field_bytes, "tracer_sum",
     )(concentration)
@@ -708,9 +709,11 @@
         (
             vmem(parts, -(-groups * group_rows // SUB) * SUB, width),
             pltpu.VMEM((parts, width, rows // SUB * LANES), jnp.bfloat16),
-            vmem(max(parts, SUB), width), vmem(bricks, LANES), dma((1,)),
+            vmem(max(parts, SUB), width), vmem(bricks, LANES),
+            vmem(2 * levels * SUB, width), pltpu.VMEM((2 * levels * SUB, width), jnp.bfloat16),
+            vmem(levels * SUB, rows // SUB * LANES), dma((1,)),
         ),
-        10, field_bytes * 8, field_bytes, "soundings",
+        16, field_bytes * 8, field_bytes, "soundings",
     )(received, sums)
     forcing_rims = exchange_small(*rims)
 
@@ -741,7 +744,7 @@
         (vmem(chunks, rows, LANES), vmem(2, levels, LANES)),
     )
     (result,) = advance(
-        False, unroll, [HBM] * 2 + [VMEM] * 4, (in_hbm(stepped), in_hbm(kept), *exchange(*rims)),
+        False, largest(unroll, 4, 3, 2, 1), [HBM] * 2 + [VMEM] * 4, (in_hbm(stepped), in_hbm(kept), *exchange(*rims)),
         (f32(*field.shape),), (HBM,),
         (vmem(*weight_shape), vmem(*rim_shape), vmem(*edge_shape), vmem(levels * tracers, rows, LANES)),
     )

time: 59.9 us -> 61 us (1.018)
  Pallas kernels: 30 us -> 31.2 us
    pallas_call x2, Pallas kernels: 17.4 us -> 18.4 us  [advance(): call(functools.partial(step, levels, tracers, rows, chunks, per_chunk, to...]
  transfers between devices with their start and end apart: 14 -> 14, of which waited for: 2 -> 3; matrix products, arithmetic and copies ran while one was open for 0% -> 0% of each run, Pallas kernels for 31% -> 32%
where the time goes in v12:
time: 61 us; the launch traced here: 60.3 us
  Pallas kernels  31.2 us (51%)
  starting transfers between devices  24.8 us (41%)
  waiting for transfers between devices  3.55 us (6%)
  between operations  0.76 us (1%)
    pallas_call x2, Pallas kernels, advance(): call(functools.partial(step, levels, tracers, rows, chunks, per_chunk, to...  18.4 us
    ppermute x8, starting transfers between devices, turn(): lax.ppermute(value, axis, [(i, (i + by) % count) for i in range(count)])  7.35 us
    all_to_all x1, starting transfers between devices, per_device(): lax.all_to_all(packed.reshape(-1, 1, LANES), ('lon', 'lat'), split_axis=0...  7.3 us
    all_to_all x1, starting transfers between devices, per_device(): lax.all_to_all(back.reshape(bricks, 1, LANES), ('lon', 'lat'), split_axis...  5.21 us
    pallas_call x1, Pallas kernels, per_device(): call(functools.partial(first_rims, levels, tracers, rows, chunks, per_chu...  3.81 us
    ppermute x2, starting transfers between devices, exchange(): lax.ppermute(a_rim, 'lat', [(j, partner(j, 0)) for j in range(lats)])  3.57 us
    pallas_call x1, Pallas kernels, per_device(): call(functools.partial(soundings, levels, rows, group_rows, cap, chunks,...  2.93 us
    pallas_call x1, Pallas kernels, per_device(): call(functools.partial(coefficients, levels, tracers, rows, per_chunk, un...  2.52 us
  transfers between devices with their start and end apart: 14, of which 3 were waited for; matrix products, arithmetic and copies ran while one was open for 0% of the time, Pallas kernels for 32%

profile of v12, /device:TPU:0, one launch (start us, length us, event | category | flops | bytes accessed | tf_op | source)
XLA Modules:
  0.0 60.3 jit_solution(3164397357284383100)
XLA Ops:
  0.6 2.2 %pack.1 = f32[608,128]{1,0:T(8,128)} custom-call(f32[576,128]{1,0:T(8,128)} %bitcast.29, s32[8,128]{1,0:T(8,128)} %bitcast.30, f32[8,128]{1,0:T(8,128)} %bitcast.31, f32[8,128]{1,0:T(8,128)} %bitcast.32), custom_call_target="tpu_custom_call" | custom-call | flops 10 | bytes 800000 | tf_op jit(solution)/shard_map/pack/pallas_call | solution.py:663
  2.8 7.3 %all-to-all-start = ((f32[608,1,128]{2,1,0:T(1,128)}), f32[608,1,128]{2,1,0:T(1,128)S(1)}, u32[]{:S(2)}, u32[]{:S(2)}) async-start(f32[608,1,128]{2,1,0:T(1,128)} %bitcast.10), calls=%async_computation | async-start | bytes 622592 | tf_op jit(solution)/shard_map/all_to_all | solution.py:674
  10.1 0.0 copy-start
  10.1 3.8 %first_rims.1 = (f32[2,144,128]{2,1,0:T(8,128)S(1)}, f32[648,128]{1,0:T(8,128)S(1)}, f32[648,128]{1,0:T(8,128)S(1)}) custom-call(f32[9216,128]{1,0:T(8,128)} %bitcast.21, f32[1152,128]{1,0:T(8,128)} %bitcast.24, f32[1152,128]{1,0:T(8,128)} %bitcast.26), custom_call_target="tpu_custom_call" | custom-call | flops 4718592 | bytes 9437184 | tf_op jit(solution)/shard_map/first_rims/pallas_call | solution.py:680
  13.9 1.8 %collective-permute-start.2 = (f32[648,128]{1,0:T(8,128)S(1)}, f32[648,128]{1,0:T(8,128)S(1)}, u32[]{:S(2)}, u32[]{:S(2)}) collective-permute-start(f32[648,128]{1,0:T(8,128)S(1)} %get-tuple-element.21), channel_id=1, source_target_pairs={{0,1},{1,0},{2,3},{3,2},{4,5},{5,4},{6,7},{7,6},{8,9},{9,8},{10,11... | collective-permute-start | bytes 995336 | tf_op jit(solution)/shard_map/ppermute | solution.py:629
  15.8 0.7 %collective-permute-start.3 = (f32[648,128]{1,0:T(8,128)S(1)}, f32[648,128]{1,0:T(8,128)S(1)}, u32[]{:S(2)}, u32[]{:S(2)}) collective-permute-start(f32[648,128]{1,0:T(8,128)S(1)} %get-tuple-element.22), channel_id=1, source_target_pairs={{0,0},{1,2},{2,1},{3,3},{4,4},{5,6},{6,5},{7,7},{8,8},{9,10},{10,9... | collective-permute-start | bytes 995336 | tf_op jit(solution)/shard_map/ppermute | solution.py:630
  16.4 1.9 %collective-permute-start.1 = (f32[2,144,128]{2,1,0:T(8,128)S(1)}, f32[2,144,128]{2,1,0:T(8,128)S(1)}, u32[]{:S(2)}, u32[]{:S(2)}) collective-permute-start(f32[2,144,128]{2,1,0:T(8,128)S(1)} %get-tuple-element.20), channel_id=1, source_target_pairs={{0,28},{4,0},{8,4},{12,8},{16,12},{20,16},{24,20},{28,24},{1,29},{... | collective-permute-start | bytes 442376 | tf_op jit(solution)/shard_map/ppermute | solution.py:616
  18.3 0.0 collective-permute-start
  18.3 0.0 copy-done
  18.3 0.7 %tracer_sum.1.sums = bf16[1152,256]{1,0:T(8,128)(2,1)S(1)} custom-call(f32[72,8,16,128]{3,2,1,0:T(8,128)S(1)} %copy-done), custom_call_target="tpu_custom_call" | custom-call | flops 1179648 | bytes 4718592 | tf_op jit(solution)/shard_map/tracer_sum/pallas_call | solution.py:692
  19.1 1.9 %all-to-all-done = f32[608,1,128]{2,1,0:T(1,128)S(1)} async-done(((f32[608,1,128]{2,1,0:T(1,128)}), f32[608,1,128]{2,1,0:T(1,128)S(1)}, u32[]{:S(2)}, u32[]{:S(2)}) %all-to-all-start) | async-done | bytes 311328 | tf_op jit(solution)/shard_map/all_to_all | solution.py:674
  21.0 2.9 %soundings.1 = (f32[1168,128]{1,0:T(8,128)S(1)}, f32[2,16,128]{2,1,0:T(8,128)S(1)}, f32[72,128]{1,0:T(8,128)S(1)}, f32[72,128]{1,0:T(8,128)S(1)}, f32[32,128]{1,0:T(8,128)}) custom-call(f32[608,128]{1,0:T(8,128)S(1)} %bitcast.19, bf16[1152,256]{1,0:T(8,128)(2,1)S(1)} %tracer_sum.1.sums), custom_call_target="tpu_custom_call" | custom-call | flops 37748736 | bytes 4718592 | tf_op jit(solution)/shard_map/soundings/pallas_call | solution.py:701
  23.9 2.0 %collective-permute-start.6 = (f32[72,128]{1,0:T(8,128)S(1)}, f32[72,128]{1,0:T(8,128)S(1)}, u32[]{:S(2)}, u32[]{:S(2)}) collective-permute-start(f32[72,128]{1,0:T(8,128)S(1)} %get-tuple-element.28), channel_id=1, source_target_pairs={{0,3},{1,0},{2,1},{3,2},{4,7},{5,4},{6,5},{7,6},{8,11},{9,8},{10,9... | collective-permute-start | bytes 110600 | tf_op jit(solution)/shard_map/ppermute | solution.py:616
  26.0 0.0 collective-permute-done.1.east0
  26.0 0.1 collective-permute-start.7
  26.1 0.0 collective-permute-done.west0
  26.1 2.4 %collective-permute-start.5 = (f32[2,16,128]{2,1,0:T(8,128)S(1)}, f32[2,16,128]{2,1,0:T(8,128)S(1)}, u32[]{:S(2)}, u32[]{:S(2)}) collective-permute-start(f32[2,16,128]{2,1,0:T(8,128)S(1)} %get-tuple-element.27), channel_id=1, source_target_pairs={{0,28},{4,0},{8,4},{12,8},{16,12},{20,16},{24,20},{28,24},{1,29},{... | collective-permute-start | bytes 49160 | tf_op jit(solution)/shard_map/ppermute | solution.py:616
  28.5 0.0 collective-permute-done.2.a0
  28.5 0.0 collective-permute-start.4
  28.5 0.0 collective-permute-done.3.b0
  28.5 2.5 %coefficients.1 = (f32[7,1152,128]{2,1,0:T(8,128)S(1)}, f32[2,128,128]{2,1,0:T(8,128)S(1)}, f32[2,576,128]{2,1,0:T(8,128)S(1)}) custom-call(f32[1152,128]{1,0:T(8,128)} %bitcast.25, f32[1152,128]{1,0:T(8,128)} %bitcast.27, f32[1152,128]{1,0:T(8,128)} %bitcast.28, f32[2,144,128]{2,1,0:T(8,128)S(1)} %collective-permute-done.west0, ...), custom_call_target="tpu_custom_call" | custom-call | flops 4718592 | bytes 4718592 | tf_op jit(solution)/shard_map/coefficients/pallas_call | solution.py:722
  31.0 0.0 collective-permute-done.5.refs_6_
  31.0 1.5 %collective-permute-done.4.refs_5_ = f32[2,16,128]{2,1,0:T(8,128)S(1)} collective-permute-done((f32[2,16,128]{2,1,0:T(8,128)S(1)}, f32[2,16,128]{2,1,0:T(8,128)S(1)}, u32[]{:S(2)}, u32[]{:S(2)}) %collective-permute-start.4) | collective-permute-done | bytes 16416 | tf_op jit(solution)/shard_map/ppermute | solution.py:616
  32.6 0.0 collective-permute-done.6.refs_7_
  32.6 0.0 collective-permute-done.7.refs_8_
  32.6 9.1 %step.2 = (f32[576,16,128]{2,1,0:T(8,128)}, f32[7,1152,128]{2,1,0:T(8,128)}, f32[2,128,128]{2,1,0:T(8,128)S(1)}, f32[576,128]{1,0:T(8,128)S(1)}, f32[576,128]{1,0:T(8,128)S(1)}) custom-call(f32[576,16,128]{2,1,0:T(8,128)} %bitcast.22, f32[7,1152,128]{2,1,0:T(8,128)S(1)} %get-tuple-element.23.refs_1_, f32[2,128,128]{2,1,0:T(8,128)S(1)} %get-tuple-element.24.refs_2_, ...), custom_call_target="tpu_custom_call" | custom-call | flops 37748736 | bytes 9437184 | tf_op jit(solution)/shard_map/step/pallas_call | solution.py:732
  41.6 1.7 %collective-permute-start.10 = (f32[576,128]{1,0:T(8,128)S(1)}, f32[576,128]{1,0:T(8,128)S(1)}, u32[]{:S(2)}, u32[]{:S(2)}) collective-permute-start(f32[576,128]{1,0:T(8,128)S(1)} %get-tuple-element.33), channel_id=1, source_target_pairs={{0,1},{1,0},{2,3},{3,2},{4,5},{5,4},{6,7},{7,6},{8,9},{9,8},{10,11... | collective-permute-start | bytes 884744 | tf_op jit(solution)/shard_map/ppermute | solution.py:629
  43.4 0.7 %collective-permute-start.11 = (f32[576,128]{1,0:T(8,128)S(1)}, f32[576,128]{1,0:T(8,128)S(1)}, u32[]{:S(2)}, u32[]{:S(2)}) collective-permute-start(f32[576,128]{1,0:T(8,128)S(1)} %get-tuple-element.34), channel_id=1, source_target_pairs={{0,0},{1,2},{2,1},{3,3},{4,4},{5,6},{6,5},{7,7},{8,8},{9,10},{10,9... | collective-permute-start | bytes 884744 | tf_op jit(solution)/shard_map/ppermute | solution.py:630
  44.0 0.9 %collective-permute-start.9 = (f32[2,128,128]{2,1,0:T(8,128)S(1)}, f32[2,128,128]{2,1,0:T(8,128)S(1)}, u32[]{:S(2)}, u32[]{:S(2)}) collective-permute-start(f32[2,128,128]{2,1,0:T(8,128)S(1)} %get-tuple-element.32), channel_id=1, source_target_pairs={{0,28},{4,0},{8,4},{12,8},{16,12},{20,16},{24,20},{28,24},{1,29},{... | collective-permute-start | bytes 393224 | tf_op jit(solution)/shard_map/ppermute | solution.py:616
  45.0 0.0 collective-permute-start.8
  45.0 5.2 %all-to-all-start.1 = ((f32[32,1,128]{2,1,0:T(1,128)}), f32[32,1,128]{2,1,0:T(1,128)S(1)}, u32[]{:S(2)}, u32[]{:S(2)}) async-start(f32[32,1,128]{2,1,0:T(1,128)} %bitcast.13), calls=%async_computation.1 | async-start | bytes 32768 | tf_op jit(solution)/shard_map/all_to_all | solution.py:752
  50.2 0.0 collective-permute-done.9.refs_3_
  50.2 0.1 collective-permute-done.8.refs_2_
  50.3 0.0 collective-permute-done.10.refs_4_
  50.3 0.0 collective-permute-done.11.refs_5_
  50.3 9.4 %step.3 = f32[576,16,128]{2,1,0:T(8,128)} custom-call(f32[576,16,128]{2,1,0:T(8,128)} %get-tuple-element.30.refs_0_, f32[7,1152,128]{2,1,0:T(8,128)} %get-tuple-element.31.refs_1_, f32[2,128,128]{2,1,0:T(8,128)S(1)} %collective-permute-done.8.refs_2_, f32[2,128,128]{2,1,0:T(8,128)S(1)} %collective-permute-done.9.refs_3_, ...), custom_call_target="tpu_custom_call" | custom-call | flops 37748736 | bytes 9437184 | tf_op jit(solution)/shard_map/step/pallas_call | solution.py:732
  59.6 0.0 all-to-all-done.1
  59.6 0.7 %residual.1 = f32[8,128]{1,0:T(8,128)} custom-call(f32[32,128]{1,0:T(8,128)S(1)} %bitcast.20), custom_call_target="tpu_custom_call" | custom-call | flops 10 | bytes 10000 | tf_op jit(solution)/shard_map/residual/pallas_call | solution.py:756
Async XLA Ops:
  2.8 18.2 %all-to-all-start = ((f32[608,1,128]{2,1,0:T(1,128)}), f32[608,1,128]{2,1,0:T(1,128)S(1)}, u32[]{:S(2)}, u32[]{:S(2)}) async-start(f32[608,1,128]{2,1,0:T(1,128)} %bitcast.10), calls=%async_computation | async-start | bytes 622592 | tf_op jit(solution)/shard_map/all_to_all | solution.py:674
  10.1 8.2 %copy-start = (f32[72,8,16,128]{3,2,1,0:T(8,128)S(1)}, f32[72,8,16,128]{3,2,1,0:T(8,128)}, u32[]{:S(2)}) copy-start(f32[72,8,16,128]{3,2,1,0:T(8,128)} %concentration.1) | copy-start | bytes 14155780
  13.9 14.6 %collective-permute-start.2 = (f32[648,128]{1,0:T(8,128)S(1)}, f32[648,128]{1,0:T(8,128)S(1)}, u32[]{:S(2)}, u32[]{:S(2)}) collective-permute-start(f32[648,128]{1,0:T(8,128)S(1)} %get-tuple-element.21), channel_id=1, source_target_pairs={{0,1},{1,0},{2,3},{3,2},{4,5},{5,4},{6,7},{7,6},{8,9},{9,8},{10,11... | collective-permute-start | bytes 995336 | tf_op jit(solution)/shard_map/ppermute | solution.py:629
  15.8 12.7 %collective-permute-start.3 = (f32[648,128]{1,0:T(8,128)S(1)}, f32[648,128]{1,0:T(8,128)S(1)}, u32[]{:S(2)}, u32[]{:S(2)}) collective-permute-start(f32[648,128]{1,0:T(8,128)S(1)} %get-tuple-element.22), channel_id=1, source_target_pairs={{0,0},{1,2},{2,1},{3,3},{4,4},{5,6},{6,5},{7,7},{8,8},{9,10},{10,9... | collective-permute-start | bytes 995336 | tf_op jit(solution)/shard_map/ppermute | solution.py:630
  16.4 9.5 %collective-permute-start.1 = (f32[2,144,128]{2,1,0:T(8,128)S(1)}, f32[2,144,128]{2,1,0:T(8,128)S(1)}, u32[]{:S(2)}, u32[]{:S(2)}) collective-permute-start(f32[2,144,128]{2,1,0:T(8,128)S(1)} %get-tuple-element.20), channel_id=1, source_target_pairs={{0,28},{4,0},{8,4},{12,8},{16,12},{20,16},{24,20},{28,24},{1,29},{... | collective-permute-start | bytes 442376 | tf_op jit(solution)/shard_map/ppermute | solution.py:616
  18.3 7.8 %collective-permute-start = (f32[2,144,128]{2,1,0:T(8,128)S(1)}, f32[2,144,128]{2,1,0:T(8,128)S(1)}, u32[]{:S(2)}, u32[]{:S(2)}) collective-permute-start(f32[2,144,128]{2,1,0:T(8,128)S(1)} %get-tuple-element.20), channel_id=1, source_target_pairs={{0,4},{4,8},{8,12},{12,16},{16,20},{20,24},{24,28},{28,0},{1,5},{5... | collective-permute-start | bytes 442376 | tf_op jit(solution)/shard_map/ppermute | solution.py:616
  23.9 8.6 %collective-permute-start.6 = (f32[72,128]{1,0:T(8,128)S(1)}, f32[72,128]{1,0:T(8,128)S(1)}, u32[]{:S(2)}, u32[]{:S(2)}) collective-permute-start(f32[72,128]{1,0:T(8,128)S(1)} %get-tuple-element.28), channel_id=1, source_target_pairs={{0,3},{1,0},{2,1},{3,2},{4,7},{5,4},{6,5},{7,6},{8,11},{9,8},{10,9... | collective-permute-start | bytes 110600 | tf_op jit(solution)/shard_map/ppermute | solution.py:616
  26.0 6.6 %collective-permute-start.7 = (f32[72,128]{1,0:T(8,128)S(1)}, f32[72,128]{1,0:T(8,128)S(1)}, u32[]{:S(2)}, u32[]{:S(2)}) collective-permute-start(f32[72,128]{1,0:T(8,128)S(1)} %get-tuple-element.29), channel_id=1, source_target_pairs={{0,1},{1,2},{2,3},{3,0},{4,5},{5,6},{6,7},{7,4},{8,9},{9,10},{10,1... | collective-permute-start | bytes 110600 | tf_op jit(solution)/shard_map/ppermute | solution.py:616
  26.1 4.9 %collective-permute-start.5 = (f32[2,16,128]{2,1,0:T(8,128)S(1)}, f32[2,16,128]{2,1,0:T(8,128)S(1)}, u32[]{:S(2)}, u32[]{:S(2)}) collective-permute-start(f32[2,16,128]{2,1,0:T(8,128)S(1)} %get-tuple-element.27), channel_id=1, source_target_pairs={{0,28},{4,0},{8,4},{12,8},{16,12},{20,16},{24,20},{28,24},{1,29},{... | collective-permute-start | bytes 49160 | tf_op jit(solution)/shard_map/ppermute | solution.py:616
  28.5 4.1 %collective-permute-start.4 = (f32[2,16,128]{2,1,0:T(8,128)S(1)}, f32[2,16,128]{2,1,0:T(8,128)S(1)}, u32[]{:S(2)}, u32[]{:S(2)}) collective-permute-start(f32[2,16,128]{2,1,0:T(8,128)S(1)} %get-tuple-element.27), channel_id=1, source_target_pairs={{0,4},{4,8},{8,12},{12,16},{16,20},{20,24},{24,28},{28,0},{1,5},{5... | collective-permute-start | bytes 49160 | tf_op jit(solution)/shard_map/ppermute | solution.py:616
  41.6 8.6 %collective-permute-start.10 = (f32[576,128]{1,0:T(8,128)S(1)}, f32[576,128]{1,0:T(8,128)S(1)}, u32[]{:S(2)}, u32[]{:S(2)}) collective-permute-start(f32[576,128]{1,0:T(8,128)S(1)} %get-tuple-element.33), channel_id=1, source_target_pairs={{0,1},{1,0},{2,3},{3,2},{4,5},{5,4},{6,7},{7,6},{8,9},{9,8},{10,11... | collective-permute-start | bytes 884744 | tf_op jit(solution)/shard_map/ppermute | solution.py:629
  43.4 6.9 %collective-permute-start.11 = (f32[576,128]{1,0:T(8,128)S(1)}, f32[576,128]{1,0:T(8,128)S(1)}, u32[]{:S(2)}, u32[]{:S(2)}) collective-permute-start(f32[576,128]{1,0:T(8,128)S(1)} %get-tuple-element.34), channel_id=1, source_target_pairs={{0,0},{1,2},{2,1},{3,3},{4,4},{5,6},{6,5},{7,7},{8,8},{9,10},{10,9... | collective-permute-start | bytes 884744 | tf_op jit(solution)/shard_map/ppermute | solution.py:630
  44.0 6.1 %collective-permute-start.9 = (f32[2,128,128]{2,1,0:T(8,128)S(1)}, f32[2,128,128]{2,1,0:T(8,128)S(1)}, u32[]{:S(2)}, u32[]{:S(2)}) collective-permute-start(f32[2,128,128]{2,1,0:T(8,128)S(1)} %get-tuple-element.32), channel_id=1, source_target_pairs={{0,28},{4,0},{8,4},{12,8},{16,12},{20,16},{24,20},{28,24},{1,29},{... | collective-permute-start | bytes 393224 | tf_op jit(solution)/shard_map/ppermute | solution.py:616
  45.0 5.3 %collective-permute-start.8 = (f32[2,128,128]{2,1,0:T(8,128)S(1)}, f32[2,128,128]{2,1,0:T(8,128)S(1)}, u32[]{:S(2)}, u32[]{:S(2)}) collective-permute-start(f32[2,128,128]{2,1,0:T(8,128)S(1)} %get-tuple-element.32), channel_id=1, source_target_pairs={{0,4},{4,8},{8,12},{12,16},{16,20},{20,24},{24,28},{28,0},{1,5},{5... | collective-permute-start | bytes 393224 | tf_op jit(solution)/shard_map/ppermute | solution.py:616
  45.0 14.7 %all-to-all-start.1 = ((f32[32,1,128]{2,1,0:T(1,128)}), f32[32,1,128]{2,1,0:T(1,128)S(1)}, u32[]{:S(2)}, u32[]{:S(2)}) async-start(f32[32,1,128]{2,1,0:T(1,128)} %bitcast.13), calls=%async_computation.1 | async-start | bytes 32768 | tf_op jit(solution)/shard_map/all_to_all | solution.py:752

commit v13 on v11

--- a/solution.py
+++ b/solution.py
@@ -310,14 +310,24 @@
     def part(ref, b, size, offset=0):
         return ref.at[pl.ds(pl.multiple_of(b * unroll * size + offset, SUB), unroll * size)]
 
-    def turned_rims(b, source, count, first_row):
+    def in_turn(body, carry):
+        group = rim_now.shape[0]
+
+        def turn_of(i, carry):
+            for n in range(group):
+                carry = body(i * group + n, n, carry)
+            return carry
+
+        return lax.fori_loop(0, blocks // group, turn_of, carry)
+
+    def turned_rims(b, n, source, count, first_row):
         chunk, q = b * unroll // per_chunk, b * unroll % per_chunk
         for r in range(0, count, SUB):
             turned = pltpu.roll(source[chunk, pl.ds(r, SUB), :], (LANES - 2 * q) % LANES, 1)
-            rim_now[pl.ds(first_row + r, SUB), :] = turned
-
-    def side(u, r):
-        return lambda h: pltpu.roll(rim_now[pl.ds(r + h * SUB, SUB), :], LANES - 1 - 2 * u, 1)
+            rim_now[n, pl.ds(first_row + r, SUB), :] = turned
+
+    def side(n, u, r):
+        return lambda h: pltpu.roll(rim_now[n, pl.ds(r + h * SUB, SUB), :], LANES - 1 - 2 * u, 1)
 
     def weights_of(b):
         co_part = weights.at[:, pl.ds(pl.multiple_of(b * unroll * rows, SUB), unroll * rows)]
@@ -332,15 +342,15 @@
 
         return lambda u: [one(u, h) for h in range(halves)]
 
-    def forward_block(b, solved):
+    def forward_block(b, n, solved):
         load(b).wait()
         if not first:
             load_weights(b).wait()
-        turned_rims(b, rim, plane, 0)
+        turned_rims(b, n, rim, plane, 0)
         cells, co_of = part(flat, b, plane, rows), weights_of(b)
         edge = edges.at[:, pl.ds(pl.multiple_of(b * unroll * tracers, SUB), unroll * tracers)]
         if first:
-            turned_rims(b, f_rim, rows, plane)
+            turned_rims(b, n, f_rim, rows, plane)
             f_cells = part(forcing, b, rows, SUB)
             f_edge = f_edges.at[:, pl.ds(pl.multiple_of(b * unroll, SUB), unroll)]
         else:
@@ -349,11 +359,11 @@
             co = co_of(u)
             new = []
             if first:
-                extra = stencil((forcing, b * unroll * rows + SUB), f_cells, u * rows, side(u, plane), f_edge, u, co)
+                extra = stencil((forcing, b * unroll * rows + SUB), f_cells, u * rows, side(n, u, plane), f_edge, u, co)
                 for t in range(tracers):
                     here = u * plane + t * rows
                     near = (flat, b * unroll * plane + rows)
-                    values = stencil(near, cells, here, side(u, t * rows), edge, u * tracers + t, co)
+                    values = stencil(near, cells, here, side(n, u, t * rows), edge, u * tracers + t, co)
                     for h in range(halves):
                         value = values[h] + extra[h] + co[h][6] * solved[h * tracers + t]
                         new.append(value)
@@ -364,7 +374,7 @@
                     for t in range(tracers):
                         here = u * plane + t * rows
                         (value,) = stencil(
-                            None, cells, here, side(u, t * rows), edge, u * tracers + t, co, (h,)
+                            None, cells, here, side(n, u, t * rows), edge, u * tracers + t, co, (h,)
                         )
                         value = value + co[h][6] * solved[h * tracers + t]
                         new.append(value)
@@ -374,11 +384,11 @@
 
     zero = jnp.zeros((SUB, LANES), jnp.float32)
     zeros = (zero,) * (tracers * halves)
-    lax.fori_loop(0, blocks, forward_block, zeros)
+    in_turn(forward_block, zeros)
     if not first:
         above_copy.wait()
 
-    def backward_block(i, later):
+    def backward_block(i, n, later):
         b = blocks - 1 - i
         cells = part(solved_ref, b, plane, solved_at * rows)
         factors = part(above, b, rows)
@@ -395,7 +405,7 @@
         store(b).start()
         return later
 
-    lax.fori_loop(0, blocks, backward_block, zeros)
+    in_turn(backward_block, zeros)
     if first:
         for chunk in range(chunks):
             put_rims(flat, rows, levels, per_chunk, chunk, side_ref, 0, plane)
@@ -729,7 +739,7 @@
         return call(
             functools.partial(step, levels, tracers, rows, chunks, per_chunk, together, first),
             specs, outs, out_specs,
-            (vmem(levels * tracers + 2, rows, LANES), vmem(plane + rows, LANES))
+            (vmem(levels * tracers + 2, rows, LANES), vmem(largest(levels // together, 3, 2, 1), plane + rows, LANES))
             + scratch + (dma((2 * (levels // together) + 5,)),),
             22, field_bytes * 8, field_bytes * 2, "step",
         )(*operands)

time: 59.9 us -> 59.9 us (level)
  no operation moved by 1% of the time
where the time goes in v13:
time: 59.9 us; the launch traced here: 59.2 us
  Pallas kernels  30 us (50%)
  starting transfers between devices  24.9 us (42%)
  waiting for transfers between devices  3.49 us (6%)
  between operations  0.79 us (1%)
    pallas_call x2, Pallas kernels, advance(): call(functools.partial(step, levels, tracers, rows, chunks, per_chunk, to...  17.3 us
    ppermute x8, starting transfers between devices, turn(): lax.ppermute(value, axis, [(i, (i + by) % count) for i in range(count)])  7.5 us
    all_to_all x1, starting transfers between devices, per_device(): lax.all_to_all(packed.reshape(-1, 1, LANES), ('lon', 'lat'), split_axis=0...  7.3 us
    all_to_all x1, starting transfers between devices, per_device(): lax.all_to_all(back.reshape(bricks, 1, LANES), ('lon', 'lat'), split_axis...  5.36 us
    pallas_call x1, Pallas kernels, per_device(): call(functools.partial(first_rims, levels, tracers, rows, chunks, per_chu...  3.81 us
    ppermute x2, starting transfers between devices, exchange(): lax.ppermute(a_rim, 'lat', [(j, partner(j, 0)) for j in range(lats)])  3.42 us
    pallas_call x1, Pallas kernels, per_device(): call(functools.partial(soundings, levels, rows, group_rows, cap, chunks,...  2.74 us
    pallas_call x1, Pallas kernels, per_device(): call(functools.partial(coefficients, levels, tracers, rows, per_chunk, un...  2.52 us
  transfers between devices with their start and end apart: 14, of which 2 were waited for; matrix products, arithmetic and copies ran while one was open for 0% of the time, Pallas kernels for 31%

profile of v13, /device:TPU:0, one launch (start us, length us, event | category | flops | bytes accessed | tf_op | source)
XLA Modules:
  0.0 59.2 jit_solution(15686724736881136080)
XLA Ops:
  0.6 2.2 %pack.1 = f32[608,128]{1,0:T(8,128)} custom-call(f32[576,128]{1,0:T(8,128)} %bitcast.29, s32[8,128]{1,0:T(8,128)} %bitcast.30, f32[8,128]{1,0:T(8,128)} %bitcast.31, f32[8,128]{1,0:T(8,128)} %bitcast.32), custom_call_target="tpu_custom_call" | custom-call | flops 10 | bytes 800000 | tf_op jit(solution)/shard_map/pack/pallas_call | solution.py:672
  2.8 7.3 %all-to-all-start = ((f32[608,1,128]{2,1,0:T(1,128)}), f32[608,1,128]{2,1,0:T(1,128)S(1)}, u32[]{:S(2)}, u32[]{:S(2)}) async-start(f32[608,1,128]{2,1,0:T(1,128)} %bitcast.10), calls=%async_computation | async-start | bytes 622592 | tf_op jit(solution)/shard_map/all_to_all | solution.py:683
  10.1 0.0 copy-start
  10.1 3.8 %first_rims.1 = (f32[2,144,128]{2,1,0:T(8,128)S(1)}, f32[648,128]{1,0:T(8,128)S(1)}, f32[648,128]{1,0:T(8,128)S(1)}) custom-call(f32[9216,128]{1,0:T(8,128)} %bitcast.21, f32[1152,128]{1,0:T(8,128)} %bitcast.24, f32[1152,128]{1,0:T(8,128)} %bitcast.26), custom_call_target="tpu_custom_call" | custom-call | flops 4718592 | bytes 9437184 | tf_op jit(solution)/shard_map/first_rims/pallas_call | solution.py:689
  13.9 1.8 %collective-permute-start.2 = (f32[648,128]{1,0:T(8,128)S(1)}, f32[648,128]{1,0:T(8,128)S(1)}, u32[]{:S(2)}, u32[]{:S(2)}) collective-permute-start(f32[648,128]{1,0:T(8,128)S(1)} %get-tuple-element.21), channel_id=1, source_target_pairs={{0,1},{1,0},{2,3},{3,2},{4,5},{5,4},{6,7},{7,6},{8,9},{9,8},{10,11... | collective-permute-start | bytes 995336 | tf_op jit(solution)/shard_map/ppermute | solution.py:638
  15.8 0.7 %collective-permute-start.3 = (f32[648,128]{1,0:T(8,128)S(1)}, f32[648,128]{1,0:T(8,128)S(1)}, u32[]{:S(2)}, u32[]{:S(2)}) collective-permute-start(f32[648,128]{1,0:T(8,128)S(1)} %get-tuple-element.22), channel_id=1, source_target_pairs={{0,0},{1,2},{2,1},{3,3},{4,4},{5,6},{6,5},{7,7},{8,8},{9,10},{10,9... | collective-permute-start | bytes 995336 | tf_op jit(solution)/shard_map/ppermute | solution.py:639
  16.4 1.9 %collective-permute-start.1 = (f32[2,144,128]{2,1,0:T(8,128)S(1)}, f32[2,144,128]{2,1,0:T(8,128)S(1)}, u32[]{:S(2)}, u32[]{:S(2)}) collective-permute-start(f32[2,144,128]{2,1,0:T(8,128)S(1)} %get-tuple-element.20), channel_id=1, source_target_pairs={{0,28},{4,0},{8,4},{12,8},{16,12},{20,16},{24,20},{28,24},{1,29},{... | collective-permute-start | bytes 442376 | tf_op jit(solution)/shard_map/ppermute | solution.py:625
  18.3 0.0 collective-permute-start
  18.3 0.0 copy-done
  18.3 0.7 %tracer_sum.1.sums = bf16[2,576,256]{2,1,0:T(8,128)(2,1)S(1)} custom-call(f32[72,8,16,128]{3,2,1,0:T(8,128)S(1)} %copy-done), custom_call_target="tpu_custom_call" | custom-call | flops 1179648 | bytes 4718592 | tf_op jit(solution)/shard_map/tracer_sum/pallas_call | solution.py:701
  19.1 1.9 %all-to-all-done = f32[608,1,128]{2,1,0:T(1,128)S(1)} async-done(((f32[608,1,128]{2,1,0:T(1,128)}), f32[608,1,128]{2,1,0:T(1,128)S(1)}, u32[]{:S(2)}, u32[]{:S(2)}) %all-to-all-start) | async-done | bytes 311328 | tf_op jit(solution)/shard_map/all_to_all | solution.py:683
  21.0 2.7 %soundings.1 = (f32[1168,128]{1,0:T(8,128)S(1)}, f32[2,16,128]{2,1,0:T(8,128)S(1)}, f32[72,128]{1,0:T(8,128)S(1)}, f32[72,128]{1,0:T(8,128)S(1)}, f32[32,128]{1,0:T(8,128)}) custom-call(f32[608,128]{1,0:T(8,128)S(1)} %bitcast.19, bf16[2,576,256]{2,1,0:T(8,128)(2,1)S(1)} %tracer_sum.1.sums), custom_call_target="tpu_custom_call" | custom-call | flops 37748736 | bytes 4718592 | tf_op jit(solution)/shard_map/soundings/pallas_call | solution.py:710
  23.8 2.0 %collective-permute-start.6 = (f32[72,128]{1,0:T(8,128)S(1)}, f32[72,128]{1,0:T(8,128)S(1)}, u32[]{:S(2)}, u32[]{:S(2)}) collective-permute-start(f32[72,128]{1,0:T(8,128)S(1)} %get-tuple-element.28), channel_id=1, source_target_pairs={{0,3},{1,0},{2,1},{3,2},{4,7},{5,4},{6,5},{7,6},{8,11},{9,8},{10,9... | collective-permute-start | bytes 110600 | tf_op jit(solution)/shard_map/ppermute | solution.py:625
  25.8 0.0 collective-permute-done.1.east0
  25.8 0.1 collective-permute-start.7
  25.9 0.0 collective-permute-done.west0
  25.9 2.5 %collective-permute-start.5 = (f32[2,16,128]{2,1,0:T(8,128)S(1)}, f32[2,16,128]{2,1,0:T(8,128)S(1)}, u32[]{:S(2)}, u32[]{:S(2)}) collective-permute-start(f32[2,16,128]{2,1,0:T(8,128)S(1)} %get-tuple-element.27), channel_id=1, source_target_pairs={{0,28},{4,0},{8,4},{12,8},{16,12},{20,16},{24,20},{28,24},{1,29},{... | collective-permute-start | bytes 49160 | tf_op jit(solution)/shard_map/ppermute | solution.py:625
  28.4 0.0 collective-permute-done.2.a0
  28.4 0.0 collective-permute-start.4
  28.5 0.0 collective-permute-done.3.b0
  28.5 2.5 %coefficients.1 = (f32[7,1152,128]{2,1,0:T(8,128)S(1)}, f32[2,128,128]{2,1,0:T(8,128)S(1)}, f32[2,576,128]{2,1,0:T(8,128)S(1)}) custom-call(f32[1152,128]{1,0:T(8,128)} %bitcast.25, f32[1152,128]{1,0:T(8,128)} %bitcast.27, f32[1152,128]{1,0:T(8,128)} %bitcast.28, f32[2,144,128]{2,1,0:T(8,128)S(1)} %collective-permute-done.west0, ...), custom_call_target="tpu_custom_call" | custom-call | flops 4718592 | bytes 4718592 | tf_op jit(solution)/shard_map/coefficients/pallas_call | solution.py:729
  31.0 0.0 collective-permute-done.5.refs_6_
  31.0 1.5 %collective-permute-done.4.refs_5_ = f32[2,16,128]{2,1,0:T(8,128)S(1)} collective-permute-done((f32[2,16,128]{2,1,0:T(8,128)S(1)}, f32[2,16,128]{2,1,0:T(8,128)S(1)}, u32[]{:S(2)}, u32[]{:S(2)}) %collective-permute-start.4) | collective-permute-done | bytes 16416 | tf_op jit(solution)/shard_map/ppermute | solution.py:625
  32.5 0.0 collective-permute-done.6.refs_7_
  32.5 0.0 collective-permute-done.7.refs_8_
  32.5 9.0 %step.2 = (f32[576,16,128]{2,1,0:T(8,128)}, f32[7,1152,128]{2,1,0:T(8,128)}, f32[2,128,128]{2,1,0:T(8,128)S(1)}, f32[576,128]{1,0:T(8,128)S(1)}, f32[576,128]{1,0:T(8,128)S(1)}) custom-call(f32[576,16,128]{2,1,0:T(8,128)} %bitcast.22, f32[7,1152,128]{2,1,0:T(8,128)S(1)} %get-tuple-element.23.refs_1_, f32[2,128,128]{2,1,0:T(8,128)S(1)} %get-tuple-element.24.refs_2_, ...), custom_call_target="tpu_custom_call" | custom-call | flops 37748736 | bytes 9437184 | tf_op jit(solution)/shard_map/step/pallas_call | solution.py:739
  41.6 1.6 %collective-permute-start.10 = (f32[576,128]{1,0:T(8,128)S(1)}, f32[576,128]{1,0:T(8,128)S(1)}, u32[]{:S(2)}, u32[]{:S(2)}) collective-permute-start(f32[576,128]{1,0:T(8,128)S(1)} %get-tuple-element.33), channel_id=1, source_target_pairs={{0,1},{1,0},{2,3},{3,2},{4,5},{5,4},{6,7},{7,6},{8,9},{9,8},{10,11... | collective-permute-start | bytes 884744 | tf_op jit(solution)/shard_map/ppermute | solution.py:638
  43.1 0.7 %collective-permute-start.11 = (f32[576,128]{1,0:T(8,128)S(1)}, f32[576,128]{1,0:T(8,128)S(1)}, u32[]{:S(2)}, u32[]{:S(2)}) collective-permute-start(f32[576,128]{1,0:T(8,128)S(1)} %get-tuple-element.34), channel_id=1, source_target_pairs={{0,0},{1,2},{2,1},{3,3},{4,4},{5,6},{6,5},{7,7},{8,8},{9,10},{10,9... | collective-permute-start | bytes 884744 | tf_op jit(solution)/shard_map/ppermute | solution.py:639
  43.8 0.9 %collective-permute-start.9 = (f32[2,128,128]{2,1,0:T(8,128)S(1)}, f32[2,128,128]{2,1,0:T(8,128)S(1)}, u32[]{:S(2)}, u32[]{:S(2)}) collective-permute-start(f32[2,128,128]{2,1,0:T(8,128)S(1)} %get-tuple-element.32), channel_id=1, source_target_pairs={{0,28},{4,0},{8,4},{12,8},{16,12},{20,16},{24,20},{28,24},{1,29},{... | collective-permute-start | bytes 393224 | tf_op jit(solution)/shard_map/ppermute | solution.py:625
  44.7 0.0 collective-permute-start.8
  44.7 5.4 %all-to-all-start.1 = ((f32[32,1,128]{2,1,0:T(1,128)}), f32[32,1,128]{2,1,0:T(1,128)S(1)}, u32[]{:S(2)}, u32[]{:S(2)}) async-start(f32[32,1,128]{2,1,0:T(1,128)} %bitcast.13), calls=%async_computation.1 | async-start | bytes 32768 | tf_op jit(solution)/shard_map/all_to_all | solution.py:759
  50.1 0.0 collective-permute-done.9.refs_3_
  50.1 0.0 collective-permute-done.8.refs_2_
  50.1 0.0 collective-permute-done.10.refs_4_
  50.1 0.0 collective-permute-done.11.refs_5_
  50.2 8.3 %step.3 = f32[576,16,128]{2,1,0:T(8,128)} custom-call(f32[576,16,128]{2,1,0:T(8,128)} %get-tuple-element.30.refs_0_, f32[7,1152,128]{2,1,0:T(8,128)} %get-tuple-element.31.refs_1_, f32[2,128,128]{2,1,0:T(8,128)S(1)} %collective-permute-done.8.refs_2_, f32[2,128,128]{2,1,0:T(8,128)S(1)} %collective-permute-done.9.refs_3_, ...), custom_call_target="tpu_custom_call" | custom-call | flops 37748736 | bytes 9437184 | tf_op jit(solution)/shard_map/step/pallas_call | solution.py:739
  58.5 0.0 all-to-all-done.1
  58.5 0.7 %residual.1 = f32[8,128]{1,0:T(8,128)} custom-call(f32[32,128]{1,0:T(8,128)S(1)} %bitcast.20), custom_call_target="tpu_custom_call" | custom-call | flops 10 | bytes 10000 | tf_op jit(solution)/shard_map/residual/pallas_call | solution.py:763
Async XLA Ops:
  2.8 18.2 %all-to-all-start = ((f32[608,1,128]{2,1,0:T(1,128)}), f32[608,1,128]{2,1,0:T(1,128)S(1)}, u32[]{:S(2)}, u32[]{:S(2)}) async-start(f32[608,1,128]{2,1,0:T(1,128)} %bitcast.10), calls=%async_computation | async-start | bytes 622592 | tf_op jit(solution)/shard_map/all_to_all | solution.py:683
  10.1 8.2 %copy-start = (f32[72,8,16,128]{3,2,1,0:T(8,128)S(1)}, f32[72,8,16,128]{3,2,1,0:T(8,128)}, u32[]{:S(2)}) copy-start(f32[72,8,16,128]{3,2,1,0:T(8,128)} %concentration.1) | copy-start | bytes 14155780
  13.9 14.5 %collective-permute-start.2 = (f32[648,128]{1,0:T(8,128)S(1)}, f32[648,128]{1,0:T(8,128)S(1)}, u32[]{:S(2)}, u32[]{:S(2)}) collective-permute-start(f32[648,128]{1,0:T(8,128)S(1)} %get-tuple-element.21), channel_id=1, source_target_pairs={{0,1},{1,0},{2,3},{3,2},{4,5},{5,4},{6,7},{7,6},{8,9},{9,8},{10,11... | collective-permute-start | bytes 995336 | tf_op jit(solution)/shard_map/ppermute | solution.py:638
  15.8 12.7 %collective-permute-start.3 = (f32[648,128]{1,0:T(8,128)S(1)}, f32[648,128]{1,0:T(8,128)S(1)}, u32[]{:S(2)}, u32[]{:S(2)}) collective-permute-start(f32[648,128]{1,0:T(8,128)S(1)} %get-tuple-element.22), channel_id=1, source_target_pairs={{0,0},{1,2},{2,1},{3,3},{4,4},{5,6},{6,5},{7,7},{8,8},{9,10},{10,9... | collective-permute-start | bytes 995336 | tf_op jit(solution)/shard_map/ppermute | solution.py:639
  16.4 9.3 %collective-permute-start.1 = (f32[2,144,128]{2,1,0:T(8,128)S(1)}, f32[2,144,128]{2,1,0:T(8,128)S(1)}, u32[]{:S(2)}, u32[]{:S(2)}) collective-permute-start(f32[2,144,128]{2,1,0:T(8,128)S(1)} %get-tuple-element.20), channel_id=1, source_target_pairs={{0,28},{4,0},{8,4},{12,8},{16,12},{20,16},{24,20},{28,24},{1,29},{... | collective-permute-start | bytes 442376 | tf_op jit(solution)/shard_map/ppermute | solution.py:625
  18.3 7.6 %collective-permute-start = (f32[2,144,128]{2,1,0:T(8,128)S(1)}, f32[2,144,128]{2,1,0:T(8,128)S(1)}, u32[]{:S(2)}, u32[]{:S(2)}) collective-permute-start(f32[2,144,128]{2,1,0:T(8,128)S(1)} %get-tuple-element.20), channel_id=1, source_target_pairs={{0,4},{4,8},{8,12},{12,16},{16,20},{20,24},{24,28},{28,0},{1,5},{5... | collective-permute-start | bytes 442376 | tf_op jit(solution)/shard_map/ppermute | solution.py:625
  23.8 8.8 %collective-permute-start.6 = (f32[72,128]{1,0:T(8,128)S(1)}, f32[72,128]{1,0:T(8,128)S(1)}, u32[]{:S(2)}, u32[]{:S(2)}) collective-permute-start(f32[72,128]{1,0:T(8,128)S(1)} %get-tuple-element.28), channel_id=1, source_target_pairs={{0,3},{1,0},{2,1},{3,2},{4,7},{5,4},{6,5},{7,6},{8,11},{9,8},{10,9... | collective-permute-start | bytes 110600 | tf_op jit(solution)/shard_map/ppermute | solution.py:625
  25.8 6.7 %collective-permute-start.7 = (f32[72,128]{1,0:T(8,128)S(1)}, f32[72,128]{1,0:T(8,128)S(1)}, u32[]{:S(2)}, u32[]{:S(2)}) collective-permute-start(f32[72,128]{1,0:T(8,128)S(1)} %get-tuple-element.29), channel_id=1, source_target_pairs={{0,1},{1,2},{2,3},{3,0},{4,5},{5,6},{6,7},{7,4},{8,9},{9,10},{10,1... | collective-permute-start | bytes 110600 | tf_op jit(solution)/shard_map/ppermute | solution.py:625
  25.9 5.1 %collective-permute-start.5 = (f32[2,16,128]{2,1,0:T(8,128)S(1)}, f32[2,16,128]{2,1,0:T(8,128)S(1)}, u32[]{:S(2)}, u32[]{:S(2)}) collective-permute-start(f32[2,16,128]{2,1,0:T(8,128)S(1)} %get-tuple-element.27), channel_id=1, source_target_pairs={{0,28},{4,0},{8,4},{12,8},{16,12},{20,16},{24,20},{28,24},{1,29},{... | collective-permute-start | bytes 49160 | tf_op jit(solution)/shard_map/ppermute | solution.py:625
  28.4 4.1 %collective-permute-start.4 = (f32[2,16,128]{2,1,0:T(8,128)S(1)}, f32[2,16,128]{2,1,0:T(8,128)S(1)}, u32[]{:S(2)}, u32[]{:S(2)}) collective-permute-start(f32[2,16,128]{2,1,0:T(8,128)S(1)} %get-tuple-element.27), channel_id=1, source_target_pairs={{0,4},{4,8},{8,12},{12,16},{16,20},{20,24},{24,28},{28,0},{1,5},{5... | collective-permute-start | bytes 49160 | tf_op jit(solution)/shard_map/ppermute | solution.py:625
  41.6 8.6 %collective-permute-start.10 = (f32[576,128]{1,0:T(8,128)S(1)}, f32[576,128]{1,0:T(8,128)S(1)}, u32[]{:S(2)}, u32[]{:S(2)}) collective-permute-start(f32[576,128]{1,0:T(8,128)S(1)} %get-tuple-element.33), channel_id=1, source_target_pairs={{0,1},{1,0},{2,3},{3,2},{4,5},{5,4},{6,7},{7,6},{8,9},{9,8},{10,11... | collective-permute-start | bytes 884744 | tf_op jit(solution)/shard_map/ppermute | solution.py:638
  43.1 7.0 %collective-permute-start.11 = (f32[576,128]{1,0:T(8,128)S(1)}, f32[576,128]{1,0:T(8,128)S(1)}, u32[]{:S(2)}, u32[]{:S(2)}) collective-permute-start(f32[576,128]{1,0:T(8,128)S(1)} %get-tuple-element.34), channel_id=1, source_target_pairs={{0,0},{1,2},{2,1},{3,3},{4,4},{5,6},{6,5},{7,7},{8,8},{9,10},{10,9... | collective-permute-start | bytes 884744 | tf_op jit(solution)/shard_map/ppermute | solution.py:639
  43.8 6.3 %collective-permute-start.9 = (f32[2,128,128]{2,1,0:T(8,128)S(1)}, f32[2,128,128]{2,1,0:T(8,128)S(1)}, u32[]{:S(2)}, u32[]{:S(2)}) collective-permute-start(f32[2,128,128]{2,1,0:T(8,128)S(1)} %get-tuple-element.32), channel_id=1, source_target_pairs={{0,28},{4,0},{8,4},{12,8},{16,12},{20,16},{24,20},{28,24},{1,29},{... | collective-permute-start | bytes 393224 | tf_op jit(solution)/shard_map/ppermute | solution.py:625
  44.7 5.4 %collective-permute-start.8 = (f32[2,128,128]{2,1,0:T(8,128)S(1)}, f32[2,128,128]{2,1,0:T(8,128)S(1)}, u32[]{:S(2)}, u32[]{:S(2)}) collective-permute-start(f32[2,128,128]{2,1,0:T(8,128)S(1)} %get-tuple-element.32), channel_id=1, source_target_pairs={{0,4},{4,8},{8,12},{12,16},{16,20},{20,24},{24,28},{28,0},{1,5},{5... | collective-permute-start | bytes 393224 | tf_op jit(solution)/shard_map/ppermute | solution.py:625
  44.7 13.7 %all-to-all-start.1 = ((f32[32,1,128]{2,1,0:T(1,128)}), f32[32,1,128]{2,1,0:T(1,128)S(1)}, u32[]{:S(2)}, u32[]{:S(2)}) async-start(f32[32,1,128]{2,1,0:T(1,128)} %bitcast.13), calls=%async_computation.1 | async-start | bytes 32768 | tf_op jit(solution)/shard_map/all_to_all | solution.py:759
